TPU v7x, 32 devices: a whole 2x2x4 slice. The times are simulated.
32 devices in a mesh: rows: 16 (over z, y, core), seq: 2 (over x).
Axes of the slice: x: 2, y: 2, z: 4, core: 2. Of those that a mesh axis runs over, the one named last changes fastest.
Arguments:
- enc_ids: int32 [16, 1024], P('rows', 'seq'), may hold values from 0 to 32127
- enc_segs: int32 [16, 1024], P('rows'), may hold values from 0 to 3, as said below
- sentinel: int32 [16, 1024], P('rows', 'seq'), may hold values 0 or 1
- mode: int32 [16, 4], P('rows'), may hold values from 0 to 2
- dec_ids: int32 [16, 512], P('rows', 'seq'), may hold values from 0 to 32127
- dec_segs: int32 [16, 512], P('rows'), may hold values from 0 to 3
- target_ids: int32 [16, 512], P('rows', 'seq'), may hold values from 0 to 32127
- target_mask: int32 [16, 512], P('rows', 'seq'), may hold values 0 or 1
- buckets: int32 [2, 2048], replicated, may hold values from 0 to 31
- embed: float32 [32128, 768], P(('rows', 'seq')), may hold values from -9 to 9
- attn_in: float32 [3, 768, 2304], P(None, ('rows', 'seq')), may hold values from -0.21875 to 0.21875
- attn_out: float32 [3, 768, 768], P(None, ('rows', 'seq')), may hold values from -0.875 to 0.875
- ffn_in: float32 [2, 768, 4096], P(None, ('rows', 'seq')), may hold values from -0.21875 to 0.21875
- ffn_out: float32 [2, 2048, 768], P(None, ('rows', 'seq')), may hold values from -0.25 to 0.25
- rel_table: float32 [2, 384], P(None, ('rows', 'seq')), may hold values from -6 to 6
- gains: float32 [7, 768], P(None, ('rows', 'seq')), may hold values from 0.5 to 1.5
- m_embed: float32 [32128, 768], P(('rows', 'seq')), may hold values from -2.3841858e-06 to 2.3841858e-06
- v_embed: float32 [32128, 768], P(('rows', 'seq')), may hold values from 2.4274484e-15 to 9.709794e-15
- m_attn_in: float32 [3, 768, 2304], P(None, ('rows', 'seq')), may hold values from -2.3841858e-06 to 2.3841858e-06
- v_attn_in: float32 [3, 768, 2304], P(None, ('rows', 'seq')), may hold values from 2.4274484e-15 to 9.709794e-15
- m_attn_out: float32 [3, 768, 768], P(None, ('rows', 'seq')), may hold values from -2.3841858e-06 to 2.3841858e-06
- v_attn_out: float32 [3, 768, 768], P(None, ('rows', 'seq')), may hold values from 2.4274484e-15 to 9.709794e-15
- m_ffn_in: float32 [2, 768, 4096], P(None, ('rows', 'seq')), may hold values from -2.3841858e-06 to 2.3841858e-06
- v_ffn_in: float32 [2, 768, 4096], P(None, ('rows', 'seq')), may hold values from 2.4274484e-15 to 9.709794e-15
- m_ffn_out: float32 [2, 2048, 768], P(None, ('rows', 'seq')), may hold values from -2.3841858e-06 to 2.3841858e-06
- v_ffn_out: float32 [2, 2048, 768], P(None, ('rows', 'seq')), may hold values from 2.4274484e-15 to 9.709794e-15
- m_rel: float32 [2, 384], P(None, ('rows', 'seq')), may hold values from -9.536743e-06 to 9.536743e-06
- v_rel: float32 [2, 384], P(None, ('rows', 'seq')), may hold values from 3.8839175e-14 to 1.553567e-13
- m_gains: float32 [7, 768], P(None, ('rows', 'seq')), may hold values from -9.536743e-06 to 9.536743e-06
- v_gains: float32 [7, 768], P(None, ('rows', 'seq')), may hold values from 3.8839175e-14 to 1.553567e-13
Outputs:
- loss: float32 [], replicated
- grad_norm: float32 [], replicated
- clipped_embed_grad: float32 [32128, 768], P(('rows', 'seq'))
- new_v_embed: float32 [32128, 768], P(('rows', 'seq'))
- new_embed: float32 [32128, 768], P(('rows', 'seq'))
- new_m_attn_in: float32 [3, 768, 2304], P(None, ('rows', 'seq'))
- new_v_attn_in: float32 [3, 768, 2304], P(None, ('rows', 'seq'))
- new_attn_in: float32 [3, 768, 2304], P(None, ('rows', 'seq'))
- new_m_attn_out: float32 [3, 768, 768], P(None, ('rows', 'seq'))
- new_v_attn_out: float32 [3, 768, 768], P(None, ('rows', 'seq'))
- new_attn_out: float32 [3, 768, 768], P(None, ('rows', 'seq'))
- new_m_ffn_in: float32 [2, 768, 4096], P(None, ('rows', 'seq'))
- new_v_ffn_in: float32 [2, 768, 4096], P(None, ('rows', 'seq'))
- new_ffn_in: float32 [2, 768, 4096], P(None, ('rows', 'seq'))
- new_m_ffn_out: float32 [2, 2048, 768], P(None, ('rows', 'seq'))
- new_v_ffn_out: float32 [2, 2048, 768], P(None, ('rows', 'seq'))
- new_ffn_out: float32 [2, 2048, 768], P(None, ('rows', 'seq'))
- new_m_rel: float32 [2, 384], P(None, ('rows', 'seq'))
- new_v_rel: float32 [2, 384], P(None, ('rows', 'seq'))
- new_rel_table: float32 [2, 384], P(None, ('rows', 'seq'))
- new_m_gains: float32 [7, 768], P(None, ('rows', 'seq'))
- new_v_gains: float32 [7, 768], P(None, ('rows', 'seq'))
- new_gains: float32 [7, 768], P(None, ('rows', 'seq'))
Inputs may be any that keep to these rules, and one draw needn't show every extreme that they name: Every row holds all 4 examples in enc_segs and in dec_segs, numbered alike and never falling along the row; decoder example s reads encoder example s.
All inputs are finite; a program needn't handle non-finite values. No bound on the sum of `sentinel` or of `target_mask` on one device may be relied on, other than what follows from the above.
Results may differ from a plain program's by a relative error of at most 0.012.
The roundings to bfloat16 on the way count: a program that leaves them out, or rounds other values in their place, can miss the bound.
Values may be sent and summed in bfloat16 or wider, within the bound.
A program may use at most 448 MiB of HBM per device.

v0:
```python
import jax
import jax.numpy as jnp
from jax import lax
from jax.sharding import PartitionSpec as P

D = 768
HEADS = 12
HEAD_DIM = 64
FF = 2048
V = 32128
BUCKETS = 32
STEP = 10


masked_out = -1e30
clip_limit = 0.01


def rms_scale(values, gain):
    return values * lax.rsqrt(jnp.mean(values * values, axis=-1, keepdims=True) + 1e-06) * gain


def norm_pull(values, gain, factor, upstream):
    _, pull = jax.vjp(lambda left, right: rms_scale(left, right) * factor, values, gain)
    return pull(upstream)


def gate_up(both):
    return jax.nn.gelu(both[:, :FF], approximate=True) * both[:, FF:]


def project(left, right):
    return jnp.dot(left, right, preferred_element_type=jnp.float32)


def weight_grad(inputs, grads):
    return jnp.einsum("td,te->de", inputs, grads, preferred_element_type=jnp.float32)


def input_grad(grads, weight):
    return jnp.einsum("te,de->td", grads, weight, preferred_element_type=jnp.float32)


def offset_window(lookup_matrix, bucket_row, q_start, k_start, q_len, k_len):
    width = q_len + k_len - 1
    offset = bucket_row.shape[0] // 2
    window = lax.dynamic_slice_in_dim(bucket_row, k_start - q_start + offset - (q_len - 1), width)
    picks = (window[:, None] == jnp.arange(BUCKETS, dtype=jnp.int32)[None]).astype(jnp.float32)
    per_offset = jnp.einsum("nb,bh->hn", picks, lookup_matrix.astype(jnp.float32))
    return (per_offset, picks)


def diagonal_spread(per_offset, q_len, k_len):
    width = per_offset.shape[1]
    rolled = jnp.roll(per_offset, -(q_len - 1), axis=1)
    flat = jnp.tile(rolled, (1, q_len))[:, : q_len * (width - 1)]
    return flat.reshape(per_offset.shape[0], q_len, width - 1)[:, :, :k_len]


def diagonal_collect(grid, width):
    heads, q_len, k_len = grid.shape
    padded = jnp.pad(grid, ((0, 0), (0, 0), (0, width - 1 - k_len)))
    flat = jnp.pad(padded.reshape(heads, q_len * (width - 1)), ((0, 0), (0, q_len)))
    summed = jnp.sum(flat.reshape(heads, q_len, width), axis=1)
    return jnp.roll(summed, q_len - 1, axis=1)


def block_scores(query3, keys3, q_pos, k_pos, q_seg, k_seg, causal, lookup_matrix, bucket_row):
    scores = jnp.einsum(
        "qhd,khd->hqk", query3, keys3, preferred_element_type=jnp.float32
    ) * HEAD_DIM ** (-0.5)
    picks = None
    if lookup_matrix is not None:
        per_offset, picks = offset_window(
            lookup_matrix, bucket_row, q_pos[0], k_pos[0], q_pos.shape[0], k_pos.shape[0]
        )
        scores = scores + diagonal_spread(per_offset, q_pos.shape[0], k_pos.shape[0])
    allowed = q_seg[:, None] == k_seg[None, :]
    if causal:
        allowed = allowed & (k_pos[None, :] <= q_pos[:, None])
    return (jnp.where(allowed[None], scores, masked_out), picks)


def key_blocks(keyval_b, k_pos, k_seg):
    total = keyval_b.shape[0]
    block = min(256, total)
    number = total // block
    keys = keyval_b[:, :D].reshape(number, block, HEADS, HEAD_DIM)
    values = keyval_b[:, D:].reshape(number, block, HEADS, HEAD_DIM)
    return (keys, values, k_pos.reshape(number, block), k_seg.reshape(number, block))


def attend_forward(
    query_b, keyval_b, q_pos, k_pos, q_seg, k_seg, causal, lookup_matrix, bucket_row
):
    length = query_b.shape[0]
    query3 = query_b.reshape(length, HEADS, HEAD_DIM)
    blocks = key_blocks(keyval_b, k_pos, k_seg)

    def scores_of(item):
        return block_scores(
            query3, item[0], q_pos, item[2], q_seg, item[3], causal, lookup_matrix, bucket_row
        )[0]

    def first_pass(carry, item):
        top, total = carry
        scores = scores_of(item)
        new_top = jnp.maximum(top, jnp.max(scores, axis=-1))
        total = total * jnp.exp(top - new_top) + jnp.sum(
            jnp.exp(scores - new_top[..., None]), axis=-1
        )
        return ((new_top, total), None)

    start = (
        jnp.full((HEADS, length), masked_out, jnp.float32),
        jnp.zeros((HEADS, length), jnp.float32),
    )
    (top, total), _ = lax.scan(first_pass, start, blocks)
    lse = top + jnp.log(total)

    def second_pass(carry, item):
        probs = jnp.exp(scores_of(item) - lse[..., None]).astype(jnp.bfloat16)
        return (
            carry + jnp.einsum("hqk,khd->qhd", probs, item[1], preferred_element_type=jnp.float32),
            None,
        )

    out, _ = lax.scan(second_pass, jnp.zeros((length, HEADS, HEAD_DIM), jnp.float32), blocks)
    return (out.reshape(length, D), lse)


def attend_backward(
    grad_b, query_b, keyval_b, lse, q_pos, k_pos, q_seg, k_seg, causal, lookup_matrix, bucket_row
):
    length = query_b.shape[0]
    query3 = query_b.reshape(length, HEADS, HEAD_DIM)
    grad3 = grad_b.reshape(length, HEADS, HEAD_DIM)
    blocks = key_blocks(keyval_b, k_pos, k_seg)

    def pieces(item):
        scores, picks = block_scores(
            query3, item[0], q_pos, item[2], q_seg, item[3], causal, lookup_matrix, bucket_row
        )
        probs = jnp.exp(scores - lse[..., None])
        d_probs = jnp.einsum("qhd,khd->hqk", grad3, item[1], preferred_element_type=jnp.float32)
        return (probs, d_probs, picks)

    def delta_pass(carry, item):
        probs, d_probs, _ = pieces(item)
        return (carry + jnp.sum(probs * d_probs, axis=-1), None)

    delta, _ = lax.scan(delta_pass, jnp.zeros((HEADS, length), jnp.float32), blocks)

    def grad_pass(carry, item):
        d_query, d_table = carry
        probs, d_probs, picks = pieces(item)
        score_gradient = (probs * (d_probs - delta[..., None])).astype(jnp.bfloat16)
        d_query = d_query + jnp.einsum(
            "hqk,khd->qhd", score_gradient, item[0], preferred_element_type=jnp.float32
        )
        d_keys = jnp.einsum(
            "hqk,qhd->khd", score_gradient, query3, preferred_element_type=jnp.float32
        ) * HEAD_DIM ** (-0.5)
        d_values = jnp.einsum(
            "hqk,qhd->khd", probs.astype(jnp.bfloat16), grad3, preferred_element_type=jnp.float32
        )
        if picks is not None:
            d_offset = diagonal_collect(score_gradient.astype(jnp.float32), picks.shape[0])
            d_table = d_table + jnp.einsum("nb,hn->bh", picks, d_offset)
        joined = jnp.concatenate([d_keys.reshape(-1, D), d_values.reshape(-1, D)], axis=1)
        return ((d_query, d_table), joined)

    start = (
        jnp.zeros((length, HEADS, HEAD_DIM), jnp.float32),
        jnp.zeros((BUCKETS, HEADS), jnp.float32),
    )
    (d_query, d_table), d_keyval = lax.scan(grad_pass, start, blocks)
    return (d_query.reshape(length, D) * HEAD_DIM ** (-0.5), d_keyval.reshape(-1, 2 * D), d_table)


def ffn_forward(resid, gain, w_in, w_out):
    normed = rms_scale(resid, gain).astype(jnp.bfloat16)
    both = project(normed, w_in)
    hidden = gate_up(both).astype(jnp.bfloat16)
    return (resid + project(hidden, w_out), (normed, both, hidden))


def ffn_backward(upstream, resid, gain, w_in, w_out, saved):
    normed, both, hidden = saved
    grad_b = upstream.astype(jnp.bfloat16)
    d_out = weight_grad(hidden, grad_b)
    _, pull = jax.vjp(gate_up, both)
    (d_both,) = pull(input_grad(grad_b, w_out))
    d_both_b = d_both.astype(jnp.bfloat16)
    d_in = weight_grad(normed, d_both_b)
    d_resid, d_gain = norm_pull(resid, gain, 1.0, input_grad(d_both_b, w_in))
    return (upstream + d_resid, d_gain, d_in, d_out)


def branch_backward(upstream, out_b, w_out):
    grad_b = upstream.astype(jnp.bfloat16)
    return (weight_grad(out_b, grad_b), input_grad(grad_b, w_out).astype(jnp.bfloat16))


def head_stats(hidden_b, targets):

    def fold(carry, piece, start):
        top, total, picked = carry
        logits = jnp.einsum("td,vd->tv", hidden_b, piece, preferred_element_type=jnp.float32)
        columns = jnp.arange(piece.shape[0], dtype=jnp.int32)
        new_top = jnp.maximum(top, jnp.max(logits, axis=1))
        total = jnp.sum(jnp.exp(logits - new_top[:, None]), axis=1)
        picked = jnp.sum(jnp.where(columns[None] == targets[:, None], logits, 0.0), axis=1)
        return (new_top, total, picked)

    return fold


def head_gradient_list(hidden_b, targets, weight, lse, piece):
    logits = jnp.einsum("td,vd->tv", hidden_b, piece, preferred_element_type=jnp.float32)
    columns = jnp.arange(piece.shape[0], dtype=jnp.int32)
    hits = (columns[None] == targets[:, None]).astype(jnp.float32)
    grad_b = ((jnp.exp(logits - lse[:, None]) - hits) * weight[:, None]).astype(jnp.bfloat16)
    d_hidden = project(grad_b, piece)
    return (d_hidden, grad_b)


def adamw(weight, grad, first_m, second_m, count, rate, decay):
    first_new = 0.9 * first_m + 0.1 * grad
    second_new = 0.999 * second_m + 0.001 * grad * grad
    first_hat = first_new / (1.0 - 0.9**count)
    second_hat = second_new / (1.0 - 0.999**count)
    return (
        first_new,
        second_new,
        weight - rate * (first_hat / (jnp.sqrt(second_hat) + 1e-08) + decay * weight),
    )


def body(
    enc_ids,
    enc_segs,
    sentinel,
    mode,
    dec_ids,
    dec_segs,
    target_ids,
    target_mask,
    buckets,
    embed,
    attn_in,
    attn_out,
    ffn_in,
    ffn_out,
    rel_table,
    gains,
    m_embed,
    v_embed,
    m_attn_in,
    v_attn_in,
    m_attn_out,
    v_attn_out,
    m_ffn_in,
    v_ffn_in,
    m_ffn_out,
    v_ffn_out,
    m_rel,
    v_rel,
    m_gains,
    v_gains,
):
    enc_count = enc_ids.shape[1]
    dec_count = dec_ids.shape[1]
    seq_index = lax.axis_index("seq")
    enc_all = jnp.arange(enc_segs.shape[1], dtype=jnp.int32)
    dec_all = jnp.arange(dec_segs.shape[1], dtype=jnp.int32)
    enc_pos = seq_index * enc_count + jnp.arange(enc_count, dtype=jnp.int32)
    dec_pos = seq_index * dec_count + jnp.arange(dec_count, dtype=jnp.int32)
    enc_seg_all = enc_segs[0]
    dec_seg_all = dec_segs[0]
    enc_seg = lax.dynamic_slice_in_dim(enc_seg_all, seq_index * enc_count, enc_count)
    dec_seg = lax.dynamic_slice_in_dim(dec_seg_all, seq_index * dec_count, dec_count)
    prior_all = jnp.concatenate([enc_seg_all[:1], enc_seg_all[:-1]])
    prior = lax.dynamic_slice_in_dim(prior_all, seq_index * enc_count, enc_count)
    first = (enc_pos == 0) | (enc_seg != prior)
    mode_of = jnp.sum(
        jnp.where(
            enc_seg[:, None] == jnp.arange(mode.shape[1], dtype=jnp.int32)[None], mode[0][None], 0
        ),
        axis=1,
    )
    enc_tok = jnp.where(sentinel[0] == 1, V - 1 - enc_seg, enc_ids[0])
    enc_tok = jnp.where(first, V - 101 - mode_of, enc_tok)
    all_ids = jnp.concatenate([enc_tok, dec_ids[0]])
    enc_wi, enc_wo, enc_fi, enc_fo, enc_rel, enc_gain = (
        lax.all_gather(attn_in[0:1].astype(jnp.bfloat16), ("rows", "seq"), axis=1, tiled=True),
        lax.all_gather(attn_out[0:1].astype(jnp.bfloat16), ("rows", "seq"), axis=1, tiled=True),
        lax.all_gather(ffn_in[0:1].astype(jnp.bfloat16), ("rows", "seq"), axis=1, tiled=True),
        lax.all_gather(ffn_out[0:1].astype(jnp.bfloat16), ("rows", "seq"), axis=1, tiled=True),
        lax.all_gather(rel_table[0:1].astype(jnp.bfloat16), ("rows", "seq"), axis=1, tiled=True),
        lax.all_gather(gains[0:3].astype(jnp.bfloat16), ("rows", "seq"), axis=1, tiled=True),
    )
    dec_wi, dec_wo, dec_fi, dec_fo, dec_rel, dec_gain = (
        lax.all_gather(attn_in[1:3].astype(jnp.bfloat16), ("rows", "seq"), axis=1, tiled=True),
        lax.all_gather(attn_out[1:3].astype(jnp.bfloat16), ("rows", "seq"), axis=1, tiled=True),
        lax.all_gather(ffn_in[1:2].astype(jnp.bfloat16), ("rows", "seq"), axis=1, tiled=True),
        lax.all_gather(ffn_out[1:2].astype(jnp.bfloat16), ("rows", "seq"), axis=1, tiled=True),
        lax.all_gather(rel_table[1:2].astype(jnp.bfloat16), ("rows", "seq"), axis=1, tiled=True),
        lax.all_gather(gains[3:7].astype(jnp.bfloat16), ("rows", "seq"), axis=1, tiled=True),
    )
    enc_gain = enc_gain.astype(jnp.float32)
    dec_gain = dec_gain.astype(jnp.float32)
    enc_table = enc_rel[0].reshape(BUCKETS, HEADS)
    dec_table = dec_rel[0].reshape(BUCKETS, HEADS)
    cross_wi = dec_wi[1]
    piece = lax.all_gather(embed.astype(jnp.bfloat16), ("rows", "seq"), axis=0, tiled=True)
    local = all_ids
    inside = (local >= 0) & (local < piece.shape[0])
    rows_got = jnp.take(piece, jnp.clip(local, 0, piece.shape[0] - 1), axis=0).astype(jnp.float32)
    looked = jnp.where(inside[:, None], rows_got, 0.0)
    enc_x0 = looked[:enc_count]
    dec_y0 = looked[enc_count:]
    enc_n1 = rms_scale(enc_x0, enc_gain[0]).astype(jnp.bfloat16)
    enc_qkv = project(enc_n1, enc_wi[0]).astype(jnp.bfloat16)
    dec_n1 = rms_scale(dec_y0, dec_gain[0]).astype(jnp.bfloat16)
    dec_qkv = project(dec_n1, dec_wi[0]).astype(jnp.bfloat16)
    encoder_key_value, dec_kv = (
        lax.all_gather(enc_qkv[:, D:], "seq", axis=0, tiled=True),
        lax.all_gather(dec_qkv[:, D:], "seq", axis=0, tiled=True),
    )
    enc_args = (enc_pos, enc_all, enc_seg, enc_seg_all, False, enc_table, buckets[0])
    enc_att, enc_lse = attend_forward(enc_qkv[:, :D], encoder_key_value, *enc_args)
    enc_ob = enc_att.astype(jnp.bfloat16)
    enc_x1 = enc_x0 + project(enc_ob, enc_wo[0])
    enc_x2, enc_saved = ffn_forward(enc_x1, enc_gain[1], enc_fi[0], enc_fo[0])
    enc_out = rms_scale(enc_x2, enc_gain[2]).astype(jnp.bfloat16)
    cross_kv = lax.all_gather(
        project(enc_out, cross_wi[:, D:]).astype(jnp.bfloat16), "seq", axis=0, tiled=True
    )
    dec_args = (dec_pos, dec_all, dec_seg, dec_seg_all, True, dec_table, buckets[1])
    dec_att, dec_lse = attend_forward(dec_qkv[:, :D], dec_kv, *dec_args)
    dec_ob = dec_att.astype(jnp.bfloat16)
    dec_y1 = dec_y0 + project(dec_ob, dec_wo[0])
    cross_n = rms_scale(dec_y1, dec_gain[1]).astype(jnp.bfloat16)
    cross_q = project(cross_n, cross_wi[:, :D]).astype(jnp.bfloat16)
    cross_args = (dec_pos, enc_all, dec_seg, enc_seg_all, False, None, None)
    cross_att, cross_lse = attend_forward(cross_q, cross_kv, *cross_args)
    cross_ob = cross_att.astype(jnp.bfloat16)
    dec_y2 = dec_y1 + project(cross_ob, dec_wo[1])
    dec_y3, dec_saved = ffn_forward(dec_y2, dec_gain[2], dec_fi[0], dec_fo[0])
    head_scale = D ** (-0.5)
    hidden_b = (rms_scale(dec_y3, dec_gain[3]) * head_scale).astype(jnp.bfloat16)
    targets = target_ids[0]
    weight = target_mask[0].astype(jnp.float32)
    stats_fold = head_stats(hidden_b, targets)
    stats_start = (
        jnp.full((dec_count,), masked_out, jnp.float32),
        jnp.zeros((dec_count,), jnp.float32),
        jnp.zeros((dec_count,), jnp.float32),
    )
    top, total, picked = stats_fold(
        stats_start,
        lax.all_gather(embed.astype(jnp.bfloat16), ("rows", "seq"), axis=0, tiled=True),
        jnp.int32(0),
    )
    lse = top + jnp.log(total)
    d_hidden, logit_grads = head_gradient_list(
        hidden_b,
        targets,
        weight,
        lse,
        lax.all_gather(embed.astype(jnp.bfloat16), ("rows", "seq"), axis=0, tiled=True),
    )
    loss_local = jnp.sum(weight * (lse - picked))
    d_y3, d_gain_final = norm_pull(dec_y3, dec_gain[3], head_scale, d_hidden)
    d_y2, d_gain_dffn, d_dec_fi, d_dec_fo = ffn_backward(
        d_y3, dec_y2, dec_gain[2], dec_fi[0], dec_fo[0], dec_saved
    )
    d_cross_wo, d_cross_ob = branch_backward(d_y2, cross_ob, dec_wo[1])
    d_cross_q, d_cross_kv_all, _ = attend_backward(
        d_cross_ob, cross_q, cross_kv, cross_lse, *cross_args
    )
    d_cross_kv = lax.psum_scatter(
        d_cross_kv_all.astype(jnp.bfloat16), "seq", scatter_dimension=0, tiled=True
    )
    d_cross_qb = d_cross_q.astype(jnp.bfloat16)
    d_cross_wq = weight_grad(cross_n, d_cross_qb)
    d_y1_norm, d_gain_cross = norm_pull(
        dec_y1, dec_gain[1], 1.0, input_grad(d_cross_qb, cross_wi[:, :D])
    )
    d_y1 = d_y2 + d_y1_norm
    d_cross_wkv = weight_grad(enc_out, d_cross_kv)
    d_dec_wo, d_dec_ob = branch_backward(d_y1, dec_ob, dec_wo[0])
    d_dec_q, d_dec_kv_all, d_dec_table = attend_backward(
        d_dec_ob, dec_qkv[:, :D], dec_kv, dec_lse, *dec_args
    )
    d_x2, d_gain_efin = norm_pull(enc_x2, enc_gain[2], 1.0, input_grad(d_cross_kv, cross_wi[:, D:]))
    d_x1, d_gain_effn, d_enc_fi, d_enc_fo = ffn_backward(
        d_x2, enc_x1, enc_gain[1], enc_fi[0], enc_fo[0], enc_saved
    )
    d_enc_wo, d_enc_ob = branch_backward(d_x1, enc_ob, enc_wo[0])
    d_enc_q, d_enc_kv_all, d_enc_table = attend_backward(
        d_enc_ob, enc_qkv[:, :D], encoder_key_value, enc_lse, *enc_args
    )
    d_enc_kv, d_dec_kv = (
        lax.psum_scatter(
            d_enc_kv_all.astype(jnp.bfloat16), "seq", scatter_dimension=0, tiled=True
        ).astype(jnp.float32),
        lax.psum_scatter(
            d_dec_kv_all.astype(jnp.bfloat16), "seq", scatter_dimension=0, tiled=True
        ).astype(jnp.float32),
    )
    d_enc_qkv = jnp.concatenate([d_enc_q, d_enc_kv], axis=1).astype(jnp.bfloat16)
    d_enc_wi = weight_grad(enc_n1, d_enc_qkv)
    d_x0_norm, d_gain_eatt = norm_pull(enc_x0, enc_gain[0], 1.0, input_grad(d_enc_qkv, enc_wi[0]))
    d_x0 = d_x1 + d_x0_norm
    d_dec_qkv = jnp.concatenate([d_dec_q, d_dec_kv], axis=1).astype(jnp.bfloat16)
    d_dec_wi = weight_grad(dec_n1, d_dec_qkv)
    d_y0_norm, d_gain_datt = norm_pull(dec_y0, dec_gain[0], 1.0, input_grad(d_dec_qkv, dec_wi[0]))
    d_y0 = d_y1 + d_y0_norm
    d_inputs = jnp.concatenate([d_x0, d_y0])
    count = lax.axis_size(("rows", "seq")) * embed.shape[0]
    term = jnp.einsum("tv,td->vd", logit_grads, hidden_b, preferred_element_type=jnp.float32)
    local = all_ids
    inside = (local >= 0) & (local < count)
    grad_embed = lax.psum_scatter(
        term
        + jax.ops.segment_sum(
            jnp.where(inside[:, None], d_inputs, 0.0),
            jnp.clip(local, 0, count - 1),
            num_segments=count,
        ),
        ("rows", "seq"),
        scatter_dimension=0,
        tiled=True,
    )
    full_grads = (
        jnp.stack([d_enc_wi, d_dec_wi, jnp.concatenate([d_cross_wq, d_cross_wkv], axis=1)]),
        jnp.stack([d_enc_wo, d_dec_wo, d_cross_wo]),
        jnp.stack([d_enc_fi, d_dec_fi]),
        jnp.stack([d_enc_fo, d_dec_fo]),
        jnp.stack([d_enc_table.reshape(-1), d_dec_table.reshape(-1)]),
        jnp.stack(
            [
                d_gain_eatt,
                d_gain_effn,
                d_gain_efin,
                d_gain_datt,
                d_gain_cross,
                d_gain_dffn,
                d_gain_final,
            ]
        ),
    )
    owned = (
        lax.psum_scatter(full_grads[0], ("rows", "seq"), scatter_dimension=1, tiled=True),
        lax.psum_scatter(full_grads[1], ("rows", "seq"), scatter_dimension=1, tiled=True),
        lax.psum_scatter(full_grads[2], ("rows", "seq"), scatter_dimension=1, tiled=True),
        lax.psum_scatter(full_grads[3], ("rows", "seq"), scatter_dimension=1, tiled=True),
        lax.psum_scatter(full_grads[4], ("rows", "seq"), scatter_dimension=1, tiled=True),
        lax.psum_scatter(full_grads[5], ("rows", "seq"), scatter_dimension=1, tiled=True),
    )
    grads = (grad_embed,) + tuple(owned)
    squares = sum((jnp.sum(item * item) for item in grads))
    count_local = jnp.sum(weight)
    count_all, loss_all, squares_all = lax.psum((count_local, loss_local, squares), ("rows", "seq"))
    grad_norm = jnp.sqrt(squares_all) / count_all
    factor = jnp.minimum(1.0, clip_limit / grad_norm) / count_all
    weights = (embed, attn_in, attn_out, ffn_in, ffn_out, rel_table, gains)
    moments = [
        (m_embed, v_embed),
        (m_attn_in, v_attn_in),
        (m_attn_out, v_attn_out),
        (m_ffn_in, v_ffn_in),
        (m_ffn_out, v_ffn_out),
        (m_rel, v_rel),
        (m_gains, v_gains),
    ]
    settings = [
        (1.0, 0.01),
        (0.05, 0.01),
        (0.05, 0.01),
        (0.05, 0.01),
        (0.05, 0.01),
        (0.3, 0.0),
        (0.3, 0.0),
    ]
    results = [loss_all / count_all, grad_norm]
    for slot_number, (param, grad, pair, setting) in enumerate(
        zip(weights, grads, moments, settings)
    ):
        clipped = grad * factor
        first_new, second_new, new_param = adamw(
            param, clipped, pair[0], pair[1], float(STEP), setting[0], setting[1]
        )
        results.extend((clipped if slot_number == 0 else first_new, second_new, new_param))
    return tuple(results)


def solution(mesh):
    in_specs = (
        P("rows", "seq"),
        P("rows", None),
        P("rows", "seq"),
        P("rows", None),
        P("rows", "seq"),
        P("rows", None),
        P("rows", "seq"),
        P("rows", "seq"),
        P(),
        P(("rows", "seq"), None),
        P(None, ("rows", "seq"), None),
        P(None, ("rows", "seq"), None),
        P(None, ("rows", "seq"), None),
        P(None, ("rows", "seq"), None),
        P(None, ("rows", "seq")),
        P(None, ("rows", "seq")),
        P(("rows", "seq"), None),
        P(("rows", "seq"), None),
        P(None, ("rows", "seq"), None),
        P(None, ("rows", "seq"), None),
        P(None, ("rows", "seq"), None),
        P(None, ("rows", "seq"), None),
        P(None, ("rows", "seq"), None),
        P(None, ("rows", "seq"), None),
        P(None, ("rows", "seq"), None),
        P(None, ("rows", "seq"), None),
        P(None, ("rows", "seq")),
        P(None, ("rows", "seq")),
        P(None, ("rows", "seq")),
        P(None, ("rows", "seq")),
    )
    out_specs = (
        P(),
        P(),
        P(("rows", "seq"), None),
        P(("rows", "seq"), None),
        P(("rows", "seq"), None),
        P(None, ("rows", "seq"), None),
        P(None, ("rows", "seq"), None),
        P(None, ("rows", "seq"), None),
        P(None, ("rows", "seq"), None),
        P(None, ("rows", "seq"), None),
        P(None, ("rows", "seq"), None),
        P(None, ("rows", "seq"), None),
        P(None, ("rows", "seq"), None),
        P(None, ("rows", "seq"), None),
        P(None, ("rows", "seq"), None),
        P(None, ("rows", "seq"), None),
        P(None, ("rows", "seq"), None),
        P(None, ("rows", "seq")),
        P(None, ("rows", "seq")),
        P(None, ("rows", "seq")),
        P(None, ("rows", "seq")),
        P(None, ("rows", "seq")),
        P(None, ("rows", "seq")),
    )
    return jax.shard_map(body, mesh=mesh, in_specs=in_specs, out_specs=out_specs, check_vma=False)
```

profile of v0, /device:TPU:0, one launch (start us, length us, event | category | flops | bytes accessed | tf_op | source)
XLA Modules:
  0.0 6273.9 jit_solution(951221955652553043)
XLA Ops:
  12.7 70.8 %all-gather.2 = bf16[32,24,3]{1,2,0:T(4,128)(2,1)S(1)} all-gather(bf16[1,24,3]{1,2,0:T(4,128)(2,1)S(1)} %slice_bitcast_fusion.10), channel_id=1, replica_groups=mesh['rows'=16,'seq'=2] {'rows','seq'}, dimensions={0}, use_global_device_ids=true | all-gather | bytes 4752 | tf_op jit(solution)/shard_map/all_gather | solution.py:301
  88.9 197.2 %all-gather.38.cloned.1.call-done = bf16[32,1004,768]{2,1,0:T(8,128)(2,1)} async-done(((bf16[1,1004,768]{2,1,0:T(8,128)(2,1)}), bf16[32,1004,768]{2,1,0:T(8,128)(2,1)}) %all-gather.38.cloned.1.call-update) | async-done | bytes 49348624 | tf_op jit(solution)/shard_map/all_gather | solution.py:316
  286.2 38.5 reshape.1224
  358.9 66.6 %all-gather.1 = bf16[32,24,4]{1,2,0:T(4,128)(2,1)S(1)} all-gather(bf16[1,24,4]{1,2,0:T(4,128)(2,1)S(1)} %slice_bitcast_fusion.11), channel_id=1, replica_groups=mesh['rows'=16,'seq'=2] {'rows','seq'}, dimensions={0}, use_global_device_ids=true | all-gather | bytes 6336 | tf_op jit(solution)/shard_map/all_gather | solution.py:309
  434.4 37.4 all-reduce.16
  485.7 522.0 %while.182 = (s32[]{:T(128)}, f32[12,512]{1,0:T(8,128)S(1)}, f32[12,512]{1,0:T(8,128)S(1)}, s32[512]{0:T(512)}, s32[4,256]{1,0:T(4,128)}, /*index=5*/bf16[4,256,...) while((s32[]{:T(128)}, f32[12,512]{1,0:T(8,128)S(1)}, ...), condition=%wide.region_12.13_spmd.clone, body=%wide.region_9.12_spmd.clone.sunk | while | flops 211548384 | bytes 177888464 | solution.py:118
  516.8 29.6 tile.157
  563.5 37.8 reshape.1307
  637.3 29.6 tile.157
  684.3 37.7 reshape.1307
  804.6 37.7 reshape.1307
  924.7 37.7 reshape.1307
  1011.8 472.0 %while.183 = (s32[]{:T(128)}, f32[512,12,64]{0,2,1:T(8,128)}, bf16[4,256,12,64]{1,3,2,0:T(8,128)(2,1)}, s32[512]{0:T(512)}, s32[4,256]{1,0:T(4,128)}, /*index=5*...) while((s32[]{:T(128)}, f32[512,12,64]{0,2,1:T(8,128)}, ...), condition=%wide.region_14.15_spmd.clone, body=%wide.region_13.14_spmd.clone.sunk | while | flops 412057824 | bytes 168558288 | solution.py:128
  1069.8 37.7 reshape.1308
  1186.0 37.7 reshape.1308
  1302.7 37.7 reshape.1308
  1419.5 37.7 reshape.1308
  1520.5 90.9 %while.180 = (s32[]{:T(128)}, f32[12,256]{1,0:T(8,128)S(1)}, f32[12,256]{1,0:T(8,128)}, s32[256]{0:T(256)}, s32[2,256]{1,0:T(2,128)}, /*index=5*/s32[2,256]{1,0:...) while((s32[]{:T(128)}, f32[12,256]{1,0:T(8,128)S(1)}, ...), condition=%wide.region_5.6_spmd.clone, body=%wide.region_2.5_spmd.clone.sunk | while | flops 106008792 | bytes 70409480 | solution.py:118
  1614.7 89.4 %while.181 = (s32[]{:T(128)}, f32[256,12,64]{0,2,1:T(8,128)}, bf16[2,256,12,64]{1,3,2,0:T(8,128)(2,1)}, s32[256]{0:T(256)}, s32[2,256]{1,0:T(2,128)}, /*index=5*...) while((s32[]{:T(128)}, f32[256,12,64]{0,2,1:T(8,128)}, ...), condition=%wide.region_7.8_spmd.clone, body=%wide.region_6.7_spmd.clone.sunk | while | flops 206263520 | bytes 65838812 | solution.py:128
  1786.5 32.7 fusion.283
  1836.1 30.7 multiply_reduce_fusion.10
  1909.0 46.6 while.187
  1962.1 90.3 %while.190 = (s32[]{:T(128)}, f32[12,256]{1,0:T(8,128)}, s32[256]{0:T(256)}, s32[2,256]{1,0:T(2,128)}, s32[2,256]{1,0:T(2,128)}, /*index=5*/s32[256]{0:T(256)}, ...) while((s32[]{:T(128)}, f32[12,256]{1,0:T(8,128)}, ...), condition=%wide.region_54.55_spmd.clone, body=%wide.region_52.54_spmd.clone.sunk | while | flops 206659808 | bytes 85253976 | solution.py:152
  2052.4 168.1 %while.191 = (s32[]{:T(128)}, f32[256,12,64]{0,2,1:T(8,128)}, f32[32,12]{0,1:T(8,128)}, bf16[2,256,1536]{2,1,0:T(8,128)(2,1)}, bf16[2,256,12,64]{1,3,2,0:T(8,128...) while((s32[]{:T(128)}, f32[256,12,64]{0,2,1:T(8,128)}, ...), condition=%wide.region_57.58_spmd.clone, body=%wide.region_55.57_spmd.clone.sunk | while | flops 516146304 | bytes 143725440 | solution.py:177
  2244.3 486.7 %while.188 = (s32[]{:T(128)}, f32[12,512]{1,0:T(8,128)}, s32[512]{0:T(512)}, s32[4,256]{1,0:T(4,128)}, bf16[4,256,12,64]{1,3,2,0:T(8,128)(2,1)}, /*index=5*/bf16...) while((s32[]{:T(128)}, f32[12,512]{1,0:T(8,128)}, ...), condition=%wide.region_45.46_spmd.clone, body=%wide.region_43.45_spmd.clone.sunk | while | flops 412850400 | bytes 204046064 | solution.py:152
  2322.7 37.7 reshape.1309
  2392.1 29.5 tile.161
  2438.7 37.7 reshape.1309
  2555.4 37.7 reshape.1309
  2672.1 37.7 reshape.1309
  2732.9 939.3 %while.189 = (s32[]{:T(128)}, f32[512,12,64]{0,2,1:T(8,128)}, f32[32,12]{0,1:T(8,128)}, bf16[4,256,1536]{2,1,0:T(8,128)(2,1)}, bf16[4,256,12,64]{1,3,2,0:T(8,128...) while((s32[]{:T(128)}, f32[512,12,64]{0,2,1:T(8,128)}, ...), condition=%wide.region_48.49_spmd.clone, body=%wide.region_46.48_spmd.clone.sunk | while | flops 1032789184 | bytes 327727744 | solution.py:177
  2797.1 38.3 reshape.1311
  2875.7 31.1 reshape.1312
  2920.9 37.5 reshape.1313
  3027.5 38.3 reshape.1311
  3106.2 31.1 reshape.1312
  3151.3 37.5 reshape.1313
  3259.2 38.3 reshape.1311
  3337.9 31.1 reshape.1312
  3383.0 37.5 reshape.1313
  3490.9 38.3 reshape.1311
  3569.6 31.1 reshape.1312
  3614.7 37.5 reshape.1313
  3728.9 49.0 fusion.264
  3819.8 99.6 %scatter_fusion = f32[32128,768]{1,0:T(8,128)} fusion(f32[32128,768]{1,0:T(8,128)} %fusion.264, s32[768]{0:T(1024)S(1)} %copy-done.157, f32[768,768]{1,0:T(8,128)S(1)} %maximum_select_fusion), kind=kCustom, calls=%fused_computation.1 | custom fusion | flops 589824 | bytes 7080960 | tf_op jit(solution)/shard_map/scatter-add | solution.py:428
  3919.4 2186.0 %fusion = f32[1008,768]{1,0:T(8,128)S(1)} fusion(f32[32128,768]{1,0:T(8,128)} %scatter_fusion), kind=kCustom, calls=%all-reduce-scatter | all-reduce-scatter fusion | flops 24772608 | bytes 101793792
  6132.3 50.3 all-reduce.15
  6205.5 40.2 all-reduce.14
  (1326 shorter events, 2337.7 us)
Async XLA Ops:
  7.2 77.9 %copy-start.183 = (s32[1,512]{1,0:T(1,128)S(1)}, s32[1,512]{1,0:T(1,128)}, u32[]{:S(2)}) copy-start(s32[1,512]{1,0:T(1,128)} %param.56) | copy-start | bytes 6148
  7.2 77.9 %copy-start.191 = (s32[1,4]{1,0:T(1,128)S(1)}, s32[1,4]{1,0:T(1,128)}, u32[]{:S(2)}) copy-start(s32[1,4]{1,0:T(1,128)} %param.57) | copy-start | bytes 52
  7.2 78.7 %copy-start.181 = (s32[1,512]{1,0:T(1,128)S(1)}, s32[1,512]{1,0:T(1,128)}, u32[]{:S(2)}) copy-start(s32[1,512]{1,0:T(1,128)} %param.54) | copy-start | bytes 6148
  7.3 79.9 %copy-start.178 = (s32[1,256]{1,0:T(1,128)S(1)}, s32[1,256]{1,0:T(1,128)}, u32[]{:S(2)}) copy-start(s32[1,256]{1,0:T(1,128)} %param.58) | copy-start | bytes 3076
  7.3 278.9 %all-gather.38.cloned.1.call-start = ((), (), s32[]{:S(2)}) async-start(), calls=%async_computation.25 | async-start | bytes 51093504 | tf_op jit(solution)/shard_map/all_gather | solution.py:316
  10.6 337.5 %all-gather.22.cloned.1.call-start = ((), (), s32[]{:S(2)}) async-start(), calls=%async_computation.10 | async-start | bytes 3649536 | tf_op jit(solution)/shard_map/all_gather | solution.py:296
  11.3 415.3 %all-gather.16.cloned.1.call-start = ((), (), s32[]{:S(2)}) async-start(), calls=%async_computation.7 | async-start | bytes 7299072 | tf_op jit(solution)/shard_map/all_gather | solution.py:304
  12.1 466.9 %all-gather.24.cloned.1.call-start = ((), (), s32[]{:S(2)}) async-start(), calls=%async_computation.11 | async-start | bytes 4718592 | tf_op jit(solution)/shard_map/all_gather | solution.py:328
  88.3 243.3 %copy-start.158 = (pred[768]{0:T(1024)(128)(4,1)}, pred[768]{0:T(1024)(128)(4,1)S(1)}, u32[]{:S(2)}) copy-start(pred[768]{0:T(1024)(128)(4,1)S(1)} %get-tuple-element.4065) | copy-start | bytes 2308
  88.9 259.1 %copy-start.119 = (f32[768]{0:T(1024)}, f32[768]{0:T(1024)S(1)}, u32[]{:S(2)}) copy-start(f32[768]{0:T(1024)S(1)} %get-tuple-element.3724) | copy-start | bytes 9220
  332.7 94.5 %copy-start.9 = (f32[768,768]{1,0:T(8,128)}, f32[768,768]{1,0:T(8,128)S(1)}, u32[]{:S(2)}) copy-start(f32[768,768]{1,0:T(8,128)S(1)} %convert_select_fusion) | copy-start | bytes 7077892
  354.9 1130.6 %all-gather.26.cloned.1.call-start = ((), (), s32[]{:S(2)}) async-start(), calls=%async_computation.12 | async-start | bytes 1216512 | tf_op jit(solution)/shard_map/all_gather | solution.py:297
  357.2 1131.9 %all-gather.28.cloned.1.call-start = ((), (), s32[]{:S(2)}) async-start(), calls=%async_computation.13 | async-start | bytes 6488064 | tf_op jit(solution)/shard_map/all_gather | solution.py:298
  358.1 1143.4 %all-gather.30.cloned.1.call-start = ((), (), s32[]{:S(2)}) async-start(), calls=%async_computation.14 | async-start | bytes 3244032 | tf_op jit(solution)/shard_map/all_gather | solution.py:299
  358.9 1157.6 %all-gather.18.cloned.1.call-start = ((), (), s32[]{:S(2)}) async-start(), calls=%async_computation.8 | async-start | bytes 2359296 | tf_op jit(solution)/shard_map/all_gather | solution.py:329
  432.5 1273.0 %all-gather.20.cloned.1.call-start = ((), (), s32[]{:S(2)}) async-start(), calls=%async_computation.9 | async-start | bytes 2433024 | tf_op jit(solution)/shard_map/all_gather | solution.py:305
  433.3 1278.1 %all-gather.32.cloned.1.call-start = ((), (), s32[]{:S(2)}) async-start(), calls=%async_computation.15 | async-start | bytes 4718592 | tf_op jit(solution)/shard_map/all_gather | solution.py:337
  485.7 522.0 %copy-start.49 = (bf16[1024,768]{1,0:T(8,128)(2,1)S(1)}, bf16[1024,768]{1,0:T(8,128)(2,1)}, u32[]{:S(2)}) copy-start(bf16[1024,768]{1,0:T(8,128)(2,1)} %get-tuple-element.4056) | copy-start | bytes 4718596
  1011.8 473.6 %copy-start.10 = (f32[768,768]{1,0:T(8,128)S(1)}, f32[768,768]{1,0:T(8,128)}, u32[]{:S(2)}) copy-start(f32[768,768]{1,0:T(8,128)} %copy-done.9) | copy-start | bytes 7077892
  1509.9 265.5 %all-gather.34.cloned.1.call-start = ((), (), s32[]{:S(2)}) async-start(), calls=%async_computation.16 | async-start | bytes 6488064 | tf_op jit(solution)/shard_map/all_gather | solution.py:306
  1510.7 272.5 %all-gather.36.cloned.1.call-start = ((), (), s32[]{:S(2)}) async-start(), calls=%async_computation.17 | async-start | bytes 3244032 | tf_op jit(solution)/shard_map/all_gather | solution.py:307
  1511.2 709.4 %reduce-scatter.12.cloned.1.call-start = ((), (), s32[]{:S(2)}) async-start(), calls=%async_computation.18 | async-start | bytes 4718592 | tf_op jit(solution)/shard_map/reduce_scatter | solution.py:383
  1775.4 103.9 %copy-start.26 = (f32[256,768]{1,0:T(8,128)}, f32[256,768]{1,0:T(8,128)S(1)}, u32[]{:S(2)}) copy-start(f32[256,768]{1,0:T(8,128)S(1)} %get-tuple-element.4076) | copy-start | bytes 2359300
  1775.4 103.9 %copy-start.137 = (f32[256]{0:T(256)}, f32[256]{0:T(256)S(1)}, u32[]{:S(2)}) copy-start(f32[256]{0:T(256)S(1)} %fusion.252) | copy-start | bytes 3076
  1786.5 80.3 %copy-start.14 = (f32[256,768]{1,0:T(8,128)}, f32[256,768]{1,0:T(8,128)S(1)}, u32[]{:S(2)}) copy-start(f32[256,768]{1,0:T(8,128)S(1)} %get-tuple-element.4078) | copy-start | bytes 2359300
  1786.5 80.2 %copy-start.117 = (f32[256]{0:T(256)}, f32[256]{0:T(256)S(1)}, u32[]{:S(2)}) copy-start(f32[256]{0:T(256)S(1)} %fusion.253) | copy-start | bytes 3076
  1955.7 1822.3 %reduce-scatter.16.cloned.1.call-start = ((), (), s32[]{:S(2)}) async-start(), calls=%async_computation.20 | async-start | bytes 2359296 | tf_op jit(solution)/shard_map/reduce_scatter | solution.py:409
  2220.6 1576.2 %reduce-scatter.14.cloned.1.call-start = ((), (), s32[]{:S(2)}) async-start(), calls=%async_computation.19 | async-start | bytes 4718592 | tf_op jit(solution)/shard_map/reduce_scatter | solution.py:406
  3672.3 2521.5 %reduce-scatter.20.cloned.1.call-start = ((), (), s32[]{:S(2)}) async-start(), calls=%async_computation.22 | async-start | bytes 7299072 | tf_op jit(solution)/shard_map/reduce_scatter | solution.py:457
  3679.2 2516.3 %reduce-scatter.24.cloned.1.call-start = ((), (), s32[]{:S(2)}) async-start(), calls=%async_computation.24 | async-start | bytes 12976128 | tf_op jit(solution)/shard_map/reduce_scatter | solution.py:459
  3696.1 2501.1 %reduce-scatter.22.cloned.1.call-start = ((), (), s32[]{:S(2)}) async-start(), calls=%async_computation.23 | async-start | bytes 25952256 | tf_op jit(solution)/shard_map/reduce_scatter | solution.py:458
  3724.8 2474.3 %reduce-scatter.18.cloned.1.call-start = ((), (), s32[]{:S(2)}) async-start(), calls=%async_computation.21 | async-start | bytes 21897216 | tf_op jit(solution)/shard_map/reduce_scatter | solution.py:456
  3728.9 49.1 copy-start.11
  3919.3 2211.1 %copy-start.186 = (s32[1,256]{1,0:T(1,128)S(1)}, s32[1,256]{1,0:T(1,128)}, u32[]{:S(2)}) copy-start(s32[1,256]{1,0:T(1,128)} %param.61) | copy-start | bytes 3076
  3919.3 2211.7 %copy-start.172 = (f32[768]{0:T(1024)S(1)}, f32[768]{0:T(1024)}, u32[]{:S(2)}) copy-start(f32[768]{0:T(1024)} %get-tuple-element.3716) | copy-start | bytes 9220
  3919.4 2211.7 %copy-start.171 = (f32[768]{0:T(1024)S(1)}, f32[768]{0:T(1024)}, u32[]{:S(2)}) copy-start(f32[768]{0:T(1024)} %get-tuple-element.3714) | copy-start | bytes 9220
  3919.4 2211.7 %copy-start.170 = (f32[768]{0:T(1024)S(1)}, f32[768]{0:T(1024)}, u32[]{:S(2)}) copy-start(f32[768]{0:T(1024)} %get-tuple-element.3712) | copy-start | bytes 9220
  3919.4 2211.7 %copy-start.164 = (f32[32,12]{0,1:T(8,128)S(1)}, f32[32,12]{0,1:T(8,128)}, u32[]{:S(2)}) copy-start(f32[32,12]{0,1:T(8,128)} %get-tuple-element.2275) | copy-start | bytes 4612
  3919.4 2211.9 %copy-start.174 = (f32[768]{0:T(1024)S(1)}, f32[768]{0:T(1024)}, u32[]{:S(2)}) copy-start(f32[768]{0:T(1024)} %get-tuple-element.3710) | copy-start | bytes 9220
  3919.4 2211.9 %copy-start.173 = (f32[768]{0:T(1024)S(1)}, f32[768]{0:T(1024)}, u32[]{:S(2)}) copy-start(f32[768]{0:T(1024)} %get-tuple-element.3708) | copy-start | bytes 9220
  6105.4 78.6 %copy-start.31 = (f32[1008,768]{1,0:T(8,128)}, f32[1008,768]{1,0:T(8,128)S(1)}, u32[]{:S(2)}) copy-start(f32[1008,768]{1,0:T(8,128)S(1)} %fusion) | copy-start | bytes 9289732
  6105.4 78.5 %collective-permute-start = (f32[124,768]{1,0:T(8,128)S(1)}, f32[124,768]{1,0:T(8,128)}, u32[]{:S(2)}, u32[]{:S(2)}) collective-permute-start(f32[124,768]{1,0:T(8,128)S(1)} %slice.835), channel_id=1, source_target_pairs={{0,1},{1,2},{2,3},{3,4},{4,5},{5,6},{6,7},{7,8},{8,9},{9,10},{10,1... | collective-permute-start | bytes 1142792
  6192.4 57.4 copy-start.156
  6192.4 57.4 copy-start.179
  6192.4 57.4 copy-start.180
  6192.4 58.1 copy-start.188
  6192.5 58.1 copy-start.189
  6192.5 58.1 copy-start.190
  (207 other events, 927.7 us)
Sparse Core Ops, SparseCore 0:
  11.6 274.5 all-gather.37
  289.7 58.3 all-gather.21
  351.5 71.5 all-gather.15
  424.5 44.4 all-gather.23
  472.4 54.4 all-gather.25
  530.2 68.4 all-gather.27
  602.2 57.5 all-gather.29
  661.9 26.0 all-gather.17
  691.4 57.4 all-gather.19
  1510.0 46.0 all-gather.31
  1559.6 69.3 all-gather.33
  1632.3 57.5 all-gather.35
  1955.8 44.3 reduce-scatter.11
  2220.7 27.4 reduce-scatter.15
  3672.5 44.7 reduce-scatter.13
  3723.7 119.1 reduce-scatter.19
  3848.8 197.3 reduce-scatter.23
  4053.6 299.8 reduce-scatter.21
  4359.8 269.2 reduce-scatter.17
where the time goes:
time: 6300 us; the launch traced here: 6270 us
  local copies, waits for them, and re-layouts  2550 us (40%)
  blocking collectives  2450 us (39%)
  matrix products  499 us (8%)
  other arithmetic  392 us (6%)
  waiting for transfers between devices  214 us (3%)
  loops' own time  115 us (2%)
    unnamed x3, blocking collectives  2270 us
    another operation x48, local copies, waits for them, and re-layouts, diagonal_spread(): flat = jnp.tile(rolled, (1, q_len))[:, :q_len * (width - 1)]  694 us
    reshape x24, local copies, waits for them, and re-layouts, diagonal_spread(): return flat.reshape(per_offset.shape[0], q_len, width - 1)[:, :, :k_len]  682 us
    slice x24, local copies, waits for them, and re-layouts, diagonal_spread(): flat = jnp.tile(rolled, (1, q_len))[:, :q_len * (width - 1)]  331 us
    all_gather x1, waiting for transfers between devices, body(): lax.all_gather(embed.astype(jnp.bfloat16), ('rows', 'seq'), axis=0, tiled...  197 us
    reshape x6, local copies, waits for them, and re-layouts, diagonal_collect(): summed = jnp.sum(flat.reshape(heads, q_len, width), axis=1)  168 us
    while x140, local copies, waits for them, and re-layouts  146 us
    reshape x6, local copies, waits for them, and re-layouts, diagonal_collect(): padded.reshape(heads, q_len * (width - 1))  143 us
  transfers between devices with their start and end apart: 20, of which 2 were waited for; matrix products, arithmetic and copies ran while one was open for 86% of the time, Pallas kernels for 0%

commit v1 on v0

v1 whole, which is shorter than its diff:
```python
import functools

import jax
import jax.numpy as jnp
from jax import lax
from jax.experimental import pallas as pl
from jax.experimental.pallas import tpu as pltpu
from jax.sharding import Mesh
from jax.sharding import PartitionSpec as P

D = 768
HEADS = 12
HEAD_DIM = 64
FF = 2048
V = 32128
BUCKETS = 32
STEP = 10

masked_out = -1e30
clip_limit = 0.01
ALL = ("z", "p", "core", "seq")
PLANE = ("p", "core", "seq")
bf16 = jnp.bfloat16
f32 = jnp.float32
VMEM_LIMIT = 56 * 1024 * 1024


def rms_scale(values, gain):
    return values * lax.rsqrt(jnp.mean(values * values, axis=-1, keepdims=True) + 1e-06) * gain


def norm_pull(values, gain, factor, upstream):
    _, pull = jax.vjp(lambda left, right: rms_scale(left, right) * factor, values, gain)
    return pull(upstream)


def gate_up(both):
    return jax.nn.gelu(both[:, :FF], approximate=True) * both[:, FF:]


def project(left, right):
    return jnp.dot(left, right, preferred_element_type=f32)


def weight_grad(inputs, grads):
    return jnp.einsum("td,te->de", inputs, grads, preferred_element_type=f32)


def input_grad(grads, weight):
    return jnp.einsum("te,de->td", grads, weight, preferred_element_type=f32)


def dot_nt(a, b):
    return lax.dot_general(a, b, (((1,), (1,)), ((), ())), preferred_element_type=f32)


def dot_tn(a, b):
    return lax.dot_general(a, b, (((0,), (0,)), ((), ())), preferred_element_type=f32)


def dot_nn(a, b):
    return lax.dot_general(a, b, (((1,), (0,)), ((), ())), preferred_element_type=f32)


def spread(eight, rows, width):
    total = eight.shape[-1]
    grid = eight
    have = 8
    while have < rows:
        grid = jnp.concatenate([pltpu.roll(grid, total - have, 1), grid], axis=0)
        have *= 2
    return grid[:, :width]


def collect(grid, total):
    rows, width = grid.shape
    have = jnp.concatenate([grid, jnp.zeros((rows, total - width), f32)], axis=1)
    while rows > 8:
        rows //= 2
        have = pltpu.roll(have[:rows], rows, 1) + have[rows:]
    return have


def probs_of(cfg, refs, block, head):
    bq, has_bias, causal = cfg
    rows = slice(block * bq, (block + 1) * bq)
    cols = slice(head * HEAD_DIM, (head + 1) * HEAD_DIM)
    query = refs["q"][rows, cols]
    scores = []
    for part in range(2):
        keys = refs["k"][part][:, cols]
        s = dot_nt(query, keys) * HEAD_DIM ** (-0.5)
        if has_bias:
            s = s + spread(refs["x8"][block, part, head], bq, keys.shape[0])
        allowed = refs["qseg"][rows, :] == refs["kseg"][part]
        if causal:
            allowed = allowed & (refs["kpos"][part] <= refs["qpos"][rows, :])
        scores.append(jnp.where(allowed, s, masked_out))
    top = jnp.maximum(
        jnp.max(scores[0], axis=1, keepdims=True), jnp.max(scores[1], axis=1, keepdims=True)
    )
    exps = [jnp.exp(s - top) for s in scores]
    total = jnp.sum(exps[0], axis=1, keepdims=True) + jnp.sum(exps[1], axis=1, keepdims=True)
    scale = 1.0 / total
    return query, [e * scale for e in exps]


def name_refs(cfg, refs):
    bq, has_bias, causal = cfg
    it = iter(refs)
    named = {"q": next(it)}
    k0, v0, k1, v1 = next(it), next(it), next(it), next(it)
    named["k"], named["v"] = (k0, k1), (v0, v1)
    ids = next(it), next(it), next(it), next(it), next(it), next(it)
    named["qseg"], named["kseg"] = ids[0], (ids[1][...], ids[2][...])
    named["qpos"], named["kpos"] = ids[3], (ids[4][...], ids[5][...])
    if has_bias:
        named["x8"] = next(it)
    return named, list(it)


def attend_forward_kernel(cfg, *refs):
    named, (out,) = name_refs(cfg, refs)
    bq = cfg[0]
    for block in range(named["q"].shape[0] // bq):
        for head in range(2):
            cols = slice(head * HEAD_DIM, (head + 1) * HEAD_DIM)
            _, probs = probs_of(cfg, named, block, head)
            acc = dot_nn(probs[0].astype(bf16), named["v"][0][:, cols])
            acc = acc + dot_nn(probs[1].astype(bf16), named["v"][1][:, cols])
            out[block * bq : (block + 1) * bq, cols] = acc.astype(bf16)


def attend_backward_kernel(cfg, *refs):
    named, rest = name_refs(cfg, refs)
    bq, has_bias, causal = cfg
    if has_bias:
        grad, dq, own, other, y8 = rest
    else:
        grad, dq, own, other = rest
    blocks = named["q"].shape[0] // bq
    for head in range(2):
        cols = slice(head * HEAD_DIM, (head + 1) * HEAD_DIM)
        dk, dv = [None, None], [None, None]
        for block in range(blocks):
            rows = slice(block * bq, (block + 1) * bq)
            query, probs = probs_of(cfg, named, block, head)
            do = grad[rows, cols]
            dp = [dot_nt(do, named["v"][part][:, cols]) for part in range(2)]
            delta = jnp.sum(probs[0] * dp[0], axis=1, keepdims=True) + jnp.sum(
                probs[1] * dp[1], axis=1, keepdims=True
            )
            acc = None
            for part in range(2):
                ds = (probs[part] * (dp[part] - delta)).astype(bf16)
                term = dot_nn(ds, named["k"][part][:, cols])
                acc = term if acc is None else acc + term
                k_term = dot_tn(query, ds)
                v_term = dot_tn(do, probs[part].astype(bf16))
                dk[part] = k_term if dk[part] is None else dk[part] + k_term
                dv[part] = v_term if dv[part] is None else dv[part] + v_term
                if has_bias:
                    y8[block, part, head] = collect(ds.astype(f32), y8.shape[-1])
            dq[rows, cols] = (acc * HEAD_DIM ** (-0.5)).astype(bf16)
        for part, target in enumerate((own, other)):
            target[0, :, cols] = (dk[part] * HEAD_DIM ** (-0.5)).T.astype(target.dtype)
            target[1, :, cols] = dv[part].T.astype(target.dtype)


def attend_specs(q_len, k_len, has_bias, x8):
    whole = lambda shape: pl.BlockSpec(shape, lambda i: (0,) * len(shape))
    kv = [
        pl.BlockSpec((k_len, 128), lambda i: (0, i)),
        pl.BlockSpec((k_len, 128), lambda i: (0, i + 6)),
    ]
    specs = [pl.BlockSpec((q_len, 128), lambda i: (0, i))] + kv + kv
    specs += [whole((q_len, 1)), whole((1, k_len)), whole((1, k_len))] * 2
    if has_bias:
        specs.append(
            pl.BlockSpec((x8.shape[0], 2, 2, 8, x8.shape[-1]), lambda i: (0, 0, i, 0, 0))
        )
    return specs


def attend_args(q, kv_own, kv_other, ids, x8):
    args = [q, kv_own, kv_own, kv_other, kv_other] + list(ids)
    if x8 is not None:
        args.append(x8)
    return args


def attend_cost(q_len, k_len, products):
    size = HEADS * q_len * 2 * k_len
    return pl.CostEstimate(
        flops=2 * products * size * HEAD_DIM, bytes_accessed=8 * D * (q_len + 4 * k_len),
        transcendentals=size,
    )


def attend_forward(q, kv_own, kv_other, ids, x8, causal):
    q_len, k_len = q.shape[0], kv_own.shape[0]
    cfg = (256, x8 is not None, causal)
    return pl.pallas_call(
        functools.partial(attend_forward_kernel, cfg),
        grid=(HEADS // 2,),
        in_specs=attend_specs(q_len, k_len, x8 is not None, x8),
        out_specs=pl.BlockSpec((q_len, 128), lambda i: (0, i)),
        out_shape=jax.ShapeDtypeStruct((q_len, D), bf16),
        compiler_params=pltpu.CompilerParams(vmem_limit_bytes=VMEM_LIMIT),
        cost_estimate=attend_cost(q_len, k_len, 2),
    )(*attend_args(q, kv_own, kv_other, ids, x8))


def attend_backward(grad, q, kv_own, kv_other, ids, x8, causal):
    q_len, k_len = q.shape[0], kv_own.shape[0]
    cfg = (256, x8 is not None, causal)
    kv_spec = pl.BlockSpec((2, k_len, 128), lambda i: (0, 0, i))
    out_specs = [pl.BlockSpec((q_len, 128), lambda i: (0, i)), kv_spec, kv_spec]
    out_shape = [
        jax.ShapeDtypeStruct((q_len, D), bf16),
        jax.ShapeDtypeStruct((2, k_len, D), f32),
        jax.ShapeDtypeStruct((2, k_len, D), bf16),
    ]
    if x8 is not None:
        out_specs.append(
            pl.BlockSpec((x8.shape[0], 2, 2, 8, x8.shape[-1]), lambda i: (0, 0, i, 0, 0))
        )
        out_shape.append(jax.ShapeDtypeStruct(x8.shape, f32))
    return pl.pallas_call(
        functools.partial(attend_backward_kernel, cfg),
        grid=(HEADS // 2,),
        in_specs=attend_specs(q_len, k_len, x8 is not None, x8)
        + [pl.BlockSpec((q_len, 128), lambda i: (0, i))],
        out_specs=out_specs,
        out_shape=out_shape,
        compiler_params=pltpu.CompilerParams(vmem_limit_bytes=VMEM_LIMIT),
        cost_estimate=attend_cost(q_len, k_len, 5),
    )(*attend_args(q, kv_own, kv_other, ids, x8), grad)


def bias_bases(core, q_len, k_len, offset):
    bases = []
    for block in range(q_len // 256):
        for part in range(2):
            k_start = (core if part == 0 else 1 - core) * k_len
            q_start = core * q_len + block * 256
            bases.append(k_start - q_start - 255 + offset)
    return bases


def bias_eights(table, bucket_row, core, q_len, k_len):
    size = bucket_row.shape[0]
    picks = (bucket_row[None, :] == jnp.arange(BUCKETS, dtype=jnp.int32)[:, None]).astype(bf16)
    per_offset = jnp.einsum("bh,bn->hn", table, picks, preferred_element_type=f32)
    per_offset = jnp.pad(per_offset, ((0, 0), (0, 16)))
    width = k_len + 256
    found = []
    for base in bias_bases(core, q_len, k_len, size // 2):
        window = lax.dynamic_slice_in_dim(per_offset, base, width + 7, axis=1)
        found.append(jnp.stack([window[:, 7 - r : 7 - r + width] for r in range(8)], axis=1))
    return jnp.stack(found).reshape(q_len // 256, 2, HEADS, 8, width), picks


def bias_gradient(y8, picks, core, q_len, k_len):
    size = picks.shape[1]
    width = k_len + 256
    total = jnp.zeros((HEADS, size + 16), f32)
    flat = y8.reshape(-1, HEADS, 8, width)
    for number, base in enumerate(bias_bases(core, q_len, k_len, size // 2)):
        window = sum(
            jnp.pad(flat[number, :, r], ((0, 0), (7 - r, r))) for r in range(8)
        )
        old = lax.dynamic_slice_in_dim(total, base, width + 7, axis=1)
        total = lax.dynamic_update_slice_in_dim(total, old + window, base, axis=1)
    return jnp.einsum(
        "bn,hn->bh", picks.astype(f32), total[:, :size], precision=lax.Precision.HIGHEST
    )


def head_stats_kernel(count, hid, tab, tgt, lse_out, pick_out):
    logits = dot_nt(tab[...], hid[...])
    row = lax.broadcasted_iota(jnp.int32, logits.shape, 0)
    pick_out[...] = jnp.sum(jnp.where(row == tgt[...], logits, 0.0), axis=0, keepdims=True)
    logits = jnp.where(row < count, logits, masked_out)
    top = jnp.max(logits, axis=0, keepdims=True)
    lse_out[...] = top + jnp.log(jnp.sum(jnp.exp(logits - top), axis=0, keepdims=True))


def head_grad_kernel(count, hid, tab, tgt, msk, lse, dhid, dtab):
    logits = dot_nt(tab[...], hid[...])
    row = lax.broadcasted_iota(jnp.int32, logits.shape, 0)
    soft = jnp.exp(jnp.where(row < count, logits, masked_out) - lse[...])
    grad = ((soft - jnp.where(row == tgt[...], 1.0, 0.0)) * msk[...]).astype(bf16)
    dhid[...] = dot_tn(grad, tab[...]).astype(bf16)
    term = dot_nn(grad, hid[...])

    @pl.when(pl.program_id(0) == 0)
    def _():
        dtab[...] = term

    @pl.when(pl.program_id(0) != 0)
    def _():
        dtab[...] += term


def head_stats(hidden, table, targets, count):
    tokens, rows = hidden.shape[0], table.shape[0]
    block = 512
    line = pl.BlockSpec((1, block), lambda i: (0, i))
    return pl.pallas_call(
        functools.partial(head_stats_kernel, count),
        grid=(tokens // block,),
        in_specs=[
            pl.BlockSpec((block, D), lambda i: (i, 0)),
            pl.BlockSpec((rows, D), lambda i: (0, 0)),
            line,
        ],
        out_specs=[line, line],
        out_shape=[jax.ShapeDtypeStruct((1, tokens), f32)] * 2,
        compiler_params=pltpu.CompilerParams(vmem_limit_bytes=VMEM_LIMIT),
        cost_estimate=pl.CostEstimate(
            flops=2 * tokens * rows * D, bytes_accessed=2 * tokens * D, transcendentals=tokens * rows
        ),
    )(hidden, table, targets)


def head_grad(hidden, table, targets, mask, lse, count):
    tokens, rows = hidden.shape[0], table.shape[0]
    block = 512
    line = pl.BlockSpec((1, block), lambda i: (0, i))
    return pl.pallas_call(
        functools.partial(head_grad_kernel, count),
        grid=(tokens // block,),
        in_specs=[
            pl.BlockSpec((block, D), lambda i: (i, 0)),
            pl.BlockSpec((rows, D), lambda i: (0, 0)),
            line,
            line,
            line,
        ],
        out_specs=[
            pl.BlockSpec((block, D), lambda i: (i, 0)),
            pl.BlockSpec((rows, D), lambda i: (0, 0)),
        ],
        out_shape=[
            jax.ShapeDtypeStruct((tokens, D), bf16),
            jax.ShapeDtypeStruct((rows, D), f32),
        ],
        compiler_params=pltpu.CompilerParams(vmem_limit_bytes=VMEM_LIMIT),
        cost_estimate=pl.CostEstimate(
            flops=6 * tokens * rows * D, bytes_accessed=4 * tokens * D, transcendentals=tokens * rows
        ),
    )(hidden, table, targets, mask, lse)


def place_kernel(ids, grads, out):
    rows = out.shape[0]
    row = lax.broadcasted_iota(jnp.int32, (rows, ids.shape[1]), 0) + pl.program_id(0) * rows
    hot = jnp.where(row == ids[...], 1.0, 0.0).astype(bf16)
    out[...] = dot_nn(hot, grads[...]).astype(bf16)


def place_rows(ids, grads, parts, rows):
    tokens = grads.shape[0]
    return pl.pallas_call(
        place_kernel,
        grid=(parts,),
        in_specs=[
            pl.BlockSpec((1, tokens), lambda i: (0, 0)),
            pl.BlockSpec((tokens, D), lambda i: (0, 0)),
        ],
        out_specs=pl.BlockSpec((rows, D), lambda i: (i, 0)),
        out_shape=jax.ShapeDtypeStruct((parts * rows, D), bf16),
        compiler_params=pltpu.CompilerParams(vmem_limit_bytes=VMEM_LIMIT),
        cost_estimate=pl.CostEstimate(
            flops=2 * tokens * parts * rows * D, bytes_accessed=2 * parts * rows * D, transcendentals=0
        ),
    )(ids, grads)


def gather_axis(value, axis):
    size = lax.axis_size(axis)
    me = lax.axis_index(axis)
    got = [value]
    for step in range(1, size):
        got.append(lax.ppermute(value, axis, [(i, (i + step) % size) for i in range(size)]))
    stacked = jnp.stack(got)
    return jnp.take(stacked, (me - jnp.arange(size, dtype=jnp.int32)) % size, axis=0)


def gather_small(value, axes):
    shape = value.shape
    for axis in reversed(axes):
        value = gather_axis(value, axis)
        value = value.reshape((-1,) + shape)
    return value


def fold_all(value, combine):
    for axis in reversed(ALL):
        size = lax.axis_size(axis)
        hop = 1
        while hop < size:
            other = lax.ppermute(value, axis, [(i, i ^ hop) for i in range(size)])
            value = combine(value, other)
            hop *= 2
    return value


def swap_core(value):
    return lax.ppermute(value, "core", [(0, 1), (1, 0)])


def add_logs(left, right):
    top = jnp.maximum(left, right)
    return top + jnp.log(jnp.exp(left - top) + jnp.exp(right - top))


def ffn_forward(resid, gain, w_in, w_out):
    normed = rms_scale(resid, gain).astype(bf16)
    both = project(normed, w_in)
    hidden = gate_up(both).astype(bf16)
    return (resid + project(hidden, w_out), (normed, both, hidden))


def ffn_backward(upstream, resid, gain, w_in, w_out, saved):
    normed, both, hidden = saved
    grad_b = upstream.astype(bf16)
    d_out = weight_grad(hidden, grad_b).astype(bf16)
    _, pull = jax.vjp(gate_up, both)
    (d_both,) = pull(input_grad(grad_b, w_out))
    d_both_b = d_both.astype(bf16)
    d_in = weight_grad(normed, d_both_b).astype(bf16)
    d_resid, d_gain = norm_pull(resid, gain, 1.0, input_grad(d_both_b, w_in))
    return (upstream + d_resid, d_gain, d_in, d_out)


def branch_backward(upstream, out_b, w_out):
    grad_b = upstream.astype(bf16)
    return (weight_grad(out_b, grad_b).astype(bf16), input_grad(grad_b, w_out).astype(bf16))


def adamw(weight, grad, first_m, second_m, count, rate, decay):
    first_new = 0.9 * first_m + 0.1 * grad
    second_new = 0.999 * second_m + 0.001 * grad * grad
    first_hat = first_new / (1.0 - 0.9**count)
    second_hat = second_new / (1.0 - 0.999**count)
    return (
        first_new,
        second_new,
        weight - rate * (first_hat / (jnp.sqrt(second_hat) + 1e-08) + decay * weight),
    )


def body(
    enc_ids,
    enc_segs,
    sentinel,
    mode,
    dec_ids,
    dec_segs,
    target_ids,
    target_mask,
    buckets,
    embed,
    attn_in,
    attn_out,
    ffn_in,
    ffn_out,
    rel_table,
    gains,
    m_embed,
    v_embed,
    m_attn_in,
    v_attn_in,
    m_attn_out,
    v_attn_out,
    m_ffn_in,
    v_ffn_in,
    m_ffn_out,
    v_ffn_out,
    m_rel,
    v_rel,
    m_gains,
    v_gains,
):
    core = lax.axis_index("core")
    z_at = lax.axis_index("z")
    z_size = lax.axis_size("z")
    plane_size = lax.axis_size(PLANE)
    device = lax.axis_index(ALL)
    shard = embed.shape[0]
    padded = -(-shard // 16) * 16
    enc_count, dec_count = enc_ids.shape[1], dec_ids.shape[1]
    enc_len, dec_len = enc_segs.shape[1], dec_segs.shape[1]

    table_b = jnp.pad(embed.astype(bf16), ((0, padded - shard), (0, 0)))
    plane_table = lax.all_gather(table_b, PLANE, axis=0, tiled=True)
    misc = jnp.concatenate([gains.T, rel_table.reshape(-1, 1)], axis=1)
    misc = jnp.pad(misc, ((0, 0), (0, 120)))
    shard_in = attn_in.shape[1]
    enc_pack = lax.all_gather(
        jnp.concatenate([attn_in[0], ffn_in[0], attn_out[0], misc], axis=1).astype(bf16),
        ALL,
        axis=0,
        tiled=True,
    )
    fo_pack = lax.all_gather(ffn_out.astype(bf16), ALL, axis=1, tiled=True)
    dec_pack = lax.all_gather(
        jnp.concatenate(
            [attn_in[1], attn_in[2], ffn_in[1], attn_out[1], attn_out[2]], axis=1
        ).astype(bf16),
        ALL,
        axis=0,
        tiled=True,
    )
    cut = lambda pack, start, width: lax.slice_in_dim(pack, start, start + width, axis=1)
    enc_wi, enc_fi = cut(enc_pack, 0, 3 * D), cut(enc_pack, 3 * D, 2 * FF)
    enc_wo, misc_all = cut(enc_pack, 3 * D + 2 * FF, D), cut(enc_pack, 4 * D + 2 * FF, 128)
    dec_wi, cross_wi = cut(dec_pack, 0, 3 * D), cut(dec_pack, 3 * D, 3 * D)
    dec_fi = cut(dec_pack, 6 * D, 2 * FF)
    dec_wo, cross_wo = cut(dec_pack, 6 * D + 2 * FF, D), cut(dec_pack, 7 * D + 2 * FF, D)
    enc_fo, dec_fo = fo_pack[0], fo_pack[1]
    gain = misc_all[:, :7].T.astype(f32)
    rel_all = jnp.transpose(misc_all[:, 7].reshape(-1, 2, rel_table.shape[1]), (1, 0, 2))
    rel_all = rel_all.reshape(2, BUCKETS, HEADS)

    flat = jnp.concatenate(
        [
            enc_ids[0],
            sentinel[0],
            dec_ids[0],
            target_ids[0],
            target_mask[0],
            enc_segs[0],
            dec_segs[0],
            jnp.pad(mode[0], (0, 128 - mode.shape[1])),
        ]
    )
    flat = lax.ppermute(flat, ("core", "seq"), [(0, 0), (1, 2), (2, 1), (3, 3)])
    sizes = [enc_count, enc_count, dec_count, dec_count, dec_count, enc_len, dec_len]
    pieces, start = [], 0
    for size in sizes:
        pieces.append(flat[start : start + size])
        start += size
    enc_id, sent, dec_id, targets, mask_i, enc_seg_all, dec_seg_all = pieces
    mode_row = flat[start : start + mode.shape[1]]
    mask = mask_i.astype(f32)

    enc_seg = lax.dynamic_slice_in_dim(enc_seg_all, core * enc_count, enc_count)
    enc_seg_other = lax.dynamic_slice_in_dim(enc_seg_all, (1 - core) * enc_count, enc_count)
    dec_seg = lax.dynamic_slice_in_dim(dec_seg_all, core * dec_count, dec_count)
    dec_seg_other = lax.dynamic_slice_in_dim(dec_seg_all, (1 - core) * dec_count, dec_count)
    enc_range = jnp.arange(enc_count, dtype=jnp.int32)
    dec_range = jnp.arange(dec_count, dtype=jnp.int32)
    enc_pos, enc_pos_other = core * enc_count + enc_range, (1 - core) * enc_count + enc_range
    dec_pos, dec_pos_other = core * dec_count + dec_range, (1 - core) * dec_count + dec_range
    prior_all = jnp.concatenate([enc_seg_all[:1], enc_seg_all[:-1]])
    prior = lax.dynamic_slice_in_dim(prior_all, core * enc_count, enc_count)
    first = (enc_pos == 0) | (enc_seg != prior)
    mode_of = jnp.sum(
        jnp.where(
            enc_seg[:, None] == jnp.arange(mode.shape[1], dtype=jnp.int32)[None], mode_row[None], 0
        ),
        axis=1,
    )
    enc_tok = jnp.where(sent == 1, V - 1 - enc_seg, enc_id)
    enc_tok = jnp.where(first, V - 101 - mode_of, enc_tok)
    local_ids = jnp.concatenate([enc_tok, dec_id])

    line_ids = gather_small(local_ids, ("z",))
    line_flat = line_ids.reshape(-1)
    plane_rows = plane_size * shard
    rel_id = line_flat - z_at * plane_rows
    inside = (rel_id >= 0) & (rel_id < plane_rows)
    place = jnp.where(inside, (rel_id // shard) * padded + rel_id % shard, -1)
    got = jnp.take(plane_table, jnp.maximum(place, 0), axis=0)
    got = jnp.where(inside[:, None], got, jnp.zeros((), bf16))
    looked = lax.psum_scatter(got, "z", scatter_dimension=0, tiled=True).astype(f32)
    enc_x0, dec_y0 = looked[:enc_count], looked[enc_count:]

    enc_x8, enc_picks = bias_eights(rel_all[0], buckets[0], core, enc_count, enc_count)
    dec_x8, dec_picks = bias_eights(rel_all[1], buckets[1], core, dec_count, dec_count)
    col, line = (lambda v: v[:, None]), (lambda v: v[None, :])
    enc_info = (
        col(enc_seg), line(enc_seg), line(enc_seg_other),
        col(enc_pos), line(enc_pos), line(enc_pos_other),
    )
    dec_info = (
        col(dec_seg), line(dec_seg), line(dec_seg_other),
        col(dec_pos), line(dec_pos), line(dec_pos_other),
    )
    cross_info = (
        col(dec_seg), line(enc_seg), line(enc_seg_other),
        col(dec_pos), line(enc_pos), line(enc_pos_other),
    )

    enc_n1 = rms_scale(enc_x0, gain[0]).astype(bf16)
    enc_q = project(enc_n1, enc_wi[:, :D]).astype(bf16)
    enc_kv = project(enc_n1, enc_wi[:, D:]).astype(bf16)
    enc_kv2 = swap_core(enc_kv)
    enc_ob = attend_forward(enc_q, enc_kv, enc_kv2, enc_info, enc_x8, False)
    enc_x1 = enc_x0 + project(enc_ob, enc_wo)
    enc_x2, enc_saved = ffn_forward(enc_x1, gain[1], enc_fi, enc_fo)
    enc_out = rms_scale(enc_x2, gain[2]).astype(bf16)

    dec_n1 = rms_scale(dec_y0, gain[3]).astype(bf16)
    dec_q = project(dec_n1, dec_wi[:, :D]).astype(bf16)
    dec_kv = project(dec_n1, dec_wi[:, D:]).astype(bf16)
    dec_kv2 = swap_core(dec_kv)
    dec_ob = attend_forward(dec_q, dec_kv, dec_kv2, dec_info, dec_x8, True)
    dec_y1 = dec_y0 + project(dec_ob, dec_wo)
    cross_kv = project(enc_out, cross_wi[:, D:]).astype(bf16)
    cross_kv2 = swap_core(cross_kv)
    cross_n = rms_scale(dec_y1, gain[4]).astype(bf16)
    cross_q = project(cross_n, cross_wi[:, :D]).astype(bf16)
    cross_ob = attend_forward(cross_q, cross_kv, cross_kv2, cross_info, None, False)
    dec_y2 = dec_y1 + project(cross_ob, cross_wo)
    dec_y3, dec_saved = ffn_forward(dec_y2, gain[5], dec_fi, dec_fo)
    head_scale = D ** (-0.5)
    hidden_b = (rms_scale(dec_y3, gain[6]) * head_scale).astype(bf16)

    hidden_all = lax.all_gather(hidden_b, ALL, axis=0, tiled=True)
    info = gather_small(jnp.stack([targets, mask_i]), ALL)
    targets_all = info[:, 0].reshape(1, -1) - device * shard
    mask_all = info[:, 1].reshape(1, -1).astype(f32)
    lse_part, picked = head_stats(hidden_all, table_b, targets_all, shard)
    lse = fold_all(lse_part, add_logs)
    d_hidden_all, head_embed = head_grad(
        hidden_all, table_b, targets_all, mask_all, lse, shard
    )
    d_hidden = lax.psum_scatter(d_hidden_all, ALL, scatter_dimension=0, tiled=True).astype(f32)
    lse_mine = lax.dynamic_slice_in_dim(lse[0], device * dec_count, dec_count)
    loss_local = jnp.sum(mask * lse_mine) - jnp.sum(mask_all * picked)

    d_y3, d_gain_final = norm_pull(dec_y3, gain[6], head_scale, d_hidden)
    d_y2, d_gain_dffn, d_dec_fi, d_dec_fo = ffn_backward(
        d_y3, dec_y2, gain[5], dec_fi, dec_fo, dec_saved
    )
    d_cross_wo, d_cross_ob = branch_backward(d_y2, cross_ob, cross_wo)
    d_cross_q, own, other = attend_backward(
        d_cross_ob, cross_q, cross_kv, cross_kv2, cross_info, None, False
    )
    got = (own + swap_core(other).astype(f32)).astype(bf16)
    d_cross_kv = jnp.concatenate([got[0], got[1]], axis=1)
    d_cross_wq = weight_grad(cross_n, d_cross_q)
    d_y1_norm, d_gain_cross = norm_pull(
        dec_y1, gain[4], 1.0, input_grad(d_cross_q, cross_wi[:, :D])
    )
    d_y1 = d_y2 + d_y1_norm
    d_cross_wkv = weight_grad(enc_out, d_cross_kv)
    d_dec_wo, d_dec_ob = branch_backward(d_y1, dec_ob, dec_wo)
    d_dec_q, own, other, dec_y8 = attend_backward(
        d_dec_ob, dec_q, dec_kv, dec_kv2, dec_info, dec_x8, True
    )
    got = (own + swap_core(other).astype(f32)).astype(bf16)
    d_dec_qkv = jnp.concatenate([d_dec_q, got[0], got[1]], axis=1)
    d_dec_table = bias_gradient(dec_y8, dec_picks, core, dec_count, dec_count)
    d_dec_wi = weight_grad(dec_n1, d_dec_qkv)
    d_y0_norm, d_gain_datt = norm_pull(dec_y0, gain[3], 1.0, input_grad(d_dec_qkv, dec_wi))
    d_y0 = d_y1 + d_y0_norm
    dec_grads = lax.psum_scatter(
        jnp.concatenate(
            [
                d_dec_wi.astype(bf16),
                d_cross_wq.astype(bf16),
                d_cross_wkv.astype(bf16),
                d_dec_fi,
                d_dec_wo,
                d_cross_wo,
            ],
            axis=1,
        ),
        ALL,
        scatter_dimension=0,
        tiled=True,
    ).astype(f32)

    d_x2, d_gain_efin = norm_pull(
        enc_x2, gain[2], 1.0, input_grad(d_cross_kv, cross_wi[:, D:])
    )
    d_x1, d_gain_effn, d_enc_fi, d_enc_fo = ffn_backward(
        d_x2, enc_x1, gain[1], enc_fi, enc_fo, enc_saved
    )
    fo_grads = lax.psum_scatter(
        jnp.stack([d_enc_fo, d_dec_fo]), ALL, scatter_dimension=1, tiled=True
    ).astype(f32)
    d_enc_wo, d_enc_ob = branch_backward(d_x1, enc_ob, enc_wo)
    d_enc_q, own, other, enc_y8 = attend_backward(
        d_enc_ob, enc_q, enc_kv, enc_kv2, enc_info, enc_x8, False
    )
    got = (own + swap_core(other).astype(f32)).astype(bf16)
    d_enc_qkv = jnp.concatenate([d_enc_q, got[0], got[1]], axis=1)
    d_enc_table = bias_gradient(enc_y8, enc_picks, core, enc_count, enc_count)
    d_enc_wi = weight_grad(enc_n1, d_enc_qkv)
    d_x0_norm, d_gain_eatt = norm_pull(enc_x0, gain[0], 1.0, input_grad(d_enc_qkv, enc_wi))
    d_x0 = d_x1 + d_x0_norm

    d_inputs = jnp.concatenate([d_x0, d_y0]).astype(bf16)
    d_line = lax.all_gather(d_inputs, "z", axis=0, tiled=True)
    placed = place_rows(place[None, :], d_line, plane_size, padded)
    input_embed = lax.psum_scatter(placed, PLANE, scatter_dimension=0, tiled=True)
    grad_embed = head_embed[:shard] + input_embed[:shard].astype(f32)

    d_gains = jnp.stack(
        [
            d_gain_eatt,
            d_gain_effn,
            d_gain_efin,
            d_gain_datt,
            d_gain_cross,
            d_gain_dffn,
            d_gain_final,
        ]
    )
    d_rel = jnp.stack([d_enc_table.reshape(-1), d_dec_table.reshape(-1)])
    d_rel = jnp.transpose(d_rel.reshape(2, -1, rel_table.shape[1]), (1, 0, 2)).reshape(D, 1)
    d_misc = jnp.pad(jnp.concatenate([d_gains.T, d_rel], axis=1), ((0, 0), (0, 120)))
    enc_grads = lax.psum_scatter(
        jnp.concatenate([d_enc_wi.astype(bf16), d_enc_fi, d_enc_wo, d_misc.astype(bf16)], axis=1),
        ALL,
        scatter_dimension=0,
        tiled=True,
    ).astype(f32)
    owned = (
        jnp.stack(
            [cut(enc_grads, 0, 3 * D), cut(dec_grads, 0, 3 * D), cut(dec_grads, 3 * D, 3 * D)]
        ),
        jnp.stack(
            [
                cut(enc_grads, 3 * D + 2 * FF, D),
                cut(dec_grads, 6 * D + 2 * FF, D),
                cut(dec_grads, 7 * D + 2 * FF, D),
            ]
        ),
        jnp.stack([cut(enc_grads, 3 * D, 2 * FF), cut(dec_grads, 6 * D, 2 * FF)]),
        fo_grads,
        enc_grads[:, 4 * D + 2 * FF + 7].reshape(2, -1),
        enc_grads[:, 4 * D + 2 * FF : 4 * D + 2 * FF + 7].T,
    )
    grads = (grad_embed,) + owned
    squares = sum((jnp.sum(item * item) for item in grads))
    sums = fold_all(jnp.stack([jnp.sum(mask), loss_local, squares]), jnp.add)
    count_all, loss_all, squares_all = sums[0], sums[1], sums[2]
    grad_norm = jnp.sqrt(squares_all) / count_all
    factor = jnp.minimum(1.0, clip_limit / grad_norm) / count_all
    weights = (embed, attn_in, attn_out, ffn_in, ffn_out, rel_table, gains)
    moments = [
        (m_embed, v_embed),
        (m_attn_in, v_attn_in),
        (m_attn_out, v_attn_out),
        (m_ffn_in, v_ffn_in),
        (m_ffn_out, v_ffn_out),
        (m_rel, v_rel),
        (m_gains, v_gains),
    ]
    settings = [
        (1.0, 0.01),
        (0.05, 0.01),
        (0.05, 0.01),
        (0.05, 0.01),
        (0.05, 0.01),
        (0.3, 0.0),
        (0.3, 0.0),
    ]
    results = [loss_all / count_all, grad_norm]
    for slot_number, (param, grad, pair, setting) in enumerate(
        zip(weights, grads, moments, settings)
    ):
        clipped = grad * factor
        first_new, second_new, new_param = adamw(
            param, clipped, pair[0], pair[1], float(STEP), setting[0], setting[1]
        )
        results.extend((clipped if slot_number == 0 else first_new, second_new, new_param))
    return tuple(results)


def solution(mesh):
    rows = ("z", "p", "core")
    every = ALL
    inner = Mesh(mesh.devices.reshape(4, -1, 2, mesh.devices.shape[1]), ALL)
    mat = P(None, every, None)
    vec = P(None, every)
    emb = P(every, None)
    in_specs = (
        P(rows, "seq"),
        P(rows, None),
        P(rows, "seq"),
        P(rows, None),
        P(rows, "seq"),
        P(rows, None),
        P(rows, "seq"),
        P(rows, "seq"),
        P(),
        emb,
        mat,
        mat,
        mat,
        mat,
        vec,
        vec,
        emb,
        emb,
    ) + (mat,) * 8 + (vec,) * 4
    out_specs = (P(), P()) + (emb,) * 3 + (mat,) * 12 + (vec,) * 6
    return jax.shard_map(body, mesh=inner, in_specs=in_specs, out_specs=out_specs, check_vma=False)
```

time: 6300 us -> 1720 us (0.27)
  blocking collectives: 2450 us -> 0 us
  local copies, waits for them, and re-layouts: 2550 us -> 103 us
  waiting for transfers between devices: 214 us -> 1060 us
  matrix products: 499 us -> 135 us
  other arithmetic: 392 us -> 81.2 us
  Pallas kernels: 0 us -> 277 us
  loops' own time: 115 us -> 0 us
    unnamed x3 -> x0, blocking collectives: 2270 us -> none
    reshape x42 -> x2, local copies, waits for them, and re-layouts: 999 us -> 0.2 us  [the longest x1 0.11 us: body(): jnp.transpose(d_rel.reshape(2, -1, rel_table.shape[1]), (1, 0, 2))]
    another operation x56 -> x40, local copies, waits for them, and re-layouts: 699 us -> 27.6 us  [the longest x5 11.1 us: body(): jnp.stack([cut(enc_grads, 0, 3 * D), cut(dec_grads, 0, 3 * D), cut(dec_gr...]
    slice x189 -> x14, local copies, waits for them, and re-layouts: 516 us -> 6.32 us  [the longest x1 1.79 us: body(): hidden_b = (rms_scale(dec_y3, gain[6]) * head_scale).astype(bf16)]
    reduce_scatter x7 -> x4, waiting for transfers between devices: 0.04 us -> 375 us  [the longest x1 154 us: body(): lax.psum_scatter(d_hidden_all, ALL, scatter_dimension=0, tiled=True)]
    dot_general x156 -> x39, matrix products: 499 us -> 135 us  [the longest x11 55 us: input_grad(): return jnp.einsum('te,de->td', grads, weight, preferred_element_type=f32)]
    unnamed x20 -> x14, waiting for transfers between devices: 1.5 us -> 307 us
    pallas_call x0 -> x9, Pallas kernels: none -> 277 us  [the longest x3 101 us: attend_backward(): pl.pallas_call(functools.partial(attend_backward_kernel, cfg), grid=(HEAD...]
  transfers between devices with their start and end apart: 20 -> 38, of which waited for: 2 -> 30; matrix products, arithmetic and copies ran while one was open for 86% -> 14% of each run, Pallas kernels for 0% -> 10%
where the time goes in v1:
time: 1720 us; the launch traced here: 1710 us
  waiting for transfers between devices  1060 us (62%)
  Pallas kernels  277 us (16%)
  matrix products  135 us (8%)
  local copies, waits for them, and re-layouts  103 us (6%)
  other arithmetic  81.2 us (5%)
  between operations  29.8 us (2%)
  starting transfers between devices  27.6 us (2%)
    unnamed x14, waiting for transfers between devices  307 us
    reduce_scatter x1, waiting for transfers between devices, body(): lax.psum_scatter(d_hidden_all, ALL, scatter_dimension=0, tiled=True)  154 us
    all_gather x1, waiting for transfers between devices, body(): lax.all_gather(jnp.concatenate([attn_in[1], attn_in[2], ffn_in[1], attn_o...  103 us
    pallas_call x3, Pallas kernels, attend_backward(): pl.pallas_call(functools.partial(attend_backward_kernel, cfg), grid=(HEAD...  101 us
    reduce_scatter x1, waiting for transfers between devices, body(): lax.psum_scatter(got, 'z', scatter_dimension=0, tiled=True).astype(f32)  79 us
    all_gather x1, waiting for transfers between devices, body(): hidden_all = lax.all_gather(hidden_b, ALL, axis=0, tiled=True)  74.6 us
    reduce_scatter x1, waiting for transfers between devices, body(): lax.psum_scatter(jnp.stack([d_enc_fo, d_dec_fo]), ALL, scatter_dimension=...  71.3 us
    reduce_scatter x1, waiting for transfers between devices, body(): lax.psum_scatter(placed, PLANE, scatter_dimension=0, tiled=True)  70.9 us
  transfers between devices with their start and end apart: 38, of which 30 were waited for; matrix products, arithmetic and copies ran while one was open for 14% of the time, Pallas kernels for 10%

profile of v1, /device:TPU:0, one launch (start us, length us, event | category | flops | bytes accessed | tf_op | source)
XLA Modules:
  0.0 1713.0 jit_solution(11895068985407769794)
XLA Ops:
  15.8 5.0 collective-permute-start.3
  27.4 57.3 %all-gather.7.cloned.1.call-done = bf16[8064,768]{1,0:T(8,128)(2,1)} async-done(((bf16[1008,768]{1,0:T(8,128)(2,1)}), bf16[8064,768]{1,0:T(8,128)(2,1)}) %all-gather.7.cloned.1.call-update) | async-done | bytes 12386320 | tf_op jit(solution)/shard_map/all_gather | solution.py:498
  84.7 20.7 %gather_fusion.1 = bf16[3072,768]{1,0:T(8,128)(2,1)} fusion(bf16[8064,768]{1,0:T(8,128)(2,1)} %all-gather.7.cloned.1.call-done, s32[3072]{0:T(1024)S(1)} %broadcast_clamp_fusion), kind=kCustom, calls=%fused_computation.1 | custom fusion | bytes 9449472 | tf_op jit(solution)/shard_map/jit(_take)/gather | solution.py:577
  105.5 5.9 select_select_fusion
  118.2 59.9 %all-gather.9.cloned.1.call-done = bf16[768,7296]{1,0:T(8,128)(2,1)} async-done(((bf16[24,7296]{1,0:T(8,128)(2,1)}), bf16[768,7296]{1,0:T(8,128)(2,1)}) %all-gather.9.cloned.1.call-update) | async-done | bytes 11206672 | tf_op jit(solution)/shard_map/all_gather | solution.py:502
  185.2 79.0 %reduce-scatter.11.cloned.1.call-done = bf16[768,768]{1,0:T(8,128)(2,1)} async-done(((bf16[3072,768]{1,0:T(8,128)(2,1)}), bf16[768,768]{1,0:T(8,128)(2,1)}) %reduce-scatter.11.cloned.1.call-update) | async-done | bytes 1179664 | tf_op jit(solution)/shard_map/reduce_scatter | solution.py:579
  267.2 4.5 convolution_convert_fusion.8.refs_1_.refs_2_
  274.8 103.4 %all-gather.11.cloned.1.call-done = bf16[768,10240]{1,0:T(8,128)(2,1)} async-done(((bf16[24,10240]{1,0:T(8,128)(2,1)}), bf16[768,10240]{1,0:T(8,128)(2,1)}) %all-gather.11.cloned.1.call-update) | async-done | bytes 15728656 | tf_op jit(solution)/shard_map/all_gather | solution.py:509
  384.1 28.8 %shard_map.462 = bf16[512,768]{1,0:T(8,128)(2,1)} custom-call(bf16[512,768]{1,0:T(8,128)(2,1)} %convolution_convert_fusion.15.refs_0_, bf16[512,1536]{1,0:T(8,128)(2,1)} %convolution_convert_fusion.8.refs_1_.refs_2_, bf16[512,1536]{1,0:T(8,128)(2,1)} %convolution_convert_fusion.8.refs_1_.refs_2_, bf16[512,1536]{1,0:T(8,128)(2,1)} %collective-permute-done.5.refs_3_.refs_4_, ...), custom_call_target="tpu_custom_call" | custom-call | flops 1610612736 | bytes 15728640 | tf_op jit(solution)/shard_map/pallas_call | solution.py:203
  415.3 6.2 fusion.9
  421.6 3.2 copy-done.14
  427.2 22.0 %all-gather.13.cloned.1.call-done = bf16[2,2048,768]{2,1,0:T(8,128)(2,1)} async-done(((bf16[2,64,768]{2,1,0:T(8,128)(2,1)}), bf16[2,2048,768]{2,1,0:T(8,128)(2,1)}) %all-gather.13.cloned.1.call-update) | async-done | bytes 6291472 | tf_op jit(solution)/shard_map/all_gather | solution.py:508
  449.2 4.9 multiply_reduce_fusion.7
  454.1 4.9 convolution_convert_fusion.7.refs_1_.refs_2_
  469.7 14.3 shard_map.461
  488.8 12.0 shard_map.463
  503.0 4.9 fusion.5
  526.7 3.3 collective-permute-done.11
  533.0 74.6 %all-gather.15.cloned.1.call-done.hid = bf16[8192,768]{1,0:T(8,128)(2,1)} async-done(((bf16[256,768]{1,0:T(8,128)(2,1)}), bf16[8192,768]{1,0:T(8,128)(2,1)}) %all-gather.15.cloned.1.call-update) | async-done | bytes 12582928 | tf_op jit(solution)/shard_map/all_gather | solution.py:623
  607.7 25.2 %shard_map.464 = (f32[1,8192]{1,0:T(1,128)}, f32[1,8192]{1,0:T(1,128)}) custom-call(bf16[8192,768]{1,0:T(8,128)(2,1)} %all-gather.15.cloned.1.call-done.hid, bf16[1008,768]{1,0:T(8,128)(2,1)} %pad.200.tab, s32[1,8192]{1,0:T(1,128)} %bitcast.594), custom_call_target="tpu_custom_call" | custom-call | flops 12683575296 | bytes 12582912 | tf_op jit(solution)/shard_map/pallas_call | solution.py:310
  653.1 52.5 %shard_map.465 = (bf16[8192,768]{1,0:T(8,128)(2,1)}, f32[1008,768]{1,0:T(8,128)}) custom-call(bf16[8192,768]{1,0:T(8,128)(2,1)} %all-gather.15.cloned.1.call-done.hid, bf16[1008,768]{1,0:T(8,128)(2,1)} %pad.200.tab, s32[1,8192]{1,0:T(1,128)} %bitcast.595, f32[1,8192]{1,0:T(1,128)} %bitcast.562, f32[1,8192]{1,0:T(1,128)} %log_add_fusion.lse), custom_call_target="tpu_custom_call" | custom-call | flops 38050725888 | bytes 25165824 | tf_op jit(solution)/shard_map/pallas_call | solution.py:331
  705.7 154.1 %reduce-scatter.13.cloned.1.call-done = bf16[256,768]{1,0:T(8,128)(2,1)} async-done(((bf16[8192,768]{1,0:T(8,128)(2,1)}), bf16[256,768]{1,0:T(8,128)(2,1)}) %reduce-scatter.13.cloned.1.call-update) | async-done | bytes 393232 | tf_op jit(solution)/shard_map/reduce_scatter | solution.py:632
  861.7 5.5 fusion.73
  867.2 6.8 multiply_reduce_fusion.11
  877.3 21.9 %shard_map.466 = (bf16[256,768]{1,0:T(8,128)(2,1)}, f32[2,512,768]{2,1,0:T(8,128)}, bf16[2,512,768]{2,1,0:T(8,128)(2,1)}) custom-call(bf16[256,768]{1,0:T(8,128)(2,1)} %convolution_convert_fusion.18.refs_0_, bf16[512,1536]{1,0:T(8,128)(2,1)} %convolution_convert_fusion.7.refs_1_.refs_2_, bf16[512,1536]{1,0:T(8,128)(2,1)} %convolution_convert_fusion.7.refs_1_.refs_2_, ...), custom_call_target="tpu_custom_call" | custom-call | flops 2013265920 | bytes 14155776 | tf_op jit(solution)/shard_map/pallas_call | solution.py:229
  904.9 24.6 %shard_map.468 = (bf16[256,768]{1,0:T(8,128)(2,1)}, f32[2,256,768]{2,1,0:T(8,128)}, bf16[2,256,768]{2,1,0:T(8,128)(2,1)}, f32[1,2,12,8,512]{4,3,2,1,0:T(8,128)}) custom-call(bf16[256,768]{1,0:T(8,128)(2,1)} %convolution_convert_fusion.19.refs_0_, bf16[256,1536]{1,0:T(8,128)(2,1)} %copy-done.11, bf16[256,1536]{1,0:T(8,128)(2,1)} %copy-done.11, ...), custom_call_target="tpu_custom_call" | custom-call | flops 1006632960 | bytes 7864320 | tf_op jit(solution)/shard_map/pallas_call | solution.py:229
  936.1 4.0 multiply_reduce_fusion.1
  940.5 8.3 fusion.47
  948.9 9.8 multiply_reduce_fusion.2
  959.1 3.5 convolution_convert_fusion.14.refs_12_
  962.7 54.8 %shard_map.467 = (bf16[512,768]{1,0:T(8,128)(2,1)}, f32[2,512,768]{2,1,0:T(8,128)}, bf16[2,512,768]{2,1,0:T(8,128)(2,1)}, f32[2,2,12,8,768]{4,3,2,1,0:T(8,128)}) custom-call(bf16[512,768]{1,0:T(8,128)(2,1)} %convolution_convert_fusion.15.refs_0_, bf16[512,1536]{1,0:T(8,128)(2,1)} %convolution_convert_fusion.8.refs_1_.refs_2_, ...), custom_call_target="tpu_custom_call" | custom-call | flops 4026531840 | bytes 15728640 | tf_op jit(solution)/shard_map/pallas_call | solution.py:229
  1019.1 4.1 multiply_reduce_fusion.13
  1025.2 4.8 multiply_reduce_fusion.3
  1036.0 3.4 pad_maximum_fusion
  1058.2 9.8 convolution_convert_fusion
  1068.4 3.8 convolution_convert_fusion.3
  1072.2 4.8 fusion.1
  1079.7 4.1 fusion.11
  1088.2 4.6 fusion.2
  1097.4 23.0 %all-gather.17.cloned.1.call-done.grads = bf16[3072,768]{1,0:T(8,128)(2,1)} async-done(((bf16[768,768]{1,0:T(8,128)(2,1)}), bf16[3072,768]{1,0:T(8,128)(2,1)}) %all-gather.17.cloned.1.call-update) | async-done | bytes 4718608 | tf_op jit(solution)/shard_map/all_gather | solution.py:700
  1120.4 43.3 %shard_map.469 = bf16[8064,768]{1,0:T(8,128)(2,1)} custom-call(s32[1,3072]{1,0:T(1,128)} %fusion.135.ids, bf16[3072,768]{1,0:T(8,128)(2,1)} %all-gather.17.cloned.1.call-done.grads), custom_call_target="tpu_custom_call" | custom-call | flops 38050725888 | bytes 12386304 | tf_op jit(solution)/shard_map/pallas_call | solution.py:365
  1168.4 71.3 %reduce-scatter.17.cloned.1.call-done = bf16[2,64,768]{2,1,0:T(8,128)(2,1)} async-done(((bf16[2,2048,768]{2,1,0:T(8,128)(2,1)}), bf16[2,64,768]{2,1,0:T(8,128)(2,1)}) %reduce-scatter.17.cloned.1.call-update) | async-done | bytes 196624 | tf_op jit(solution)/shard_map/reduce_scatter | solution.py:685
  1241.4 143.1 %reduce-scatter.21.cloned.1.call-done = bf16[24,7296]{1,0:T(8,128)(2,1)} async-done(((bf16[768,7296]{1,0:T(8,128)(2,1)}), bf16[24,7296]{1,0:T(8,128)(2,1)}) %reduce-scatter.21.cloned.1.call-update) | async-done | bytes 350224
  1396.7 164.1 %reduce-scatter.19.cloned.1.call-done = bf16[24,10240]{1,0:T(8,128)(2,1)} async-done(((bf16[768,10240]{1,0:T(8,128)(2,1)}), bf16[24,10240]{1,0:T(8,128)(2,1)}) %reduce-scatter.19.cloned.1.call-update) | async-done | bytes 491536
  1570.3 3.3 slice_bitcast_fusion.13
  1584.5 70.9 %reduce-scatter.15.cloned.1.call-done = bf16[1008,768]{1,0:T(8,128)(2,1)} async-done(((bf16[8064,768]{1,0:T(8,128)(2,1)}), bf16[1008,768]{1,0:T(8,128)(2,1)}) %reduce-scatter.15.cloned.1.call-update) | async-done | bytes 1548304 | tf_op jit(solution)/shard_map/reduce_scatter | solution.py:702
  1690.2 3.5 multiply_subtract_fusion.1
  1699.2 4.5 add_subtract_fusion
  (773 shorter events, 230.9 us)
Async XLA Ops:
  7.2 77.5 %all-gather.7.cloned.1.call-start = ((), (), s32[]{:S(2)}) async-start(), calls=%async_computation.6 | async-start | bytes 13934592 | tf_op jit(solution)/shard_map/all_gather | solution.py:498
  10.7 167.4 %all-gather.9.cloned.1.call-start = ((), (), s32[]{:S(2)}) async-start(), calls=%async_computation.8 | async-start | bytes 11556864 | tf_op jit(solution)/shard_map/all_gather | solution.py:502
  12.2 252.0 %reduce-scatter.11.cloned.1.call-start = ((), (), s32[]{:S(2)}) async-start(), calls=%async_computation.7 | async-start | bytes 5898240 | tf_op jit(solution)/shard_map/reduce_scatter | solution.py:579
  12.4 0.7 collective-permute-start
  13.3 104.0 %copy-start.87 = (s32[512]{0:T(512)}, s32[512]{0:T(512)S(1)}, u32[]{:S(2)}) copy-start(s32[512]{0:T(512)S(1)} %dynamic_slice.44) | copy-start | bytes 6148
  15.8 6.4 collective-permute-start.3
  20.9 4.5 collective-permute-start.2
  20.9 5.4 collective-permute-start.1
  111.4 266.7 %all-gather.11.cloned.1.call-start = ((), (), s32[]{:S(2)}) async-start(), calls=%async_computation.9 | async-start | bytes 16220160 | tf_op jit(solution)/shard_map/all_gather | solution.py:509
  112.4 336.8 %all-gather.13.cloned.1.call-start = ((), (), s32[]{:S(2)}) async-start(), calls=%async_computation.10 | async-start | bytes 6488064 | tf_op jit(solution)/shard_map/all_gather | solution.py:508
  113.2 494.5 %all-gather.15.cloned.1.call-start = ((), (), s32[]{:S(2)}) async-start(), calls=%async_computation.11 | async-start | bytes 12976128 | tf_op jit(solution)/shard_map/all_gather | solution.py:623
  115.8 157.8 %copy-start.82 = (s32[1,2048]{1,0:T(1,128)}, s32[1,2048]{1,0:T(1,128)S(1)}, u32[]{:S(2)}) copy-start(s32[1,2048]{1,0:T(1,128)S(1)} %get-tuple-element.363) | copy-start | bytes 24580
  271.7 112.4 %collective-permute-start.5 = (bf16[512,1536]{1,0:T(8,128)(2,1)}, bf16[512,1536]{1,0:T(8,128)(2,1)}, u32[]{:S(2)}, u32[]{:S(2)}) collective-permute-start(bf16[512,1536]{1,0:T(8,128)(2,1)} %convolution_convert_fusion.8.refs_1_.refs_2_), channel_id=1, source_target_pairs={{0,2},{2,0},{1,3},{3,1},{4,6},{6,4},{5,7},{7,5},{8,10},{10,8},{9,1... | collective-permute-start | bytes 4718600 | tf_op jit(solution)/shard_map/ppermute | solution.py:411
  273.9 106.9 %copy-start.122 = (f32[256]{0:T(256)}, f32[256]{0:T(256)S(1)}, u32[]{:S(2)}) copy-start(f32[256]{0:T(256)S(1)} %multiply_reduce_fusion.20) | copy-start | bytes 3076
  273.9 106.9 %copy-start.128 = (f32[256]{0:T(256)}, f32[256]{0:T(256)S(1)}, u32[]{:S(2)}) copy-start(f32[256]{0:T(256)S(1)} %fusion.153) | copy-start | bytes 3076
  380.8 88.9 %collective-permute-start.4 = (bf16[256,1536]{1,0:T(8,128)(2,1)S(1)}, bf16[256,1536]{1,0:T(8,128)(2,1)}, u32[]{:S(2)}, u32[]{:S(2)}) collective-permute-start(bf16[256,1536]{1,0:T(8,128)(2,1)S(1)} %convolution_convert_fusion.9.refs_1_.refs_2_), channel_id=1, source_target_pairs={{0,2},{2,0},{1,3},{3,1},{4,6},{6,4},{5,7},{7,5},{8,10},{10,8},{9,1... | collective-permute-start | bytes 2359304 | tf_op jit(solution)/shard_map/ppermute | solution.py:411
  459.0 29.8 %collective-permute-start.6 = (bf16[512,1536]{1,0:T(8,128)(2,1)}, bf16[512,1536]{1,0:T(8,128)(2,1)}, u32[]{:S(2)}, u32[]{:S(2)}) collective-permute-start(bf16[512,1536]{1,0:T(8,128)(2,1)} %convolution_convert_fusion.7.refs_1_.refs_2_), channel_id=1, source_target_pairs={{0,2},{2,0},{1,3},{3,1},{4,6},{6,4},{5,7},{7,5},{8,10},{10,8},{9,1... | collective-permute-start | bytes 4718600 | tf_op jit(solution)/shard_map/ppermute | solution.py:411
  511.2 350.4 %copy-start.89 = (f32[256]{0:T(256)}, f32[256]{0:T(256)S(1)}, u32[]{:S(2)}) copy-start(f32[256]{0:T(256)S(1)} %fusion.156) | copy-start | bytes 3076
  512.2 347.6 %reduce-scatter.13.cloned.1.call-start = ((), (), s32[]{:S(2)}) async-start(), calls=%async_computation.12 | async-start | bytes 12976128 | tf_op jit(solution)/shard_map/reduce_scatter | solution.py:632
  512.4 3.7 collective-permute-start.7
  516.7 1.2 collective-permute-start.8
  518.5 3.7 collective-permute-start.9
  522.8 3.9 collective-permute-start.12
  524.6 5.4 collective-permute-start.11
  525.7 5.9 collective-permute-start.10
  632.9 4.1 collective-permute-start.13
  637.9 1.3 collective-permute-start.14
  639.3 4.0 collective-permute-start.15
  643.4 4.0 collective-permute-start.16
  647.5 4.9 collective-permute-start.17
  705.6 414.8 %all-gather.17.cloned.1.call-start = ((), (), s32[]{:S(2)}) async-start(), calls=%async_computation.13 | async-start | bytes 5898240 | tf_op jit(solution)/shard_map/all_gather | solution.py:700
  899.2 30.9 %collective-permute-start.18 = (bf16[2,512,768]{2,1,0:T(8,128)(2,1)}, bf16[2,512,768]{2,1,0:T(8,128)(2,1)S(1)}, u32[]{:S(2)}, u32[]{:S(2)}) collective-permute-start(bf16[2,512,768]{2,1,0:T(8,128)(2,1)} %get-tuple-element.43), channel_id=1, source_target_pairs={{0,2},{2,0},{1,3},{3,1},{4,6},{6,4},{5,7},{7,5},{8,10},{10,8},{9,1... | collective-permute-start | bytes 4718600 | tf_op jit(solution)/shard_map/ppermute | solution.py:411
  902.1 121.1 %copy-start.9 = (f32[256,768]{1,0:T(8,128)}, f32[256,768]{1,0:T(8,128)S(1)}, u32[]{:S(2)}) copy-start(f32[256,768]{1,0:T(8,128)S(1)} %fusion.69) | copy-start | bytes 2359300
  929.5 88.1 %collective-permute-start.20 = (bf16[2,256,768]{2,1,0:T(8,128)(2,1)}, bf16[2,256,768]{2,1,0:T(8,128)(2,1)}, u32[]{:S(2)}, u32[]{:S(2)}) collective-permute-start(bf16[2,256,768]{2,1,0:T(8,128)(2,1)} %get-tuple-element.50), channel_id=1, source_target_pairs={{0,2},{2,0},{1,3},{3,1},{4,6},{6,4},{5,7},{7,5},{8,10},{10,8},{9,1... | collective-permute-start | bytes 2359304 | tf_op jit(solution)/shard_map/ppermute | solution.py:411
  1017.5 5.9 collective-permute-start.19
  1031.6 208.2 %reduce-scatter.17.cloned.1.call-start = ((), (), s32[]{:S(2)}) async-start(), calls=%async_computation.15 | async-start | bytes 6488064 | tf_op jit(solution)/shard_map/reduce_scatter | solution.py:685
  1039.4 345.1 %reduce-scatter.21.cloned.1.call-start = ((), (), s32[]{:S(2)}) async-start(), calls=%async_computation.17 | async-start | bytes 11556864
  1077.1 483.7 %reduce-scatter.19.cloned.1.call-start = ((), (), s32[]{:S(2)}) async-start(), calls=%async_computation.16 | async-start | bytes 16220160
  1096.0 559.4 %reduce-scatter.15.cloned.1.call-start = ((), (), s32[]{:S(2)}) async-start(), calls=%async_computation.14 | async-start | bytes 13934592 | tf_op jit(solution)/shard_map/reduce_scatter | solution.py:702
  1573.6 81.7 %copy-start.13 = (f32[1008,768]{1,0:T(8,128)S(1)}, f32[1008,768]{1,0:T(8,128)}, u32[]{:S(2)}) copy-start(f32[1008,768]{1,0:T(8,128)} %get-tuple-element.40) | copy-start | bytes 9289732
  1584.5 102.0 %copy-start.107 = (f32[7,24]{1,0:T(8,128)S(1)}, f32[7,24]{1,0:T(8,128)}, u32[]{:S(2)}) copy-start(f32[7,24]{1,0:T(8,128)} %param.45) | copy-start | bytes 2020
  1584.5 102.0 %copy-start.142 = (f32[7,24]{1,0:T(8,128)S(1)}, f32[7,24]{1,0:T(8,128)}, u32[]{:S(2)}) copy-start(f32[7,24]{1,0:T(8,128)} %param.59) | copy-start | bytes 2020
  1584.5 102.0 %copy-start.143 = (f32[7,24]{1,0:T(8,128)S(1)}, f32[7,24]{1,0:T(8,128)}, u32[]{:S(2)}) copy-start(f32[7,24]{1,0:T(8,128)} %param.58) | copy-start | bytes 2020
  1663.4 3.5 collective-permute-start.21
  1667.7 1.1 collective-permute-start.22
  1669.5 3.5 collective-permute-start.23
  1673.1 3.5 collective-permute-start.24
  1676.6 4.4 collective-permute-start.25
  (170 other events, 1407.7 us)
Sparse Core Ops, SparseCore 0:
  10.7 73.9 all-gather.6
  88.3 89.7 all-gather.8
  180.4 83.7 reduce-scatter.10
  267.5 110.5 all-gather.10
  381.4 67.7 all-gather.12
  512.3 95.3 all-gather.14
  705.7 153.9 reduce-scatter.12
  1031.7 88.6 all-gather.16
  1127.0 112.7 reduce-scatter.16
  1245.8 138.6 reduce-scatter.20
  1391.6 169.1 reduce-scatter.18
  1564.8 90.5 reduce-scatter.14

commit v2 on v1

--- a/solution.py
+++ b/solution.py
@@ -278,7 +278,7 @@
 
 
 def head_stats_kernel(count, hid, tab, tgt, lse_out, pick_out):
-    logits = dot_nt(tab[...], hid[...])
+    logits = dot_nt(tab[...], hid[...].reshape(-1, D))
     row = lax.broadcasted_iota(jnp.int32, logits.shape, 0)
     pick_out[...] = jnp.sum(jnp.where(row == tgt[...], logits, 0.0), axis=0, keepdims=True)
     logits = jnp.where(row < count, logits, masked_out)
@@ -287,12 +287,13 @@
 
 
 def head_grad_kernel(count, hid, tab, tgt, msk, lse, dhid, dtab):
-    logits = dot_nt(tab[...], hid[...])
+    tokens = hid[...].reshape(-1, D)
+    logits = dot_nt(tab[...], tokens)
     row = lax.broadcasted_iota(jnp.int32, logits.shape, 0)
     soft = jnp.exp(jnp.where(row < count, logits, masked_out) - lse[...])
     grad = ((soft - jnp.where(row == tgt[...], 1.0, 0.0)) * msk[...]).astype(bf16)
-    dhid[...] = dot_tn(grad, tab[...]).astype(bf16)
-    term = dot_nn(grad, hid[...])
+    dhid[...] = dot_tn(grad, tab[...]).astype(bf16).reshape(dhid.shape)
+    term = dot_nn(grad, tokens)
 
     @pl.when(pl.program_id(0) == 0)
     def _():
@@ -304,15 +305,16 @@
 
 
 def head_stats(hidden, table, targets, count):
-    tokens, rows = hidden.shape[0], table.shape[0]
-    block = 512
-    line = pl.BlockSpec((1, block), lambda i: (0, i))
+    devices, each, _ = hidden.shape
+    tokens, rows = devices * each, table.shape[0]
+    steps = devices // 4
+    line = pl.BlockSpec((1, 2 * each), lambda h, i: (0, h * steps + i))
     return pl.pallas_call(
         functools.partial(head_stats_kernel, count),
-        grid=(tokens // block,),
+        grid=(2, steps),
         in_specs=[
-            pl.BlockSpec((block, D), lambda i: (i, 0)),
-            pl.BlockSpec((rows, D), lambda i: (0, 0)),
+            pl.BlockSpec((4, each // 2, D), lambda h, i: (i, h, 0)),
+            pl.BlockSpec((rows, D), lambda h, i: (0, 0)),
             line,
         ],
         out_specs=[line, line],
@@ -324,26 +326,27 @@
     )(hidden, table, targets)
 
 
-def head_grad(hidden, table, targets, mask, lse, count):
-    tokens, rows = hidden.shape[0], table.shape[0]
-    block = 512
-    line = pl.BlockSpec((1, block), lambda i: (0, i))
+def head_grad(hidden, table, targets, mask, lse, count, half):
+    devices, each, _ = hidden.shape
+    tokens, rows = devices * each // 2, table.shape[0]
+    steps = devices // 4
+    line = pl.BlockSpec((1, 2 * each), lambda i: (0, half * steps + i))
     return pl.pallas_call(
         functools.partial(head_grad_kernel, count),
-        grid=(tokens // block,),
+        grid=(steps,),
         in_specs=[
-            pl.BlockSpec((block, D), lambda i: (i, 0)),
+            pl.BlockSpec((4, each // 2, D), lambda i: (i, half, 0)),
             pl.BlockSpec((rows, D), lambda i: (0, 0)),
             line,
             line,
             line,
         ],
         out_specs=[
-            pl.BlockSpec((block, D), lambda i: (i, 0)),
+            pl.BlockSpec((4, each // 2, D), lambda i: (i, 0, 0)),
             pl.BlockSpec((rows, D), lambda i: (0, 0)),
         ],
         out_shape=[
-            jax.ShapeDtypeStruct((tokens, D), bf16),
+            jax.ShapeDtypeStruct((devices, each // 2, D), bf16),
             jax.ShapeDtypeStruct((rows, D), f32),
         ],
         compiler_params=pltpu.CompilerParams(vmem_limit_bytes=VMEM_LIMIT),
@@ -353,29 +356,37 @@
     )(hidden, table, targets, mask, lse)
 
 
-def place_kernel(ids, grads, out):
+def place_kernel(first, *refs):
+    out = refs[-1]
     rows = out.shape[0]
-    row = lax.broadcasted_iota(jnp.int32, (rows, ids.shape[1]), 0) + pl.program_id(0) * rows
-    hot = jnp.where(row == ids[...], 1.0, 0.0).astype(bf16)
-    out[...] = dot_nn(hot, grads[...]).astype(bf16)
-
-
-def place_rows(ids, grads, parts, rows):
-    tokens = grads.shape[0]
+    base = (pl.program_id(0) + first) * rows
+    total = None
+    for ids, grads in zip(refs[:-1:2], refs[1:-1:2]):
+        row = lax.broadcasted_iota(jnp.int32, (rows, ids.shape[1]), 0) + base
+        hot = jnp.where(row == ids[...], 1.0, 0.0).astype(bf16)
+        term = dot_nn(hot, grads[...])
+        total = term if total is None else total + term
+    out[...] = total.astype(bf16)
+
+
+def place_rows(pairs, first, parts, rows):
+    tokens = sum(grads.shape[0] for _, grads in pairs)
+    specs, args = [], []
+    for ids, grads in pairs:
+        specs.append(pl.BlockSpec(ids.shape, lambda i: (0, 0)))
+        specs.append(pl.BlockSpec(grads.shape, lambda i: (0, 0)))
+        args += [ids, grads]
     return pl.pallas_call(
-        place_kernel,
+        functools.partial(place_kernel, first),
         grid=(parts,),
-        in_specs=[
-            pl.BlockSpec((1, tokens), lambda i: (0, 0)),
-            pl.BlockSpec((tokens, D), lambda i: (0, 0)),
-        ],
+        in_specs=specs,
         out_specs=pl.BlockSpec((rows, D), lambda i: (i, 0)),
         out_shape=jax.ShapeDtypeStruct((parts * rows, D), bf16),
         compiler_params=pltpu.CompilerParams(vmem_limit_bytes=VMEM_LIMIT),
         cost_estimate=pl.CostEstimate(
             flops=2 * tokens * parts * rows * D, bytes_accessed=2 * parts * rows * D, transcendentals=0
         ),
-    )(ids, grads)
+    )(*args)
 
 
 def gather_axis(value, axis):
@@ -407,8 +418,102 @@
     return value
 
 
+def swap(value, axis):
+    return lax.ppermute(value, axis, [(0, 1), (1, 0)])
+
+
 def swap_core(value):
-    return lax.ppermute(value, "core", [(0, 1), (1, 0)])
+    return swap(value, "core")
+
+
+def add16(left, right):
+    return (left.astype(f32) + right.astype(f32)).astype(bf16)
+
+
+def pick(value, index, dim):
+    return lax.dynamic_index_in_dim(value, index, dim, keepdims=False)
+
+
+def scatter_pair(value, axis, dim):
+    if lax.axis_size(axis) != 2:
+        return lax.psum_scatter(value, axis, scatter_dimension=dim, tiled=False)
+    me = lax.axis_index(axis)
+    got = swap(pick(value, 1 - me, dim), axis)
+    return add16(pick(value, me, dim), got)
+
+
+def scatter_chain(value, seq_first):
+    sizes = tuple(lax.axis_size(axis) for axis in ALL)
+    value = value.reshape(sizes + (-1, value.shape[-1]))
+    value = scatter_pair(value, "core", 2)
+    if seq_first:
+        value = scatter_pair(scatter_pair(value, "seq", 2), "p", 1)
+    else:
+        value = scatter_pair(scatter_pair(value, "p", 1), "seq", 1)
+    size, me = sizes[0], lax.axis_index("z")
+    total = pick(value, me, 0).astype(f32)
+    for hop in range(1, size):
+        send = pick(value, (me + hop) % size, 0)
+        got = lax.ppermute(send, "z", [(i, (i + hop) % size) for i in range(size)])
+        total = total + got.astype(f32)
+    return total
+
+
+def line_gather(value, axis):
+    size = lax.axis_size(axis)
+    ups, downs = [value], [value]
+    for _ in range(1, size):
+        ups.append(lax.ppermute(ups[-1], axis, [(i, i + 1) for i in range(size - 1)]))
+        downs.append(lax.ppermute(downs[-1], axis, [(i + 1, i) for i in range(size - 1)]))
+    return [value] + [ups[k] + downs[size - k] for k in range(1, size)]
+
+
+def line_scatter(parts, axis):
+    size = lax.axis_size(axis)
+    up, down = None, None
+    for step in range(1, size):
+        far = size - step
+        send_up, send_down = parts[size - far], parts[far]
+        if up is not None:
+            send_up, send_down = send_up + up, send_down + down
+        up = lax.ppermute(send_up, axis, [(i, i + 1) for i in range(step)])
+        down = lax.ppermute(send_down, axis, [(size - 1 - i, size - 2 - i) for i in range(step)])
+    return parts[0].astype(f32) + up.astype(f32) + down.astype(f32)
+
+
+def plane_gather(table):
+    if lax.axis_size("p") != 2:
+        return lax.all_gather(table, PLANE, axis=0, tiled=True)
+    half = table.shape[0] // 2
+    by_seq, by_p = swap(table, "seq"), swap(table, "p")
+    far = [swap(by_p[:half], "seq"), swap(by_seq[half:], "p")]
+    mine = [table, by_seq, by_p] + far
+    return jnp.concatenate(mine + [swap_core(item) for item in mine])
+
+
+def plane_slot(owner):
+    if lax.axis_size("p") != 2:
+        return owner
+    other = owner ^ lax.axis_index(PLANE)
+    return ((other >> 1) & 1) * 4 + (other >> 2) * 2 + (other & 1)
+
+
+def plane_scatter(pairs, rows):
+    count = lax.axis_size(PLANE)
+    if lax.axis_size("p") != 2:
+        placed = place_rows(pairs, 0, count, rows)
+        return lax.psum_scatter(placed, PLANE, scatter_dimension=0, tiled=True).astype(f32)
+    away = swap_core(place_rows(pairs, 4, 4, rows))
+    home = place_rows(pairs, 0, 4, rows)
+    half = rows // 2
+    part = lambda first, last: add16(home[first:last], away[first:last])
+    got_low = swap(part(3 * rows, 3 * rows + half), "seq")
+    got_high = swap(part(3 * rows + half, 4 * rows), "p")
+    seq_high = add16(part(rows + half, 2 * rows), got_high)
+    p_low = add16(part(2 * rows, 2 * rows + half), got_low)
+    from_seq = swap(jnp.concatenate([part(rows, rows + half), seq_high]), "seq")
+    from_p = swap(jnp.concatenate([p_low, part(2 * rows + half, 3 * rows)]), "p")
+    return part(0, rows).astype(f32) + from_seq.astype(f32) + from_p.astype(f32)
 
 
 def add_logs(left, right):
@@ -490,37 +595,33 @@
     plane_size = lax.axis_size(PLANE)
     device = lax.axis_index(ALL)
     shard = embed.shape[0]
-    padded = -(-shard // 16) * 16
+    padded = (shard // 16 + 1) * 16
     enc_count, dec_count = enc_ids.shape[1], dec_ids.shape[1]
     enc_len, dec_len = enc_segs.shape[1], dec_segs.shape[1]
 
     table_b = jnp.pad(embed.astype(bf16), ((0, padded - shard), (0, 0)))
-    plane_table = lax.all_gather(table_b, PLANE, axis=0, tiled=True)
     misc = jnp.concatenate([gains.T, rel_table.reshape(-1, 1)], axis=1)
     misc = jnp.pad(misc, ((0, 0), (0, 120)))
     shard_in = attn_in.shape[1]
+    flat_out = ffn_out.astype(bf16).reshape(2, shard_in, -1)
+    enc_cast = jnp.concatenate([attn_in[0], ffn_in[0], attn_out[0], misc], axis=1).astype(bf16)
     enc_pack = lax.all_gather(
-        jnp.concatenate([attn_in[0], ffn_in[0], attn_out[0], misc], axis=1).astype(bf16),
-        ALL,
-        axis=0,
-        tiled=True,
-    )
-    fo_pack = lax.all_gather(ffn_out.astype(bf16), ALL, axis=1, tiled=True)
-    dec_pack = lax.all_gather(
-        jnp.concatenate(
-            [attn_in[1], attn_in[2], ffn_in[1], attn_out[1], attn_out[2]], axis=1
-        ).astype(bf16),
-        ALL,
-        axis=0,
-        tiled=True,
-    )
+        jnp.concatenate([enc_cast, flat_out[0]], axis=1), ALL, axis=0, tiled=True
+    )
+    dec_cast = jnp.concatenate(
+        [attn_in[1], attn_in[2], ffn_in[1], attn_out[1], attn_out[2]], axis=1
+    ).astype(bf16)
+    dec_cast = jnp.concatenate([dec_cast, flat_out[1]], axis=1)
+    dec_cast, _ = lax.optimization_barrier((dec_cast, enc_pack[0, 0]))
+    dec_pack = lax.all_gather(dec_cast, ALL, axis=0, tiled=True)
     cut = lambda pack, start, width: lax.slice_in_dim(pack, start, start + width, axis=1)
     enc_wi, enc_fi = cut(enc_pack, 0, 3 * D), cut(enc_pack, 3 * D, 2 * FF)
     enc_wo, misc_all = cut(enc_pack, 3 * D + 2 * FF, D), cut(enc_pack, 4 * D + 2 * FF, 128)
     dec_wi, cross_wi = cut(dec_pack, 0, 3 * D), cut(dec_pack, 3 * D, 3 * D)
     dec_fi = cut(dec_pack, 6 * D, 2 * FF)
     dec_wo, cross_wo = cut(dec_pack, 6 * D + 2 * FF, D), cut(dec_pack, 7 * D + 2 * FF, D)
-    enc_fo, dec_fo = fo_pack[0], fo_pack[1]
+    enc_fo = cut(enc_pack, 4 * D + 2 * FF + 128, FF).reshape(FF, D)
+    dec_fo = cut(dec_pack, 8 * D + 2 * FF, FF).reshape(FF, D)
     gain = misc_all[:, :7].T.astype(f32)
     rel_all = jnp.transpose(misc_all[:, 7].reshape(-1, 2, rel_table.shape[1]), (1, 0, 2))
     rel_all = rel_all.reshape(2, BUCKETS, HEADS)
@@ -568,16 +669,21 @@
     enc_tok = jnp.where(first, V - 101 - mode_of, enc_tok)
     local_ids = jnp.concatenate([enc_tok, dec_id])
 
-    line_ids = gather_small(local_ids, ("z",))
-    line_flat = line_ids.reshape(-1)
+    plane_table = plane_gather(table_b)
+    line_ids = line_gather(local_ids, "z")
     plane_rows = plane_size * shard
-    rel_id = line_flat - z_at * plane_rows
-    inside = (rel_id >= 0) & (rel_id < plane_rows)
-    place = jnp.where(inside, (rel_id // shard) * padded + rel_id % shard, -1)
-    got = jnp.take(plane_table, jnp.maximum(place, 0), axis=0)
-    got = jnp.where(inside[:, None], got, jnp.zeros((), bf16))
-    looked = lax.psum_scatter(got, "z", scatter_dimension=0, tiled=True).astype(f32)
-    enc_x0, dec_y0 = looked[:enc_count], looked[enc_count:]
+    places = []
+    for ids in line_ids:
+        rel_id = ids - z_at * plane_rows
+        inside = (rel_id >= 0) & (rel_id < plane_rows)
+        places.append(
+            jnp.where(inside, plane_slot(rel_id // shard) * padded + rel_id % shard, shard)
+        )
+    enc_places = [item[:enc_count] for item in places]
+    dec_places = [item[enc_count:] for item in places]
+    look = lambda item: jnp.take(plane_table, item, axis=0, mode="clip")
+    enc_x0 = line_scatter([look(item) for item in enc_places], "z")
+    dec_y0 = line_scatter([look(item) for item in dec_places], "z")
 
     enc_x8, enc_picks = bias_eights(rel_all[0], buckets[0], core, enc_count, enc_count)
     dec_x8, dec_picks = bias_eights(rel_all[1], buckets[1], core, dec_count, dec_count)
@@ -621,17 +727,24 @@
     hidden_b = (rms_scale(dec_y3, gain[6]) * head_scale).astype(bf16)
 
     hidden_all = lax.all_gather(hidden_b, ALL, axis=0, tiled=True)
+    hidden_all = hidden_all.reshape(-1, dec_count, D)
     info = gather_small(jnp.stack([targets, mask_i]), ALL)
-    targets_all = info[:, 0].reshape(1, -1) - device * shard
-    mask_all = info[:, 1].reshape(1, -1).astype(f32)
+    info = jnp.transpose(info.reshape(-1, 2, 2, dec_count // 2), (1, 2, 0, 3)).reshape(2, 1, -1)
+    targets_all = info[0] - device * shard
+    mask_all = info[1].astype(f32)
     lse_part, picked = head_stats(hidden_all, table_b, targets_all, shard)
     lse = fold_all(lse_part, add_logs)
-    d_hidden_all, head_embed = head_grad(
-        hidden_all, table_b, targets_all, mask_all, lse, shard
-    )
-    d_hidden = lax.psum_scatter(d_hidden_all, ALL, scatter_dimension=0, tiled=True).astype(f32)
-    lse_mine = lax.dynamic_slice_in_dim(lse[0], device * dec_count, dec_count)
-    loss_local = jnp.sum(mask * lse_mine) - jnp.sum(mask_all * picked)
+    halves = [
+        head_grad(hidden_all, table_b, targets_all, mask_all, lse, shard, half) for half in range(2)
+    ]
+    head_embed = halves[0][1] + halves[1][1]
+    d_hidden = jnp.concatenate(
+        [scatter_chain(item[0], number == 0) for number, item in enumerate(halves)]
+    )
+    lse_mine = lax.dynamic_slice_in_dim(
+        lse.reshape(2, -1), device * (dec_count // 2), dec_count // 2, axis=1
+    )
+    loss_local = jnp.sum(mask * lse_mine.reshape(-1)) - jnp.sum(mask_all * picked)
 
     d_y3, d_gain_final = norm_pull(dec_y3, gain[6], head_scale, d_hidden)
     d_y2, d_gain_dffn, d_dec_fi, d_dec_fo = ffn_backward(
@@ -659,22 +772,20 @@
     d_dec_wi = weight_grad(dec_n1, d_dec_qkv)
     d_y0_norm, d_gain_datt = norm_pull(dec_y0, gain[3], 1.0, input_grad(d_dec_qkv, dec_wi))
     d_y0 = d_y1 + d_y0_norm
-    dec_grads = lax.psum_scatter(
-        jnp.concatenate(
-            [
-                d_dec_wi.astype(bf16),
-                d_cross_wq.astype(bf16),
-                d_cross_wkv.astype(bf16),
-                d_dec_fi,
-                d_dec_wo,
-                d_cross_wo,
-            ],
-            axis=1,
-        ),
-        ALL,
-        scatter_dimension=0,
-        tiled=True,
-    ).astype(f32)
+    d_dec_rest = jnp.concatenate(
+        [
+            d_dec_wi.astype(bf16),
+            d_cross_wq.astype(bf16),
+            d_cross_wkv.astype(bf16),
+            d_dec_wo,
+            d_cross_wo,
+        ],
+        axis=1,
+    )
+    g_dec_fi = scatter_chain(d_dec_fi, True)
+    g_dec_fo = scatter_chain(d_dec_fo, False)
+    g_dec_rest = scatter_chain(d_dec_rest, False)
+    dec_lines = line_gather(d_y0.astype(bf16), "z")
 
     d_x2, d_gain_efin = norm_pull(
         enc_x2, gain[2], 1.0, input_grad(d_cross_kv, cross_wi[:, D:])
@@ -682,9 +793,8 @@
     d_x1, d_gain_effn, d_enc_fi, d_enc_fo = ffn_backward(
         d_x2, enc_x1, gain[1], enc_fi, enc_fo, enc_saved
     )
-    fo_grads = lax.psum_scatter(
-        jnp.stack([d_enc_fo, d_dec_fo]), ALL, scatter_dimension=1, tiled=True
-    ).astype(f32)
+    g_enc_fi = scatter_chain(d_enc_fi, True)
+    g_enc_fo = scatter_chain(d_enc_fo, False)
     d_enc_wo, d_enc_ob = branch_backward(d_x1, enc_ob, enc_wo)
     d_enc_q, own, other, enc_y8 = attend_backward(
         d_enc_ob, enc_q, enc_kv, enc_kv2, enc_info, enc_x8, False
@@ -696,11 +806,14 @@
     d_x0_norm, d_gain_eatt = norm_pull(enc_x0, gain[0], 1.0, input_grad(d_enc_qkv, enc_wi))
     d_x0 = d_x1 + d_x0_norm
 
-    d_inputs = jnp.concatenate([d_x0, d_y0]).astype(bf16)
-    d_line = lax.all_gather(d_inputs, "z", axis=0, tiled=True)
-    placed = place_rows(place[None, :], d_line, plane_size, padded)
-    input_embed = lax.psum_scatter(placed, PLANE, scatter_dimension=0, tiled=True)
-    grad_embed = head_embed[:shard] + input_embed[:shard].astype(f32)
+    enc_lines = line_gather(d_x0.astype(bf16), "z")
+    far_place = lambda item: jnp.where(item == shard, -1, item)[None, :]
+    pairs = [
+        (far_place(item), grads)
+        for item, grads in zip(enc_places + dec_places, enc_lines + dec_lines)
+    ]
+    input_embed = plane_scatter(pairs, padded)
+    grad_embed = head_embed[:shard] + input_embed[:shard]
 
     d_gains = jnp.stack(
         [
@@ -716,27 +829,19 @@
     d_rel = jnp.stack([d_enc_table.reshape(-1), d_dec_table.reshape(-1)])
     d_rel = jnp.transpose(d_rel.reshape(2, -1, rel_table.shape[1]), (1, 0, 2)).reshape(D, 1)
     d_misc = jnp.pad(jnp.concatenate([d_gains.T, d_rel], axis=1), ((0, 0), (0, 120)))
-    enc_grads = lax.psum_scatter(
-        jnp.concatenate([d_enc_wi.astype(bf16), d_enc_fi, d_enc_wo, d_misc.astype(bf16)], axis=1),
-        ALL,
-        scatter_dimension=0,
-        tiled=True,
-    ).astype(f32)
+    g_enc_wi = scatter_chain(d_enc_wi.astype(bf16), True)
+    g_enc_rest = scatter_chain(
+        jnp.concatenate([d_enc_wo, d_misc.astype(bf16)], axis=1), False
+    )
     owned = (
+        jnp.stack([g_enc_wi, cut(g_dec_rest, 0, 3 * D), cut(g_dec_rest, 3 * D, 3 * D)]),
         jnp.stack(
-            [cut(enc_grads, 0, 3 * D), cut(dec_grads, 0, 3 * D), cut(dec_grads, 3 * D, 3 * D)]
+            [cut(g_enc_rest, 0, D), cut(g_dec_rest, 6 * D, D), cut(g_dec_rest, 7 * D, D)]
         ),
-        jnp.stack(
-            [
-                cut(enc_grads, 3 * D + 2 * FF, D),
-                cut(dec_grads, 6 * D + 2 * FF, D),
-                cut(dec_grads, 7 * D + 2 * FF, D),
-            ]
-        ),
-        jnp.stack([cut(enc_grads, 3 * D, 2 * FF), cut(dec_grads, 6 * D, 2 * FF)]),
-        fo_grads,
-        enc_grads[:, 4 * D + 2 * FF + 7].reshape(2, -1),
-        enc_grads[:, 4 * D + 2 * FF : 4 * D + 2 * FF + 7].T,
+        jnp.stack([g_enc_fi, g_dec_fi]),
+        jnp.stack([g_enc_fo, g_dec_fo]),
+        g_enc_rest[:, D + 7].reshape(2, -1),
+        g_enc_rest[:, D : D + 7].T,
     )
     grads = (grad_embed,) + owned
     squares = sum((jnp.sum(item * item) for item in grads))

time: 1720 us -> 1540 us (0.90)
  waiting for transfers between devices: 1060 us -> 488 us
  starting transfers between devices: 27.6 us -> 209 us
  local copies, waits for them, and re-layouts: 103 us -> 254 us
  other arithmetic: 81.2 us -> 149 us
  matrix products: 135 us -> 116 us
    reduce_scatter x4 -> x0, waiting for transfers between devices: 375 us -> none  [the longest x1 154 us: body(): lax.psum_scatter(d_hidden_all, ALL, scatter_dimension=0, tiled=True)]
    ppermute x6 -> x104, waiting for transfers between devices: 0.02 us -> 375 us  [the longest x47 216 us: swap(): return lax.ppermute(value, axis, [(0, 1), (1, 0)])]
    unnamed x14 -> x3, waiting for transfers between devices: 307 us -> 0.05 us
    all_gather x5 -> x2, waiting for transfers between devices: 266 us -> 0.04 us  [the longest x1 0.02 us: body(): lax.all_gather(jnp.concatenate([enc_cast, flat_out[0]], axis=1), ALL, axi...]
    ppermute x6 -> x104, starting transfers between devices: 1.37 us -> 192 us  [the longest x47 58.7 us: swap(): return lax.ppermute(value, axis, [(0, 1), (1, 0)])]
    convert_element_type x4 -> x33, other arithmetic: 2.77 us -> 54.9 us  [the longest x29 51.6 us: add16(): return (left.astype(f32) + right.astype(f32)).astype(bf16)]
    gather x1 -> x8, local copies, waits for them, and re-layouts: 20.7 us -> 65.3 us  [body(): look = lambda item: jnp.take(plane_table, item, axis=0, mode='clip')]
    dynamic_slice x1 -> x17, local copies, waits for them, and re-layouts: 0.65 us -> 36.5 us  [pick(): return lax.dynamic_index_in_dim(value, index, dim, keepdims=False)]
  transfers between devices with their start and end apart: 38 -> 124, of which waited for: 30 -> 53; matrix products, arithmetic and copies ran while one was open for 14% -> 27% of each run, Pallas kernels for 10% -> 13%
where the time goes in v2:
time: 1540 us; the launch traced here: 1530 us
  waiting for transfers between devices  488 us (32%)
  Pallas kernels  285 us (19%)
  local copies, waits for them, and re-layouts  254 us (16%)
  starting transfers between devices  209 us (14%)
  other arithmetic  149 us (10%)
  matrix products  116 us (8%)
  between operations  30.2 us (2%)
    ppermute x47, waiting for transfers between devices, swap(): return lax.ppermute(value, axis, [(0, 1), (1, 0)])  216 us
    pallas_call x3, Pallas kernels, attend_backward(): pl.pallas_call(functools.partial(attend_backward_kernel, cfg), grid=(HEAD...  101 us
    ppermute x27, waiting for transfers between devices, scatter_chain(): got = lax.ppermute(send, 'z', [(i, (i + hop) % size) for i in range(size)])  77.8 us
    all_gather x1, waiting for transfers between devices, body(): hidden_all = lax.all_gather(hidden_b, ALL, axis=0, tiled=True)  75.7 us
    gather x8, local copies, waits for them, and re-layouts, body(): look = lambda item: jnp.take(plane_table, item, axis=0, mode='clip')  65.3 us
    unnamed x480, local copies, waits for them, and re-layouts  59.7 us
    ppermute x47, starting transfers between devices, swap(): return lax.ppermute(value, axis, [(0, 1), (1, 0)])  58.7 us
    pallas_call x2, Pallas kernels, head_grad(): pl.pallas_call(functools.partial(head_grad_kernel, count), grid=(steps,),...  56.3 us
  transfers between devices with their start and end apart: 124, of which 53 were waited for; matrix products, arithmetic and copies ran while one was open for 27% of the time, Pallas kernels for 13%

profile of v2, /device:TPU:0, one launch (start us, length us, event | category | flops | bytes accessed | tf_op | source)
XLA Modules:
  0.0 1531.4 jit_solution(11695873221305397983)
XLA Ops:
  56.9 18.5 %collective-permute-done.1 = bf16[1008,768]{1,0:T(8,128)(2,1)S(1)} collective-permute-done((bf16[1008,768]{1,0:T(8,128)(2,1)}, bf16[1008,768]{1,0:T(8,128)(2,1)S(1)}, u32[]{:S(2)}, u32[]{:S(2)}) %collective-permute-start.1) | collective-permute-done | bytes 1548320 | tf_op jit(solution)/shard_map/ppermute | solution.py:422
  75.4 23.7 %collective-permute-start.6 = (bf16[1008,768]{1,0:T(8,128)(2,1)S(1)}, bf16[1008,768]{1,0:T(8,128)(2,1)S(1)}, u32[]{:S(2)}, u32[]{:S(2)}) collective-permute-start(bf16[1008,768]{1,0:T(8,128)(2,1)S(1)} %collective-permute-done.1), channel_id=1, source_target_pairs={{0,2},{2,0},{1,3},{3,1},{4,6},{6,4},{5,7},{7,5},{8,10},{10,8},{9,1... | collective-permute-start | bytes 4644872 | tf_op jit(solution)/shard_map/ppermute | solution.py:422
  106.0 30.3 %collective-permute-done.3 = bf16[504,768]{1,0:T(8,128)(2,1)S(1)} collective-permute-done((bf16[504,768]{1,0:T(8,128)(2,1)S(1)}, bf16[504,768]{1,0:T(8,128)(2,1)S(1)}, u32[]{:S(2)}, u32[]{:S(2)}) %collective-permute-start.3) | collective-permute-done | bytes 774176 | tf_op jit(solution)/shard_map/ppermute | solution.py:422
  147.1 8.8 gather_fusion.7
  161.2 8.5 gather_fusion.5
  172.6 7.6 gather_fusion.3
  182.2 7.5 gather_fusion.1
  191.8 8.5 gather_fusion.6
  200.3 8.2 gather_fusion.2
  226.5 25.6 %collective-permute-done.17 = bf16[256,768]{1,0:T(8,128)(2,1)} collective-permute-done((bf16[256,768]{1,0:T(8,128)(2,1)}, bf16[256,768]{1,0:T(8,128)(2,1)}, u32[]{:S(2)}, u32[]{:S(2)}) %collective-permute-start.17) | collective-permute-done | bytes 393248 | tf_op jit(solution)/shard_map/ppermute | solution.py:479
  254.0 10.3 collective-permute-start.18
  269.4 8.4 collective-permute-start.25
  278.3 8.6 gather_fusion.4
  286.9 7.6 gather_fusion
  295.9 38.7 %collective-permute-done.28 = bf16[512,768]{1,0:T(8,128)(2,1)S(1)} collective-permute-done((bf16[512,768]{1,0:T(8,128)(2,1)}, bf16[512,768]{1,0:T(8,128)(2,1)S(1)}, u32[]{:S(2)}, u32[]{:S(2)}) %collective-permute-start.28) | collective-permute-done | bytes 786464 | tf_op jit(solution)/shard_map/ppermute | solution.py:480
  354.3 6.6 reshape.681
  365.0 28.7 %shard_map.462 = bf16[512,768]{1,0:T(8,128)(2,1)} custom-call(bf16[512,768]{1,0:T(8,128)(2,1)} %convolution_convert_fusion.15.refs_0_, bf16[512,1536]{1,0:T(8,128)(2,1)} %convolution_convert_fusion.8.refs_1_.refs_2_, bf16[512,1536]{1,0:T(8,128)(2,1)} %convolution_convert_fusion.8.refs_1_.refs_2_, bf16[512,1536]{1,0:T(8,128)(2,1)} %collective-permute-done.29.refs_3_.refs_4_, ...), custom_call_target="tpu_custom_call" | custom-call | flops 1610612736 | bytes 15728640 | tf_op jit(solution)/shard_map/pallas_call | solution.py:203
  396.2 6.2 fusion.12
  428.6 13.9 shard_map.461
  447.3 12.0 shard_map.463
  496.6 75.7 %all-gather.8.cloned.1.call-done = bf16[8192,768]{1,0:T(8,128)(2,1)} async-done(((bf16[256,768]{1,0:T(8,128)(2,1)}), bf16[8192,768]{1,0:T(8,128)(2,1)}) %all-gather.8.cloned.1.call-update) | async-done | bytes 12582928 | tf_op jit(solution)/shard_map/all_gather | solution.py:729
  572.2 25.5 %shard_map.464 = (f32[1,8192]{1,0:T(1,128)}, f32[1,8192]{1,0:T(1,128)}) custom-call(bf16[32,256,768]{2,1,0:T(8,128)(2,1)} %bitcast.854, bf16[1008,768]{1,0:T(8,128)(2,1)} %get-tuple-element.317.tab, s32[1,8192]{1,0:T(1,128)} %bitcast.811), custom_call_target="tpu_custom_call" | custom-call | flops 12683575296 | bytes 12582912 | tf_op jit(solution)/shard_map/pallas_call | solution.py:312
  619.8 27.9 %shard_map.466 = (bf16[32,128,768]{2,1,0:T(8,128)(2,1)}, f32[1008,768]{1,0:T(8,128)}) custom-call(bf16[32,256,768]{2,1,0:T(8,128)(2,1)} %bitcast.855, bf16[1008,768]{1,0:T(8,128)(2,1)} %get-tuple-element.317.tab, s32[1,8192]{1,0:T(1,128)} %bitcast.812, f32[1,8192]{1,0:T(1,128)} %bitcast.788, f32[1,8192]{1,0:T(1,128)} %get-tuple-element.284.lse), custom_call_target="tpu_custom_call" | custom-call | flops 19025362944 | bytes 12582912 | tf_op jit(solution)/shard_map/pallas_call | solution.py:334
  653.1 28.3 %shard_map.465 = (bf16[32,128,768]{2,1,0:T(8,128)(2,1)}, f32[1008,768]{1,0:T(8,128)}) custom-call(bf16[32,256,768]{2,1,0:T(8,128)(2,1)} %bitcast.856, bf16[1008,768]{1,0:T(8,128)(2,1)} %get-tuple-element.317.tab, s32[1,8192]{1,0:T(1,128)} %bitcast.813, f32[1,8192]{1,0:T(1,128)} %bitcast.789, f32[1,8192]{1,0:T(1,128)} %get-tuple-element.284.lse), custom_call_target="tpu_custom_call" | custom-call | flops 19025362944 | bytes 12582912 | tf_op jit(solution)/shard_map/pallas_call | solution.py:334
  703.6 27.0 %collective-permute-done.49 = bf16[4,2,128,768]{3,2,0,1:T(8,128)(2,1)} collective-permute-done((bf16[4,2,128,768]{3,2,0,1:T(8,128)(2,1)}, bf16[4,2,128,768]{3,2,0,1:T(8,128)(2,1)}, u32[]{:S(2)}, u32[]{:S(2)}) %collective-permute-start.49) | collective-permute-done | bytes 1572896 | tf_op jit(solution)/shard_map/ppermute | solution.py:422
  748.0 6.3 collective-permute-done.50
  764.2 8.2 collective-permute-start.45
  772.4 12.6 collective-permute-done.52
  785.1 6.2 collective-permute-done.46
  809.8 21.9 %shard_map.467 = (bf16[256,768]{1,0:T(8,128)(2,1)}, f32[2,512,768]{2,1,0:T(8,128)}, bf16[2,512,768]{2,1,0:T(8,128)(2,1)}) custom-call(bf16[256,768]{1,0:T(8,128)(2,1)} %convolution_convert_fusion.18.refs_0_, bf16[512,1536]{1,0:T(8,128)(2,1)} %convolution_convert_fusion.7.refs_1_.refs_2_, bf16[512,1536]{1,0:T(8,128)(2,1)} %convolution_convert_fusion.7.refs_1_.refs_2_, ...), custom_call_target="tpu_custom_call" | custom-call | flops 2013265920 | bytes 14155776 | tf_op jit(solution)/shard_map/pallas_call | solution.py:229
  837.6 24.5 %shard_map.469 = (bf16[256,768]{1,0:T(8,128)(2,1)}, f32[2,256,768]{2,1,0:T(8,128)}, bf16[2,256,768]{2,1,0:T(8,128)(2,1)}, f32[1,2,12,8,512]{4,3,2,1,0:T(8,128)}) custom-call(bf16[256,768]{1,0:T(8,128)(2,1)} %convolution_convert_fusion.19.refs_0_, bf16[256,1536]{1,0:T(8,128)(2,1)} %convolution_convert_fusion.9.refs_1_.refs_2_, ...), custom_call_target="tpu_custom_call" | custom-call | flops 1006632960 | bytes 7864320 | tf_op jit(solution)/shard_map/pallas_call | solution.py:229
  891.0 9.1 collective-permute-done.64
  915.0 7.3 fusion.63
  922.3 9.9 multiply_reduce_fusion.2
  935.7 54.7 %shard_map.468 = (bf16[512,768]{1,0:T(8,128)(2,1)}, f32[2,512,768]{2,1,0:T(8,128)}, bf16[2,512,768]{2,1,0:T(8,128)(2,1)}, f32[2,2,12,8,768]{4,3,2,1,0:T(8,128)}) custom-call(bf16[512,768]{1,0:T(8,128)(2,1)} %convolution_convert_fusion.15.refs_0_, bf16[512,1536]{1,0:T(8,128)(2,1)} %convolution_convert_fusion.8.refs_1_.refs_2_, ...), custom_call_target="tpu_custom_call" | custom-call | flops 4026531840 | bytes 15728640 | tf_op jit(solution)/shard_map/pallas_call | solution.py:229
  1014.9 7.0 convolution_convert_fusion
  1146.7 10.1 collective-permute-done.106
  1179.1 11.6 collective-permute-done.90
  1196.4 13.9 collective-permute-done.109
  1252.8 23.6 %shard_map.471 = bf16[4032,768]{1,0:T(8,128)(2,1)} custom-call(s32[1,512]{1,0:T(1,128)} %bitcast.837, bf16[512,768]{1,0:T(8,128)(2,1)} %fusion.53.refs_1_, s32[1,512]{1,0:T(1,128)} %bitcast.833, bf16[512,768]{1,0:T(8,128)(2,1)} %add.1529.refs_3_, s32[1,512]{1,0:T(1,128)} %bitcast.831, bf16[512,768]{1,0:T(8,128)(2,1)} %add.1530.refs_5_, s32[1,512]{1,0:T(1,128)} %bitcast.835, ...), custom_call_target="tpu_custom_call" | custom-call | flops 19025362944 | bytes 6193152 | tf_op jit(solution)/shard_map/pallas_call | solution.py:379
  1276.5 23.7 %shard_map.470 = bf16[4032,768]{1,0:T(8,128)(2,1)} custom-call(s32[1,512]{1,0:T(1,128)} %bitcast.838, bf16[512,768]{1,0:T(8,128)(2,1)} %fusion.53.refs_1_, s32[1,512]{1,0:T(1,128)} %bitcast.834, bf16[512,768]{1,0:T(8,128)(2,1)} %add.1529.refs_3_, s32[1,512]{1,0:T(1,128)} %bitcast.832, bf16[512,768]{1,0:T(8,128)(2,1)} %add.1530.refs_5_, s32[1,512]{1,0:T(1,128)} %bitcast.836, ...), custom_call_target="tpu_custom_call" | custom-call | flops 19025362944 | bytes 6193152 | tf_op jit(solution)/shard_map/pallas_call | solution.py:379
  1306.0 8.5 collective-permute-done.76
  1327.8 6.6 collective-permute-done.102
  1341.0 55.7 %collective-permute-done.94 = bf16[4,24,4096]{2,1,0:T(8,128)(2,1)S(1)} collective-permute-done((bf16[4,24,4096]{2,1,0:T(8,128)(2,1)S(1)}, bf16[4,24,4096]{2,1,0:T(8,128)(2,1)S(1)}, u32[]{:S(2)}, u32[]{:S(2)}) %collective-permute-start.94) | collective-permute-done | bytes 786464 | tf_op jit(solution)/shard_map/ppermute | solution.py:422
  1406.6 7.6 collective-permute-done.96
  1419.9 14.2 collective-permute-done.82
  1437.0 8.4 collective-permute-done.72
  1454.3 19.8 %collective-permute-done.73 = bf16[1008,768]{1,0:T(8,128)(2,1)S(1)} collective-permute-done((bf16[1008,768]{1,0:T(8,128)(2,1)S(1)}, bf16[1008,768]{1,0:T(8,128)(2,1)S(1)}, u32[]{:S(2)}, u32[]{:S(2)}) %collective-permute-start.73) | collective-permute-done | bytes 1548320 | tf_op jit(solution)/shard_map/ppermute | solution.py:422
  (1079 shorter events, 657.3 us)
Async XLA Ops:
  7.2 330.2 %all-gather.4.cloned.1.call-start = ((), (), s32[]{:S(2)}) async-start(), calls=%async_computation | async-start | bytes 14800896 | tf_op jit(solution)/shard_map/all_gather | solution.py:608
  21.1 387.6 %all-gather.6.cloned.1.call-start = ((), (), s32[]{:S(2)}) async-start(), calls=%async_computation.1 | async-start | bytes 19464192 | tf_op jit(solution)/shard_map/all_gather | solution.py:616
  22.8 549.4 %all-gather.8.cloned.1.call-start = ((), (), s32[]{:S(2)}) async-start(), calls=%async_computation.2 | async-start | bytes 12976128 | tf_op jit(solution)/shard_map/all_gather | solution.py:729
  25.0 50.4 %collective-permute-start.1 = (bf16[1008,768]{1,0:T(8,128)(2,1)}, bf16[1008,768]{1,0:T(8,128)(2,1)S(1)}, u32[]{:S(2)}, u32[]{:S(2)}) collective-permute-start(bf16[1008,768]{1,0:T(8,128)(2,1)} %get-tuple-element.317.tab), channel_id=1, source_target_pairs={{0,1},{1,0},{2,3},{3,2},{4,5},{5,4},{6,7},{7,6},{8,9},{9,8},{10,11... | collective-permute-start | bytes 4644872 | tf_op jit(solution)/shard_map/ppermute | solution.py:422
  27.9 71.2 %collective-permute-start.2 = (bf16[1008,768]{1,0:T(8,128)(2,1)}, bf16[1008,768]{1,0:T(8,128)(2,1)S(1)}, u32[]{:S(2)}, u32[]{:S(2)}) collective-permute-start(bf16[1008,768]{1,0:T(8,128)(2,1)} %get-tuple-element.317.tab), channel_id=1, source_target_pairs={{0,4},{4,0},{1,5},{5,1},{2,6},{6,2},{3,7},{7,3},{8,12},{12,8},{9,1... | collective-permute-start | bytes 4644872 | tf_op jit(solution)/shard_map/ppermute | solution.py:422
  29.5 110.6 %collective-permute-start.5 = (bf16[1008,768]{1,0:T(8,128)(2,1)}, bf16[1008,768]{1,0:T(8,128)(2,1)}, u32[]{:S(2)}, u32[]{:S(2)}) collective-permute-start(bf16[1008,768]{1,0:T(8,128)(2,1)} %get-tuple-element.317.tab), channel_id=1, source_target_pairs={{0,2},{2,0},{1,3},{3,1},{4,6},{6,4},{5,7},{7,5},{8,10},{10,8},{9,1... | collective-permute-start | bytes 4644872 | tf_op jit(solution)/shard_map/ppermute | solution.py:422
  52.3 46.9 %collective-permute-start.12 = (s32[768]{0:T(1024)S(1)}, s32[768]{0:T(1024)S(1)}, u32[]{:S(2)}, u32[]{:S(2)}) collective-permute-start(s32[768]{0:T(1024)S(1)} %collective-permute-done.11), channel_id=1, source_target_pairs={{0,8},{8,16},{16,24},{1,9},{9,17},{17,25},{2,10},{10,18},{18,26},{... | collective-permute-start | bytes 9224 | tf_op jit(solution)/shard_map/ppermute | solution.py:466
  75.4 67.3 %collective-permute-start.6 = (bf16[1008,768]{1,0:T(8,128)(2,1)S(1)}, bf16[1008,768]{1,0:T(8,128)(2,1)S(1)}, u32[]{:S(2)}, u32[]{:S(2)}) collective-permute-start(bf16[1008,768]{1,0:T(8,128)(2,1)S(1)} %collective-permute-done.1), channel_id=1, source_target_pairs={{0,2},{2,0},{1,3},{3,1},{4,6},{6,4},{5,7},{7,5},{8,10},{10,8},{9,1... | collective-permute-start | bytes 4644872 | tf_op jit(solution)/shard_map/ppermute | solution.py:422
  99.1 44.8 %collective-permute-start.7 = (bf16[1008,768]{1,0:T(8,128)(2,1)S(1)}, bf16[1008,768]{1,0:T(8,128)(2,1)S(1)}, u32[]{:S(2)}, u32[]{:S(2)}) collective-permute-start(bf16[1008,768]{1,0:T(8,128)(2,1)S(1)} %collective-permute-done.2), channel_id=1, source_target_pairs={{0,2},{2,0},{1,3},{3,1},{4,6},{6,4},{5,7},{7,5},{8,10},{10,8},{9,1... | collective-permute-start | bytes 4644872 | tf_op jit(solution)/shard_map/ppermute | solution.py:422
  99.3 37.0 %collective-permute-start.3 = (bf16[504,768]{1,0:T(8,128)(2,1)S(1)}, bf16[504,768]{1,0:T(8,128)(2,1)S(1)}, u32[]{:S(2)}, u32[]{:S(2)}) collective-permute-start(bf16[504,768]{1,0:T(8,128)(2,1)S(1)} %slice.881), channel_id=1, source_target_pairs={{0,1},{1,0},{2,3},{3,2},{4,5},{5,4},{6,7},{7,6},{8,9},{9,8},{10,11... | collective-permute-start | bytes 2322440 | tf_op jit(solution)/shard_map/ppermute | solution.py:422
  101.9 36.2 %collective-permute-start.4 = (bf16[504,768]{1,0:T(8,128)(2,1)S(1)}, bf16[504,768]{1,0:T(8,128)(2,1)S(1)}, u32[]{:S(2)}, u32[]{:S(2)}) collective-permute-start(bf16[504,768]{1,0:T(8,128)(2,1)S(1)} %slice.882), channel_id=1, source_target_pairs={{0,4},{4,0},{1,5},{5,1},{2,6},{6,2},{3,7},{7,3},{8,12},{12,8},{9,1... | collective-permute-start | bytes 2322440 | tf_op jit(solution)/shard_map/ppermute | solution.py:422
  155.9 52.6 %collective-permute-start.23 = (bf16[512,768]{1,0:T(8,128)(2,1)S(1)}, bf16[512,768]{1,0:T(8,128)(2,1)}, u32[]{:S(2)}, u32[]{:S(2)}) collective-permute-start(bf16[512,768]{1,0:T(8,128)(2,1)S(1)} %gather_fusion.7), channel_id=1, source_target_pairs={{0,8},{1,9},{2,10},{3,11},{4,12},{5,13},{6,14},{7,15}} | collective-permute-start | bytes 2359304 | tf_op jit(solution)/shard_map/ppermute | solution.py:479
  169.7 38.8 %collective-permute-start.26 = (bf16[512,768]{1,0:T(8,128)(2,1)S(1)}, bf16[512,768]{1,0:T(8,128)(2,1)}, u32[]{:S(2)}, u32[]{:S(2)}) collective-permute-start(bf16[512,768]{1,0:T(8,128)(2,1)S(1)} %gather_fusion.5), channel_id=1, source_target_pairs={{24,16},{25,17},{26,18},{27,19},{28,20},{29,21},{30,22},{31,23}} | collective-permute-start | bytes 2359304 | tf_op jit(solution)/shard_map/ppermute | solution.py:480
  180.2 33.8 %collective-permute-start.16 = (bf16[256,768]{1,0:T(8,128)(2,1)S(1)}, bf16[256,768]{1,0:T(8,128)(2,1)}, u32[]{:S(2)}, u32[]{:S(2)}) collective-permute-start(bf16[256,768]{1,0:T(8,128)(2,1)S(1)} %gather_fusion.3), channel_id=1, source_target_pairs={{0,8},{1,9},{2,10},{3,11},{4,12},{5,13},{6,14},{7,15}} | collective-permute-start | bytes 1179656 | tf_op jit(solution)/shard_map/ppermute | solution.py:479
  211.1 53.7 %collective-permute-start.27 = (bf16[512,768]{1,0:T(8,128)(2,1)}, bf16[512,768]{1,0:T(8,128)(2,1)}, u32[]{:S(2)}, u32[]{:S(2)}) collective-permute-start(bf16[512,768]{1,0:T(8,128)(2,1)} %get-tuple-element.374), channel_id=1, source_target_pairs={{24,16},{16,8},{25,17},{17,9},{26,18},{18,10},{27,19},{19,11},{28,... | collective-permute-start | bytes 2359304 | tf_op jit(solution)/shard_map/ppermute | solution.py:480
  212.7 55.6 %collective-permute-start.24 = (bf16[512,768]{1,0:T(8,128)(2,1)}, bf16[512,768]{1,0:T(8,128)(2,1)S(1)}, u32[]{:S(2)}, u32[]{:S(2)}) collective-permute-start(bf16[512,768]{1,0:T(8,128)(2,1)} %get-tuple-element.373), channel_id=1, source_target_pairs={{0,8},{8,16},{1,9},{9,17},{2,10},{10,18},{3,11},{11,19},{4,12},{12... | collective-permute-start | bytes 2359304 | tf_op jit(solution)/shard_map/ppermute | solution.py:479
  216.8 35.3 %collective-permute-start.17 = (bf16[256,768]{1,0:T(8,128)(2,1)}, bf16[256,768]{1,0:T(8,128)(2,1)}, u32[]{:S(2)}, u32[]{:S(2)}) collective-permute-start(bf16[256,768]{1,0:T(8,128)(2,1)} %get-tuple-element.404), channel_id=1, source_target_pairs={{0,8},{8,16},{1,9},{9,17},{2,10},{10,18},{3,11},{11,19},{4,12},{12... | collective-permute-start | bytes 1179656 | tf_op jit(solution)/shard_map/ppermute | solution.py:479
  225.2 69.3 %collective-permute-start.21 = (bf16[256,768]{1,0:T(8,128)(2,1)}, bf16[256,768]{1,0:T(8,128)(2,1)S(1)}, u32[]{:S(2)}, u32[]{:S(2)}) collective-permute-start(bf16[256,768]{1,0:T(8,128)(2,1)} %add.1421), channel_id=1, source_target_pairs={{24,16},{16,8},{8,0},{25,17},{17,9},{9,1},{26,18},{18,10},{10,2},{... | collective-permute-start | bytes 1179656 | tf_op jit(solution)/shard_map/ppermute | solution.py:480
  254.0 40.7 %collective-permute-start.18 = (bf16[256,768]{1,0:T(8,128)(2,1)}, bf16[256,768]{1,0:T(8,128)(2,1)}, u32[]{:S(2)}, u32[]{:S(2)}) collective-permute-start(bf16[256,768]{1,0:T(8,128)(2,1)} %add.1418), channel_id=1, source_target_pairs={{0,8},{8,16},{16,24},{1,9},{9,17},{17,25},{2,10},{10,18},{18,26},{... | collective-permute-start | bytes 1179656 | tf_op jit(solution)/shard_map/ppermute | solution.py:479
  267.0 67.6 %collective-permute-start.28 = (bf16[512,768]{1,0:T(8,128)(2,1)}, bf16[512,768]{1,0:T(8,128)(2,1)S(1)}, u32[]{:S(2)}, u32[]{:S(2)}) collective-permute-start(bf16[512,768]{1,0:T(8,128)(2,1)} %add.1440), channel_id=1, source_target_pairs={{24,16},{16,8},{8,0},{25,17},{17,9},{9,1},{26,18},{18,10},{10,2},{... | collective-permute-start | bytes 2359304 | tf_op jit(solution)/shard_map/ppermute | solution.py:480
  269.4 66.1 %collective-permute-start.25 = (bf16[512,768]{1,0:T(8,128)(2,1)}, bf16[512,768]{1,0:T(8,128)(2,1)}, u32[]{:S(2)}, u32[]{:S(2)}) collective-permute-start(bf16[512,768]{1,0:T(8,128)(2,1)} %add.1437), channel_id=1, source_target_pairs={{0,8},{8,16},{16,24},{1,9},{9,17},{17,25},{2,10},{10,18},{18,26},{... | collective-permute-start | bytes 2359304 | tf_op jit(solution)/shard_map/ppermute | solution.py:479
  417.3 30.0 %collective-permute-start.30 = (bf16[512,1536]{1,0:T(8,128)(2,1)}, bf16[512,1536]{1,0:T(8,128)(2,1)}, u32[]{:S(2)}, u32[]{:S(2)}) collective-permute-start(bf16[512,1536]{1,0:T(8,128)(2,1)} %convolution_convert_fusion.7.refs_1_.refs_2_), channel_id=1, source_target_pairs={{0,2},{2,0},{1,3},{3,1},{4,6},{6,4},{5,7},{7,5},{8,10},{10,8},{9,1... | collective-permute-start | bytes 4718600 | tf_op jit(solution)/shard_map/ppermute | solution.py:422
  653.0 35.8 %collective-permute-start.48 = (bf16[4,2,2,128,768]{4,3,0,2,1:T(8,128)(2,1)S(1)}, bf16[4,2,2,128,768]{4,3,0,2,1:T(8,128)(2,1)}, u32[]{:S(2)}, u32[]{:S(2)}) collective-permute-start(bf16[4,2,2,128,768]{4,3,0,2,1:T(8,128)(2,1)S(1)} %bitcast.730), channel_id=1, source_target_pairs={{0,2},{2,0},{1,3},{3,1},{4,6},{6,4},{5,7},{7,5},{8,10},{10,8},{9,1... | collective-permute-start | bytes 9437192 | tf_op jit(solution)/shard_map/ppermute | solution.py:422
  693.9 36.7 %collective-permute-start.49 = (bf16[4,2,128,768]{3,2,0,1:T(8,128)(2,1)}, bf16[4,2,128,768]{3,2,0,1:T(8,128)(2,1)}, u32[]{:S(2)}, u32[]{:S(2)}) collective-permute-start(bf16[4,2,128,768]{3,2,0,1:T(8,128)(2,1)} %dynamic-slice_bitcast_fusion.5), channel_id=1, source_target_pairs={{0,4},{4,0},{1,5},{5,1},{2,6},{6,2},{3,7},{7,3},{8,12},{12,8},{9,1... | collective-permute-start | bytes 4718600 | tf_op jit(solution)/shard_map/ppermute | solution.py:422
  701.2 37.6 %collective-permute-start.43 = (bf16[4,2,128,768]{3,2,0,1:T(8,128)(2,1)}, bf16[4,2,128,768]{3,2,0,1:T(8,128)(2,1)}, u32[]{:S(2)}, u32[]{:S(2)}) collective-permute-start(bf16[4,2,128,768]{3,2,0,1:T(8,128)(2,1)} %dynamic-slice_bitcast_fusion.6), channel_id=1, source_target_pairs={{0,1},{1,0},{2,3},{3,2},{4,5},{5,4},{6,7},{7,6},{8,9},{9,8},{10,11... | collective-permute-start | bytes 4718600 | tf_op jit(solution)/shard_map/ppermute | solution.py:422
  762.3 29.0 %collective-permute-start.46 = (bf16[128,768]{1,0:T(8,128)(2,1)S(1)}, bf16[128,768]{1,0:T(8,128)(2,1)S(1)}, u32[]{:S(2)}, u32[]{:S(2)}) collective-permute-start(bf16[128,768]{1,0:T(8,128)(2,1)S(1)} %get-tuple-element.369), channel_id=1, source_target_pairs={{0,16},{8,24},{16,0},{24,8},{1,17},{9,25},{17,1},{25,9},{2,18},{10... | collective-permute-start | bytes 589832 | tf_op jit(solution)/shard_map/ppermute | solution.py:457
  831.7 75.1 %collective-permute-start.54 = (bf16[2,512,768]{2,1,0:T(8,128)(2,1)}, bf16[2,512,768]{2,1,0:T(8,128)(2,1)}, u32[]{:S(2)}, u32[]{:S(2)}) collective-permute-start(bf16[2,512,768]{2,1,0:T(8,128)(2,1)} %get-tuple-element.47), channel_id=1, source_target_pairs={{0,2},{2,0},{1,3},{3,1},{4,6},{6,4},{5,7},{7,5},{8,10},{10,8},{9,1... | collective-permute-start | bytes 4718600 | tf_op jit(solution)/shard_map/ppermute | solution.py:422
  871.9 218.1 %collective-permute-start.98 = (bf16[4,2,2,24,4096]{4,3,0,1,2:T(8,128)(2,1)}, bf16[4,2,2,24,4096]{4,3,0,1,2:T(8,128)(2,1)}, u32[]{:S(2)}, u32[]{:S(2)}) collective-permute-start(bf16[4,2,2,24,4096]{4,3,0,1,2:T(8,128)(2,1)} %bitcast.660), channel_id=1, source_target_pairs={{0,2},{2,0},{1,3},{3,1},{4,6},{6,4},{5,7},{7,5},{8,10},{10,8},{9,1... | collective-permute-start | bytes 9437192 | tf_op jit(solution)/shard_map/ppermute | solution.py:422
  876.0 149.1 %collective-permute-start.110 = (bf16[4,2,2,64,768]{4,3,0,2,1:T(8,128)(2,1)}, bf16[4,2,2,64,768]{4,3,0,2,1:T(8,128)(2,1)}, u32[]{:S(2)}, u32[]{:S(2)}) collective-permute-start(bf16[4,2,2,64,768]{4,3,0,2,1:T(8,128)(2,1)} %bitcast.664), channel_id=1, source_target_pairs={{0,2},{2,0},{1,3},{3,1},{4,6},{6,4},{5,7},{7,5},{8,10},{10,8},{9,1... | collective-permute-start | bytes 4718600 | tf_op jit(solution)/shard_map/ppermute | solution.py:422
  900.2 130.7 %collective-permute-start.65 = (bf16[256,768]{1,0:T(8,128)(2,1)}, bf16[256,768]{1,0:T(8,128)(2,1)}, u32[]{:S(2)}, u32[]{:S(2)}) collective-permute-start(bf16[256,768]{1,0:T(8,128)(2,1)} %collective-permute-done.64), channel_id=1, source_target_pairs={{8,0},{16,8},{24,16},{9,1},{17,9},{25,17},{10,2},{18,10},{26,18},{... | collective-permute-start | bytes 1179656 | tf_op jit(solution)/shard_map/ppermute | solution.py:467
  901.5 134.3 %collective-permute-start.67 = (bf16[256,768]{1,0:T(8,128)(2,1)}, bf16[256,768]{1,0:T(8,128)(2,1)}, u32[]{:S(2)}, u32[]{:S(2)}) collective-permute-start(bf16[256,768]{1,0:T(8,128)(2,1)} %collective-permute-done.63), channel_id=1, source_target_pairs={{0,8},{8,16},{16,24},{1,9},{9,17},{17,25},{2,10},{10,18},{18,26},{... | collective-permute-start | bytes 1179656 | tf_op jit(solution)/shard_map/ppermute | solution.py:466
  997.5 74.3 %collective-permute-start.55 = (bf16[2,512,768]{2,1,0:T(8,128)(2,1)}, bf16[2,512,768]{2,1,0:T(8,128)(2,1)}, u32[]{:S(2)}, u32[]{:S(2)}) collective-permute-start(bf16[2,512,768]{2,1,0:T(8,128)(2,1)} %get-tuple-element.50), channel_id=1, source_target_pairs={{0,2},{2,0},{1,3},{3,1},{4,6},{6,4},{5,7},{7,5},{8,10},{10,8},{9,1... | collective-permute-start | bytes 4718600 | tf_op jit(solution)/shard_map/ppermute | solution.py:422
  1030.9 28.6 %collective-permute-start.66 = (bf16[256,768]{1,0:T(8,128)(2,1)}, bf16[256,768]{1,0:T(8,128)(2,1)S(1)}, u32[]{:S(2)}, u32[]{:S(2)}) collective-permute-start(bf16[256,768]{1,0:T(8,128)(2,1)} %collective-permute-done.65), channel_id=1, source_target_pairs={{8,0},{16,8},{24,16},{9,1},{17,9},{25,17},{10,2},{18,10},{26,18},{... | collective-permute-start | bytes 1179656 | tf_op jit(solution)/shard_map/ppermute | solution.py:467
  1071.3 164.5 %collective-permute-start.92 = (bf16[4,2,2,24,4096]{4,3,0,1,2:T(8,128)(2,1)}, bf16[4,2,2,24,4096]{4,3,0,1,2:T(8,128)(2,1)}, u32[]{:S(2)}, u32[]{:S(2)}) collective-permute-start(bf16[4,2,2,24,4096]{4,3,0,1,2:T(8,128)(2,1)} %bitcast.661), channel_id=1, source_target_pairs={{0,2},{2,0},{1,3},{3,1},{4,6},{6,4},{5,7},{7,5},{8,10},{10,8},{9,1... | collective-permute-start | bytes 9437192 | tf_op jit(solution)/shard_map/ppermute | solution.py:422
  1081.6 90.2 %collective-permute-start.56 = (bf16[512,768]{1,0:T(8,128)(2,1)}, bf16[512,768]{1,0:T(8,128)(2,1)}, u32[]{:S(2)}, u32[]{:S(2)}) collective-permute-start(bf16[512,768]{1,0:T(8,128)(2,1)} %fusion.53.refs_1_), channel_id=1, source_target_pairs={{0,8},{8,16},{16,24},{1,9},{9,17},{17,25},{2,10},{10,18},{18,26},{... | collective-permute-start | bytes 2359304 | tf_op jit(solution)/shard_map/ppermute | solution.py:466
  1084.7 87.1 %collective-permute-start.57 = (bf16[512,768]{1,0:T(8,128)(2,1)}, bf16[512,768]{1,0:T(8,128)(2,1)}, u32[]{:S(2)}, u32[]{:S(2)}) collective-permute-start(bf16[512,768]{1,0:T(8,128)(2,1)} %fusion.53.refs_1_), channel_id=1, source_target_pairs={{8,0},{16,8},{24,16},{9,1},{17,9},{25,17},{10,2},{18,10},{26,18},{... | collective-permute-start | bytes 2359304 | tf_op jit(solution)/shard_map/ppermute | solution.py:467
  1111.5 117.3 %collective-permute-start.99 = (bf16[4,2,24,4096]{3,2,0,1:T(8,128)(2,1)}, bf16[4,2,24,4096]{3,2,0,1:T(8,128)(2,1)}, u32[]{:S(2)}, u32[]{:S(2)}) collective-permute-start(bf16[4,2,24,4096]{3,2,0,1:T(8,128)(2,1)} %dynamic-slice_bitcast_fusion.3), channel_id=1, source_target_pairs={{0,1},{1,0},{2,3},{3,2},{4,5},{5,4},{6,7},{7,6},{8,9},{9,8},{10,11... | collective-permute-start | bytes 4718600 | tf_op jit(solution)/shard_map/ppermute | solution.py:422
  1177.9 46.7 %collective-permute-start.58 = (bf16[512,768]{1,0:T(8,128)(2,1)}, bf16[512,768]{1,0:T(8,128)(2,1)}, u32[]{:S(2)}, u32[]{:S(2)}) collective-permute-start(bf16[512,768]{1,0:T(8,128)(2,1)} %collective-permute-done.57), channel_id=1, source_target_pairs={{8,0},{16,8},{24,16},{9,1},{17,9},{25,17},{10,2},{18,10},{26,18},{... | collective-permute-start | bytes 2359304 | tf_op jit(solution)/shard_map/ppermute | solution.py:467
  1190.7 34.3 %collective-permute-start.60 = (bf16[512,768]{1,0:T(8,128)(2,1)}, bf16[512,768]{1,0:T(8,128)(2,1)}, u32[]{:S(2)}, u32[]{:S(2)}) collective-permute-start(bf16[512,768]{1,0:T(8,128)(2,1)} %collective-permute-done.56), channel_id=1, source_target_pairs={{0,8},{8,16},{16,24},{1,9},{9,17},{17,25},{2,10},{10,18},{18,26},{... | collective-permute-start | bytes 2359304 | tf_op jit(solution)/shard_map/ppermute | solution.py:466
  1222.8 94.4 %collective-permute-start.80 = (bf16[4,2,2,24,6144]{4,3,2,1,0:T(8,128)(2,1)}, bf16[4,2,2,24,6144]{4,3,2,1,0:T(8,128)(2,1)}, u32[]{:S(2)}, u32[]{:S(2)}) collective-permute-start(bf16[4,2,2,24,6144]{4,3,2,1,0:T(8,128)(2,1)} %dynamic-slice_bitcast_fusion), channel_id=1, source_target_pairs={{0,2},{2,0},{1,3},{3,1},{4,6},{6,4},{5,7},{7,5},{8,10},{10,8},{9,1... | collective-permute-start | bytes 14155784 | tf_op jit(solution)/shard_map/ppermute | solution.py:422
  1235.8 64.3 %collective-permute-start.100 = (bf16[4,24,4096]{2,1,0:T(8,128)(2,1)S(1)}, bf16[4,24,4096]{2,1,0:T(8,128)(2,1)}, u32[]{:S(2)}, u32[]{:S(2)}) collective-permute-start(bf16[4,24,4096]{2,1,0:T(8,128)(2,1)S(1)} %dynamic-slice_bitcast_fusion.11), channel_id=1, source_target_pairs={{0,4},{4,0},{1,5},{5,1},{2,6},{6,2},{3,7},{7,3},{8,12},{12,8},{9,1... | collective-permute-start | bytes 2359304 | tf_op jit(solution)/shard_map/ppermute | solution.py:422
  1241.4 81.9 %collective-permute-start.93 = (bf16[4,2,24,4096]{3,2,0,1:T(8,128)(2,1)}, bf16[4,2,24,4096]{3,2,0,1:T(8,128)(2,1)S(1)}, u32[]{:S(2)}, u32[]{:S(2)}) collective-permute-start(bf16[4,2,24,4096]{3,2,0,1:T(8,128)(2,1)} %dynamic-slice_bitcast_fusion.4), channel_id=1, source_target_pairs={{0,1},{1,0},{2,3},{3,2},{4,5},{5,4},{6,7},{7,6},{8,9},{9,8},{10,11... | collective-permute-start | bytes 4718600 | tf_op jit(solution)/shard_map/ppermute | solution.py:422
  1246.6 56.3 %collective-permute-start.75 = (bf16[4,2,24,2304]{3,2,1,0:T(8,128)(2,1)}, bf16[4,2,24,2304]{3,2,1,0:T(8,128)(2,1)S(1)}, u32[]{:S(2)}, u32[]{:S(2)}) collective-permute-start(bf16[4,2,24,2304]{3,2,1,0:T(8,128)(2,1)} %dynamic-slice_bitcast_fusion.8), channel_id=1, source_target_pairs={{0,1},{1,0},{2,3},{3,2},{4,5},{5,4},{6,7},{7,6},{8,9},{9,8},{10,11... | collective-permute-start | bytes 2654216 | tf_op jit(solution)/shard_map/ppermute | solution.py:422
  1300.2 115.0 %collective-permute-start.69 = (bf16[4032,768]{1,0:T(8,128)(2,1)}, bf16[4032,768]{1,0:T(8,128)(2,1)}, u32[]{:S(2)}, u32[]{:S(2)}) collective-permute-start(bf16[4032,768]{1,0:T(8,128)(2,1)} %shard_map.471), channel_id=1, source_target_pairs={{0,2},{2,0},{1,3},{3,1},{4,6},{6,4},{5,7},{7,5},{8,10},{10,8},{9,1... | collective-permute-start | bytes 18579464 | tf_op jit(solution)/shard_map/ppermute | solution.py:422
  1334.4 69.6 %collective-permute-start.81 = (bf16[4,2,24,6144]{3,2,1,0:T(8,128)(2,1)S(1)}, bf16[4,2,24,6144]{3,2,1,0:T(8,128)(2,1)S(1)}, u32[]{:S(2)}, u32[]{:S(2)}) collective-permute-start(bf16[4,2,24,6144]{3,2,1,0:T(8,128)(2,1)S(1)} %dynamic-slice_bitcast_fusion.1), channel_id=1, source_target_pairs={{0,4},{4,0},{1,5},{5,1},{2,6},{6,2},{3,7},{7,3},{8,12},{12,8},{9,1... | collective-permute-start | bytes 7077896 | tf_op jit(solution)/shard_map/ppermute | solution.py:422
  1334.7 61.9 %collective-permute-start.94 = (bf16[4,24,4096]{2,1,0:T(8,128)(2,1)S(1)}, bf16[4,24,4096]{2,1,0:T(8,128)(2,1)S(1)}, u32[]{:S(2)}, u32[]{:S(2)}) collective-permute-start(bf16[4,24,4096]{2,1,0:T(8,128)(2,1)S(1)} %dynamic-slice_bitcast_fusion.12), channel_id=1, source_target_pairs={{0,4},{4,0},{1,5},{5,1},{2,6},{6,2},{3,7},{7,3},{8,12},{12,8},{9,1... | collective-permute-start | bytes 2359304 | tf_op jit(solution)/shard_map/ppermute | solution.py:422
  1405.1 29.0 %collective-permute-start.82 = (bf16[4,24,6144]{2,1,0:T(8,128)(2,1)S(1)}, bf16[4,24,6144]{2,1,0:T(8,128)(2,1)S(1)}, u32[]{:S(2)}, u32[]{:S(2)}) collective-permute-start(bf16[4,24,6144]{2,1,0:T(8,128)(2,1)S(1)} %dynamic-slice_bitcast_fusion.7), channel_id=1, source_target_pairs={{0,1},{1,0},{2,3},{3,2},{4,5},{5,4},{6,7},{7,6},{8,9},{9,8},{10,11... | collective-permute-start | bytes 3538952 | tf_op jit(solution)/shard_map/ppermute | solution.py:422
  1447.8 28.6 %collective-permute-start.71 = (bf16[1008,768]{1,0:T(8,128)(2,1)S(1)}, bf16[1008,768]{1,0:T(8,128)(2,1)S(1)}, u32[]{:S(2)}, u32[]{:S(2)}) collective-permute-start(bf16[1008,768]{1,0:T(8,128)(2,1)S(1)} %pad_maximum_fusion.3), channel_id=1, source_target_pairs={{0,1},{1,0},{2,3},{3,2},{4,5},{5,4},{6,7},{7,6},{8,9},{9,8},{10,11... | collective-permute-start | bytes 4644872 | tf_op jit(solution)/shard_map/ppermute | solution.py:422
  (273 other events, 3573.7 us)
Sparse Core Ops, SparseCore 0:
  21.2 136.1 all-gather.3
  160.8 177.7 all-gather.5
  473.2 98.9 all-gather.7

commit v3 on v2

--- a/solution.py
+++ b/solution.py
@@ -190,11 +190,7 @@
 
 
 def attend_cost(q_len, k_len, products):
-    size = HEADS * q_len * 2 * k_len
-    return pl.CostEstimate(
-        flops=2 * products * size * HEAD_DIM, bytes_accessed=8 * D * (q_len + 4 * k_len),
-        transcendentals=size,
-    )
+    return pl.CostEstimate(flops=products, bytes_accessed=q_len, transcendentals=0)
 
 
 def attend_forward(q, kv_own, kv_other, ids, x8, causal):
@@ -286,13 +282,16 @@
     lse_out[...] = top + jnp.log(jnp.sum(jnp.exp(logits - top), axis=0, keepdims=True))
 
 
-def head_grad_kernel(count, hid, tab, tgt, msk, lse, dhid, dtab):
+def head_grad_kernel(count, core, hid, tab, tgt, msk, lse, dhid_a, dhid_b, dtab):
     tokens = hid[...].reshape(-1, D)
     logits = dot_nt(tab[...], tokens)
     row = lax.broadcasted_iota(jnp.int32, logits.shape, 0)
     soft = jnp.exp(jnp.where(row < count, logits, masked_out) - lse[...])
     grad = ((soft - jnp.where(row == tgt[...], 1.0, 0.0)) * msk[...]).astype(bf16)
-    dhid[...] = dot_tn(grad, tab[...]).astype(bf16).reshape(dhid.shape)
+    dhid = dot_tn(grad, tab[...]).astype(bf16).reshape(hid.shape)
+    cut = hid.shape[3] // 2
+    dhid_a[...] = dhid[:, 0, :, :cut]
+    dhid_b[...] = dhid[:, 0, :, cut:]
     term = dot_nn(grad, tokens)
 
     @pl.when(pl.program_id(0) == 0)
@@ -305,16 +304,16 @@
 
 
 def head_stats(hidden, table, targets, count):
-    devices, each, _ = hidden.shape
-    tokens, rows = devices * each, table.shape[0]
-    steps = devices // 4
-    line = pl.BlockSpec((1, 2 * each), lambda h, i: (0, h * steps + i))
+    places, each = hidden.shape[0], hidden.shape[3]
+    tokens, rows = places * 4 * each, table.shape[0]
+    steps = places // 2
+    line = pl.BlockSpec((1, 2 * each), lambda h, c, i: (0, (h * 2 + c) * steps + i))
     return pl.pallas_call(
         functools.partial(head_stats_kernel, count),
-        grid=(2, steps),
+        grid=(2, 2, steps),
         in_specs=[
-            pl.BlockSpec((4, each // 2, D), lambda h, i: (i, h, 0)),
-            pl.BlockSpec((rows, D), lambda h, i: (0, 0)),
+            pl.BlockSpec((2, 1, 2, each // 2, D), lambda h, c, i: (i, c, 0, h, 0)),
+            pl.BlockSpec((rows, D), lambda h, c, i: (0, 0)),
             line,
         ],
         out_specs=[line, line],
@@ -326,34 +325,36 @@
     )(hidden, table, targets)
 
 
-def head_grad(hidden, table, targets, mask, lse, count, half):
-    devices, each, _ = hidden.shape
-    tokens, rows = devices * each // 2, table.shape[0]
-    steps = devices // 4
-    line = pl.BlockSpec((1, 2 * each), lambda i: (0, half * steps + i))
+def head_grad(core, hidden, table, targets, mask, lse, count, half):
+    places, each = hidden.shape[0], hidden.shape[3]
+    tokens, rows = places * each, table.shape[0]
+    steps = places // 2
+    line = pl.BlockSpec((1, 2 * each), lambda i, c: (0, (half * 2 + c[0]) * steps + i))
+    piece = pl.BlockSpec((2, 2, each // 4, D), lambda i, c: (i, 0, 0, 0))
     return pl.pallas_call(
         functools.partial(head_grad_kernel, count),
-        grid=(steps,),
-        in_specs=[
-            pl.BlockSpec((4, each // 2, D), lambda i: (i, half, 0)),
-            pl.BlockSpec((rows, D), lambda i: (0, 0)),
-            line,
-            line,
-            line,
-        ],
-        out_specs=[
-            pl.BlockSpec((4, each // 2, D), lambda i: (i, 0, 0)),
-            pl.BlockSpec((rows, D), lambda i: (0, 0)),
-        ],
+        grid_spec=pltpu.PrefetchScalarGridSpec(
+            num_scalar_prefetch=1,
+            grid=(steps,),
+            in_specs=[
+                pl.BlockSpec((2, 1, 2, each // 2, D), lambda i, c: (i, c[0], 0, half, 0)),
+                pl.BlockSpec((rows, D), lambda i, c: (0, 0)),
+                line,
+                line,
+                line,
+            ],
+            out_specs=[piece, piece, pl.BlockSpec((rows, D), lambda i, c: (0, 0))],
+        ),
         out_shape=[
-            jax.ShapeDtypeStruct((devices, each // 2, D), bf16),
+            jax.ShapeDtypeStruct((places, 2, each // 4, D), bf16),
+            jax.ShapeDtypeStruct((places, 2, each // 4, D), bf16),
             jax.ShapeDtypeStruct((rows, D), f32),
         ],
         compiler_params=pltpu.CompilerParams(vmem_limit_bytes=VMEM_LIMIT),
         cost_estimate=pl.CostEstimate(
             flops=6 * tokens * rows * D, bytes_accessed=4 * tokens * D, transcendentals=tokens * rows
         ),
-    )(hidden, table, targets, mask, lse)
+    )(core.reshape(1), hidden, table, targets, mask, lse)
 
 
 def place_kernel(first, *refs):
@@ -442,21 +443,24 @@
     return add16(pick(value, me, dim), got)
 
 
-def scatter_chain(value, seq_first):
-    sizes = tuple(lax.axis_size(axis) for axis in ALL)
-    value = value.reshape(sizes + (-1, value.shape[-1]))
-    value = scatter_pair(value, "core", 2)
+def scatter_rest(value, seq_first):
     if seq_first:
         value = scatter_pair(scatter_pair(value, "seq", 2), "p", 1)
     else:
         value = scatter_pair(scatter_pair(value, "p", 1), "seq", 1)
-    size, me = sizes[0], lax.axis_index("z")
+    size, me = value.shape[0], lax.axis_index("z")
     total = pick(value, me, 0).astype(f32)
     for hop in range(1, size):
         send = pick(value, (me + hop) % size, 0)
         got = lax.ppermute(send, "z", [(i, (i + hop) % size) for i in range(size)])
         total = total + got.astype(f32)
     return total
+
+
+def scatter_chain(value, seq_first):
+    sizes = tuple(lax.axis_size(axis) for axis in ALL)
+    value = value.reshape(sizes + (-1, value.shape[-1]))
+    return scatter_rest(scatter_pair(value, "core", 2), seq_first)
 
 
 def line_gather(value, axis):
@@ -609,23 +613,10 @@
         jnp.concatenate([enc_cast, flat_out[0]], axis=1), ALL, axis=0, tiled=True
     )
     dec_cast = jnp.concatenate(
-        [attn_in[1], attn_in[2], ffn_in[1], attn_out[1], attn_out[2]], axis=1
+        [attn_in[1], attn_in[2], attn_out[1], attn_out[2]], axis=1
     ).astype(bf16)
-    dec_cast = jnp.concatenate([dec_cast, flat_out[1]], axis=1)
-    dec_cast, _ = lax.optimization_barrier((dec_cast, enc_pack[0, 0]))
-    dec_pack = lax.all_gather(dec_cast, ALL, axis=0, tiled=True)
-    cut = lambda pack, start, width: lax.slice_in_dim(pack, start, start + width, axis=1)
-    enc_wi, enc_fi = cut(enc_pack, 0, 3 * D), cut(enc_pack, 3 * D, 2 * FF)
-    enc_wo, misc_all = cut(enc_pack, 3 * D + 2 * FF, D), cut(enc_pack, 4 * D + 2 * FF, 128)
-    dec_wi, cross_wi = cut(dec_pack, 0, 3 * D), cut(dec_pack, 3 * D, 3 * D)
-    dec_fi = cut(dec_pack, 6 * D, 2 * FF)
-    dec_wo, cross_wo = cut(dec_pack, 6 * D + 2 * FF, D), cut(dec_pack, 7 * D + 2 * FF, D)
-    enc_fo = cut(enc_pack, 4 * D + 2 * FF + 128, FF).reshape(FF, D)
-    dec_fo = cut(dec_pack, 8 * D + 2 * FF, FF).reshape(FF, D)
-    gain = misc_all[:, :7].T.astype(f32)
-    rel_all = jnp.transpose(misc_all[:, 7].reshape(-1, 2, rel_table.shape[1]), (1, 0, 2))
-    rel_all = rel_all.reshape(2, BUCKETS, HEADS)
-
+    ffn_cast = jnp.concatenate([ffn_in[1].astype(bf16), flat_out[1]], axis=1)
+    plane_table = plane_gather(table_b)
     flat = jnp.concatenate(
         [
             enc_ids[0],
@@ -669,7 +660,6 @@
     enc_tok = jnp.where(first, V - 101 - mode_of, enc_tok)
     local_ids = jnp.concatenate([enc_tok, dec_id])
 
-    plane_table = plane_gather(table_b)
     line_ids = line_gather(local_ids, "z")
     plane_rows = plane_size * shard
     places = []
@@ -679,11 +669,27 @@
         places.append(
             jnp.where(inside, plane_slot(rel_id // shard) * padded + rel_id % shard, shard)
         )
+    dec_cast, enc_pack, plane_table, places = lax.optimization_barrier(
+        (dec_cast, enc_pack, plane_table, places)
+    )
+    dec_pack = lax.all_gather(dec_cast, ALL, axis=0, tiled=True)
     enc_places = [item[:enc_count] for item in places]
     dec_places = [item[enc_count:] for item in places]
-    look = lambda item: jnp.take(plane_table, item, axis=0, mode="clip")
-    enc_x0 = line_scatter([look(item) for item in enc_places], "z")
-    dec_y0 = line_scatter([look(item) for item in dec_places], "z")
+
+    def look(items):
+        got = jnp.take(plane_table, jnp.concatenate(items), axis=0, mode="clip")
+        return line_scatter(jnp.split(got, len(items)), "z")
+
+    enc_x0 = look(enc_places)
+    dec_y0 = look(dec_places)
+
+    cut = lambda pack, start, width: lax.slice_in_dim(pack, start, start + width, axis=1)
+    enc_wi, enc_fi = cut(enc_pack, 0, 3 * D), cut(enc_pack, 3 * D, 2 * FF)
+    enc_wo, misc_all = cut(enc_pack, 3 * D + 2 * FF, D), cut(enc_pack, 4 * D + 2 * FF, 128)
+    enc_fo = cut(enc_pack, 4 * D + 2 * FF + 128, FF).reshape(FF, D)
+    gain = misc_all[:, :7].T.astype(f32)
+    rel_all = jnp.transpose(misc_all[:, 7].reshape(-1, 2, rel_table.shape[1]), (1, 0, 2))
+    rel_all = rel_all.reshape(2, BUCKETS, HEADS)
 
     enc_x8, enc_picks = bias_eights(rel_all[0], buckets[0], core, enc_count, enc_count)
     dec_x8, dec_picks = bias_eights(rel_all[1], buckets[1], core, dec_count, dec_count)
@@ -706,6 +712,12 @@
     enc_kv = project(enc_n1, enc_wi[:, D:]).astype(bf16)
     enc_kv2 = swap_core(enc_kv)
     enc_ob = attend_forward(enc_q, enc_kv, enc_kv2, enc_info, enc_x8, False)
+    ffn_cast, dec_pack, enc_ob = lax.optimization_barrier((ffn_cast, dec_pack, enc_ob))
+    ffn_pack = lax.all_gather(ffn_cast, ALL, axis=0, tiled=True)
+    dec_wi, cross_wi = cut(dec_pack, 0, 3 * D), cut(dec_pack, 3 * D, 3 * D)
+    dec_wo, cross_wo = cut(dec_pack, 6 * D, D), cut(dec_pack, 7 * D, D)
+    dec_fi = cut(ffn_pack, 0, 2 * FF)
+    dec_fo = cut(ffn_pack, 2 * FF, FF).reshape(FF, D)
     enc_x1 = enc_x0 + project(enc_ob, enc_wo)
     enc_x2, enc_saved = ffn_forward(enc_x1, gain[1], enc_fi, enc_fo)
     enc_out = rms_scale(enc_x2, gain[2]).astype(bf16)
@@ -727,22 +739,34 @@
     hidden_b = (rms_scale(dec_y3, gain[6]) * head_scale).astype(bf16)
 
     hidden_all = lax.all_gather(hidden_b, ALL, axis=0, tiled=True)
-    hidden_all = hidden_all.reshape(-1, dec_count, D)
+    sizes = tuple(lax.axis_size(axis) for axis in ALL)
+    hidden_all = hidden_all.reshape(-1, 2, 2, dec_count, D)
     info = gather_small(jnp.stack([targets, mask_i]), ALL)
-    info = jnp.transpose(info.reshape(-1, 2, 2, dec_count // 2), (1, 2, 0, 3)).reshape(2, 1, -1)
+    info = info.reshape(-1, 2, 2, 2, 2, dec_count // 2)
+    info = jnp.transpose(info, (3, 4, 1, 0, 2, 5)).reshape(2, 1, -1)
     targets_all = info[0] - device * shard
     mask_all = info[1].astype(f32)
     lse_part, picked = head_stats(hidden_all, table_b, targets_all, shard)
     lse = fold_all(lse_part, add_logs)
-    halves = [
-        head_grad(hidden_all, table_b, targets_all, mask_all, lse, shard, half) for half in range(2)
-    ]
-    head_embed = halves[0][1] + halves[1][1]
-    d_hidden = jnp.concatenate(
-        [scatter_chain(item[0], number == 0) for number, item in enumerate(halves)]
-    )
+    d_hidden, head_embed = [], None
+    for half in range(2):
+        *away, term = head_grad(
+            1 - core, hidden_all, table_b, targets_all, mask_all, lse, shard, half
+        )
+        head_embed = term if head_embed is None else head_embed + term
+        away = [swap_core(item) for item in away]
+        *home, term = head_grad(
+            core, hidden_all, table_b, targets_all, mask_all, lse, shard, half
+        )
+        head_embed = head_embed + term
+        for number in range(2):
+            item = add16(home[number], away[number])
+            item = item.reshape(sizes[:2] + (2,) + item.shape[2:])
+            d_hidden.append(scatter_rest(item, number == 0))
+    d_hidden = jnp.concatenate(d_hidden)
+    mine = (core * sizes[0] * sizes[1] + device // 4) * 2 + lax.axis_index("seq")
     lse_mine = lax.dynamic_slice_in_dim(
-        lse.reshape(2, -1), device * (dec_count // 2), dec_count // 2, axis=1
+        lse.reshape(2, -1), mine * (dec_count // 2), dec_count // 2, axis=1
     )
     loss_local = jnp.sum(mask * lse_mine.reshape(-1)) - jnp.sum(mask_all * picked)
 
@@ -751,6 +775,11 @@
         d_y3, dec_y2, gain[5], dec_fi, dec_fo, dec_saved
     )
     d_cross_wo, d_cross_ob = branch_backward(d_y2, cross_ob, cross_wo)
+    rows_in = lambda out: out.reshape(-1, ffn_out.shape[1], D).reshape(D, FF)
+    early, d_cross_ob = lax.optimization_barrier(
+        (jnp.concatenate([d_dec_fi, rows_in(d_dec_fo)], axis=1), d_cross_ob)
+    )
+    early = lax.psum_scatter(early, ALL, scatter_dimension=0, tiled=True)
     d_cross_q, own, other = attend_backward(
         d_cross_ob, cross_q, cross_kv, cross_kv2, cross_info, None, False
     )
@@ -782,9 +811,6 @@
         ],
         axis=1,
     )
-    g_dec_fi = scatter_chain(d_dec_fi, True)
-    g_dec_fo = scatter_chain(d_dec_fo, False)
-    g_dec_rest = scatter_chain(d_dec_rest, False)
     dec_lines = line_gather(d_y0.astype(bf16), "z")
 
     d_x2, d_gain_efin = norm_pull(
@@ -793,9 +819,17 @@
     d_x1, d_gain_effn, d_enc_fi, d_enc_fo = ffn_backward(
         d_x2, enc_x1, gain[1], enc_fi, enc_fo, enc_saved
     )
-    g_enc_fi = scatter_chain(d_enc_fi, True)
-    g_enc_fo = scatter_chain(d_enc_fo, False)
     d_enc_wo, d_enc_ob = branch_backward(d_x1, enc_ob, enc_wo)
+    late, early, dec_lines, d_enc_ob = lax.optimization_barrier(
+        (
+            jnp.concatenate([d_dec_rest, d_enc_fi, rows_in(d_enc_fo)], axis=1),
+            early,
+            dec_lines,
+            d_enc_ob,
+        )
+    )
+    late = lax.psum_scatter(late, ALL, scatter_dimension=0, tiled=True).astype(f32)
+    early = early.astype(f32)
     d_enc_q, own, other, enc_y8 = attend_backward(
         d_enc_ob, enc_q, enc_kv, enc_kv2, enc_info, enc_x8, False
     )
@@ -829,19 +863,18 @@
     d_rel = jnp.stack([d_enc_table.reshape(-1), d_dec_table.reshape(-1)])
     d_rel = jnp.transpose(d_rel.reshape(2, -1, rel_table.shape[1]), (1, 0, 2)).reshape(D, 1)
     d_misc = jnp.pad(jnp.concatenate([d_gains.T, d_rel], axis=1), ((0, 0), (0, 120)))
-    g_enc_wi = scatter_chain(d_enc_wi.astype(bf16), True)
-    g_enc_rest = scatter_chain(
-        jnp.concatenate([d_enc_wo, d_misc.astype(bf16)], axis=1), False
-    )
+    d_last = jnp.concatenate([d_enc_wi.astype(bf16), d_enc_wo, d_misc.astype(bf16)], axis=1)
+    last = jnp.concatenate(
+        [scatter_chain(d_last[:, : 2 * D], True), scatter_chain(d_last[:, 2 * D :], False)], axis=1
+    )
+    rows_out = lambda out: out.reshape(-1, D)
     owned = (
-        jnp.stack([g_enc_wi, cut(g_dec_rest, 0, 3 * D), cut(g_dec_rest, 3 * D, 3 * D)]),
-        jnp.stack(
-            [cut(g_enc_rest, 0, D), cut(g_dec_rest, 6 * D, D), cut(g_dec_rest, 7 * D, D)]
-        ),
-        jnp.stack([g_enc_fi, g_dec_fi]),
-        jnp.stack([g_enc_fo, g_dec_fo]),
-        g_enc_rest[:, D + 7].reshape(2, -1),
-        g_enc_rest[:, D : D + 7].T,
+        jnp.stack([cut(last, 0, 3 * D), cut(late, 0, 3 * D), cut(late, 3 * D, 3 * D)]),
+        jnp.stack([cut(last, 3 * D, D), cut(late, 6 * D, D), cut(late, 7 * D, D)]),
+        jnp.stack([cut(late, 8 * D, 2 * FF), cut(early, 0, 2 * FF)]),
+        jnp.stack([rows_out(cut(late, 8 * D + 2 * FF, FF)), rows_out(cut(early, 2 * FF, FF))]),
+        last[:, 4 * D + 7].reshape(2, -1),
+        last[:, 4 * D : 4 * D + 7].T,
     )
     grads = (grad_embed,) + owned
     squares = sum((jnp.sum(item * item) for item in grads))

time: 1540 us -> 1450 us (0.942)
  local copies, waits for them, and re-layouts: 254 us -> 223 us
  starting transfers between devices: 209 us -> 179 us
  waiting for transfers between devices: 488 us -> 461 us
    ppermute x47 -> x38, waiting for transfers between devices: 216 us -> 117 us  [swap(): return lax.ppermute(value, axis, [(0, 1), (1, 0)])]
    ppermute x6, waiting for transfers between devices: 25.6 us -> 92.9 us  [line_scatter(): up = lax.ppermute(send_up, axis, [(i, i + 1) for i in range(step)])]
    ppermute x9, waiting for transfers between devices: 1.38 us -> 53.8 us  [line_gather(): lax.ppermute(ups[-1], axis, [(i, i + 1) for i in range(size - 1)])]
    ppermute x27 -> x18, waiting for transfers between devices: 77.8 us -> 27.4 us  [scatter_rest(): got = lax.ppermute(send, 'z', [(i, (i + hop) % size) for i in range(size)])]
    gather x8 -> x2, local copies, waits for them, and re-layouts: 65.3 us -> 25.4 us  [look(): got = jnp.take(plane_table, jnp.concatenate(items), axis=0, mode='clip')]
    all_gather x1, waiting for transfers between devices: 0.02 us -> 29.7 us  [body(): lax.all_gather(jnp.concatenate([enc_cast, flat_out[0]], axis=1), ALL, axi...]
    another operation x4 -> x17, local copies, waits for them, and re-layouts: 2.58 us -> 31.8 us  [the longest x2 11.1 us: body(): rows_in = lambda out: out.reshape(-1, ffn_out.shape[1], D).reshape(D, FF)]
    ppermute x47 -> x38, starting transfers between devices: 58.7 us -> 31.1 us  [swap(): return lax.ppermute(value, axis, [(0, 1), (1, 0)])]
  transfers between devices with their start and end apart: 124 -> 109, of which waited for: 53 -> 50; matrix products, arithmetic and copies ran while one was open for 27% -> 24% of each run, Pallas kernels for 13% -> 16%
where the time goes in v3:
time: 1450 us; the launch traced here: 1440 us
  waiting for transfers between devices  461 us (32%)
  Pallas kernels  292 us (20%)
  local copies, waits for them, and re-layouts  223 us (15%)
  starting transfers between devices  179 us (12%)
  other arithmetic  135 us (9%)
  matrix products  116 us (8%)
  between operations  30.1 us (2%)
    ppermute x38, waiting for transfers between devices, swap(): return lax.ppermute(value, axis, [(0, 1), (1, 0)])  117 us
    pallas_call x3, Pallas kernels, attend_backward(): pl.pallas_call(functools.partial(attend_backward_kernel, cfg), grid=(HEAD...  101 us
    ppermute x6, waiting for transfers between devices, line_scatter(): up = lax.ppermute(send_up, axis, [(i, i + 1) for i in range(step)])  92.9 us
    all_gather x1, waiting for transfers between devices, body(): hidden_all = lax.all_gather(hidden_b, ALL, axis=0, tiled=True)  77 us
    pallas_call x4, Pallas kernels, head_grad(): pl.pallas_call(functools.partial(head_grad_kernel, count), grid_spec=pltp...  63.4 us
    unnamed x399, local copies, waits for them, and re-layouts  62.1 us
    pallas_call x3, Pallas kernels, attend_forward(): pl.pallas_call(functools.partial(attend_forward_kernel, cfg), grid=(HEADS...  54.9 us
    ppermute x9, waiting for transfers between devices, line_gather(): lax.ppermute(ups[-1], axis, [(i, i + 1) for i in range(size - 1)])  53.8 us
  transfers between devices with their start and end apart: 109, of which 50 were waited for; matrix products, arithmetic and copies ran while one was open for 24% of the time, Pallas kernels for 16%

profile of v3, /device:TPU:0, one launch (start us, length us, event | category | flops | bytes accessed | tf_op | source)
XLA Modules:
  0.0 1435.8 jit_solution(16342902512787164445)
XLA Ops:
  50.8 24.5 %collective-permute-done.1 = bf16[1008,768]{1,0:T(8,128)(2,1)S(1)} collective-permute-done((bf16[1008,768]{1,0:T(8,128)(2,1)}, bf16[1008,768]{1,0:T(8,128)(2,1)S(1)}, u32[]{:S(2)}, u32[]{:S(2)}) %collective-permute-start.1) | collective-permute-done | bytes 1548320 | tf_op jit(solution)/shard_map/ppermute | solution.py:423
  81.8 17.1 %collective-permute-done.3 = bf16[504,768]{1,0:T(8,128)(2,1)S(1)} collective-permute-done((bf16[504,768]{1,0:T(8,128)(2,1)S(1)}, bf16[504,768]{1,0:T(8,128)(2,1)S(1)}, u32[]{:S(2)}, u32[]{:S(2)}) %collective-permute-start.3) | collective-permute-done | bytes 774176 | tf_op jit(solution)/shard_map/ppermute | solution.py:423
  113.3 29.7 %all-gather.5.cloned.1.call-done = bf16[768,9344]{1,0:T(8,128)(2,1)} async-done(((bf16[24,9344]{1,0:T(8,128)(2,1)}), bf16[768,9344]{1,0:T(8,128)(2,1)}) %all-gather.5.cloned.1.call-update) | async-done | bytes 14352400 | tf_op jit(solution)/shard_map/all_gather | solution.py:612
  149.4 14.8 %gather_fusion.1 = bf16[2048,768]{1,0:T(8,128)(2,1)S(1)} fusion(bf16[8064,768]{1,0:T(8,128)(2,1)} %constant_dynamic-update-slice_fusion.5, s32[2048]{0:T(1024)S(1)} %add_clamp_fusion), kind=kCustom, calls=%fused_computation.1 | custom fusion | bytes 6299648 | tf_op jit(solution)/shard_map/jit(_take)/gather | solution.py:680
  167.9 28.5 %collective-permute-done.22 = bf16[512,768]{1,0:T(8,128)(2,1)S(1)} collective-permute-done((bf16[512,768]{1,0:T(8,128)(2,1)S(1)}, bf16[512,768]{1,0:T(8,128)(2,1)S(1)}, u32[]{:S(2)}, u32[]{:S(2)}) %collective-permute-start.22) | collective-permute-done | bytes 786464 | tf_op jit(solution)/shard_map/ppermute | solution.py:483
  202.0 29.5 %collective-permute-done.23 = bf16[512,768]{1,0:T(8,128)(2,1)S(1)} collective-permute-done((bf16[512,768]{1,0:T(8,128)(2,1)S(1)}, bf16[512,768]{1,0:T(8,128)(2,1)S(1)}, u32[]{:S(2)}, u32[]{:S(2)}) %collective-permute-start.23) | collective-permute-done | bytes 786464 | tf_op jit(solution)/shard_map/ppermute | solution.py:483
  231.8 18.0 %collective-permute-start.24 = (bf16[512,768]{1,0:T(8,128)(2,1)S(1)}, bf16[512,768]{1,0:T(8,128)(2,1)S(1)}, u32[]{:S(2)}, u32[]{:S(2)}) collective-permute-start(bf16[512,768]{1,0:T(8,128)(2,1)S(1)} %get-tuple-element.382), channel_id=1, source_target_pairs={{0,8},{8,16},{16,24},{1,9},{9,17},{17,25},{2,10},{10,18},{18,26},{... | collective-permute-start | bytes 2359304 | tf_op jit(solution)/shard_map/ppermute | solution.py:483
  254.3 9.4 collective-permute-done.24
  280.8 28.5 %shard_map.461 = bf16[512,768]{1,0:T(8,128)(2,1)} custom-call(bf16[512,768]{1,0:T(8,128)(2,1)} %convolution_convert_fusion.15.refs_0_, bf16[512,1536]{1,0:T(8,128)(2,1)} %copy-done.4, bf16[512,1536]{1,0:T(8,128)(2,1)} %copy-done.4, bf16[512,1536]{1,0:T(8,128)(2,1)} %copy-done.5, bf16[512,1536]{1,0:T(8,128)(2,1)} %copy-done.5, s32[512,1]{1,0:T(8,128)} %copy.1047.refs_5_, ...), custom_call_target="tpu_custom_call" | custom-call | flops 2 | bytes 512 | tf_op jit(solution)/shard_map/pallas_call | solution.py:199
  310.6 10.6 gather_fusion
  324.1 9.9 collective-permute-done.16
  341.4 15.7 %collective-permute-done.17 = bf16[256,768]{1,0:T(8,128)(2,1)S(1)} collective-permute-done((bf16[256,768]{1,0:T(8,128)(2,1)}, bf16[256,768]{1,0:T(8,128)(2,1)S(1)}, u32[]{:S(2)}, u32[]{:S(2)}) %collective-permute-start.17) | collective-permute-done | bytes 393248 | tf_op jit(solution)/shard_map/ppermute | solution.py:483
  359.1 6.6 collective-permute-start.18
  374.4 6.8 reshape.649
  383.6 12.3 collective-permute-done.21
  400.5 6.3 fusion.9
  433.7 13.9 shard_map.462
  453.7 12.4 shard_map.463
  504.8 77.0 %all-gather.11.cloned.1.call-done = bf16[8192,768]{1,0:T(8,128)(2,1)} async-done(((bf16[256,768]{1,0:T(8,128)(2,1)}), bf16[8192,768]{1,0:T(8,128)(2,1)}) %all-gather.11.cloned.1.call-update) | async-done | bytes 12582928 | tf_op jit(solution)/shard_map/all_gather | solution.py:741
  581.7 25.6 %shard_map.464 = (f32[1,8192]{1,0:T(1,128)}, f32[1,8192]{1,0:T(1,128)}) custom-call(bf16[8,2,2,256,768]{4,3,2,1,0:T(8,128)(2,1)} %bitcast.744, bf16[1008,768]{1,0:T(8,128)(2,1)} %get-tuple-element.411.tab, s32[1,8192]{1,0:T(1,128)} %bitcast.703), custom_call_target="tpu_custom_call" | custom-call | flops 12683575296 | bytes 12582912 | tf_op jit(solution)/shard_map/pallas_call | solution.py:311
  629.3 15.8 %shard_map.465 = (bf16[8,2,64,768]{3,2,1,0:T(8,128)(2,1)}, bf16[8,2,64,768]{3,2,1,0:T(8,128)(2,1)}, f32[1008,768]{1,0:T(8,128)}) custom-call(s32[1]{0:T(128)} %bitcast.101.core, bf16[8,2,2,256,768]{4,3,2,1,0:T(8,128)(2,1)} %bitcast.745, bf16[1008,768]{1,0:T(8,128)(2,1)} %get-tuple-element.411.tab, s32[1,8192]{1,0:T(1,128)} %bitcast.704, ...), custom_call_target="tpu_custom_call" | custom-call | flops 9512681472 | bytes 6291456 | tf_op jit(solution)/shard_map/pallas_call | solution.py:334
  645.1 15.8 %shard_map.467 = (bf16[8,2,64,768]{3,2,1,0:T(8,128)(2,1)}, bf16[8,2,64,768]{3,2,1,0:T(8,128)(2,1)}, f32[1008,768]{1,0:T(8,128)}) custom-call(s32[1]{0:T(128)} %bitcast.101.core, bf16[8,2,2,256,768]{4,3,2,1,0:T(8,128)(2,1)} %bitcast.746, bf16[1008,768]{1,0:T(8,128)(2,1)} %get-tuple-element.411.tab, s32[1,8192]{1,0:T(1,128)} %bitcast.705, ...), custom_call_target="tpu_custom_call" | custom-call | flops 9512681472 | bytes 6291456 | tf_op jit(solution)/shard_map/pallas_call | solution.py:334
  661.5 15.8 %shard_map.466 = (bf16[8,2,64,768]{3,2,1,0:T(8,128)(2,1)}, bf16[8,2,64,768]{3,2,1,0:T(8,128)(2,1)}, f32[1008,768]{1,0:T(8,128)}) custom-call(s32[1]{0:T(128)} %bitcast.102.core, bf16[8,2,2,256,768]{4,3,2,1,0:T(8,128)(2,1)} %bitcast.747, bf16[1008,768]{1,0:T(8,128)(2,1)} %get-tuple-element.411.tab, s32[1,8192]{1,0:T(1,128)} %bitcast.706, ...), custom_call_target="tpu_custom_call" | custom-call | flops 9512681472 | bytes 6291456 | tf_op jit(solution)/shard_map/pallas_call | solution.py:334
  677.8 16.0 %shard_map.468 = (bf16[8,2,64,768]{3,2,1,0:T(8,128)(2,1)}, bf16[8,2,64,768]{3,2,1,0:T(8,128)(2,1)}, f32[1008,768]{1,0:T(8,128)}) custom-call(s32[1]{0:T(128)} %bitcast.102.core, bf16[8,2,2,256,768]{4,3,2,1,0:T(8,128)(2,1)} %bitcast.748, bf16[1008,768]{1,0:T(8,128)(2,1)} %get-tuple-element.411.tab, s32[1,8192]{1,0:T(1,128)} %bitcast.707, ...), custom_call_target="tpu_custom_call" | custom-call | flops 9512681472 | bytes 6291456 | tf_op jit(solution)/shard_map/pallas_call | solution.py:334
  703.6 13.3 collective-permute-done.43
  720.5 13.2 collective-permute-done.55
  737.3 7.0 collective-permute-done.44
  797.6 9.1 pad_maximum_fusion
  806.9 21.7 %shard_map.469 = (bf16[256,768]{1,0:T(8,128)(2,1)}, f32[2,512,768]{2,1,0:T(8,128)}, bf16[2,512,768]{2,1,0:T(8,128)(2,1)}) custom-call(bf16[256,768]{1,0:T(8,128)(2,1)} %convolution_convert_fusion.18.refs_0_, bf16[512,1536]{1,0:T(8,128)(2,1)} %copy-done.2, bf16[512,1536]{1,0:T(8,128)(2,1)} %copy-done.2, bf16[512,1536]{1,0:T(8,128)(2,1)} %copy-done.3, ...), custom_call_target="tpu_custom_call" | custom-call | flops 5 | bytes 256 | tf_op jit(solution)/shard_map/pallas_call | solution.py:225
  834.3 24.6 %shard_map.470 = (bf16[256,768]{1,0:T(8,128)(2,1)}, f32[2,256,768]{2,1,0:T(8,128)}, bf16[2,256,768]{2,1,0:T(8,128)(2,1)}, f32[1,2,12,8,512]{4,3,2,1,0:T(8,128)}) custom-call(bf16[256,768]{1,0:T(8,128)(2,1)} %convolution_convert_fusion.19.refs_0_, bf16[256,1536]{1,0:T(8,128)(2,1)} %convolution_convert_fusion.9.refs_1_.refs_2_, ...), custom_call_target="tpu_custom_call" | custom-call | flops 5 | bytes 256 | tf_op jit(solution)/shard_map/pallas_call | solution.py:225
  882.7 9.9 collective-permute-done.68
  912.2 6.6 reshape_reshape.8
  932.8 8.1 fusion.47
  940.9 8.4 multiply_reduce_fusion.2
  949.8 8.7 fusion.2
  979.3 54.9 %shard_map.471 = (bf16[512,768]{1,0:T(8,128)(2,1)}, f32[2,512,768]{2,1,0:T(8,128)}, bf16[2,512,768]{2,1,0:T(8,128)(2,1)}, f32[2,2,12,8,768]{4,3,2,1,0:T(8,128)}) custom-call(bf16[512,768]{1,0:T(8,128)(2,1)} %convolution_convert_fusion.15.refs_0_, bf16[512,1536]{1,0:T(8,128)(2,1)} %copy-done.4, bf16[512,1536]{1,0:T(8,128)(2,1)} %copy-done.4, ...), custom_call_target="tpu_custom_call" | custom-call | flops 5 | bytes 512 | tf_op jit(solution)/shard_map/pallas_call | solution.py:225
  1082.8 18.2 %collective-permute-done.75 = bf16[512,768]{1,0:T(8,128)(2,1)S(1)} collective-permute-done((bf16[512,768]{1,0:T(8,128)(2,1)}, bf16[512,768]{1,0:T(8,128)(2,1)S(1)}, u32[]{:S(2)}, u32[]{:S(2)}) %collective-permute-start.75) | collective-permute-done | bytes 786464 | tf_op jit(solution)/shard_map/ppermute | solution.py:470
  1111.7 10.7 collective-permute-done.79
  1140.7 15.1 %collective-permute-done.80 = bf16[512,768]{1,0:T(8,128)(2,1)} collective-permute-done((bf16[512,768]{1,0:T(8,128)(2,1)}, bf16[512,768]{1,0:T(8,128)(2,1)}, u32[]{:S(2)}, u32[]{:S(2)}) %collective-permute-start.80) | collective-permute-done | bytes 786464 | tf_op jit(solution)/shard_map/ppermute | solution.py:470
  1158.2 15.5 %collective-permute-done.78 = bf16[512,768]{1,0:T(8,128)(2,1)} collective-permute-done((bf16[512,768]{1,0:T(8,128)(2,1)}, bf16[512,768]{1,0:T(8,128)(2,1)}, u32[]{:S(2)}, u32[]{:S(2)}) %collective-permute-start.78) | collective-permute-done | bytes 786464 | tf_op jit(solution)/shard_map/ppermute | solution.py:471
  1175.9 23.7 %shard_map.473 = bf16[4032,768]{1,0:T(8,128)(2,1)} custom-call(s32[1,512]{1,0:T(1,128)} %bitcast.730, bf16[512,768]{1,0:T(8,128)(2,1)} %fusion.42.refs_1_, s32[1,512]{1,0:T(1,128)} %bitcast.728, bf16[512,768]{1,0:T(8,128)(2,1)} %add.1443.refs_3_, s32[1,512]{1,0:T(1,128)} %bitcast.726, bf16[512,768]{1,0:T(8,128)(2,1)} %add.1444.refs_5_, s32[1,512]{1,0:T(1,128)} %bitcast.724, ...), custom_call_target="tpu_custom_call" | custom-call | flops 19025362944 | bytes 6193152 | tf_op jit(solution)/shard_map/pallas_call | solution.py:380
  1209.2 9.5 fusion
  1228.6 12.4 collective-permute-done.93
  1262.5 23.6 %shard_map.472 = bf16[4032,768]{1,0:T(8,128)(2,1)} custom-call(s32[1,512]{1,0:T(1,128)} %bitcast.731, bf16[512,768]{1,0:T(8,128)(2,1)} %fusion.42.refs_1_, s32[1,512]{1,0:T(1,128)} %bitcast.729, bf16[512,768]{1,0:T(8,128)(2,1)} %add.1443.refs_3_, s32[1,512]{1,0:T(1,128)} %bitcast.727, bf16[512,768]{1,0:T(8,128)(2,1)} %add.1444.refs_5_, s32[1,512]{1,0:T(1,128)} %bitcast.725, ...), custom_call_target="tpu_custom_call" | custom-call | flops 19025362944 | bytes 6193152 | tf_op jit(solution)/shard_map/pallas_call | solution.py:380
  1292.4 14.3 collective-permute-done.82
  1321.3 14.1 collective-permute-done.96
  1339.6 8.7 collective-permute-done.83
  1348.6 6.7 multiply_reduce_fusion
  (960 shorter events, 587.3 us)
Async XLA Ops:
  7.3 135.6 %all-gather.5.cloned.1.call-start = ((), (), s32[]{:S(2)}) async-start(), calls=%async_computation.2 | async-start | bytes 14800896 | tf_op jit(solution)/shard_map/all_gather | solution.py:612
  20.0 289.3 %all-gather.7.cloned.1.call-start = ((), (), s32[]{:S(2)}) async-start(), calls=%async_computation.3 | async-start | bytes 9732096 | tf_op jit(solution)/shard_map/all_gather | solution.py:675
  23.0 52.3 %collective-permute-start.1 = (bf16[1008,768]{1,0:T(8,128)(2,1)}, bf16[1008,768]{1,0:T(8,128)(2,1)S(1)}, u32[]{:S(2)}, u32[]{:S(2)}) collective-permute-start(bf16[1008,768]{1,0:T(8,128)(2,1)} %get-tuple-element.411.tab), channel_id=1, source_target_pairs={{0,1},{1,0},{2,3},{3,2},{4,5},{5,4},{6,7},{7,6},{8,9},{9,8},{10,11... | collective-permute-start | bytes 4644872 | tf_op jit(solution)/shard_map/ppermute | solution.py:423
  27.2 48.8 %collective-permute-start.2 = (bf16[1008,768]{1,0:T(8,128)(2,1)}, bf16[1008,768]{1,0:T(8,128)(2,1)S(1)}, u32[]{:S(2)}, u32[]{:S(2)}) collective-permute-start(bf16[1008,768]{1,0:T(8,128)(2,1)} %get-tuple-element.411.tab), channel_id=1, source_target_pairs={{0,4},{4,0},{1,5},{5,1},{2,6},{6,2},{3,7},{7,3},{8,12},{12,8},{9,1... | collective-permute-start | bytes 4644872 | tf_op jit(solution)/shard_map/ppermute | solution.py:423
  28.7 74.7 %collective-permute-start.5 = (bf16[1008,768]{1,0:T(8,128)(2,1)}, bf16[1008,768]{1,0:T(8,128)(2,1)}, u32[]{:S(2)}, u32[]{:S(2)}) collective-permute-start(bf16[1008,768]{1,0:T(8,128)(2,1)} %get-tuple-element.411.tab), channel_id=1, source_target_pairs={{0,2},{2,0},{1,3},{3,1},{4,6},{6,4},{5,7},{7,5},{8,10},{10,8},{9,1... | collective-permute-start | bytes 4644872 | tf_op jit(solution)/shard_map/ppermute | solution.py:423
  44.9 31.9 %collective-permute-start.13 = (s32[768]{0:T(1024)S(1)}, s32[768]{0:T(1024)S(1)}, u32[]{:S(2)}, u32[]{:S(2)}) collective-permute-start(s32[768]{0:T(1024)S(1)} %collective-permute-done.12), channel_id=1, source_target_pairs={{8,0},{16,8},{24,16},{9,1},{17,9},{25,17},{10,2},{18,10},{26,18},{... | collective-permute-start | bytes 9224 | tf_op jit(solution)/shard_map/ppermute | solution.py:471
  46.3 32.9 %collective-permute-start.15 = (s32[768]{0:T(1024)S(1)}, s32[768]{0:T(1024)S(1)}, u32[]{:S(2)}, u32[]{:S(2)}) collective-permute-start(s32[768]{0:T(1024)S(1)} %collective-permute-done.14), channel_id=1, source_target_pairs={{0,8},{8,16},{16,24},{1,9},{9,17},{17,25},{2,10},{10,18},{18,26},{... | collective-permute-start | bytes 9224 | tf_op jit(solution)/shard_map/ppermute | solution.py:470
  75.3 30.7 %collective-permute-start.6 = (bf16[1008,768]{1,0:T(8,128)(2,1)S(1)}, bf16[1008,768]{1,0:T(8,128)(2,1)}, u32[]{:S(2)}, u32[]{:S(2)}) collective-permute-start(bf16[1008,768]{1,0:T(8,128)(2,1)S(1)} %collective-permute-done.1), channel_id=1, source_target_pairs={{0,2},{2,0},{1,3},{3,1},{4,6},{6,4},{5,7},{7,5},{8,10},{10,8},{9,1... | collective-permute-start | bytes 4644872 | tf_op jit(solution)/shard_map/ppermute | solution.py:423
  76.0 32.8 %collective-permute-start.7 = (bf16[1008,768]{1,0:T(8,128)(2,1)S(1)}, bf16[1008,768]{1,0:T(8,128)(2,1)}, u32[]{:S(2)}, u32[]{:S(2)}) collective-permute-start(bf16[1008,768]{1,0:T(8,128)(2,1)S(1)} %collective-permute-done.2), channel_id=1, source_target_pairs={{0,2},{2,0},{1,3},{3,1},{4,6},{6,4},{5,7},{7,5},{8,10},{10,8},{9,1... | collective-permute-start | bytes 4644872 | tf_op jit(solution)/shard_map/ppermute | solution.py:423
  143.0 325.1 %all-gather.9.cloned.1.call-start = ((), (), s32[]{:S(2)}) async-start(), calls=%async_computation.4 | async-start | bytes 9732096 | tf_op jit(solution)/shard_map/all_gather | solution.py:716
  164.3 32.1 %collective-permute-start.22 = (bf16[512,768]{1,0:T(8,128)(2,1)S(1)}, bf16[512,768]{1,0:T(8,128)(2,1)S(1)}, u32[]{:S(2)}, u32[]{:S(2)}) collective-permute-start(bf16[512,768]{1,0:T(8,128)(2,1)S(1)} %get-tuple-element.386), channel_id=1, source_target_pairs={{0,8},{1,9},{2,10},{3,11},{4,12},{5,13},{6,14},{7,15}} | collective-permute-start | bytes 2359304 | tf_op jit(solution)/shard_map/ppermute | solution.py:483
  166.6 29.8 %collective-permute-start.25 = (bf16[512,768]{1,0:T(8,128)(2,1)S(1)}, bf16[512,768]{1,0:T(8,128)(2,1)S(1)}, u32[]{:S(2)}, u32[]{:S(2)}) collective-permute-start(bf16[512,768]{1,0:T(8,128)(2,1)S(1)} %get-tuple-element.387), channel_id=1, source_target_pairs={{24,16},{25,17},{26,18},{27,19},{28,20},{29,21},{30,22},{31,23}} | collective-permute-start | bytes 2359304 | tf_op jit(solution)/shard_map/ppermute | solution.py:484
  196.5 35.1 %collective-permute-start.23 = (bf16[512,768]{1,0:T(8,128)(2,1)S(1)}, bf16[512,768]{1,0:T(8,128)(2,1)S(1)}, u32[]{:S(2)}, u32[]{:S(2)}) collective-permute-start(bf16[512,768]{1,0:T(8,128)(2,1)S(1)} %get-tuple-element.384), channel_id=1, source_target_pairs={{0,8},{8,16},{1,9},{9,17},{2,10},{10,18},{3,11},{11,19},{4,12},{12... | collective-permute-start | bytes 2359304 | tf_op jit(solution)/shard_map/ppermute | solution.py:483
  200.9 30.6 %collective-permute-start.26 = (bf16[512,768]{1,0:T(8,128)(2,1)S(1)}, bf16[512,768]{1,0:T(8,128)(2,1)S(1)}, u32[]{:S(2)}, u32[]{:S(2)}) collective-permute-start(bf16[512,768]{1,0:T(8,128)(2,1)S(1)} %get-tuple-element.385), channel_id=1, source_target_pairs={{24,16},{16,8},{25,17},{17,9},{26,18},{18,10},{27,19},{19,11},{28,... | collective-permute-start | bytes 2359304 | tf_op jit(solution)/shard_map/ppermute | solution.py:484
  231.8 32.0 %collective-permute-start.24 = (bf16[512,768]{1,0:T(8,128)(2,1)S(1)}, bf16[512,768]{1,0:T(8,128)(2,1)S(1)}, u32[]{:S(2)}, u32[]{:S(2)}) collective-permute-start(bf16[512,768]{1,0:T(8,128)(2,1)S(1)} %get-tuple-element.382), channel_id=1, source_target_pairs={{0,8},{8,16},{16,24},{1,9},{9,17},{17,25},{2,10},{10,18},{18,26},{... | collective-permute-start | bytes 2359304 | tf_op jit(solution)/shard_map/ppermute | solution.py:483
  309.4 272.4 %all-gather.11.cloned.1.call-start = ((), (), s32[]{:S(2)}) async-start(), calls=%async_computation.5 | async-start | bytes 12976128 | tf_op jit(solution)/shard_map/all_gather | solution.py:741
  359.1 24.5 %collective-permute-start.18 = (bf16[256,768]{1,0:T(8,128)(2,1)}, bf16[256,768]{1,0:T(8,128)(2,1)S(1)}, u32[]{:S(2)}, u32[]{:S(2)}) collective-permute-start(bf16[256,768]{1,0:T(8,128)(2,1)} %get-tuple-element.405), channel_id=1, source_target_pairs={{0,8},{8,16},{16,24},{1,9},{9,17},{17,25},{2,10},{10,18},{18,26},{... | collective-permute-start | bytes 1179656 | tf_op jit(solution)/shard_map/ppermute | solution.py:483
  365.6 30.2 %collective-permute-start.21 = (bf16[256,768]{1,0:T(8,128)(2,1)}, bf16[256,768]{1,0:T(8,128)(2,1)}, u32[]{:S(2)}, u32[]{:S(2)}) collective-permute-start(bf16[256,768]{1,0:T(8,128)(2,1)} %get-tuple-element.406), channel_id=1, source_target_pairs={{24,16},{16,8},{8,0},{25,17},{17,9},{9,1},{26,18},{18,10},{10,2},{... | collective-permute-start | bytes 1179656 | tf_op jit(solution)/shard_map/ppermute | solution.py:484
  417.3 35.2 %collective-permute-start.30 = (bf16[512,1536]{1,0:T(8,128)(2,1)S(1)}, bf16[512,1536]{1,0:T(8,128)(2,1)S(1)}, u32[]{:S(2)}, u32[]{:S(2)}) collective-permute-start(bf16[512,1536]{1,0:T(8,128)(2,1)S(1)} %convolution_convert_fusion.7.refs_1_.refs_2_), channel_id=1, source_target_pairs={{0,2},{2,0},{1,3},{3,1},{4,6},{6,4},{5,7},{7,5},{8,10},{10,8},{9,1... | collective-permute-start | bytes 4718600 | tf_op jit(solution)/shard_map/ppermute | solution.py:423
  486.1 483.0 %reduce-scatter.7.cloned.1.call-start = ((), (), s32[]{:S(2)}) async-start(), calls=%async_computation.6 | async-start | bytes 9732096
  660.9 32.9 %collective-permute-start.42 = (bf16[8,2,64,768]{3,2,1,0:T(8,128)(2,1)}, bf16[8,2,64,768]{3,2,1,0:T(8,128)(2,1)}, u32[]{:S(2)}, u32[]{:S(2)}) collective-permute-start(bf16[8,2,64,768]{3,2,1,0:T(8,128)(2,1)} %get-tuple-element.84), channel_id=1, source_target_pairs={{0,2},{2,0},{1,3},{3,1},{4,6},{6,4},{5,7},{7,5},{8,10},{10,8},{9,1... | collective-permute-start | bytes 4718600 | tf_op jit(solution)/shard_map/ppermute | solution.py:423
  661.0 36.9 %collective-permute-start.48 = (bf16[8,2,64,768]{3,2,1,0:T(8,128)(2,1)}, bf16[8,2,64,768]{3,2,1,0:T(8,128)(2,1)S(1)}, u32[]{:S(2)}, u32[]{:S(2)}) collective-permute-start(bf16[8,2,64,768]{3,2,1,0:T(8,128)(2,1)} %get-tuple-element.86), channel_id=1, source_target_pairs={{0,2},{2,0},{1,3},{3,1},{4,6},{6,4},{5,7},{7,5},{8,10},{10,8},{9,1... | collective-permute-start | bytes 4718600 | tf_op jit(solution)/shard_map/ppermute | solution.py:423
  677.4 24.3 %collective-permute-start.60 = (bf16[8,2,64,768]{3,2,1,0:T(8,128)(2,1)}, bf16[8,2,64,768]{3,2,1,0:T(8,128)(2,1)S(1)}, u32[]{:S(2)}, u32[]{:S(2)}) collective-permute-start(bf16[8,2,64,768]{3,2,1,0:T(8,128)(2,1)} %get-tuple-element.90), channel_id=1, source_target_pairs={{0,2},{2,0},{1,3},{3,1},{4,6},{6,4},{5,7},{7,5},{8,10},{10,8},{9,1... | collective-permute-start | bytes 4718600 | tf_op jit(solution)/shard_map/ppermute | solution.py:423
  700.5 33.2 %collective-permute-start.55 = (bf16[4,2,64,768]{3,2,0,1:T(8,128)(2,1)S(1)}, bf16[4,2,64,768]{3,2,0,1:T(8,128)(2,1)S(1)}, u32[]{:S(2)}, u32[]{:S(2)}) collective-permute-start(bf16[4,2,64,768]{3,2,0,1:T(8,128)(2,1)S(1)} %bitcast.620), channel_id=1, source_target_pairs={{0,1},{1,0},{2,3},{3,2},{4,5},{5,4},{6,7},{7,6},{8,9},{9,8},{10,11... | collective-permute-start | bytes 2359304 | tf_op jit(solution)/shard_map/ppermute | solution.py:423
  702.4 33.6 %collective-permute-start.61 = (bf16[4,2,64,768]{3,2,0,1:T(8,128)(2,1)S(1)}, bf16[4,2,64,768]{3,2,0,1:T(8,128)(2,1)S(1)}, u32[]{:S(2)}, u32[]{:S(2)}) collective-permute-start(bf16[4,2,64,768]{3,2,0,1:T(8,128)(2,1)S(1)} %bitcast.621), channel_id=1, source_target_pairs={{0,4},{4,0},{1,5},{5,1},{2,6},{6,2},{3,7},{7,3},{8,12},{12,8},{9,1... | collective-permute-start | bytes 2359304 | tf_op jit(solution)/shard_map/ppermute | solution.py:423
  717.1 27.2 %collective-permute-start.44 = (bf16[4,64,768]{2,1,0:T(8,128)(2,1)S(1)}, bf16[4,64,768]{2,1,0:T(8,128)(2,1)S(1)}, u32[]{:S(2)}, u32[]{:S(2)}) collective-permute-start(bf16[4,64,768]{2,1,0:T(8,128)(2,1)S(1)} %dynamic-slice_bitcast_fusion.9), channel_id=1, source_target_pairs={{0,4},{4,0},{1,5},{5,1},{2,6},{6,2},{3,7},{7,3},{8,12},{12,8},{9,1... | collective-permute-start | bytes 1179656 | tf_op jit(solution)/shard_map/ppermute | solution.py:423
  719.3 27.3 %collective-permute-start.50 = (bf16[4,64,768]{2,1,0:T(8,128)(2,1)S(1)}, bf16[4,64,768]{2,1,0:T(8,128)(2,1)S(1)}, u32[]{:S(2)}, u32[]{:S(2)}) collective-permute-start(bf16[4,64,768]{2,1,0:T(8,128)(2,1)S(1)} %dynamic-slice_bitcast_fusion.8), channel_id=1, source_target_pairs={{0,1},{1,0},{2,3},{3,2},{4,5},{5,4},{6,7},{7,6},{8,9},{9,8},{10,11... | collective-permute-start | bytes 1179656 | tf_op jit(solution)/shard_map/ppermute | solution.py:423
  806.7 548.7 %reduce-scatter.9.cloned.1.call-start = ((), (), s32[]{:S(2)}) async-start(), calls=%async_computation.7 | async-start | bytes 19464192
  859.0 40.4 %collective-permute-start.66 = (bf16[2,512,768]{2,1,0:T(8,128)(2,1)}, bf16[2,512,768]{2,1,0:T(8,128)(2,1)}, u32[]{:S(2)}, u32[]{:S(2)}) collective-permute-start(bf16[2,512,768]{2,1,0:T(8,128)(2,1)} %get-tuple-element.93), channel_id=1, source_target_pairs={{0,2},{2,0},{1,3},{3,1},{4,6},{6,4},{5,7},{7,5},{8,10},{10,8},{9,1... | collective-permute-start | bytes 4718600 | tf_op jit(solution)/shard_map/ppermute | solution.py:423
  892.5 26.3 %collective-permute-start.72 = (bf16[256,768]{1,0:T(8,128)(2,1)S(1)}, bf16[256,768]{1,0:T(8,128)(2,1)}, u32[]{:S(2)}, u32[]{:S(2)}) collective-permute-start(bf16[256,768]{1,0:T(8,128)(2,1)S(1)} %collective-permute-done.68), channel_id=1, source_target_pairs={{0,8},{8,16},{16,24},{1,9},{9,17},{17,25},{2,10},{10,18},{18,26},{... | collective-permute-start | bytes 1179656 | tf_op jit(solution)/shard_map/ppermute | solution.py:470
  897.7 26.6 %collective-permute-start.70 = (bf16[256,768]{1,0:T(8,128)(2,1)}, bf16[256,768]{1,0:T(8,128)(2,1)}, u32[]{:S(2)}, u32[]{:S(2)}) collective-permute-start(bf16[256,768]{1,0:T(8,128)(2,1)} %collective-permute-done.69), channel_id=1, source_target_pairs={{8,0},{16,8},{24,16},{9,1},{17,9},{25,17},{10,2},{18,10},{26,18},{... | collective-permute-start | bytes 1179656 | tf_op jit(solution)/shard_map/ppermute | solution.py:471
  918.8 46.4 %collective-permute-start.73 = (bf16[256,768]{1,0:T(8,128)(2,1)}, bf16[256,768]{1,0:T(8,128)(2,1)}, u32[]{:S(2)}, u32[]{:S(2)}) collective-permute-start(bf16[256,768]{1,0:T(8,128)(2,1)} %collective-permute-done.72), channel_id=1, source_target_pairs={{0,8},{8,16},{16,24},{1,9},{9,17},{17,25},{2,10},{10,18},{18,26},{... | collective-permute-start | bytes 1179656 | tf_op jit(solution)/shard_map/ppermute | solution.py:470
  924.3 43.0 %collective-permute-start.71 = (bf16[256,768]{1,0:T(8,128)(2,1)}, bf16[256,768]{1,0:T(8,128)(2,1)}, u32[]{:S(2)}, u32[]{:S(2)}) collective-permute-start(bf16[256,768]{1,0:T(8,128)(2,1)} %collective-permute-done.70), channel_id=1, source_target_pairs={{8,0},{16,8},{24,16},{9,1},{17,9},{25,17},{10,2},{18,10},{26,18},{... | collective-permute-start | bytes 1179656 | tf_op jit(solution)/shard_map/ppermute | solution.py:471
  1061.1 39.9 %collective-permute-start.75 = (bf16[512,768]{1,0:T(8,128)(2,1)}, bf16[512,768]{1,0:T(8,128)(2,1)S(1)}, u32[]{:S(2)}, u32[]{:S(2)}) collective-permute-start(bf16[512,768]{1,0:T(8,128)(2,1)} %fusion.42.refs_1_), channel_id=1, source_target_pairs={{0,8},{8,16},{16,24},{1,9},{9,17},{17,25},{2,10},{10,18},{18,26},{... | collective-permute-start | bytes 2359304 | tf_op jit(solution)/shard_map/ppermute | solution.py:470
  1066.0 40.2 %collective-permute-start.76 = (bf16[512,768]{1,0:T(8,128)(2,1)}, bf16[512,768]{1,0:T(8,128)(2,1)}, u32[]{:S(2)}, u32[]{:S(2)}) collective-permute-start(bf16[512,768]{1,0:T(8,128)(2,1)} %fusion.42.refs_1_), channel_id=1, source_target_pairs={{8,0},{16,8},{24,16},{9,1},{17,9},{25,17},{10,2},{18,10},{26,18},{... | collective-permute-start | bytes 2359304 | tf_op jit(solution)/shard_map/ppermute | solution.py:471
  1122.3 33.4 %collective-permute-start.80 = (bf16[512,768]{1,0:T(8,128)(2,1)}, bf16[512,768]{1,0:T(8,128)(2,1)}, u32[]{:S(2)}, u32[]{:S(2)}) collective-permute-start(bf16[512,768]{1,0:T(8,128)(2,1)} %collective-permute-done.79), channel_id=1, source_target_pairs={{0,8},{8,16},{16,24},{1,9},{9,17},{17,25},{2,10},{10,18},{18,26},{... | collective-permute-start | bytes 2359304 | tf_op jit(solution)/shard_map/ppermute | solution.py:470
  1127.7 46.0 %collective-permute-start.78 = (bf16[512,768]{1,0:T(8,128)(2,1)}, bf16[512,768]{1,0:T(8,128)(2,1)}, u32[]{:S(2)}, u32[]{:S(2)}) collective-permute-start(bf16[512,768]{1,0:T(8,128)(2,1)} %collective-permute-done.77), channel_id=1, source_target_pairs={{8,0},{16,8},{24,16},{9,1},{17,9},{25,17},{10,2},{18,10},{26,18},{... | collective-permute-start | bytes 2359304 | tf_op jit(solution)/shard_map/ppermute | solution.py:471
  1131.3 71.7 %collective-permute-start.92 = (bf16[4,2,2,24,1664]{4,3,2,1,0:T(8,128)(2,1)}, bf16[4,2,2,24,1664]{4,3,2,1,0:T(8,128)(2,1)}, u32[]{:S(2)}, u32[]{:S(2)}) collective-permute-start(bf16[4,2,2,24,1664]{4,3,2,1,0:T(8,128)(2,1)} %get-tuple-element.389), channel_id=1, source_target_pairs={{0,2},{2,0},{1,3},{3,1},{4,6},{6,4},{5,7},{7,5},{8,10},{10,8},{9,1... | collective-permute-start | bytes 3833864 | tf_op jit(solution)/shard_map/ppermute | solution.py:423
  1137.7 61.9 %collective-permute-start.86 = (bf16[4,2,2,24,1536]{4,3,2,1,0:T(8,128)(2,1)S(1)}, bf16[4,2,2,24,1536]{4,3,2,1,0:T(8,128)(2,1)S(1)}, u32[]{:S(2)}, u32[]{:S(2)}) collective-permute-start(bf16[4,2,2,24,1536]{4,3,2,1,0:T(8,128)(2,1)S(1)} %dynamic-slice_bitcast_fusion.1), channel_id=1, source_target_pairs={{0,2},{2,0},{1,3},{3,1},{4,6},{6,4},{5,7},{7,5},{8,10},{10,8},{9,1... | collective-permute-start | bytes 3538952 | tf_op jit(solution)/shard_map/ppermute | solution.py:423
  1199.5 86.6 %collective-permute-start.81 = (bf16[4032,768]{1,0:T(8,128)(2,1)}, bf16[4032,768]{1,0:T(8,128)(2,1)}, u32[]{:S(2)}, u32[]{:S(2)}) collective-permute-start(bf16[4032,768]{1,0:T(8,128)(2,1)} %shard_map.473), channel_id=1, source_target_pairs={{0,2},{2,0},{1,3},{3,1},{4,6},{6,4},{5,7},{7,5},{8,10},{10,8},{9,1... | collective-permute-start | bytes 18579464 | tf_op jit(solution)/shard_map/ppermute | solution.py:423
  1201.8 23.4 %collective-permute-start.87 = (bf16[4,2,24,1536]{3,2,1,0:T(8,128)(2,1)}, bf16[4,2,24,1536]{3,2,1,0:T(8,128)(2,1)}, u32[]{:S(2)}, u32[]{:S(2)}) collective-permute-start(bf16[4,2,24,1536]{3,2,1,0:T(8,128)(2,1)} %dynamic-slice_bitcast_fusion.2), channel_id=1, source_target_pairs={{0,1},{1,0},{2,3},{3,2},{4,5},{5,4},{6,7},{7,6},{8,9},{9,8},{10,11... | collective-permute-start | bytes 1769480 | tf_op jit(solution)/shard_map/ppermute | solution.py:423
  1228.1 24.3 %collective-permute-start.88 = (bf16[4,24,1536]{2,1,0:T(8,128)(2,1)}, bf16[4,24,1536]{2,1,0:T(8,128)(2,1)}, u32[]{:S(2)}, u32[]{:S(2)}) collective-permute-start(bf16[4,24,1536]{2,1,0:T(8,128)(2,1)} %dynamic-slice_bitcast_fusion.10), channel_id=1, source_target_pairs={{0,4},{4,0},{1,5},{5,1},{2,6},{6,2},{3,7},{7,3},{8,12},{12,8},{9,1... | collective-permute-start | bytes 884744 | tf_op jit(solution)/shard_map/ppermute | solution.py:423
  1254.9 58.9 %collective-permute-start.89 = (bf16[24,1536]{1,0:T(8,128)(2,1)}, bf16[24,1536]{1,0:T(8,128)(2,1)S(1)}, u32[]{:S(2)}, u32[]{:S(2)}) collective-permute-start(bf16[24,1536]{1,0:T(8,128)(2,1)} %get-tuple-element.477), channel_id=1, source_target_pairs={{0,8},{8,16},{16,24},{24,0},{1,9},{9,17},{17,25},{25,1},{2,10},{10... | collective-permute-start | bytes 221192 | tf_op jit(solution)/shard_map/ppermute | solution.py:455
  1255.6 60.7 %collective-permute-start.90 = (bf16[24,1536]{1,0:T(8,128)(2,1)}, bf16[24,1536]{1,0:T(8,128)(2,1)S(1)}, u32[]{:S(2)}, u32[]{:S(2)}) collective-permute-start(bf16[24,1536]{1,0:T(8,128)(2,1)} %get-tuple-element.479), channel_id=1, source_target_pairs={{0,16},{8,24},{16,0},{24,8},{1,17},{9,25},{17,1},{25,9},{2,18},{10... | collective-permute-start | bytes 221192 | tf_op jit(solution)/shard_map/ppermute | solution.py:455
  1255.6 61.2 %collective-permute-start.91 = (bf16[24,1536]{1,0:T(8,128)(2,1)}, bf16[24,1536]{1,0:T(8,128)(2,1)}, u32[]{:S(2)}, u32[]{:S(2)}) collective-permute-start(bf16[24,1536]{1,0:T(8,128)(2,1)} %get-tuple-element.478), channel_id=1, source_target_pairs={{0,24},{8,0},{16,8},{24,16},{1,25},{9,1},{17,9},{25,17},{2,26},{10... | collective-permute-start | bytes 221192 | tf_op jit(solution)/shard_map/ppermute | solution.py:455
  1308.0 27.4 %collective-permute-start.96 = (bf16[24,1664]{0,1:T(8,128)(2,1)S(1)}, bf16[24,1664]{0,1:T(8,128)(2,1)S(1)}, u32[]{:S(2)}, u32[]{:S(2)}) collective-permute-start(bf16[24,1664]{0,1:T(8,128)(2,1)S(1)} %get-tuple-element.392), channel_id=1, source_target_pairs={{0,16},{8,24},{16,0},{24,8},{1,17},{9,25},{17,1},{25,9},{2,18},{10... | collective-permute-start | bytes 239624 | tf_op jit(solution)/shard_map/ppermute | solution.py:455
  1316.3 32.0 %collective-permute-start.83 = (bf16[1008,768]{1,0:T(8,128)(2,1)}, bf16[1008,768]{1,0:T(8,128)(2,1)S(1)}, u32[]{:S(2)}, u32[]{:S(2)}) collective-permute-start(bf16[1008,768]{1,0:T(8,128)(2,1)} %pad_maximum_fusion.5), channel_id=1, source_target_pairs={{0,1},{1,0},{2,3},{3,2},{4,5},{5,4},{6,7},{7,6},{8,9},{9,8},{10,11... | collective-permute-start | bytes 4644872 | tf_op jit(solution)/shard_map/ppermute | solution.py:423
  1316.8 31.8 %collective-permute-start.85 = (bf16[1008,768]{1,0:T(8,128)(2,1)}, bf16[1008,768]{1,0:T(8,128)(2,1)}, u32[]{:S(2)}, u32[]{:S(2)}) collective-permute-start(bf16[1008,768]{1,0:T(8,128)(2,1)} %pad_maximum_fusion.6), channel_id=1, source_target_pairs={{0,4},{4,0},{1,5},{5,1},{2,6},{6,2},{3,7},{7,3},{8,12},{12,8},{9,1... | collective-permute-start | bytes 4644872 | tf_op jit(solution)/shard_map/ppermute | solution.py:423
  (216 other events, 3521.9 us)
Sparse Core Ops, SparseCore 0:
  20.2 122.7 all-gather.4
  146.4 99.7 all-gather.6
  309.5 95.4 all-gather.8
  486.2 95.5 all-gather.10
  806.8 142.8 reduce-scatter.6
  970.9 235.6 reduce-scatter.8

commit v4 on v3

--- a/solution.py
+++ b/solution.py
@@ -62,9 +62,18 @@
     return lax.dot_general(a, b, (((1,), (0,)), ((), ())), preferred_element_type=f32)
 
 
-def spread(eight, rows, width):
-    total = eight.shape[-1]
-    grid = eight
+def shifted_rows(grid, back):
+    total = grid.shape[-1]
+    row = 7 - lax.broadcasted_iota(jnp.int32, grid.shape, 0)
+    for bit in (1, 2, 4):
+        moved = pltpu.roll(grid, bit if back else total - bit, 1)
+        grid = jnp.where((row & bit) != 0, moved, grid)
+    return grid
+
+
+def spread(line, rows, width):
+    total = line.shape[-1]
+    grid = shifted_rows(jnp.broadcast_to(line, (8, total)), False)
     have = 8
     while have < rows:
         grid = jnp.concatenate([pltpu.roll(grid, total - have, 1), grid], axis=0)
@@ -78,7 +87,7 @@
     while rows > 8:
         rows //= 2
         have = pltpu.roll(have[:rows], rows, 1) + have[rows:]
-    return have
+    return jnp.sum(shifted_rows(have, True), axis=0, keepdims=True)
 
 
 def probs_of(cfg, refs, block, head):
@@ -91,7 +100,7 @@
         keys = refs["k"][part][:, cols]
         s = dot_nt(query, keys) * HEAD_DIM ** (-0.5)
         if has_bias:
-            s = s + spread(refs["x8"][block, part, head], bq, keys.shape[0])
+            s = s + spread(refs["x8"][head, pl.ds(block * 2 + part, 1), :], bq, keys.shape[0])
         allowed = refs["qseg"][rows, :] == refs["kseg"][part]
         if causal:
             allowed = allowed & (refs["kpos"][part] <= refs["qpos"][rows, :])
@@ -160,7 +169,8 @@
                 dk[part] = k_term if dk[part] is None else dk[part] + k_term
                 dv[part] = v_term if dv[part] is None else dv[part] + v_term
                 if has_bias:
-                    y8[block, part, head] = collect(ds.astype(f32), y8.shape[-1])
+                    line = collect(ds.astype(f32), y8.shape[-1])
+                    y8[head, pl.ds(block * 2 + part, 1), :] = line
             dq[rows, cols] = (acc * HEAD_DIM ** (-0.5)).astype(bf16)
         for part, target in enumerate((own, other)):
             target[0, :, cols] = (dk[part] * HEAD_DIM ** (-0.5)).T.astype(target.dtype)
@@ -176,9 +186,7 @@
     specs = [pl.BlockSpec((q_len, 128), lambda i: (0, i))] + kv + kv
     specs += [whole((q_len, 1)), whole((1, k_len)), whole((1, k_len))] * 2
     if has_bias:
-        specs.append(
-            pl.BlockSpec((x8.shape[0], 2, 2, 8, x8.shape[-1]), lambda i: (0, 0, i, 0, 0))
-        )
+        specs.append(pl.BlockSpec((2,) + x8.shape[1:], lambda i: (i, 0, 0)))
     return specs
 
 
@@ -218,9 +226,7 @@
         jax.ShapeDtypeStruct((2, k_len, D), bf16),
     ]
     if x8 is not None:
-        out_specs.append(
-            pl.BlockSpec((x8.shape[0], 2, 2, 8, x8.shape[-1]), lambda i: (0, 0, i, 0, 0))
-        )
+        out_specs.append(pl.BlockSpec((2,) + x8.shape[1:], lambda i: (i, 0, 0)))
         out_shape.append(jax.ShapeDtypeStruct(x8.shape, f32))
     return pl.pallas_call(
         functools.partial(attend_backward_kernel, cfg),
@@ -244,33 +250,25 @@
     return bases
 
 
-def bias_eights(table, bucket_row, core, q_len, k_len):
-    size = bucket_row.shape[0]
+def bias_windows(array, core, q_len, k_len):
+    size = array.shape[1]
+    array = jnp.pad(array, ((0, 0), (0, 16)))
+    bases = bias_bases(core, q_len, k_len, size // 2)
+    cut = lambda base: lax.dynamic_slice_in_dim(array, base, k_len + 256, axis=1)
+    return jnp.stack([cut(base) for base in bases], axis=1)
+
+
+def bias_lines(table, bucket_row, core, q_len, k_len):
     picks = (bucket_row[None, :] == jnp.arange(BUCKETS, dtype=jnp.int32)[:, None]).astype(bf16)
     per_offset = jnp.einsum("bh,bn->hn", table, picks, preferred_element_type=f32)
-    per_offset = jnp.pad(per_offset, ((0, 0), (0, 16)))
-    width = k_len + 256
-    found = []
-    for base in bias_bases(core, q_len, k_len, size // 2):
-        window = lax.dynamic_slice_in_dim(per_offset, base, width + 7, axis=1)
-        found.append(jnp.stack([window[:, 7 - r : 7 - r + width] for r in range(8)], axis=1))
-    return jnp.stack(found).reshape(q_len // 256, 2, HEADS, 8, width), picks
-
-
-def bias_gradient(y8, picks, core, q_len, k_len):
-    size = picks.shape[1]
-    width = k_len + 256
-    total = jnp.zeros((HEADS, size + 16), f32)
-    flat = y8.reshape(-1, HEADS, 8, width)
-    for number, base in enumerate(bias_bases(core, q_len, k_len, size // 2)):
-        window = sum(
-            jnp.pad(flat[number, :, r], ((0, 0), (7 - r, r))) for r in range(8)
-        )
-        old = lax.dynamic_slice_in_dim(total, base, width + 7, axis=1)
-        total = lax.dynamic_update_slice_in_dim(total, old + window, base, axis=1)
-    return jnp.einsum(
-        "bn,hn->bh", picks.astype(f32), total[:, :size], precision=lax.Precision.HIGHEST
-    )
+    return (
+        bias_windows(per_offset, core, q_len, k_len),
+        bias_windows(picks.astype(f32), core, q_len, k_len),
+    )
+
+
+def bias_gradient(y8, picks):
+    return jnp.einsum("bnw,hnw->bh", picks, y8, precision=lax.Precision.HIGHEST)
 
 
 def head_stats_kernel(count, hid, tab, tgt, lse_out, pick_out):
@@ -371,7 +369,6 @@
 
 
 def place_rows(pairs, first, parts, rows):
-    tokens = sum(grads.shape[0] for _, grads in pairs)
     specs, args = [], []
     for ids, grads in pairs:
         specs.append(pl.BlockSpec(ids.shape, lambda i: (0, 0)))
@@ -384,9 +381,7 @@
         out_specs=pl.BlockSpec((rows, D), lambda i: (i, 0)),
         out_shape=jax.ShapeDtypeStruct((parts * rows, D), bf16),
         compiler_params=pltpu.CompilerParams(vmem_limit_bytes=VMEM_LIMIT),
-        cost_estimate=pl.CostEstimate(
-            flops=2 * tokens * parts * rows * D, bytes_accessed=2 * parts * rows * D, transcendentals=0
-        ),
+        cost_estimate=pl.CostEstimate(flops=1, bytes_accessed=rows, transcendentals=0),
     )(*args)
 
 
@@ -457,10 +452,13 @@
     return total
 
 
+def scatter_core(value):
+    sizes = tuple(lax.axis_size(axis) for axis in ALL)
+    return scatter_pair(value.reshape(sizes + (-1, value.shape[-1])), "core", 2)
+
+
 def scatter_chain(value, seq_first):
-    sizes = tuple(lax.axis_size(axis) for axis in ALL)
-    value = value.reshape(sizes + (-1, value.shape[-1]))
-    return scatter_rest(scatter_pair(value, "core", 2), seq_first)
+    return scatter_rest(scatter_core(value), seq_first)
 
 
 def line_gather(value, axis):
@@ -502,11 +500,13 @@
     return ((other >> 1) & 1) * 4 + (other >> 2) * 2 + (other & 1)
 
 
-def plane_scatter(pairs, rows):
+def plane_scatter(pairs, rows, before):
+    pairs, before = lax.optimization_barrier((pairs, before))
     count = lax.axis_size(PLANE)
     if lax.axis_size("p") != 2:
         placed = place_rows(pairs, 0, count, rows)
-        return lax.psum_scatter(placed, PLANE, scatter_dimension=0, tiled=True).astype(f32)
+        placed = lax.psum_scatter(placed, PLANE, scatter_dimension=0, tiled=True)
+        return placed.astype(f32), before
     away = swap_core(place_rows(pairs, 4, 4, rows))
     home = place_rows(pairs, 0, 4, rows)
     half = rows // 2
@@ -517,7 +517,7 @@
     p_low = add16(part(2 * rows, 2 * rows + half), got_low)
     from_seq = swap(jnp.concatenate([part(rows, rows + half), seq_high]), "seq")
     from_p = swap(jnp.concatenate([p_low, part(2 * rows + half, 3 * rows)]), "p")
-    return part(0, rows).astype(f32) + from_seq.astype(f32) + from_p.astype(f32)
+    return part(0, rows).astype(f32) + from_seq.astype(f32) + from_p.astype(f32), before
 
 
 def add_logs(left, right):
@@ -680,8 +680,8 @@
         got = jnp.take(plane_table, jnp.concatenate(items), axis=0, mode="clip")
         return line_scatter(jnp.split(got, len(items)), "z")
 
-    enc_x0 = look(enc_places)
-    dec_y0 = look(dec_places)
+    looked = look(places)
+    enc_x0, dec_y0 = looked[:enc_count], looked[enc_count:]
 
     cut = lambda pack, start, width: lax.slice_in_dim(pack, start, start + width, axis=1)
     enc_wi, enc_fi = cut(enc_pack, 0, 3 * D), cut(enc_pack, 3 * D, 2 * FF)
@@ -691,8 +691,8 @@
     rel_all = jnp.transpose(misc_all[:, 7].reshape(-1, 2, rel_table.shape[1]), (1, 0, 2))
     rel_all = rel_all.reshape(2, BUCKETS, HEADS)
 
-    enc_x8, enc_picks = bias_eights(rel_all[0], buckets[0], core, enc_count, enc_count)
-    dec_x8, dec_picks = bias_eights(rel_all[1], buckets[1], core, dec_count, dec_count)
+    enc_x8, enc_picks = bias_lines(rel_all[0], buckets[0], core, enc_count, enc_count)
+    dec_x8, dec_picks = bias_lines(rel_all[1], buckets[1], core, dec_count, dec_count)
     col, line = (lambda v: v[:, None]), (lambda v: v[None, :])
     enc_info = (
         col(enc_seg), line(enc_seg), line(enc_seg_other),
@@ -797,7 +797,7 @@
     )
     got = (own + swap_core(other).astype(f32)).astype(bf16)
     d_dec_qkv = jnp.concatenate([d_dec_q, got[0], got[1]], axis=1)
-    d_dec_table = bias_gradient(dec_y8, dec_picks, core, dec_count, dec_count)
+    d_dec_table = bias_gradient(dec_y8, dec_picks)
     d_dec_wi = weight_grad(dec_n1, d_dec_qkv)
     d_y0_norm, d_gain_datt = norm_pull(dec_y0, gain[3], 1.0, input_grad(d_dec_qkv, dec_wi))
     d_y0 = d_y1 + d_y0_norm
@@ -819,23 +819,24 @@
     d_x1, d_gain_effn, d_enc_fi, d_enc_fo = ffn_backward(
         d_x2, enc_x1, gain[1], enc_fi, enc_fo, enc_saved
     )
+    early, d_x1 = lax.optimization_barrier((early, d_x1))
     d_enc_wo, d_enc_ob = branch_backward(d_x1, enc_ob, enc_wo)
-    late, early, dec_lines, d_enc_ob = lax.optimization_barrier(
-        (
-            jnp.concatenate([d_dec_rest, d_enc_fi, rows_in(d_enc_fo)], axis=1),
-            early,
-            dec_lines,
-            d_enc_ob,
-        )
-    )
-    late = lax.psum_scatter(late, ALL, scatter_dimension=0, tiled=True).astype(f32)
+    d_enc_low, d_enc_high = d_enc_fi[:, :3456], jnp.concatenate([d_enc_fi[:, 3456:], d_enc_wo], 1)
+    enc_sums = [scatter_core(item) for item in (d_enc_low, d_enc_high, d_enc_fo)]
+    late, dec_lines, enc_sums, d_enc_ob = lax.optimization_barrier(
+        (d_dec_rest, dec_lines, enc_sums, d_enc_ob)
+    )
+    late = lax.psum_scatter(late, ALL, scatter_dimension=0, tiled=True)
     early = early.astype(f32)
+    g_low, g_high, g_fo = [
+        scatter_rest(item, number == 0) for number, item in enumerate(enc_sums)
+    ]
     d_enc_q, own, other, enc_y8 = attend_backward(
         d_enc_ob, enc_q, enc_kv, enc_kv2, enc_info, enc_x8, False
     )
     got = (own + swap_core(other).astype(f32)).astype(bf16)
     d_enc_qkv = jnp.concatenate([d_enc_q, got[0], got[1]], axis=1)
-    d_enc_table = bias_gradient(enc_y8, enc_picks, core, enc_count, enc_count)
+    d_enc_table = bias_gradient(enc_y8, enc_picks)
     d_enc_wi = weight_grad(enc_n1, d_enc_qkv)
     d_x0_norm, d_gain_eatt = norm_pull(enc_x0, gain[0], 1.0, input_grad(d_enc_qkv, enc_wi))
     d_x0 = d_x1 + d_x0_norm
@@ -846,7 +847,8 @@
         (far_place(item), grads)
         for item, grads in zip(enc_places + dec_places, enc_lines + dec_lines)
     ]
-    input_embed = plane_scatter(pairs, padded)
+    input_embed, late = plane_scatter(pairs, padded, late)
+    late = late.astype(f32)
     grad_embed = head_embed[:shard] + input_embed[:shard]
 
     d_gains = jnp.stack(
@@ -863,22 +865,25 @@
     d_rel = jnp.stack([d_enc_table.reshape(-1), d_dec_table.reshape(-1)])
     d_rel = jnp.transpose(d_rel.reshape(2, -1, rel_table.shape[1]), (1, 0, 2)).reshape(D, 1)
     d_misc = jnp.pad(jnp.concatenate([d_gains.T, d_rel], axis=1), ((0, 0), (0, 120)))
-    d_last = jnp.concatenate([d_enc_wi.astype(bf16), d_enc_wo, d_misc.astype(bf16)], axis=1)
-    last = jnp.concatenate(
-        [scatter_chain(d_last[:, : 2 * D], True), scatter_chain(d_last[:, 2 * D :], False)], axis=1
-    )
+    d_last = jnp.concatenate([d_enc_wi.astype(bf16), d_misc.astype(bf16)], axis=1)
+    last = [scatter_chain(d_last[:, :1152], True), scatter_chain(d_last[:, 1152:], False)]
+    squares = sum(
+        (jnp.sum(item * item) for item in (grad_embed, early, late, g_low, g_high, g_fo, *last))
+    )
+    sums = fold_all(jnp.stack([jnp.sum(mask), loss_local, squares]), jnp.add)
+    last = jnp.concatenate(last, axis=1)
     rows_out = lambda out: out.reshape(-1, D)
     owned = (
         jnp.stack([cut(last, 0, 3 * D), cut(late, 0, 3 * D), cut(late, 3 * D, 3 * D)]),
-        jnp.stack([cut(last, 3 * D, D), cut(late, 6 * D, D), cut(late, 7 * D, D)]),
-        jnp.stack([cut(late, 8 * D, 2 * FF), cut(early, 0, 2 * FF)]),
-        jnp.stack([rows_out(cut(late, 8 * D + 2 * FF, FF)), rows_out(cut(early, 2 * FF, FF))]),
-        last[:, 4 * D + 7].reshape(2, -1),
-        last[:, 4 * D : 4 * D + 7].T,
+        jnp.stack([cut(g_high, 640, D), cut(late, 6 * D, D), cut(late, 7 * D, D)]),
+        jnp.stack(
+            [jnp.concatenate([g_low, cut(g_high, 0, 640)], axis=1), cut(early, 0, 2 * FF)]
+        ),
+        jnp.stack([g_fo, rows_out(cut(early, 2 * FF, FF))]),
+        last[:, 3 * D + 7].reshape(2, -1),
+        last[:, 3 * D : 3 * D + 7].T,
     )
     grads = (grad_embed,) + owned
-    squares = sum((jnp.sum(item * item) for item in grads))
-    sums = fold_all(jnp.stack([jnp.sum(mask), loss_local, squares]), jnp.add)
     count_all, loss_all, squares_all = sums[0], sums[1], sums[2]
     grad_norm = jnp.sqrt(squares_all) / count_all
     factor = jnp.minimum(1.0, clip_limit / grad_norm) / count_all

time: 1450 us -> 1470 us (1.014)
  other arithmetic: 135 us -> 167 us
  local copies, waits for them, and re-layouts: 223 us -> 198 us
  Pallas kernels: 292 us -> 311 us
    ppermute x38 -> x47, waiting for transfers between devices: 117 us -> 165 us  [swap(): return lax.ppermute(value, axis, [(0, 1), (1, 0)])]
    ppermute x9, waiting for transfers between devices: 53.8 us -> 18.1 us  [line_gather(): lax.ppermute(ups[-1], axis, [(i, i + 1) for i in range(size - 1)])]
    ppermute x18 -> x27, waiting for transfers between devices: 27.4 us -> 54.7 us  [scatter_rest(): got = lax.ppermute(send, 'z', [(i, (i + hop) % size) for i in range(size)])]
    ppermute x6 -> x3, starting transfers between devices: 37.9 us -> 11.3 us  [line_scatter(): up = lax.ppermute(send_up, axis, [(i, i + 1) for i in range(step)])]
    all_gather x1, waiting for transfers between devices: 77 us -> 52 us  [body(): hidden_all = lax.all_gather(hidden_b, ALL, axis=0, tiled=True)]
    another operation x33 -> x14, local copies, waits for them, and re-layouts: 28.6 us -> 6.21 us  [the longest x1 1.81 us: body(): jnp.stack([jnp.concatenate([g_low, cut(g_high, 0, 640)], axis=1), cut(ear...]
    ppermute x18 -> x27, starting transfers between devices: 29 us -> 50 us  [scatter_rest(): got = lax.ppermute(send, 'z', [(i, (i + hop) % size) for i in range(size)])]
    unnamed x399 -> x389, local copies, waits for them, and re-layouts: 62.1 us -> 48.3 us
  transfers between devices with their start and end apart: 109 -> 121, of which waited for: 50 -> 53; matrix products, arithmetic and copies ran while one was open for 24% -> 25% of each run, Pallas kernels for 16% -> 17%
where the time goes in v4:
time: 1470 us; the launch traced here: 1460 us
  waiting for transfers between devices  454 us (31%)
  Pallas kernels  311 us (21%)
  local copies, waits for them, and re-layouts  198 us (13%)
  starting transfers between devices  179 us (12%)
  other arithmetic  167 us (11%)
  matrix products  118 us (8%)
  between operations  30.3 us (2%)
    ppermute x47, waiting for transfers between devices, swap(): return lax.ppermute(value, axis, [(0, 1), (1, 0)])  165 us
    pallas_call x3, Pallas kernels, attend_backward(): pl.pallas_call(functools.partial(attend_backward_kernel, cfg), grid=(HEAD...  112 us
    ppermute x3, waiting for transfers between devices, line_scatter(): up = lax.ppermute(send_up, axis, [(i, i + 1) for i in range(step)])  97.5 us
    pallas_call x4, Pallas kernels, head_grad(): pl.pallas_call(functools.partial(head_grad_kernel, count), grid_spec=pltp...  63.4 us
    pallas_call x3, Pallas kernels, attend_forward(): pl.pallas_call(functools.partial(attend_forward_kernel, cfg), grid=(HEADS...  62.3 us
    ppermute x27, waiting for transfers between devices, scatter_rest(): got = lax.ppermute(send, 'z', [(i, (i + hop) % size) for i in range(size)])  54.7 us
    all_gather x1, waiting for transfers between devices, body(): hidden_all = lax.all_gather(hidden_b, ALL, axis=0, tiled=True)  52 us
    ppermute x27, starting transfers between devices, scatter_rest(): got = lax.ppermute(send, 'z', [(i, (i + hop) % size) for i in range(size)])  50 us
  transfers between devices with their start and end apart: 121, of which 53 were waited for; matrix products, arithmetic and copies ran while one was open for 25% of the time, Pallas kernels for 17%

profile of v4, /device:TPU:0, one launch (start us, length us, event | category | flops | bytes accessed | tf_op | source)
XLA Modules:
  0.0 1456.2 jit_solution(8756907032284644644)
XLA Ops:
  42.9 28.0 %collective-permute-done.1 = bf16[1008,768]{1,0:T(8,128)(2,1)} collective-permute-done((bf16[1008,768]{1,0:T(8,128)(2,1)}, bf16[1008,768]{1,0:T(8,128)(2,1)}, u32[]{:S(2)}, u32[]{:S(2)}) %collective-permute-start.1) | collective-permute-done | bytes 1548320 | tf_op jit(solution)/shard_map/ppermute | solution.py:418
  80.0 18.7 %collective-permute-done.3 = bf16[504,768]{1,0:T(8,128)(2,1)S(1)} collective-permute-done((bf16[504,768]{1,0:T(8,128)(2,1)S(1)}, bf16[504,768]{1,0:T(8,128)(2,1)S(1)}, u32[]{:S(2)}, u32[]{:S(2)}) %collective-permute-start.3) | collective-permute-done | bytes 774176 | tf_op jit(solution)/shard_map/ppermute | solution.py:418
  113.2 26.6 %all-gather.5.cloned.1.call-done = bf16[768,9344]{1,0:T(8,128)(2,1)} async-done(((bf16[24,9344]{1,0:T(8,128)(2,1)}), bf16[768,9344]{1,0:T(8,128)(2,1)}) %all-gather.5.cloned.1.call-update) | async-done | bytes 14352400 | tf_op jit(solution)/shard_map/all_gather | solution.py:612
  139.9 20.7 %gather_fusion = bf16[3072,768]{1,0:T(8,128)(2,1)} fusion(bf16[8064,768]{1,0:T(8,128)(2,1)} %constant_dynamic-update-slice_fusion.4, s32[3072]{0:T(1024)S(1)} %add_clamp_fusion), kind=kCustom, calls=%fused_computation | custom fusion | bytes 9449472 | tf_op jit(solution)/shard_map/jit(_take)/gather | solution.py:680
  165.6 39.2 %collective-permute-done.16 = bf16[768,768]{1,0:T(8,128)(2,1)S(1)} collective-permute-done((bf16[768,768]{1,0:T(8,128)(2,1)S(1)}, bf16[768,768]{1,0:T(8,128)(2,1)S(1)}, u32[]{:S(2)}, u32[]{:S(2)}) %collective-permute-start.16) | collective-permute-done | bytes 1179680 | tf_op jit(solution)/shard_map/ppermute | solution.py:481
  214.5 39.3 %collective-permute-done.17 = bf16[768,768]{1,0:T(8,128)(2,1)S(1)} collective-permute-done((bf16[768,768]{1,0:T(8,128)(2,1)}, bf16[768,768]{1,0:T(8,128)(2,1)S(1)}, u32[]{:S(2)}, u32[]{:S(2)}) %collective-permute-start.17) | collective-permute-done | bytes 1179680 | tf_op jit(solution)/shard_map/ppermute | solution.py:481
  266.9 18.9 %collective-permute-done.18 = bf16[768,768]{1,0:T(8,128)(2,1)S(1)} collective-permute-done((bf16[768,768]{1,0:T(8,128)(2,1)}, bf16[768,768]{1,0:T(8,128)(2,1)S(1)}, u32[]{:S(2)}, u32[]{:S(2)}) %collective-permute-start.18) | collective-permute-done | bytes 1179680 | tf_op jit(solution)/shard_map/ppermute | solution.py:481
  304.5 35.4 %shard_map.461 = bf16[512,768]{1,0:T(8,128)(2,1)} custom-call(bf16[512,768]{1,0:T(8,128)(2,1)} %convolution_convert_fusion.15.refs_0_, bf16[512,1536]{1,0:T(8,128)(2,1)} %convolution_convert_fusion.8.refs_1_.refs_2_, bf16[512,1536]{1,0:T(8,128)(2,1)} %convolution_convert_fusion.8.refs_1_.refs_2_, bf16[512,1536]{1,0:T(8,128)(2,1)} %collective-permute-done.22.refs_3_.refs_4_, ...), custom_call_target="tpu_custom_call" | custom-call | flops 2 | bytes 512 | tf_op jit(solution)/shard_map/pallas_call | solution.py:207
  346.7 7.1 reshape.668
  358.6 5.6 fusion.7
  380.4 14.7 %shard_map.462 = bf16[256,768]{1,0:T(8,128)(2,1)} custom-call(bf16[256,768]{1,0:T(8,128)(2,1)} %convolution_convert_fusion.19.refs_0_, bf16[256,1536]{1,0:T(8,128)(2,1)} %copy-done.6, bf16[256,1536]{1,0:T(8,128)(2,1)} %copy-done.6, bf16[256,1536]{1,0:T(8,128)(2,1)} %copy-done.7, bf16[256,1536]{1,0:T(8,128)(2,1)} %copy-done.7, s32[256,1]{1,0:T(8,128)} %copy.508.refs_5_, ...), custom_call_target="tpu_custom_call" | custom-call | flops 2 | bytes 256 | tf_op jit(solution)/shard_map/pallas_call | solution.py:207
  400.8 12.2 shard_map.463
  432.3 6.6 reshape.669
  486.9 52.0 %all-gather.11.cloned.1.call-done = bf16[8192,768]{1,0:T(8,128)(2,1)} async-done(((bf16[256,768]{1,0:T(8,128)(2,1)}), bf16[8192,768]{1,0:T(8,128)(2,1)}) %all-gather.11.cloned.1.call-update) | async-done | bytes 12582928 | tf_op jit(solution)/shard_map/all_gather | solution.py:741
  538.9 25.4 %shard_map.464 = (f32[1,8192]{1,0:T(1,128)}, f32[1,8192]{1,0:T(1,128)}) custom-call(bf16[8,2,2,256,768]{4,3,2,1,0:T(8,128)(2,1)} %bitcast.508, bf16[1008,768]{1,0:T(8,128)(2,1)} %get-tuple-element.431.tab, s32[1,8192]{1,0:T(1,128)} %bitcast.468), custom_call_target="tpu_custom_call" | custom-call | flops 12683575296 | bytes 12582912 | tf_op jit(solution)/shard_map/pallas_call | solution.py:309
  589.3 15.8 %shard_map.465 = (bf16[8,2,64,768]{3,2,1,0:T(8,128)(2,1)}, bf16[8,2,64,768]{3,2,1,0:T(8,128)(2,1)}, f32[1008,768]{1,0:T(8,128)}) custom-call(s32[1]{0:T(128)} %bitcast.54.core, bf16[8,2,2,256,768]{4,3,2,1,0:T(8,128)(2,1)} %bitcast.509, bf16[1008,768]{1,0:T(8,128)(2,1)} %get-tuple-element.431.tab, s32[1,8192]{1,0:T(1,128)} %bitcast.469, f32[1,8192]{1,0:T(1,128)} %bitcast.447, ...), custom_call_target="tpu_custom_call" | custom-call | flops 9512681472 | bytes 6291456 | tf_op jit(solution)/shard_map/pallas_call | solution.py:332
  605.1 15.8 %shard_map.467 = (bf16[8,2,64,768]{3,2,1,0:T(8,128)(2,1)}, bf16[8,2,64,768]{3,2,1,0:T(8,128)(2,1)}, f32[1008,768]{1,0:T(8,128)}) custom-call(s32[1]{0:T(128)} %bitcast.54.core, bf16[8,2,2,256,768]{4,3,2,1,0:T(8,128)(2,1)} %bitcast.510, bf16[1008,768]{1,0:T(8,128)(2,1)} %get-tuple-element.431.tab, s32[1,8192]{1,0:T(1,128)} %bitcast.470, f32[1,8192]{1,0:T(1,128)} %bitcast.448, ...), custom_call_target="tpu_custom_call" | custom-call | flops 9512681472 | bytes 6291456 | tf_op jit(solution)/shard_map/pallas_call | solution.py:332
  621.5 15.8 %shard_map.466 = (bf16[8,2,64,768]{3,2,1,0:T(8,128)(2,1)}, bf16[8,2,64,768]{3,2,1,0:T(8,128)(2,1)}, f32[1008,768]{1,0:T(8,128)}) custom-call(s32[1]{0:T(128)} %bitcast.55.core, bf16[8,2,2,256,768]{4,3,2,1,0:T(8,128)(2,1)} %bitcast.511, bf16[1008,768]{1,0:T(8,128)(2,1)} %get-tuple-element.431.tab, s32[1,8192]{1,0:T(1,128)} %bitcast.471, f32[1,8192]{1,0:T(1,128)} %bitcast.449, ...), custom_call_target="tpu_custom_call" | custom-call | flops 9512681472 | bytes 6291456 | tf_op jit(solution)/shard_map/pallas_call | solution.py:332
  637.9 16.0 %shard_map.468 = (bf16[8,2,64,768]{3,2,1,0:T(8,128)(2,1)}, bf16[8,2,64,768]{3,2,1,0:T(8,128)(2,1)}, f32[1008,768]{1,0:T(8,128)}) custom-call(s32[1]{0:T(128)} %bitcast.55.core, bf16[8,2,2,256,768]{4,3,2,1,0:T(8,128)(2,1)} %bitcast.512, bf16[1008,768]{1,0:T(8,128)(2,1)} %get-tuple-element.431.tab, s32[1,8192]{1,0:T(1,128)} %bitcast.472, f32[1,8192]{1,0:T(1,128)} %bitcast.450, ...), custom_call_target="tpu_custom_call" | custom-call | flops 9512681472 | bytes 6291456 | tf_op jit(solution)/shard_map/pallas_call | solution.py:332
  663.6 13.3 collective-permute-done.37
  680.5 13.2 collective-permute-done.49
  697.4 7.0 collective-permute-done.38
  754.9 6.6 reshape_reshape.4
  761.5 9.1 pad_maximum_fusion
  770.8 21.7 %shard_map.469 = (bf16[256,768]{1,0:T(8,128)(2,1)}, f32[2,512,768]{2,1,0:T(8,128)}, bf16[2,512,768]{2,1,0:T(8,128)(2,1)}) custom-call(bf16[256,768]{1,0:T(8,128)(2,1)} %convolution_convert_fusion.18.refs_0_, bf16[512,1536]{1,0:T(8,128)(2,1)} %copy-done, bf16[512,1536]{1,0:T(8,128)(2,1)} %copy-done, bf16[512,1536]{1,0:T(8,128)(2,1)} %copy-done.1, ...), custom_call_target="tpu_custom_call" | custom-call | flops 5 | bytes 256 | tf_op jit(solution)/shard_map/pallas_call | solution.py:231
  799.0 26.1 %shard_map.470 = (bf16[256,768]{1,0:T(8,128)(2,1)}, f32[2,256,768]{2,1,0:T(8,128)}, bf16[2,256,768]{2,1,0:T(8,128)(2,1)}, f32[12,2,512]{2,1,0:T(2,128)}) custom-call(bf16[256,768]{1,0:T(8,128)(2,1)} %convolution_convert_fusion.19.refs_0_, bf16[256,1536]{1,0:T(8,128)(2,1)} %copy-done.6, bf16[256,1536]{1,0:T(8,128)(2,1)} %copy-done.6, ...), custom_call_target="tpu_custom_call" | custom-call | flops 5 | bytes 256 | tf_op jit(solution)/shard_map/pallas_call | solution.py:231
  844.9 11.6 collective-permute-done.62
  876.8 6.7 fusion.54
  883.5 7.1 convolution_convert_fusion
  896.7 5.2 collective-permute-start.67
  909.8 11.3 multiply_reduce_fusion.3
  983.7 64.0 %shard_map.471 = (bf16[512,768]{1,0:T(8,128)(2,1)}, f32[2,512,768]{2,1,0:T(8,128)}, bf16[2,512,768]{2,1,0:T(8,128)(2,1)}, f32[12,4,768]{2,1,0:T(4,128)}) custom-call(bf16[512,768]{1,0:T(8,128)(2,1)} %convolution_convert_fusion.15.refs_0_, bf16[512,1536]{1,0:T(8,128)(2,1)} %convolution_convert_fusion.8.refs_1_.refs_2_, ...), custom_call_target="tpu_custom_call" | custom-call | flops 5 | bytes 512 | tf_op jit(solution)/shard_map/pallas_call | solution.py:231
  1056.2 33.8 %collective-permute-done.88 = bf16[4,2,24,1408]{3,2,1,0:T(8,128)(2,1)} collective-permute-done((bf16[4,2,24,1408]{3,2,1,0:T(8,128)(2,1)}, bf16[4,2,24,1408]{3,2,1,0:T(8,128)(2,1)}, u32[]{:S(2)}, u32[]{:S(2)}) %collective-permute-start.88) | collective-permute-done | bytes 540704 | tf_op jit(solution)/shard_map/ppermute | solution.py:418
  1094.8 6.0 collective-permute-done.89
  1106.8 5.4 collective-permute-start.92
  1127.8 17.9 %collective-permute-done.95 = bf16[64,768]{1,0:T(8,128)(2,1)S(1)} collective-permute-done((bf16[64,768]{1,0:T(8,128)(2,1)S(1)}, bf16[64,768]{1,0:T(8,128)(2,1)S(1)}, u32[]{:S(2)}, u32[]{:S(2)}) %collective-permute-start.95) | collective-permute-done | bytes 98336 | tf_op jit(solution)/shard_map/ppermute | solution.py:450
  1159.4 6.5 collective-permute-done.76
  1190.6 24.3 %shard_map.473 = bf16[4032,768]{1,0:T(8,128)(2,1)} custom-call(s32[1,512]{1,0:T(1,128)} %bitcast.479, bf16[512,768]{1,0:T(8,128)(2,1)} %copy-done.28, s32[1,512]{1,0:T(1,128)} %bitcast.477, bf16[512,768]{1,0:T(8,128)(2,1)} %add.1300.refs_3_, s32[1,512]{1,0:T(1,128)} %bitcast.475, bf16[512,768]{1,0:T(8,128)(2,1)} %add.1301.refs_5_, s32[1,512]{1,0:T(1,128)} %bitcast.473, ...), custom_call_target="tpu_custom_call" | custom-call | flops 1 | bytes 1008 | tf_op jit(solution)/shard_map/pallas_call | solution.py:377
  1226.4 6.5 collective-permute-done.86
  1242.2 5.4 fusion
  1259.0 11.1 collective-permute-done.105
  1290.0 23.7 %shard_map.472 = bf16[4032,768]{1,0:T(8,128)(2,1)} custom-call(s32[1,512]{1,0:T(1,128)} %bitcast.480, bf16[512,768]{1,0:T(8,128)(2,1)} %copy-done.28, s32[1,512]{1,0:T(1,128)} %bitcast.478, bf16[512,768]{1,0:T(8,128)(2,1)} %add.1300.refs_3_, s32[1,512]{1,0:T(1,128)} %bitcast.476, bf16[512,768]{1,0:T(8,128)(2,1)} %add.1301.refs_5_, s32[1,512]{1,0:T(1,128)} %bitcast.474, ...), custom_call_target="tpu_custom_call" | custom-call | flops 1 | bytes 1008 | tf_op jit(solution)/shard_map/pallas_call | solution.py:377
  1328.9 6.0 collective-permute-done.107
  1334.8 9.3 collective-permute-done.108
  1362.7 24.3 %collective-permute-done.80 = bf16[1008,768]{1,0:T(8,128)(2,1)} collective-permute-done((bf16[1008,768]{1,0:T(8,128)(2,1)}, bf16[1008,768]{1,0:T(8,128)(2,1)}, u32[]{:S(2)}, u32[]{:S(2)}) %collective-permute-start.80) | collective-permute-done | bytes 1548320 | tf_op jit(solution)/shard_map/ppermute | solution.py:418
  1388.6 7.2 multiply_reduce_fusion.1
  1411.1 7.6 collective-permute-start.113
  1432.1 8.3 add_subtract_fusion
  (960 shorter events, 605.8 us)
Async XLA Ops:
  7.3 132.4 %all-gather.5.cloned.1.call-start = ((), (), s32[]{:S(2)}) async-start(), calls=%async_computation.2 | async-start | bytes 14800896 | tf_op jit(solution)/shard_map/all_gather | solution.py:612
  12.0 327.9 %all-gather.7.cloned.1.call-start = ((), (), s32[]{:S(2)}) async-start(), calls=%async_computation.3 | async-start | bytes 9732096 | tf_op jit(solution)/shard_map/all_gather | solution.py:675
  16.8 54.1 %collective-permute-start.1 = (bf16[1008,768]{1,0:T(8,128)(2,1)}, bf16[1008,768]{1,0:T(8,128)(2,1)}, u32[]{:S(2)}, u32[]{:S(2)}) collective-permute-start(bf16[1008,768]{1,0:T(8,128)(2,1)} %get-tuple-element.431.tab), channel_id=1, source_target_pairs={{0,1},{1,0},{2,3},{3,2},{4,5},{5,4},{6,7},{7,6},{8,9},{9,8},{10,11... | collective-permute-start | bytes 4644872 | tf_op jit(solution)/shard_map/ppermute | solution.py:418
  21.0 50.6 %collective-permute-start.2 = (bf16[1008,768]{1,0:T(8,128)(2,1)}, bf16[1008,768]{1,0:T(8,128)(2,1)S(1)}, u32[]{:S(2)}, u32[]{:S(2)}) collective-permute-start(bf16[1008,768]{1,0:T(8,128)(2,1)} %get-tuple-element.431.tab), channel_id=1, source_target_pairs={{0,4},{4,0},{1,5},{5,1},{2,6},{6,2},{3,7},{7,3},{8,12},{12,8},{9,1... | collective-permute-start | bytes 4644872 | tf_op jit(solution)/shard_map/ppermute | solution.py:418
  22.5 80.6 %collective-permute-start.5 = (bf16[1008,768]{1,0:T(8,128)(2,1)}, bf16[1008,768]{1,0:T(8,128)(2,1)}, u32[]{:S(2)}, u32[]{:S(2)}) collective-permute-start(bf16[1008,768]{1,0:T(8,128)(2,1)} %get-tuple-element.431.tab), channel_id=1, source_target_pairs={{0,2},{2,0},{1,3},{3,1},{4,6},{6,4},{5,7},{7,5},{8,10},{10,8},{9,1... | collective-permute-start | bytes 4644872 | tf_op jit(solution)/shard_map/ppermute | solution.py:418
  37.0 36.5 %collective-permute-start.13 = (s32[768]{0:T(1024)S(1)}, s32[768]{0:T(1024)S(1)}, u32[]{:S(2)}, u32[]{:S(2)}) collective-permute-start(s32[768]{0:T(1024)S(1)} %collective-permute-done.12), channel_id=1, source_target_pairs={{8,0},{16,8},{24,16},{9,1},{17,9},{25,17},{10,2},{18,10},{26,18},{... | collective-permute-start | bytes 9224 | tf_op jit(solution)/shard_map/ppermute | solution.py:469
  38.3 37.6 %collective-permute-start.15 = (s32[768]{0:T(1024)S(1)}, s32[768]{0:T(1024)S(1)}, u32[]{:S(2)}, u32[]{:S(2)}) collective-permute-start(s32[768]{0:T(1024)S(1)} %collective-permute-done.14), channel_id=1, source_target_pairs={{0,8},{8,16},{16,24},{1,9},{9,17},{17,25},{2,10},{10,18},{18,26},{... | collective-permute-start | bytes 9224 | tf_op jit(solution)/shard_map/ppermute | solution.py:468
  70.9 35.0 %collective-permute-start.6 = (bf16[1008,768]{1,0:T(8,128)(2,1)}, bf16[1008,768]{1,0:T(8,128)(2,1)}, u32[]{:S(2)}, u32[]{:S(2)}) collective-permute-start(bf16[1008,768]{1,0:T(8,128)(2,1)} %collective-permute-done.1), channel_id=1, source_target_pairs={{0,2},{2,0},{1,3},{3,1},{4,6},{6,4},{5,7},{7,5},{8,10},{10,8},{9,1... | collective-permute-start | bytes 4644872 | tf_op jit(solution)/shard_map/ppermute | solution.py:418
  71.6 36.9 %collective-permute-start.7 = (bf16[1008,768]{1,0:T(8,128)(2,1)S(1)}, bf16[1008,768]{1,0:T(8,128)(2,1)}, u32[]{:S(2)}, u32[]{:S(2)}) collective-permute-start(bf16[1008,768]{1,0:T(8,128)(2,1)S(1)} %collective-permute-done.2), channel_id=1, source_target_pairs={{0,2},{2,0},{1,3},{3,1},{4,6},{6,4},{5,7},{7,5},{8,10},{10,8},{9,1... | collective-permute-start | bytes 4644872 | tf_op jit(solution)/shard_map/ppermute | solution.py:418
  139.8 281.3 %all-gather.9.cloned.1.call-start = ((), (), s32[]{:S(2)}) async-start(), calls=%async_computation.4 | async-start | bytes 9732096 | tf_op jit(solution)/shard_map/all_gather | solution.py:716
  162.4 42.5 %collective-permute-start.16 = (bf16[768,768]{1,0:T(8,128)(2,1)S(1)}, bf16[768,768]{1,0:T(8,128)(2,1)S(1)}, u32[]{:S(2)}, u32[]{:S(2)}) collective-permute-start(bf16[768,768]{1,0:T(8,128)(2,1)S(1)} %get-tuple-element.407), channel_id=1, source_target_pairs={{0,8},{1,9},{2,10},{3,11},{4,12},{5,13},{6,14},{7,15}} | collective-permute-start | bytes 3538952 | tf_op jit(solution)/shard_map/ppermute | solution.py:481
  164.9 40.0 %collective-permute-start.19 = (bf16[768,768]{1,0:T(8,128)(2,1)S(1)}, bf16[768,768]{1,0:T(8,128)(2,1)S(1)}, u32[]{:S(2)}, u32[]{:S(2)}) collective-permute-start(bf16[768,768]{1,0:T(8,128)(2,1)S(1)} %get-tuple-element.408), channel_id=1, source_target_pairs={{24,16},{25,17},{26,18},{27,19},{28,20},{29,21},{30,22},{31,23}} | collective-permute-start | bytes 3538952 | tf_op jit(solution)/shard_map/ppermute | solution.py:482
  207.8 46.1 %collective-permute-start.17 = (bf16[768,768]{1,0:T(8,128)(2,1)}, bf16[768,768]{1,0:T(8,128)(2,1)S(1)}, u32[]{:S(2)}, u32[]{:S(2)}) collective-permute-start(bf16[768,768]{1,0:T(8,128)(2,1)} %get-tuple-element.405), channel_id=1, source_target_pairs={{0,8},{8,16},{1,9},{9,17},{2,10},{10,18},{3,11},{11,19},{4,12},{12... | collective-permute-start | bytes 3538952 | tf_op jit(solution)/shard_map/ppermute | solution.py:481
  212.3 41.6 %collective-permute-start.20 = (bf16[768,768]{1,0:T(8,128)(2,1)}, bf16[768,768]{1,0:T(8,128)(2,1)S(1)}, u32[]{:S(2)}, u32[]{:S(2)}) collective-permute-start(bf16[768,768]{1,0:T(8,128)(2,1)} %get-tuple-element.406), channel_id=1, source_target_pairs={{24,16},{16,8},{25,17},{17,9},{26,18},{18,10},{27,19},{19,11},{28,... | collective-permute-start | bytes 3538952 | tf_op jit(solution)/shard_map/ppermute | solution.py:482
  256.8 29.1 %collective-permute-start.18 = (bf16[768,768]{1,0:T(8,128)(2,1)}, bf16[768,768]{1,0:T(8,128)(2,1)S(1)}, u32[]{:S(2)}, u32[]{:S(2)}) collective-permute-start(bf16[768,768]{1,0:T(8,128)(2,1)} %get-tuple-element.403), channel_id=1, source_target_pairs={{0,8},{8,16},{16,24},{1,9},{9,17},{17,25},{2,10},{10,18},{18,26},{... | collective-permute-start | bytes 3538952 | tf_op jit(solution)/shard_map/ppermute | solution.py:481
  261.1 29.4 %collective-permute-start.21 = (bf16[768,768]{1,0:T(8,128)(2,1)S(1)}, bf16[768,768]{1,0:T(8,128)(2,1)}, u32[]{:S(2)}, u32[]{:S(2)}) collective-permute-start(bf16[768,768]{1,0:T(8,128)(2,1)S(1)} %get-tuple-element.404), channel_id=1, source_target_pairs={{24,16},{16,8},{8,0},{25,17},{17,9},{9,1},{26,18},{18,10},{10,2},{... | collective-permute-start | bytes 3538952 | tf_op jit(solution)/shard_map/ppermute | solution.py:482
  340.0 198.9 %all-gather.11.cloned.1.call-start = ((), (), s32[]{:S(2)}) async-start(), calls=%async_computation.5 | async-start | bytes 12976128 | tf_op jit(solution)/shard_map/all_gather | solution.py:741
  444.1 492.4 %reduce-scatter.5.cloned.1.call-start = ((), (), s32[]{:S(2)}) async-start(), calls=%async_computation.6 | async-start | bytes 9732096 | tf_op jit(solution)/shard_map/reduce_scatter | solution.py:782
  620.9 32.9 %collective-permute-start.36 = (bf16[8,2,64,768]{3,2,1,0:T(8,128)(2,1)}, bf16[8,2,64,768]{3,2,1,0:T(8,128)(2,1)}, u32[]{:S(2)}, u32[]{:S(2)}) collective-permute-start(bf16[8,2,64,768]{3,2,1,0:T(8,128)(2,1)} %get-tuple-element.105), channel_id=1, source_target_pairs={{0,2},{2,0},{1,3},{3,1},{4,6},{6,4},{5,7},{7,5},{8,10},{10,8},{9,1... | collective-permute-start | bytes 4718600 | tf_op jit(solution)/shard_map/ppermute | solution.py:418
  621.0 36.9 %collective-permute-start.42 = (bf16[8,2,64,768]{3,2,1,0:T(8,128)(2,1)}, bf16[8,2,64,768]{3,2,1,0:T(8,128)(2,1)S(1)}, u32[]{:S(2)}, u32[]{:S(2)}) collective-permute-start(bf16[8,2,64,768]{3,2,1,0:T(8,128)(2,1)} %get-tuple-element.107), channel_id=1, source_target_pairs={{0,2},{2,0},{1,3},{3,1},{4,6},{6,4},{5,7},{7,5},{8,10},{10,8},{9,1... | collective-permute-start | bytes 4718600 | tf_op jit(solution)/shard_map/ppermute | solution.py:418
  660.6 33.2 %collective-permute-start.49 = (bf16[4,2,64,768]{3,2,0,1:T(8,128)(2,1)S(1)}, bf16[4,2,64,768]{3,2,0,1:T(8,128)(2,1)S(1)}, u32[]{:S(2)}, u32[]{:S(2)}) collective-permute-start(bf16[4,2,64,768]{3,2,0,1:T(8,128)(2,1)S(1)} %bitcast.441), channel_id=1, source_target_pairs={{0,1},{1,0},{2,3},{3,2},{4,5},{5,4},{6,7},{7,6},{8,9},{9,8},{10,11... | collective-permute-start | bytes 2359304 | tf_op jit(solution)/shard_map/ppermute | solution.py:418
  662.4 33.6 %collective-permute-start.55 = (bf16[4,2,64,768]{3,2,0,1:T(8,128)(2,1)S(1)}, bf16[4,2,64,768]{3,2,0,1:T(8,128)(2,1)S(1)}, u32[]{:S(2)}, u32[]{:S(2)}) collective-permute-start(bf16[4,2,64,768]{3,2,0,1:T(8,128)(2,1)S(1)} %bitcast.442), channel_id=1, source_target_pairs={{0,4},{4,0},{1,5},{5,1},{2,6},{6,2},{3,7},{7,3},{8,12},{12,8},{9,1... | collective-permute-start | bytes 2359304 | tf_op jit(solution)/shard_map/ppermute | solution.py:418
  677.2 27.3 %collective-permute-start.38 = (bf16[4,64,768]{2,1,0:T(8,128)(2,1)S(1)}, bf16[4,64,768]{2,1,0:T(8,128)(2,1)S(1)}, u32[]{:S(2)}, u32[]{:S(2)}) collective-permute-start(bf16[4,64,768]{2,1,0:T(8,128)(2,1)S(1)} %dynamic-slice_bitcast_fusion.11), channel_id=1, source_target_pairs={{0,4},{4,0},{1,5},{5,1},{2,6},{6,2},{3,7},{7,3},{8,12},{12,8},{9,1... | collective-permute-start | bytes 1179656 | tf_op jit(solution)/shard_map/ppermute | solution.py:418
  679.4 27.3 %collective-permute-start.44 = (bf16[4,64,768]{2,1,0:T(8,128)(2,1)S(1)}, bf16[4,64,768]{2,1,0:T(8,128)(2,1)S(1)}, u32[]{:S(2)}, u32[]{:S(2)}) collective-permute-start(bf16[4,64,768]{2,1,0:T(8,128)(2,1)S(1)} %dynamic-slice_bitcast_fusion.10), channel_id=1, source_target_pairs={{0,1},{1,0},{2,3},{3,2},{4,5},{5,4},{6,7},{7,6},{8,9},{9,8},{10,11... | collective-permute-start | bytes 1179656 | tf_op jit(solution)/shard_map/ppermute | solution.py:418
  770.6 418.2 %reduce-scatter.7.cloned.1.call-start = ((), (), s32[]{:S(2)}) async-start(), calls=%async_computation.7 | async-start | bytes 9732096
  825.2 37.9 %collective-permute-start.60 = (bf16[2,512,768]{2,1,0:T(8,128)(2,1)}, bf16[2,512,768]{2,1,0:T(8,128)(2,1)S(1)}, u32[]{:S(2)}, u32[]{:S(2)}) collective-permute-start(bf16[2,512,768]{2,1,0:T(8,128)(2,1)} %get-tuple-element.115), channel_id=1, source_target_pairs={{0,2},{2,0},{1,3},{3,1},{4,6},{6,4},{5,7},{7,5},{8,10},{10,8},{9,1... | collective-permute-start | bytes 4718600 | tf_op jit(solution)/shard_map/ppermute | solution.py:418
  856.5 40.2 %collective-permute-start.66 = (bf16[256,768]{1,0:T(8,128)(2,1)S(1)}, bf16[256,768]{1,0:T(8,128)(2,1)}, u32[]{:S(2)}, u32[]{:S(2)}) collective-permute-start(bf16[256,768]{1,0:T(8,128)(2,1)S(1)} %collective-permute-done.62), channel_id=1, source_target_pairs={{0,8},{8,16},{16,24},{1,9},{9,17},{17,25},{2,10},{10,18},{18,26},{... | collective-permute-start | bytes 1179656 | tf_op jit(solution)/shard_map/ppermute | solution.py:468
  861.6 40.3 %collective-permute-start.64 = (bf16[256,768]{1,0:T(8,128)(2,1)S(1)}, bf16[256,768]{1,0:T(8,128)(2,1)}, u32[]{:S(2)}, u32[]{:S(2)}) collective-permute-start(bf16[256,768]{1,0:T(8,128)(2,1)S(1)} %collective-permute-done.63), channel_id=1, source_target_pairs={{8,0},{16,8},{24,16},{9,1},{17,9},{25,17},{10,2},{18,10},{26,18},{... | collective-permute-start | bytes 1179656 | tf_op jit(solution)/shard_map/ppermute | solution.py:469
  875.3 58.1 %collective-permute-start.70 = (bf16[4,2,2,64,768]{4,3,0,2,1:T(8,128)(2,1)}, bf16[4,2,2,64,768]{4,3,0,2,1:T(8,128)(2,1)}, u32[]{:S(2)}, u32[]{:S(2)}) collective-permute-start(bf16[4,2,2,64,768]{4,3,0,2,1:T(8,128)(2,1)} %bitcast.418), channel_id=1, source_target_pairs={{0,2},{2,0},{1,3},{3,1},{4,6},{6,4},{5,7},{7,5},{8,10},{10,8},{9,1... | collective-permute-start | bytes 4718600 | tf_op jit(solution)/shard_map/ppermute | solution.py:418
  896.7 49.9 %collective-permute-start.68 = (bf16[4,2,2,24,3456]{4,3,0,1,2:T(8,128)(2,1)}, bf16[4,2,2,24,3456]{4,3,0,1,2:T(8,128)(2,1)}, u32[]{:S(2)}, u32[]{:S(2)}) collective-permute-start(bf16[4,2,2,24,3456]{4,3,0,1,2:T(8,128)(2,1)} %bitcast.417), channel_id=1, source_target_pairs={{0,2},{2,0},{1,3},{3,1},{4,6},{6,4},{5,7},{7,5},{8,10},{10,8},{9,1... | collective-permute-start | bytes 7962632 | tf_op jit(solution)/shard_map/ppermute | solution.py:418
  896.7 32.9 %collective-permute-start.67 = (bf16[256,768]{1,0:T(8,128)(2,1)}, bf16[256,768]{1,0:T(8,128)(2,1)}, u32[]{:S(2)}, u32[]{:S(2)}) collective-permute-start(bf16[256,768]{1,0:T(8,128)(2,1)} %collective-permute-done.66), channel_id=1, source_target_pairs={{0,8},{8,16},{16,24},{1,9},{9,17},{17,25},{2,10},{10,18},{18,26},{... | collective-permute-start | bytes 1179656 | tf_op jit(solution)/shard_map/ppermute | solution.py:468
  901.9 29.6 %collective-permute-start.65 = (bf16[256,768]{1,0:T(8,128)(2,1)}, bf16[256,768]{1,0:T(8,128)(2,1)}, u32[]{:S(2)}, u32[]{:S(2)}) collective-permute-start(bf16[256,768]{1,0:T(8,128)(2,1)} %collective-permute-done.64), channel_id=1, source_target_pairs={{8,0},{16,8},{24,16},{9,1},{17,9},{25,17},{10,2},{18,10},{26,18},{... | collective-permute-start | bytes 1179656 | tf_op jit(solution)/shard_map/ppermute | solution.py:469
  1047.7 64.6 %collective-permute-start.71 = (bf16[2,512,768]{2,1,0:T(8,128)(2,1)}, bf16[2,512,768]{2,1,0:T(8,128)(2,1)}, u32[]{:S(2)}, u32[]{:S(2)}) collective-permute-start(bf16[2,512,768]{2,1,0:T(8,128)(2,1)} %get-tuple-element.124), channel_id=1, source_target_pairs={{0,2},{2,0},{1,3},{3,1},{4,6},{6,4},{5,7},{7,5},{8,10},{10,8},{9,1... | collective-permute-start | bytes 4718600 | tf_op jit(solution)/shard_map/ppermute | solution.py:418
  1048.8 43.2 %collective-permute-start.93 = (bf16[4,2,64,768]{3,2,0,1:T(8,128)(2,1)}, bf16[4,2,64,768]{3,2,0,1:T(8,128)(2,1)}, u32[]{:S(2)}, u32[]{:S(2)}) collective-permute-start(bf16[4,2,64,768]{3,2,0,1:T(8,128)(2,1)} %dynamic-slice_bitcast_fusion.4), channel_id=1, source_target_pairs={{0,4},{4,0},{1,5},{5,1},{2,6},{6,2},{3,7},{7,3},{8,12},{12,8},{9,1... | collective-permute-start | bytes 2359304 | tf_op jit(solution)/shard_map/ppermute | solution.py:418
  1051.4 38.6 %collective-permute-start.88 = (bf16[4,2,24,1408]{3,2,1,0:T(8,128)(2,1)}, bf16[4,2,24,1408]{3,2,1,0:T(8,128)(2,1)}, u32[]{:S(2)}, u32[]{:S(2)}) collective-permute-start(bf16[4,2,24,1408]{3,2,1,0:T(8,128)(2,1)} %copy_bitcast_fusion.13), channel_id=1, source_target_pairs={{0,4},{4,0},{1,5},{5,1},{2,6},{6,2},{3,7},{7,3},{8,12},{12,8},{9,1... | collective-permute-start | bytes 1622024 | tf_op jit(solution)/shard_map/ppermute | solution.py:418
  1054.4 100.8 %collective-permute-start.83 = (bf16[4,2,24,3456]{3,2,0,1:T(8,128)(2,1)}, bf16[4,2,24,3456]{3,2,0,1:T(8,128)(2,1)S(1)}, u32[]{:S(2)}, u32[]{:S(2)}) collective-permute-start(bf16[4,2,24,3456]{3,2,0,1:T(8,128)(2,1)} %dynamic-slice_bitcast_fusion), channel_id=1, source_target_pairs={{0,1},{1,0},{2,3},{3,2},{4,5},{5,4},{6,7},{7,6},{8,9},{9,8},{10,11... | collective-permute-start | bytes 3981320 | tf_op jit(solution)/shard_map/ppermute | solution.py:418
  1120.2 30.9 %collective-permute-start.72 = (bf16[512,768]{1,0:T(8,128)(2,1)S(1)}, bf16[512,768]{1,0:T(8,128)(2,1)S(1)}, u32[]{:S(2)}, u32[]{:S(2)}) collective-permute-start(bf16[512,768]{1,0:T(8,128)(2,1)S(1)} %fusion.45.refs_1_), channel_id=1, source_target_pairs={{0,8},{8,16},{16,24},{1,9},{9,17},{17,25},{2,10},{10,18},{18,26},{... | collective-permute-start | bytes 2359304 | tf_op jit(solution)/shard_map/ppermute | solution.py:468
  1121.7 32.2 %collective-permute-start.73 = (bf16[512,768]{1,0:T(8,128)(2,1)S(1)}, bf16[512,768]{1,0:T(8,128)(2,1)S(1)}, u32[]{:S(2)}, u32[]{:S(2)}) collective-permute-start(bf16[512,768]{1,0:T(8,128)(2,1)S(1)} %fusion.45.refs_1_), channel_id=1, source_target_pairs={{8,0},{16,8},{24,16},{9,1},{17,9},{25,17},{10,2},{18,10},{26,18},{... | collective-permute-start | bytes 2359304 | tf_op jit(solution)/shard_map/ppermute | solution.py:469
  1156.7 58.3 %collective-permute-start.84 = (bf16[4,24,3456]{2,1,0:T(8,128)(2,1)}, bf16[4,24,3456]{2,1,0:T(8,128)(2,1)}, u32[]{:S(2)}, u32[]{:S(2)}) collective-permute-start(bf16[4,24,3456]{2,1,0:T(8,128)(2,1)} %dynamic-slice_bitcast_fusion.5), channel_id=1, source_target_pairs={{0,4},{4,0},{1,5},{5,1},{2,6},{6,2},{3,7},{7,3},{8,12},{12,8},{9,1... | collective-permute-start | bytes 1990664 | tf_op jit(solution)/shard_map/ppermute | solution.py:418
  1179.8 55.8 %collective-permute-start.98 = (bf16[4,2,2,24,1152]{4,3,2,1,0:T(8,128)(2,1)}, bf16[4,2,2,24,1152]{4,3,2,1,0:T(8,128)(2,1)}, u32[]{:S(2)}, u32[]{:S(2)}) collective-permute-start(bf16[4,2,2,24,1152]{4,3,2,1,0:T(8,128)(2,1)} %dynamic-slice_bitcast_fusion.3), channel_id=1, source_target_pairs={{0,2},{2,0},{1,3},{3,1},{4,6},{6,4},{5,7},{7,5},{8,10},{10,8},{9,1... | collective-permute-start | bytes 2654216 | tf_op jit(solution)/shard_map/ppermute | solution.py:418
  1214.9 98.8 %collective-permute-start.78 = (bf16[4032,768]{1,0:T(8,128)(2,1)}, bf16[4032,768]{1,0:T(8,128)(2,1)}, u32[]{:S(2)}, u32[]{:S(2)}) collective-permute-start(bf16[4032,768]{1,0:T(8,128)(2,1)} %shard_map.473), channel_id=1, source_target_pairs={{0,2},{2,0},{1,3},{3,1},{4,6},{6,4},{5,7},{7,5},{8,10},{10,8},{9,1... | collective-permute-start | bytes 18579464 | tf_op jit(solution)/shard_map/ppermute | solution.py:418
  1282.3 39.9 %collective-permute-start.101 = (bf16[24,1152]{1,0:T(8,128)(2,1)}, bf16[24,1152]{1,0:T(8,128)(2,1)}, u32[]{:S(2)}, u32[]{:S(2)}) collective-permute-start(bf16[24,1152]{1,0:T(8,128)(2,1)} %get-tuple-element.469), channel_id=1, source_target_pairs={{0,8},{8,16},{16,24},{24,0},{1,9},{9,17},{17,25},{25,1},{2,10},{10... | collective-permute-start | bytes 165896 | tf_op jit(solution)/shard_map/ppermute | solution.py:450
  1286.1 37.9 %collective-permute-start.102 = (bf16[24,1152]{1,0:T(8,128)(2,1)}, bf16[24,1152]{1,0:T(8,128)(2,1)}, u32[]{:S(2)}, u32[]{:S(2)}) collective-permute-start(bf16[24,1152]{1,0:T(8,128)(2,1)} %get-tuple-element.471), channel_id=1, source_target_pairs={{0,16},{8,24},{16,0},{24,8},{1,17},{9,25},{17,1},{25,9},{2,18},{10... | collective-permute-start | bytes 165896 | tf_op jit(solution)/shard_map/ppermute | solution.py:450
  1286.6 38.3 %collective-permute-start.103 = (bf16[24,1152]{1,0:T(8,128)(2,1)}, bf16[24,1152]{1,0:T(8,128)(2,1)}, u32[]{:S(2)}, u32[]{:S(2)}) collective-permute-start(bf16[24,1152]{1,0:T(8,128)(2,1)} %get-tuple-element.470), channel_id=1, source_target_pairs={{0,24},{8,0},{16,8},{24,16},{1,25},{9,1},{17,9},{25,17},{2,26},{10... | collective-permute-start | bytes 165896 | tf_op jit(solution)/shard_map/ppermute | solution.py:450
  1318.4 28.7 %collective-permute-start.79 = (bf16[504,768]{1,0:T(8,128)(2,1)}, bf16[504,768]{1,0:T(8,128)(2,1)}, u32[]{:S(2)}, u32[]{:S(2)}) collective-permute-start(bf16[504,768]{1,0:T(8,128)(2,1)} %get-tuple-element.396), channel_id=1, source_target_pairs={{0,4},{4,0},{1,5},{5,1},{2,6},{6,2},{3,7},{7,3},{8,12},{12,8},{9,1... | collective-permute-start | bytes 2322440 | tf_op jit(solution)/shard_map/ppermute | solution.py:418
  1320.5 26.6 %collective-permute-start.81 = (bf16[504,768]{1,0:T(8,128)(2,1)}, bf16[504,768]{1,0:T(8,128)(2,1)}, u32[]{:S(2)}, u32[]{:S(2)}) collective-permute-start(bf16[504,768]{1,0:T(8,128)(2,1)} %get-tuple-element.395), channel_id=1, source_target_pairs={{0,1},{1,0},{2,3},{3,2},{4,5},{5,4},{6,7},{7,6},{8,9},{9,8},{10,11... | collective-permute-start | bytes 2322440 | tf_op jit(solution)/shard_map/ppermute | solution.py:418
  1351.2 35.7 %collective-permute-start.80 = (bf16[1008,768]{1,0:T(8,128)(2,1)}, bf16[1008,768]{1,0:T(8,128)(2,1)}, u32[]{:S(2)}, u32[]{:S(2)}) collective-permute-start(bf16[1008,768]{1,0:T(8,128)(2,1)} %pad_maximum_fusion.4), channel_id=1, source_target_pairs={{0,1},{1,0},{2,3},{3,2},{4,5},{5,4},{6,7},{7,6},{8,9},{9,8},{10,11... | collective-permute-start | bytes 4644872 | tf_op jit(solution)/shard_map/ppermute | solution.py:418
  1352.8 35.7 %collective-permute-start.82 = (bf16[1008,768]{1,0:T(8,128)(2,1)}, bf16[1008,768]{1,0:T(8,128)(2,1)}, u32[]{:S(2)}, u32[]{:S(2)}) collective-permute-start(bf16[1008,768]{1,0:T(8,128)(2,1)} %pad_maximum_fusion.5), channel_id=1, source_target_pairs={{0,4},{4,0},{1,5},{5,1},{2,6},{6,2},{3,7},{7,3},{8,12},{12,8},{9,1... | collective-permute-start | bytes 4644872 | tf_op jit(solution)/shard_map/ppermute | solution.py:418
  (259 other events, 3571.4 us)
Sparse Core Ops, SparseCore 0:
  12.1 127.5 all-gather.4
  143.2 102.3 all-gather.6
  340.1 80.8 all-gather.8
  444.2 94.5 all-gather.10
  770.7 145.0 reduce-scatter.4
  954.5 147.3 reduce-scatter.6

commit v5 on v4

--- a/solution.py
+++ b/solution.py
@@ -62,18 +62,9 @@
     return lax.dot_general(a, b, (((1,), (0,)), ((), ())), preferred_element_type=f32)
 
 
-def shifted_rows(grid, back):
-    total = grid.shape[-1]
-    row = 7 - lax.broadcasted_iota(jnp.int32, grid.shape, 0)
-    for bit in (1, 2, 4):
-        moved = pltpu.roll(grid, bit if back else total - bit, 1)
-        grid = jnp.where((row & bit) != 0, moved, grid)
-    return grid
-
-
-def spread(line, rows, width):
-    total = line.shape[-1]
-    grid = shifted_rows(jnp.broadcast_to(line, (8, total)), False)
+def spread(eight, rows, width):
+    total = eight.shape[-1]
+    grid = eight
     have = 8
     while have < rows:
         grid = jnp.concatenate([pltpu.roll(grid, total - have, 1), grid], axis=0)
@@ -87,7 +78,7 @@
     while rows > 8:
         rows //= 2
         have = pltpu.roll(have[:rows], rows, 1) + have[rows:]
-    return jnp.sum(shifted_rows(have, True), axis=0, keepdims=True)
+    return have
 
 
 def probs_of(cfg, refs, block, head):
@@ -100,7 +91,7 @@
         keys = refs["k"][part][:, cols]
         s = dot_nt(query, keys) * HEAD_DIM ** (-0.5)
         if has_bias:
-            s = s + spread(refs["x8"][head, pl.ds(block * 2 + part, 1), :], bq, keys.shape[0])
+            s = s + spread(refs["x8"][head, block * 2 + part], bq, keys.shape[0])
         allowed = refs["qseg"][rows, :] == refs["kseg"][part]
         if causal:
             allowed = allowed & (refs["kpos"][part] <= refs["qpos"][rows, :])
@@ -169,8 +160,7 @@
                 dk[part] = k_term if dk[part] is None else dk[part] + k_term
                 dv[part] = v_term if dv[part] is None else dv[part] + v_term
                 if has_bias:
-                    line = collect(ds.astype(f32), y8.shape[-1])
-                    y8[head, pl.ds(block * 2 + part, 1), :] = line
+                    y8[head, block * 2 + part] = collect(ds.astype(f32), y8.shape[-1])
             dq[rows, cols] = (acc * HEAD_DIM ** (-0.5)).astype(bf16)
         for part, target in enumerate((own, other)):
             target[0, :, cols] = (dk[part] * HEAD_DIM ** (-0.5)).T.astype(target.dtype)
@@ -186,7 +176,7 @@
     specs = [pl.BlockSpec((q_len, 128), lambda i: (0, i))] + kv + kv
     specs += [whole((q_len, 1)), whole((1, k_len)), whole((1, k_len))] * 2
     if has_bias:
-        specs.append(pl.BlockSpec((2,) + x8.shape[1:], lambda i: (i, 0, 0)))
+        specs.append(pl.BlockSpec((2,) + x8.shape[1:], lambda i: (i, 0, 0, 0)))
     return specs
 
 
@@ -226,7 +216,7 @@
         jax.ShapeDtypeStruct((2, k_len, D), bf16),
     ]
     if x8 is not None:
-        out_specs.append(pl.BlockSpec((2,) + x8.shape[1:], lambda i: (i, 0, 0)))
+        out_specs.append(pl.BlockSpec((2,) + x8.shape[1:], lambda i: (i, 0, 0, 0)))
         out_shape.append(jax.ShapeDtypeStruct(x8.shape, f32))
     return pl.pallas_call(
         functools.partial(attend_backward_kernel, cfg),
@@ -251,10 +241,11 @@
 
 
 def bias_windows(array, core, q_len, k_len):
-    size = array.shape[1]
+    size, width = array.shape[1], k_len + 256
     array = jnp.pad(array, ((0, 0), (0, 16)))
+    rows = jnp.stack([array[:, 7 - r : size + 9 - r] for r in range(8)], axis=1)
     bases = bias_bases(core, q_len, k_len, size // 2)
-    cut = lambda base: lax.dynamic_slice_in_dim(array, base, k_len + 256, axis=1)
+    cut = lambda base: lax.dynamic_slice_in_dim(rows, base, width, axis=2)
     return jnp.stack([cut(base) for base in bases], axis=1)
 
 
@@ -268,7 +259,7 @@
 
 
 def bias_gradient(y8, picks):
-    return jnp.einsum("bnw,hnw->bh", picks, y8, precision=lax.Precision.HIGHEST)
+    return jnp.einsum("bnrw,hnrw->bh", picks, y8, precision=lax.Precision.HIGHEST)
 
 
 def head_stats_kernel(count, hid, tab, tgt, lse_out, pick_out):
@@ -438,11 +429,20 @@
     return add16(pick(value, me, dim), got)
 
 
-def scatter_rest(value, seq_first):
-    if seq_first:
-        value = scatter_pair(scatter_pair(value, "seq", 2), "p", 1)
-    else:
-        value = scatter_pair(scatter_pair(value, "p", 1), "seq", 1)
+def scatter_core(value):
+    sizes = tuple(lax.axis_size(axis) for axis in ALL)
+    return scatter_pair(value.reshape(sizes + (-1, value.shape[-1])), "core", 2)
+
+
+def scatter_first(value, seq_first):
+    return scatter_pair(value, "seq", 2) if seq_first else scatter_pair(value, "p", 1)
+
+
+def scatter_second(value, seq_first):
+    return scatter_pair(value, "p", 1) if seq_first else scatter_pair(value, "seq", 1)
+
+
+def scatter_last(value):
     size, me = value.shape[0], lax.axis_index("z")
     total = pick(value, me, 0).astype(f32)
     for hop in range(1, size):
@@ -452,13 +452,8 @@
     return total
 
 
-def scatter_core(value):
-    sizes = tuple(lax.axis_size(axis) for axis in ALL)
-    return scatter_pair(value.reshape(sizes + (-1, value.shape[-1])), "core", 2)
-
-
-def scatter_chain(value, seq_first):
-    return scatter_rest(scatter_core(value), seq_first)
+def scatter_rest(value, seq_first):
+    return scatter_last(scatter_second(scatter_first(value, seq_first), seq_first))
 
 
 def line_gather(value, axis):
@@ -500,15 +495,15 @@
     return ((other >> 1) & 1) * 4 + (other >> 2) * 2 + (other & 1)
 
 
-def plane_scatter(pairs, rows, before):
+def plane_scatter(pairs, rows, before, after):
     pairs, before = lax.optimization_barrier((pairs, before))
     count = lax.axis_size(PLANE)
     if lax.axis_size("p") != 2:
         placed = place_rows(pairs, 0, count, rows)
         placed = lax.psum_scatter(placed, PLANE, scatter_dimension=0, tiled=True)
-        return placed.astype(f32), before
+        return placed.astype(f32), before, after
     away = swap_core(place_rows(pairs, 4, 4, rows))
-    home = place_rows(pairs, 0, 4, rows)
+    home, after = lax.optimization_barrier((place_rows(pairs, 0, 4, rows), after))
     half = rows // 2
     part = lambda first, last: add16(home[first:last], away[first:last])
     got_low = swap(part(3 * rows, 3 * rows + half), "seq")
@@ -517,7 +512,7 @@
     p_low = add16(part(2 * rows, 2 * rows + half), got_low)
     from_seq = swap(jnp.concatenate([part(rows, rows + half), seq_high]), "seq")
     from_p = swap(jnp.concatenate([p_low, part(2 * rows + half, 3 * rows)]), "p")
-    return part(0, rows).astype(f32) + from_seq.astype(f32) + from_p.astype(f32), before
+    return part(0, rows).astype(f32) + from_seq.astype(f32) + from_p.astype(f32), before, after
 
 
 def add_logs(left, right):
@@ -775,10 +770,8 @@
         d_y3, dec_y2, gain[5], dec_fi, dec_fo, dec_saved
     )
     d_cross_wo, d_cross_ob = branch_backward(d_y2, cross_ob, cross_wo)
-    rows_in = lambda out: out.reshape(-1, ffn_out.shape[1], D).reshape(D, FF)
-    early, d_cross_ob = lax.optimization_barrier(
-        (jnp.concatenate([d_dec_fi, rows_in(d_dec_fo)], axis=1), d_cross_ob)
-    )
+    early, d_dec_fo, d_cross_ob = lax.optimization_barrier((d_dec_fi, d_dec_fo, d_cross_ob))
+    g_dec_fo = scatter_core(d_dec_fo)
     early = lax.psum_scatter(early, ALL, scatter_dimension=0, tiled=True)
     d_cross_q, own, other = attend_backward(
         d_cross_ob, cross_q, cross_kv, cross_kv2, cross_info, None, False
@@ -792,6 +785,8 @@
     d_y1 = d_y2 + d_y1_norm
     d_cross_wkv = weight_grad(enc_out, d_cross_kv)
     d_dec_wo, d_dec_ob = branch_backward(d_y1, dec_ob, dec_wo)
+    g_dec_fo, d_dec_ob = lax.optimization_barrier((g_dec_fo, d_dec_ob))
+    g_dec_fo = scatter_first(g_dec_fo, False)
     d_dec_q, own, other, dec_y8 = attend_backward(
         d_dec_ob, dec_q, dec_kv, dec_kv2, dec_info, dec_x8, True
     )
@@ -819,18 +814,17 @@
     d_x1, d_gain_effn, d_enc_fi, d_enc_fo = ffn_backward(
         d_x2, enc_x1, gain[1], enc_fi, enc_fo, enc_saved
     )
-    early, d_x1 = lax.optimization_barrier((early, d_x1))
+    early, g_dec_fo, d_x1 = lax.optimization_barrier((early, g_dec_fo, d_x1))
+    g_dec_fo = scatter_second(g_dec_fo, False)
     d_enc_wo, d_enc_ob = branch_backward(d_x1, enc_ob, enc_wo)
     d_enc_low, d_enc_high = d_enc_fi[:, :3456], jnp.concatenate([d_enc_fi[:, 3456:], d_enc_wo], 1)
     enc_sums = [scatter_core(item) for item in (d_enc_low, d_enc_high, d_enc_fo)]
-    late, dec_lines, enc_sums, d_enc_ob = lax.optimization_barrier(
-        (d_dec_rest, dec_lines, enc_sums, d_enc_ob)
+    late, dec_lines, enc_sums, g_dec_fo, d_enc_ob = lax.optimization_barrier(
+        (d_dec_rest, dec_lines, enc_sums, g_dec_fo, d_enc_ob)
     )
     late = lax.psum_scatter(late, ALL, scatter_dimension=0, tiled=True)
     early = early.astype(f32)
-    g_low, g_high, g_fo = [
-        scatter_rest(item, number == 0) for number, item in enumerate(enc_sums)
-    ]
+    enc_sums = [scatter_first(item, number == 0) for number, item in enumerate(enc_sums)]
     d_enc_q, own, other, enc_y8 = attend_backward(
         d_enc_ob, enc_q, enc_kv, enc_kv2, enc_info, enc_x8, False
     )
@@ -841,16 +835,16 @@
     d_x0_norm, d_gain_eatt = norm_pull(enc_x0, gain[0], 1.0, input_grad(d_enc_qkv, enc_wi))
     d_x0 = d_x1 + d_x0_norm
 
-    enc_lines = line_gather(d_x0.astype(bf16), "z")
+    d_x0, enc_sums = lax.optimization_barrier((d_x0.astype(bf16), enc_sums))
+    enc_sums = [scatter_second(item, number == 0) for number, item in enumerate(enc_sums)]
+    enc_lines = line_gather(d_x0, "z")
+    enc_lines, enc_sums = lax.optimization_barrier((enc_lines, enc_sums))
+    g_low, g_high, g_fo, g_dec_fo = [scatter_last(item) for item in (*enc_sums, g_dec_fo)]
     far_place = lambda item: jnp.where(item == shard, -1, item)[None, :]
     pairs = [
         (far_place(item), grads)
         for item, grads in zip(enc_places + dec_places, enc_lines + dec_lines)
     ]
-    input_embed, late = plane_scatter(pairs, padded, late)
-    late = late.astype(f32)
-    grad_embed = head_embed[:shard] + input_embed[:shard]
-
     d_gains = jnp.stack(
         [
             d_gain_eatt,
@@ -866,20 +860,24 @@
     d_rel = jnp.transpose(d_rel.reshape(2, -1, rel_table.shape[1]), (1, 0, 2)).reshape(D, 1)
     d_misc = jnp.pad(jnp.concatenate([d_gains.T, d_rel], axis=1), ((0, 0), (0, 120)))
     d_last = jnp.concatenate([d_enc_wi.astype(bf16), d_misc.astype(bf16)], axis=1)
-    last = [scatter_chain(d_last[:, :1152], True), scatter_chain(d_last[:, 1152:], False)]
+    last = [scatter_core(d_last[:, :1152]), scatter_core(d_last[:, 1152:])]
+    input_embed, late, last = plane_scatter(pairs, padded, late, last)
+    late = late.astype(f32)
+    grad_embed = head_embed[:shard] + input_embed[:shard]
+
+    last = [scatter_rest(item, number == 0) for number, item in enumerate(last)]
     squares = sum(
-        (jnp.sum(item * item) for item in (grad_embed, early, late, g_low, g_high, g_fo, *last))
+        (jnp.sum(item * item) for item in (grad_embed, early, late, g_low, g_high, g_fo, g_dec_fo, *last))
     )
     sums = fold_all(jnp.stack([jnp.sum(mask), loss_local, squares]), jnp.add)
     last = jnp.concatenate(last, axis=1)
-    rows_out = lambda out: out.reshape(-1, D)
     owned = (
         jnp.stack([cut(last, 0, 3 * D), cut(late, 0, 3 * D), cut(late, 3 * D, 3 * D)]),
         jnp.stack([cut(g_high, 640, D), cut(late, 6 * D, D), cut(late, 7 * D, D)]),
         jnp.stack(
-            [jnp.concatenate([g_low, cut(g_high, 0, 640)], axis=1), cut(early, 0, 2 * FF)]
+            [jnp.concatenate([g_low, cut(g_high, 0, 640)], axis=1), early]
         ),
-        jnp.stack([g_fo, rows_out(cut(early, 2 * FF, FF))]),
+        jnp.stack([g_fo, g_dec_fo]),
         last[:, 3 * D + 7].reshape(2, -1),
         last[:, 3 * D : 3 * D + 7].T,
     )

time: 1470 us -> 1400 us (0.952)
  waiting for transfers between devices: 454 us -> 416 us
  other arithmetic: 167 us -> 146 us
  Pallas kernels: 311 us -> 294 us
    ppermute x47 -> x50, waiting for transfers between devices: 165 us -> 106 us  [swap(): return lax.ppermute(value, axis, [(0, 1), (1, 0)])]
    all_gather x1, waiting for transfers between devices: 52 us -> 72.9 us  [body(): hidden_all = lax.all_gather(hidden_b, ALL, axis=0, tiled=True)]
    ppermute x27 -> x30, starting transfers between devices: 50 us -> 39 us  [scatter_last(): got = lax.ppermute(send, 'z', [(i, (i + hop) % size) for i in range(size)])]
    convert_element_type x29 -> x32, other arithmetic: 36.2 us -> 46.7 us  [add16(): return (left.astype(f32) + right.astype(f32)).astype(bf16)]
    unnamed x389 -> x463, local copies, waits for them, and re-layouts: 48.3 us -> 53.8 us
    ppermute x27 -> x30, waiting for transfers between devices: 54.7 us -> 52.4 us  [scatter_last(): got = lax.ppermute(send, 'z', [(i, (i + hop) % size) for i in range(size)])]
    ppermute x47 -> x50, starting transfers between devices: 40.7 us -> 42.6 us  [swap(): return lax.ppermute(value, axis, [(0, 1), (1, 0)])]
  transfers between devices with their start and end apart: 121 -> 127, of which waited for: 53 -> 56; matrix products, arithmetic and copies ran while one was open for 25% -> 27% of each run, Pallas kernels for 17% -> 14%
where the time goes in v5:
time: 1400 us; the launch traced here: 1390 us
  waiting for transfers between devices  416 us (30%)
  Pallas kernels  294 us (21%)
  local copies, waits for them, and re-layouts  205 us (15%)
  starting transfers between devices  169 us (12%)
  other arithmetic  146 us (10%)
  matrix products  129 us (9%)
  between operations  31.4 us (2%)
    ppermute x50, waiting for transfers between devices, swap(): return lax.ppermute(value, axis, [(0, 1), (1, 0)])  106 us
    pallas_call x3, Pallas kernels, attend_backward(): pl.pallas_call(functools.partial(attend_backward_kernel, cfg), grid=(HEAD...  101 us
    ppermute x3, waiting for transfers between devices, line_scatter(): up = lax.ppermute(send_up, axis, [(i, i + 1) for i in range(step)])  95.5 us
    all_gather x1, waiting for transfers between devices, body(): hidden_all = lax.all_gather(hidden_b, ALL, axis=0, tiled=True)  72.9 us
    pallas_call x4, Pallas kernels, head_grad(): pl.pallas_call(functools.partial(head_grad_kernel, count), grid_spec=pltp...  63.4 us
    pallas_call x3, Pallas kernels, attend_forward(): pl.pallas_call(functools.partial(attend_forward_kernel, cfg), grid=(HEADS...  55 us
    unnamed x463, local copies, waits for them, and re-layouts  53.8 us
    ppermute x30, waiting for transfers between devices, scatter_last(): got = lax.ppermute(send, 'z', [(i, (i + hop) % size) for i in range(size)])  52.4 us
  transfers between devices with their start and end apart: 127, of which 56 were waited for; matrix products, arithmetic and copies ran while one was open for 27% of the time, Pallas kernels for 14%

profile of v5, /device:TPU:0, one launch (start us, length us, event | category | flops | bytes accessed | tf_op | source)
XLA Modules:
  0.0 1390.0 jit_solution(1824289738478352593)
XLA Ops:
  50.7 24.4 %collective-permute-done.1 = bf16[1008,768]{1,0:T(8,128)(2,1)S(1)} collective-permute-done((bf16[1008,768]{1,0:T(8,128)(2,1)}, bf16[1008,768]{1,0:T(8,128)(2,1)S(1)}, u32[]{:S(2)}, u32[]{:S(2)}) %collective-permute-start.1) | collective-permute-done | bytes 1548320 | tf_op jit(solution)/shard_map/ppermute | solution.py:409
  81.6 17.0 %collective-permute-done.3 = bf16[504,768]{1,0:T(8,128)(2,1)S(1)} collective-permute-done((bf16[504,768]{1,0:T(8,128)(2,1)S(1)}, bf16[504,768]{1,0:T(8,128)(2,1)S(1)}, u32[]{:S(2)}, u32[]{:S(2)}) %collective-permute-start.3) | collective-permute-done | bytes 774176 | tf_op jit(solution)/shard_map/ppermute | solution.py:409
  113.0 29.8 %all-gather.5.cloned.1.call-done = bf16[768,9344]{1,0:T(8,128)(2,1)} async-done(((bf16[24,9344]{1,0:T(8,128)(2,1)}), bf16[768,9344]{1,0:T(8,128)(2,1)}) %all-gather.5.cloned.1.call-update) | async-done | bytes 14352400 | tf_op jit(solution)/shard_map/all_gather | solution.py:607
  142.9 20.7 %gather_fusion = bf16[3072,768]{1,0:T(8,128)(2,1)} fusion(bf16[8064,768]{1,0:T(8,128)(2,1)} %constant_dynamic-update-slice_fusion.4, s32[3072]{0:T(1024)S(1)} %add_clamp_fusion), kind=kCustom, calls=%fused_computation | custom fusion | bytes 9449472 | tf_op jit(solution)/shard_map/jit(_take)/gather | solution.py:675
  168.8 39.0 %collective-permute-done.16 = bf16[768,768]{1,0:T(8,128)(2,1)S(1)} collective-permute-done((bf16[768,768]{1,0:T(8,128)(2,1)S(1)}, bf16[768,768]{1,0:T(8,128)(2,1)S(1)}, u32[]{:S(2)}, u32[]{:S(2)}) %collective-permute-start.16) | collective-permute-done | bytes 1179680 | tf_op jit(solution)/shard_map/ppermute | solution.py:476
  218.0 38.8 %collective-permute-done.17 = bf16[768,768]{1,0:T(8,128)(2,1)S(1)} collective-permute-done((bf16[768,768]{1,0:T(8,128)(2,1)}, bf16[768,768]{1,0:T(8,128)(2,1)S(1)}, u32[]{:S(2)}, u32[]{:S(2)}) %collective-permute-start.17) | collective-permute-done | bytes 1179680 | tf_op jit(solution)/shard_map/ppermute | solution.py:476
  271.1 17.7 %collective-permute-done.18 = bf16[768,768]{1,0:T(8,128)(2,1)S(1)} collective-permute-done((bf16[768,768]{1,0:T(8,128)(2,1)}, bf16[768,768]{1,0:T(8,128)(2,1)S(1)}, u32[]{:S(2)}, u32[]{:S(2)}) %collective-permute-start.18) | collective-permute-done | bytes 1179680 | tf_op jit(solution)/shard_map/ppermute | solution.py:476
  296.4 4.9 convolution_convert_fusion.8.refs_1_.refs_2_
  314.4 28.6 %shard_map.461 = bf16[512,768]{1,0:T(8,128)(2,1)} custom-call(bf16[512,768]{1,0:T(8,128)(2,1)} %convolution_convert_fusion.15.refs_0_, bf16[512,1536]{1,0:T(8,128)(2,1)} %convolution_convert_fusion.8.refs_1_.refs_2_, bf16[512,1536]{1,0:T(8,128)(2,1)} %convolution_convert_fusion.8.refs_1_.refs_2_, bf16[512,1536]{1,0:T(8,128)(2,1)} %collective-permute-done.22.refs_3_.refs_4_, ...), custom_call_target="tpu_custom_call" | custom-call | flops 2 | bytes 512 | tf_op jit(solution)/shard_map/pallas_call | solution.py:197
  349.9 6.8 reshape.679
  360.2 6.2 fusion.7
  392.0 14.0 %shard_map.462 = bf16[256,768]{1,0:T(8,128)(2,1)} custom-call(bf16[256,768]{1,0:T(8,128)(2,1)} %convolution_convert_fusion.19.refs_0_, bf16[256,1536]{1,0:T(8,128)(2,1)} %copy-done.12, bf16[256,1536]{1,0:T(8,128)(2,1)} %copy-done.12, bf16[256,1536]{1,0:T(8,128)(2,1)} %collective-permute-done.23.refs_3_.refs_4_, ...), custom_call_target="tpu_custom_call" | custom-call | flops 2 | bytes 256 | tf_op jit(solution)/shard_map/pallas_call | solution.py:197
  410.8 12.4 shard_map.463
  425.3 4.9 fusion.3
  466.1 72.9 %all-gather.11.cloned.1.call-done = bf16[8192,768]{1,0:T(8,128)(2,1)} async-done(((bf16[256,768]{1,0:T(8,128)(2,1)}), bf16[8192,768]{1,0:T(8,128)(2,1)}) %all-gather.11.cloned.1.call-update) | async-done | bytes 12582928 | tf_op jit(solution)/shard_map/all_gather | solution.py:736
  539.0 25.8 %shard_map.464 = (f32[1,8192]{1,0:T(1,128)}, f32[1,8192]{1,0:T(1,128)}) custom-call(bf16[8,2,2,256,768]{4,3,2,1,0:T(8,128)(2,1)} %bitcast.655, bf16[1008,768]{1,0:T(8,128)(2,1)} %get-tuple-element.477.tab, s32[1,8192]{1,0:T(1,128)} %bitcast.614), custom_call_target="tpu_custom_call" | custom-call | flops 12683575296 | bytes 12582912 | tf_op jit(solution)/shard_map/pallas_call | solution.py:300
  586.8 15.8 %shard_map.465 = (bf16[8,2,64,768]{3,2,1,0:T(8,128)(2,1)}, bf16[8,2,64,768]{3,2,1,0:T(8,128)(2,1)}, f32[1008,768]{1,0:T(8,128)}) custom-call(s32[1]{0:T(128)} %bitcast.75.core, bf16[8,2,2,256,768]{4,3,2,1,0:T(8,128)(2,1)} %bitcast.656, bf16[1008,768]{1,0:T(8,128)(2,1)} %get-tuple-element.477.tab, s32[1,8192]{1,0:T(1,128)} %bitcast.615, f32[1,8192]{1,0:T(1,128)} %bitcast.593, ...), custom_call_target="tpu_custom_call" | custom-call | flops 9512681472 | bytes 6291456 | tf_op jit(solution)/shard_map/pallas_call | solution.py:323
  602.6 15.8 %shard_map.467 = (bf16[8,2,64,768]{3,2,1,0:T(8,128)(2,1)}, bf16[8,2,64,768]{3,2,1,0:T(8,128)(2,1)}, f32[1008,768]{1,0:T(8,128)}) custom-call(s32[1]{0:T(128)} %bitcast.75.core, bf16[8,2,2,256,768]{4,3,2,1,0:T(8,128)(2,1)} %bitcast.657, bf16[1008,768]{1,0:T(8,128)(2,1)} %get-tuple-element.477.tab, s32[1,8192]{1,0:T(1,128)} %bitcast.616, f32[1,8192]{1,0:T(1,128)} %bitcast.594, ...), custom_call_target="tpu_custom_call" | custom-call | flops 9512681472 | bytes 6291456 | tf_op jit(solution)/shard_map/pallas_call | solution.py:323
  619.0 15.8 %shard_map.466 = (bf16[8,2,64,768]{3,2,1,0:T(8,128)(2,1)}, bf16[8,2,64,768]{3,2,1,0:T(8,128)(2,1)}, f32[1008,768]{1,0:T(8,128)}) custom-call(s32[1]{0:T(128)} %bitcast.76.core, bf16[8,2,2,256,768]{4,3,2,1,0:T(8,128)(2,1)} %bitcast.658, bf16[1008,768]{1,0:T(8,128)(2,1)} %get-tuple-element.477.tab, s32[1,8192]{1,0:T(1,128)} %bitcast.617, f32[1,8192]{1,0:T(1,128)} %bitcast.595, ...), custom_call_target="tpu_custom_call" | custom-call | flops 9512681472 | bytes 6291456 | tf_op jit(solution)/shard_map/pallas_call | solution.py:323
  635.4 16.0 %shard_map.468 = (bf16[8,2,64,768]{3,2,1,0:T(8,128)(2,1)}, bf16[8,2,64,768]{3,2,1,0:T(8,128)(2,1)}, f32[1008,768]{1,0:T(8,128)}) custom-call(s32[1]{0:T(128)} %bitcast.76.core, bf16[8,2,2,256,768]{4,3,2,1,0:T(8,128)(2,1)} %bitcast.659, bf16[1008,768]{1,0:T(8,128)(2,1)} %get-tuple-element.477.tab, s32[1,8192]{1,0:T(1,128)} %bitcast.618, f32[1,8192]{1,0:T(1,128)} %bitcast.596, ...), custom_call_target="tpu_custom_call" | custom-call | flops 9512681472 | bytes 6291456 | tf_op jit(solution)/shard_map/pallas_call | solution.py:323
  662.3 13.3 collective-permute-done.37
  679.2 13.2 collective-permute-done.49
  696.0 7.0 collective-permute-done.38
  731.9 5.0 collective-permute-done.58
  742.0 4.7 convolution_convert_fusion.1
  746.6 6.8 multiply_reduce_fusion.12
  757.1 21.7 %shard_map.469 = (bf16[256,768]{1,0:T(8,128)(2,1)}, f32[2,512,768]{2,1,0:T(8,128)}, bf16[2,512,768]{2,1,0:T(8,128)(2,1)}) custom-call(bf16[256,768]{1,0:T(8,128)(2,1)} %convolution_convert_fusion.18.refs_0_, bf16[512,1536]{1,0:T(8,128)(2,1)} %convolution_convert_fusion.7.refs_1_.refs_2_, bf16[512,1536]{1,0:T(8,128)(2,1)} %convolution_convert_fusion.7.refs_1_.refs_2_, ...), custom_call_target="tpu_custom_call" | custom-call | flops 5 | bytes 256 | tf_op jit(solution)/shard_map/pallas_call | solution.py:221
  809.8 24.7 %shard_map.470 = (bf16[256,768]{1,0:T(8,128)(2,1)}, f32[2,256,768]{2,1,0:T(8,128)}, bf16[2,256,768]{2,1,0:T(8,128)(2,1)}, f32[12,2,8,512]{3,2,1,0:T(8,128)}) custom-call(bf16[256,768]{1,0:T(8,128)(2,1)} %convolution_convert_fusion.19.refs_0_, bf16[256,1536]{1,0:T(8,128)(2,1)} %copy-done.12, bf16[256,1536]{1,0:T(8,128)(2,1)} %copy-done.12, ...), custom_call_target="tpu_custom_call" | custom-call | flops 5 | bytes 256 | tf_op jit(solution)/shard_map/pallas_call | solution.py:221
  834.5 8.9 fusion.65
  843.4 7.1 convolution_convert_fusion
  855.0 9.6 multiply_reduce_fusion.3
  898.7 5.1 collective-permute-start.68
  953.3 4.7 slice_bitcast_fusion.3
  984.1 55.0 %shard_map.471 = (bf16[512,768]{1,0:T(8,128)(2,1)}, f32[2,512,768]{2,1,0:T(8,128)}, bf16[2,512,768]{2,1,0:T(8,128)(2,1)}, f32[12,4,8,768]{3,2,1,0:T(8,128)}) custom-call(bf16[512,768]{1,0:T(8,128)(2,1)} %convolution_convert_fusion.15.refs_0_, bf16[512,1536]{1,0:T(8,128)(2,1)} %convolution_convert_fusion.8.refs_1_.refs_2_, ...), custom_call_target="tpu_custom_call" | custom-call | flops 5 | bytes 512 | tf_op jit(solution)/shard_map/pallas_call | solution.py:221
  1075.6 5.0 copy.745
  1083.9 6.3 collective-permute-done.78
  1090.3 5.4 collective-permute-start.82
  1101.6 9.1 collective-permute-done.82
  1118.7 5.0 copy.720
  1139.1 23.9 %shard_map.473 = bf16[4032,768]{1,0:T(8,128)(2,1)} custom-call(s32[1,512]{1,0:T(1,128)} %bitcast.625, bf16[512,768]{1,0:T(8,128)(2,1)} %copy-done.24, s32[1,512]{1,0:T(1,128)} %bitcast.623, bf16[512,768]{1,0:T(8,128)(2,1)} %add.1343.refs_3_, s32[1,512]{1,0:T(1,128)} %bitcast.621, bf16[512,768]{1,0:T(8,128)(2,1)} %add.1344.refs_5_, s32[1,512]{1,0:T(1,128)} %bitcast.619, ...), custom_call_target="tpu_custom_call" | custom-call | flops 1 | bytes 1008 | tf_op jit(solution)/shard_map/pallas_call | solution.py:368
  1163.1 6.2 fusion
  1186.2 7.2 collective-permute-done.101
  1204.2 24.3 %shard_map.472 = bf16[4032,768]{1,0:T(8,128)(2,1)} custom-call(s32[1,512]{1,0:T(1,128)} %bitcast.626, bf16[512,768]{1,0:T(8,128)(2,1)} %copy-done.24, s32[1,512]{1,0:T(1,128)} %bitcast.624, bf16[512,768]{1,0:T(8,128)(2,1)} %add.1343.refs_3_, s32[1,512]{1,0:T(1,128)} %bitcast.622, bf16[512,768]{1,0:T(8,128)(2,1)} %add.1344.refs_5_, s32[1,512]{1,0:T(1,128)} %bitcast.620, ...), custom_call_target="tpu_custom_call" | custom-call | flops 1 | bytes 1008 | tf_op jit(solution)/shard_map/pallas_call | solution.py:368
  1266.4 17.8 %collective-permute-done.112 = bf16[4,24,1280]{2,1,0:T(8,128)(2,1)S(1)} collective-permute-done((bf16[4,24,1280]{2,1,0:T(8,128)(2,1)}, bf16[4,24,1280]{2,1,0:T(8,128)(2,1)S(1)}, u32[]{:S(2)}, u32[]{:S(2)}) %collective-permute-start.112) | collective-permute-done | bytes 245792 | tf_op jit(solution)/shard_map/ppermute | solution.py:409
  1301.2 7.2 collective-permute-done.113
  1308.4 9.8 collective-permute-done.114
  1327.1 8.5 multiply_reduce_fusion.1
  1365.8 8.3 add_subtract_fusion
  (1071 shorter events, 600.6 us)
Async XLA Ops:
  7.2 135.5 %all-gather.5.cloned.1.call-start = ((), (), s32[]{:S(2)}) async-start(), calls=%async_computation.2 | async-start | bytes 14800896 | tf_op jit(solution)/shard_map/all_gather | solution.py:607
  19.9 323.1 %all-gather.7.cloned.1.call-start = ((), (), s32[]{:S(2)}) async-start(), calls=%async_computation.3 | async-start | bytes 9732096 | tf_op jit(solution)/shard_map/all_gather | solution.py:670
  22.9 52.2 %collective-permute-start.1 = (bf16[1008,768]{1,0:T(8,128)(2,1)}, bf16[1008,768]{1,0:T(8,128)(2,1)S(1)}, u32[]{:S(2)}, u32[]{:S(2)}) collective-permute-start(bf16[1008,768]{1,0:T(8,128)(2,1)} %get-tuple-element.477.tab), channel_id=1, source_target_pairs={{0,1},{1,0},{2,3},{3,2},{4,5},{5,4},{6,7},{7,6},{8,9},{9,8},{10,11... | collective-permute-start | bytes 4644872 | tf_op jit(solution)/shard_map/ppermute | solution.py:409
  27.1 48.7 %collective-permute-start.2 = (bf16[1008,768]{1,0:T(8,128)(2,1)}, bf16[1008,768]{1,0:T(8,128)(2,1)S(1)}, u32[]{:S(2)}, u32[]{:S(2)}) collective-permute-start(bf16[1008,768]{1,0:T(8,128)(2,1)} %get-tuple-element.477.tab), channel_id=1, source_target_pairs={{0,4},{4,0},{1,5},{5,1},{2,6},{6,2},{3,7},{7,3},{8,12},{12,8},{9,1... | collective-permute-start | bytes 4644872 | tf_op jit(solution)/shard_map/ppermute | solution.py:409
  28.6 74.5 %collective-permute-start.5 = (bf16[1008,768]{1,0:T(8,128)(2,1)}, bf16[1008,768]{1,0:T(8,128)(2,1)}, u32[]{:S(2)}, u32[]{:S(2)}) collective-permute-start(bf16[1008,768]{1,0:T(8,128)(2,1)} %get-tuple-element.477.tab), channel_id=1, source_target_pairs={{0,2},{2,0},{1,3},{3,1},{4,6},{6,4},{5,7},{7,5},{8,10},{10,8},{9,1... | collective-permute-start | bytes 4644872 | tf_op jit(solution)/shard_map/ppermute | solution.py:409
  44.8 31.8 %collective-permute-start.13 = (s32[768]{0:T(1024)S(1)}, s32[768]{0:T(1024)S(1)}, u32[]{:S(2)}, u32[]{:S(2)}) collective-permute-start(s32[768]{0:T(1024)S(1)} %collective-permute-done.12), channel_id=1, source_target_pairs={{8,0},{16,8},{24,16},{9,1},{17,9},{25,17},{10,2},{18,10},{26,18},{... | collective-permute-start | bytes 9224 | tf_op jit(solution)/shard_map/ppermute | solution.py:464
  46.1 32.8 %collective-permute-start.15 = (s32[768]{0:T(1024)S(1)}, s32[768]{0:T(1024)S(1)}, u32[]{:S(2)}, u32[]{:S(2)}) collective-permute-start(s32[768]{0:T(1024)S(1)} %collective-permute-done.14), channel_id=1, source_target_pairs={{0,8},{8,16},{16,24},{1,9},{9,17},{17,25},{2,10},{10,18},{18,26},{... | collective-permute-start | bytes 9224 | tf_op jit(solution)/shard_map/ppermute | solution.py:463
  75.1 30.6 %collective-permute-start.6 = (bf16[1008,768]{1,0:T(8,128)(2,1)S(1)}, bf16[1008,768]{1,0:T(8,128)(2,1)}, u32[]{:S(2)}, u32[]{:S(2)}) collective-permute-start(bf16[1008,768]{1,0:T(8,128)(2,1)S(1)} %collective-permute-done.1), channel_id=1, source_target_pairs={{0,2},{2,0},{1,3},{3,1},{4,6},{6,4},{5,7},{7,5},{8,10},{10,8},{9,1... | collective-permute-start | bytes 4644872 | tf_op jit(solution)/shard_map/ppermute | solution.py:409
  75.8 32.6 %collective-permute-start.7 = (bf16[1008,768]{1,0:T(8,128)(2,1)S(1)}, bf16[1008,768]{1,0:T(8,128)(2,1)}, u32[]{:S(2)}, u32[]{:S(2)}) collective-permute-start(bf16[1008,768]{1,0:T(8,128)(2,1)S(1)} %collective-permute-done.2), channel_id=1, source_target_pairs={{0,2},{2,0},{1,3},{3,1},{4,6},{6,4},{5,7},{7,5},{8,10},{10,8},{9,1... | collective-permute-start | bytes 4644872 | tf_op jit(solution)/shard_map/ppermute | solution.py:409
  78.9 22.3 %collective-permute-start.4 = (bf16[504,768]{1,0:T(8,128)(2,1)S(1)}, bf16[504,768]{1,0:T(8,128)(2,1)S(1)}, u32[]{:S(2)}, u32[]{:S(2)}) collective-permute-start(bf16[504,768]{1,0:T(8,128)(2,1)S(1)} %slice.615), channel_id=1, source_target_pairs={{0,4},{4,0},{1,5},{5,1},{2,6},{6,2},{3,7},{7,3},{8,12},{12,8},{9,1... | collective-permute-start | bytes 2322440 | tf_op jit(solution)/shard_map/ppermute | solution.py:409
  142.8 282.5 %all-gather.9.cloned.1.call-start = ((), (), s32[]{:S(2)}) async-start(), calls=%async_computation.4 | async-start | bytes 9732096 | tf_op jit(solution)/shard_map/all_gather | solution.py:711
  165.3 42.4 %collective-permute-start.16 = (bf16[768,768]{1,0:T(8,128)(2,1)S(1)}, bf16[768,768]{1,0:T(8,128)(2,1)S(1)}, u32[]{:S(2)}, u32[]{:S(2)}) collective-permute-start(bf16[768,768]{1,0:T(8,128)(2,1)S(1)} %get-tuple-element.445), channel_id=1, source_target_pairs={{0,8},{1,9},{2,10},{3,11},{4,12},{5,13},{6,14},{7,15}} | collective-permute-start | bytes 3538952 | tf_op jit(solution)/shard_map/ppermute | solution.py:476
  167.9 39.9 %collective-permute-start.19 = (bf16[768,768]{1,0:T(8,128)(2,1)S(1)}, bf16[768,768]{1,0:T(8,128)(2,1)S(1)}, u32[]{:S(2)}, u32[]{:S(2)}) collective-permute-start(bf16[768,768]{1,0:T(8,128)(2,1)S(1)} %get-tuple-element.446), channel_id=1, source_target_pairs={{24,16},{25,17},{26,18},{27,19},{28,20},{29,21},{30,22},{31,23}} | collective-permute-start | bytes 3538952 | tf_op jit(solution)/shard_map/ppermute | solution.py:477
  210.7 46.1 %collective-permute-start.17 = (bf16[768,768]{1,0:T(8,128)(2,1)}, bf16[768,768]{1,0:T(8,128)(2,1)S(1)}, u32[]{:S(2)}, u32[]{:S(2)}) collective-permute-start(bf16[768,768]{1,0:T(8,128)(2,1)} %get-tuple-element.443), channel_id=1, source_target_pairs={{0,8},{8,16},{1,9},{9,17},{2,10},{10,18},{3,11},{11,19},{4,12},{12... | collective-permute-start | bytes 3538952 | tf_op jit(solution)/shard_map/ppermute | solution.py:476
  215.1 41.7 %collective-permute-start.20 = (bf16[768,768]{1,0:T(8,128)(2,1)}, bf16[768,768]{1,0:T(8,128)(2,1)S(1)}, u32[]{:S(2)}, u32[]{:S(2)}) collective-permute-start(bf16[768,768]{1,0:T(8,128)(2,1)} %get-tuple-element.444), channel_id=1, source_target_pairs={{24,16},{16,8},{25,17},{17,9},{26,18},{18,10},{27,19},{19,11},{28,... | collective-permute-start | bytes 3538952 | tf_op jit(solution)/shard_map/ppermute | solution.py:477
  259.7 29.1 %collective-permute-start.18 = (bf16[768,768]{1,0:T(8,128)(2,1)}, bf16[768,768]{1,0:T(8,128)(2,1)S(1)}, u32[]{:S(2)}, u32[]{:S(2)}) collective-permute-start(bf16[768,768]{1,0:T(8,128)(2,1)} %get-tuple-element.441), channel_id=1, source_target_pairs={{0,8},{8,16},{16,24},{1,9},{9,17},{17,25},{2,10},{10,18},{18,26},{... | collective-permute-start | bytes 3538952 | tf_op jit(solution)/shard_map/ppermute | solution.py:476
  264.1 29.5 %collective-permute-start.21 = (bf16[768,768]{1,0:T(8,128)(2,1)S(1)}, bf16[768,768]{1,0:T(8,128)(2,1)}, u32[]{:S(2)}, u32[]{:S(2)}) collective-permute-start(bf16[768,768]{1,0:T(8,128)(2,1)S(1)} %get-tuple-element.442), channel_id=1, source_target_pairs={{24,16},{16,8},{8,0},{25,17},{17,9},{9,1},{26,18},{18,10},{10,2},{... | collective-permute-start | bytes 3538952 | tf_op jit(solution)/shard_map/ppermute | solution.py:477
  343.1 195.9 %all-gather.11.cloned.1.call-start = ((), (), s32[]{:S(2)}) async-start(), calls=%async_computation.5 | async-start | bytes 12976128 | tf_op jit(solution)/shard_map/all_gather | solution.py:736
  378.0 32.8 %collective-permute-start.24 = (bf16[512,1536]{1,0:T(8,128)(2,1)}, bf16[512,1536]{1,0:T(8,128)(2,1)}, u32[]{:S(2)}, u32[]{:S(2)}) collective-permute-start(bf16[512,1536]{1,0:T(8,128)(2,1)} %convolution_convert_fusion.7.refs_1_.refs_2_), channel_id=1, source_target_pairs={{0,2},{2,0},{1,3},{3,1},{4,6},{6,4},{5,7},{7,5},{8,10},{10,8},{9,1... | collective-permute-start | bytes 4718600 | tf_op jit(solution)/shard_map/ppermute | solution.py:409
  443.2 485.0 %reduce-scatter.5.cloned.1.call-start = ((), (), s32[]{:S(2)}) async-start(), calls=%async_computation.6 | async-start | bytes 6488064 | tf_op jit(solution)/shard_map/reduce_scatter | solution.py:775
  618.5 32.9 %collective-permute-start.36 = (bf16[8,2,64,768]{3,2,1,0:T(8,128)(2,1)}, bf16[8,2,64,768]{3,2,1,0:T(8,128)(2,1)S(1)}, u32[]{:S(2)}, u32[]{:S(2)}) collective-permute-start(bf16[8,2,64,768]{3,2,1,0:T(8,128)(2,1)} %get-tuple-element.124), channel_id=1, source_target_pairs={{0,2},{2,0},{1,3},{3,1},{4,6},{6,4},{5,7},{7,5},{8,10},{10,8},{9,1... | collective-permute-start | bytes 4718600 | tf_op jit(solution)/shard_map/ppermute | solution.py:409
  618.5 38.0 %collective-permute-start.42 = (bf16[8,2,64,768]{3,2,1,0:T(8,128)(2,1)}, bf16[8,2,64,768]{3,2,1,0:T(8,128)(2,1)S(1)}, u32[]{:S(2)}, u32[]{:S(2)}) collective-permute-start(bf16[8,2,64,768]{3,2,1,0:T(8,128)(2,1)} %get-tuple-element.126), channel_id=1, source_target_pairs={{0,2},{2,0},{1,3},{3,1},{4,6},{6,4},{5,7},{7,5},{8,10},{10,8},{9,1... | collective-permute-start | bytes 4718600 | tf_op jit(solution)/shard_map/ppermute | solution.py:409
  634.8 23.7 %collective-permute-start.48 = (bf16[8,2,64,768]{3,2,1,0:T(8,128)(2,1)}, bf16[8,2,64,768]{3,2,1,0:T(8,128)(2,1)S(1)}, u32[]{:S(2)}, u32[]{:S(2)}) collective-permute-start(bf16[8,2,64,768]{3,2,1,0:T(8,128)(2,1)} %get-tuple-element.128), channel_id=1, source_target_pairs={{0,2},{2,0},{1,3},{3,1},{4,6},{6,4},{5,7},{7,5},{8,10},{10,8},{9,1... | collective-permute-start | bytes 4718600 | tf_op jit(solution)/shard_map/ppermute | solution.py:409
  634.9 25.4 %collective-permute-start.54 = (bf16[8,2,64,768]{3,2,1,0:T(8,128)(2,1)}, bf16[8,2,64,768]{3,2,1,0:T(8,128)(2,1)S(1)}, u32[]{:S(2)}, u32[]{:S(2)}) collective-permute-start(bf16[8,2,64,768]{3,2,1,0:T(8,128)(2,1)} %get-tuple-element.130), channel_id=1, source_target_pairs={{0,2},{2,0},{1,3},{3,1},{4,6},{6,4},{5,7},{7,5},{8,10},{10,8},{9,1... | collective-permute-start | bytes 4718600 | tf_op jit(solution)/shard_map/ppermute | solution.py:409
  659.2 33.2 %collective-permute-start.49 = (bf16[4,2,64,768]{3,2,0,1:T(8,128)(2,1)S(1)}, bf16[4,2,64,768]{3,2,0,1:T(8,128)(2,1)S(1)}, u32[]{:S(2)}, u32[]{:S(2)}) collective-permute-start(bf16[4,2,64,768]{3,2,0,1:T(8,128)(2,1)S(1)} %bitcast.588), channel_id=1, source_target_pairs={{0,1},{1,0},{2,3},{3,2},{4,5},{5,4},{6,7},{7,6},{8,9},{9,8},{10,11... | collective-permute-start | bytes 2359304 | tf_op jit(solution)/shard_map/ppermute | solution.py:409
  661.1 33.5 %collective-permute-start.55 = (bf16[4,2,64,768]{3,2,0,1:T(8,128)(2,1)S(1)}, bf16[4,2,64,768]{3,2,0,1:T(8,128)(2,1)S(1)}, u32[]{:S(2)}, u32[]{:S(2)}) collective-permute-start(bf16[4,2,64,768]{3,2,0,1:T(8,128)(2,1)S(1)} %bitcast.589), channel_id=1, source_target_pairs={{0,4},{4,0},{1,5},{5,1},{2,6},{6,2},{3,7},{7,3},{8,12},{12,8},{9,1... | collective-permute-start | bytes 2359304 | tf_op jit(solution)/shard_map/ppermute | solution.py:409
  675.8 27.2 %collective-permute-start.38 = (bf16[4,64,768]{2,1,0:T(8,128)(2,1)S(1)}, bf16[4,64,768]{2,1,0:T(8,128)(2,1)S(1)}, u32[]{:S(2)}, u32[]{:S(2)}) collective-permute-start(bf16[4,64,768]{2,1,0:T(8,128)(2,1)S(1)} %dynamic-slice_bitcast_fusion.16), channel_id=1, source_target_pairs={{0,4},{4,0},{1,5},{5,1},{2,6},{6,2},{3,7},{7,3},{8,12},{12,8},{9,1... | collective-permute-start | bytes 1179656 | tf_op jit(solution)/shard_map/ppermute | solution.py:409
  678.0 27.3 %collective-permute-start.44 = (bf16[4,64,768]{2,1,0:T(8,128)(2,1)S(1)}, bf16[4,64,768]{2,1,0:T(8,128)(2,1)S(1)}, u32[]{:S(2)}, u32[]{:S(2)}) collective-permute-start(bf16[4,64,768]{2,1,0:T(8,128)(2,1)S(1)} %dynamic-slice_bitcast_fusion.15), channel_id=1, source_target_pairs={{0,1},{1,0},{2,3},{3,2},{4,5},{5,4},{6,7},{7,6},{8,9},{9,8},{10,11... | collective-permute-start | bytes 1179656 | tf_op jit(solution)/shard_map/ppermute | solution.py:409
  782.9 354.4 %reduce-scatter.7.cloned.1.call-start = ((), (), s32[]{:S(2)}) async-start(), calls=%async_computation.7 | async-start | bytes 9732096
  801.4 116.0 %collective-permute-start.61 = (bf16[4,2,64,768]{3,2,0,1:T(8,128)(2,1)}, bf16[4,2,64,768]{3,2,0,1:T(8,128)(2,1)}, u32[]{:S(2)}, u32[]{:S(2)}) collective-permute-start(bf16[4,2,64,768]{3,2,0,1:T(8,128)(2,1)} %dynamic-slice_bitcast_fusion.7), channel_id=1, source_target_pairs={{0,4},{4,0},{1,5},{5,1},{2,6},{6,2},{3,7},{7,3},{8,12},{12,8},{9,1... | collective-permute-start | bytes 2359304 | tf_op jit(solution)/shard_map/ppermute | solution.py:409
  809.6 112.3 %collective-permute-start.72 = (bf16[4,2,2,64,768]{4,3,0,2,1:T(8,128)(2,1)}, bf16[4,2,2,64,768]{4,3,0,2,1:T(8,128)(2,1)}, u32[]{:S(2)}, u32[]{:S(2)}) collective-permute-start(bf16[4,2,2,64,768]{4,3,0,2,1:T(8,128)(2,1)} %bitcast.561), channel_id=1, source_target_pairs={{0,2},{2,0},{1,3},{3,1},{4,6},{6,4},{5,7},{7,5},{8,10},{10,8},{9,1... | collective-permute-start | bytes 4718600 | tf_op jit(solution)/shard_map/ppermute | solution.py:409
  853.7 22.0 %collective-permute-start.63 = (bf16[2,256,768]{2,1,0:T(8,128)(2,1)}, bf16[2,256,768]{2,1,0:T(8,128)(2,1)S(1)}, u32[]{:S(2)}, u32[]{:S(2)}) collective-permute-start(bf16[2,256,768]{2,1,0:T(8,128)(2,1)} %get-tuple-element.142), channel_id=1, source_target_pairs={{0,2},{2,0},{1,3},{3,1},{4,6},{6,4},{5,7},{7,5},{8,10},{10,8},{9,1... | collective-permute-start | bytes 2359304 | tf_op jit(solution)/shard_map/ppermute | solution.py:409
  873.8 68.1 %collective-permute-start.70 = (bf16[4,2,2,24,3456]{4,3,0,1,2:T(8,128)(2,1)}, bf16[4,2,2,24,3456]{4,3,0,1,2:T(8,128)(2,1)}, u32[]{:S(2)}, u32[]{:S(2)}) collective-permute-start(bf16[4,2,2,24,3456]{4,3,0,1,2:T(8,128)(2,1)} %bitcast.560), channel_id=1, source_target_pairs={{0,2},{2,0},{1,3},{3,1},{4,6},{6,4},{5,7},{7,5},{8,10},{10,8},{9,1... | collective-permute-start | bytes 7962632 | tf_op jit(solution)/shard_map/ppermute | solution.py:409
  975.4 77.5 %collective-permute-start.77 = (bf16[4,2,64,768]{3,2,0,1:T(8,128)(2,1)}, bf16[4,2,64,768]{3,2,0,1:T(8,128)(2,1)}, u32[]{:S(2)}, u32[]{:S(2)}) collective-permute-start(bf16[4,2,64,768]{3,2,0,1:T(8,128)(2,1)} %dynamic-slice_bitcast_fusion.6), channel_id=1, source_target_pairs={{0,4},{4,0},{1,5},{5,1},{2,6},{6,2},{3,7},{7,3},{8,12},{12,8},{9,1... | collective-permute-start | bytes 2359304 | tf_op jit(solution)/shard_map/ppermute | solution.py:409
  977.7 73.2 %collective-permute-start.76 = (bf16[4,2,24,1408]{3,2,1,0:T(8,128)(2,1)}, bf16[4,2,24,1408]{3,2,1,0:T(8,128)(2,1)}, u32[]{:S(2)}, u32[]{:S(2)}) collective-permute-start(bf16[4,2,24,1408]{3,2,1,0:T(8,128)(2,1)} %copy_bitcast_fusion.15), channel_id=1, source_target_pairs={{0,4},{4,0},{1,5},{5,1},{2,6},{6,2},{3,7},{7,3},{8,12},{12,8},{9,1... | collective-permute-start | bytes 1622024 | tf_op jit(solution)/shard_map/ppermute | solution.py:409
  979.5 75.6 %collective-permute-start.75 = (bf16[4,2,24,3456]{3,2,0,1:T(8,128)(2,1)}, bf16[4,2,24,3456]{3,2,0,1:T(8,128)(2,1)}, u32[]{:S(2)}, u32[]{:S(2)}) collective-permute-start(bf16[4,2,24,3456]{3,2,0,1:T(8,128)(2,1)} %dynamic-slice_bitcast_fusion), channel_id=1, source_target_pairs={{0,1},{1,0},{2,3},{3,2},{4,5},{5,4},{6,7},{7,6},{8,9},{9,8},{10,11... | collective-permute-start | bytes 3981320 | tf_op jit(solution)/shard_map/ppermute | solution.py:409
  980.2 63.2 %collective-permute-start.103 = (bf16[64,768]{1,0:T(8,128)(2,1)S(1)}, bf16[64,768]{1,0:T(8,128)(2,1)S(1)}, u32[]{:S(2)}, u32[]{:S(2)}) collective-permute-start(bf16[64,768]{1,0:T(8,128)(2,1)S(1)} %get-tuple-element.497), channel_id=1, source_target_pairs={{0,8},{8,16},{16,24},{24,0},{1,9},{9,17},{17,25},{25,1},{2,10},{10... | collective-permute-start | bytes 294920 | tf_op jit(solution)/shard_map/ppermute | solution.py:450
  982.4 64.8 %collective-permute-start.104 = (bf16[64,768]{1,0:T(8,128)(2,1)}, bf16[64,768]{1,0:T(8,128)(2,1)}, u32[]{:S(2)}, u32[]{:S(2)}) collective-permute-start(bf16[64,768]{1,0:T(8,128)(2,1)} %get-tuple-element.499), channel_id=1, source_target_pairs={{0,16},{8,24},{16,0},{24,8},{1,17},{9,25},{17,1},{25,9},{2,18},{10... | collective-permute-start | bytes 294920 | tf_op jit(solution)/shard_map/ppermute | solution.py:450
  1064.8 25.5 %collective-permute-start.78 = (bf16[512,768]{1,0:T(8,128)(2,1)S(1)}, bf16[512,768]{1,0:T(8,128)(2,1)}, u32[]{:S(2)}, u32[]{:S(2)}) collective-permute-start(bf16[512,768]{1,0:T(8,128)(2,1)S(1)} %fusion.54.refs_1_), channel_id=1, source_target_pairs={{0,8},{8,16},{16,24},{1,9},{9,17},{17,25},{2,10},{10,18},{18,26},{... | collective-permute-start | bytes 2359304 | tf_op jit(solution)/shard_map/ppermute | solution.py:463
  1068.3 27.4 %collective-permute-start.79 = (bf16[512,768]{1,0:T(8,128)(2,1)S(1)}, bf16[512,768]{1,0:T(8,128)(2,1)}, u32[]{:S(2)}, u32[]{:S(2)}) collective-permute-start(bf16[512,768]{1,0:T(8,128)(2,1)S(1)} %fusion.54.refs_1_), channel_id=1, source_target_pairs={{8,0},{16,8},{24,16},{9,1},{17,9},{25,17},{10,2},{18,10},{26,18},{... | collective-permute-start | bytes 2359304 | tf_op jit(solution)/shard_map/ppermute | solution.py:464
  1075.5 43.2 %collective-permute-start.88 = (bf16[4,2,2,24,1280]{4,3,2,1,0:T(8,128)(2,1)}, bf16[4,2,2,24,1280]{4,3,2,1,0:T(8,128)(2,1)}, u32[]{:S(2)}, u32[]{:S(2)}) collective-permute-start(bf16[4,2,2,24,1280]{4,3,2,1,0:T(8,128)(2,1)} %get-tuple-element.464), channel_id=1, source_target_pairs={{0,2},{2,0},{1,3},{3,1},{4,6},{6,4},{5,7},{7,5},{8,10},{10,8},{9,1... | collective-permute-start | bytes 2949128 | tf_op jit(solution)/shard_map/ppermute | solution.py:409
  1163.0 93.0 %collective-permute-start.89 = (bf16[4032,768]{1,0:T(8,128)(2,1)}, bf16[4032,768]{1,0:T(8,128)(2,1)}, u32[]{:S(2)}, u32[]{:S(2)}) collective-permute-start(bf16[4032,768]{1,0:T(8,128)(2,1)} %shard_map.473), channel_id=1, source_target_pairs={{0,2},{2,0},{1,3},{3,1},{4,6},{6,4},{5,7},{7,5},{8,10},{10,8},{9,1... | collective-permute-start | bytes 18579464 | tf_op jit(solution)/shard_map/ppermute | solution.py:409
  1260.6 26.1 %collective-permute-start.90 = (bf16[504,768]{1,0:T(8,128)(2,1)}, bf16[504,768]{1,0:T(8,128)(2,1)}, u32[]{:S(2)}, u32[]{:S(2)}) collective-permute-start(bf16[504,768]{1,0:T(8,128)(2,1)} %get-tuple-element.434), channel_id=1, source_target_pairs={{0,4},{4,0},{1,5},{5,1},{2,6},{6,2},{3,7},{7,3},{8,12},{12,8},{9,1... | collective-permute-start | bytes 2322440 | tf_op jit(solution)/shard_map/ppermute | solution.py:409
  1261.2 25.5 %collective-permute-start.92 = (bf16[504,768]{1,0:T(8,128)(2,1)}, bf16[504,768]{1,0:T(8,128)(2,1)}, u32[]{:S(2)}, u32[]{:S(2)}) collective-permute-start(bf16[504,768]{1,0:T(8,128)(2,1)} %get-tuple-element.433), channel_id=1, source_target_pairs={{0,1},{1,0},{2,3},{3,2},{4,5},{5,4},{6,7},{7,6},{8,9},{9,8},{10,11... | collective-permute-start | bytes 2322440 | tf_op jit(solution)/shard_map/ppermute | solution.py:409
  1265.4 30.2 %collective-permute-start.108 = (bf16[24,1152]{1,0:T(8,128)(2,1)S(1)}, bf16[24,1152]{1,0:T(8,128)(2,1)S(1)}, u32[]{:S(2)}, u32[]{:S(2)}) collective-permute-start(bf16[24,1152]{1,0:T(8,128)(2,1)S(1)} %get-tuple-element.520), channel_id=1, source_target_pairs={{0,8},{8,16},{16,24},{24,0},{1,9},{9,17},{17,25},{25,1},{2,10},{10... | collective-permute-start | bytes 165896 | tf_op jit(solution)/shard_map/ppermute | solution.py:450
  1266.1 31.4 %collective-permute-start.109 = (bf16[24,1152]{1,0:T(8,128)(2,1)S(1)}, bf16[24,1152]{1,0:T(8,128)(2,1)S(1)}, u32[]{:S(2)}, u32[]{:S(2)}) collective-permute-start(bf16[24,1152]{1,0:T(8,128)(2,1)S(1)} %get-tuple-element.522), channel_id=1, source_target_pairs={{0,16},{8,24},{16,0},{24,8},{1,17},{9,25},{17,1},{25,9},{2,18},{10... | collective-permute-start | bytes 165896 | tf_op jit(solution)/shard_map/ppermute | solution.py:450
  1290.8 33.5 %collective-permute-start.91 = (bf16[1008,768]{1,0:T(8,128)(2,1)}, bf16[1008,768]{1,0:T(8,128)(2,1)}, u32[]{:S(2)}, u32[]{:S(2)}) collective-permute-start(bf16[1008,768]{1,0:T(8,128)(2,1)} %pad_maximum_fusion.3), channel_id=1, source_target_pairs={{0,1},{1,0},{2,3},{3,2},{4,5},{5,4},{6,7},{7,6},{8,9},{9,8},{10,11... | collective-permute-start | bytes 4644872 | tf_op jit(solution)/shard_map/ppermute | solution.py:409
  1293.8 33.3 %collective-permute-start.93 = (bf16[1008,768]{1,0:T(8,128)(2,1)}, bf16[1008,768]{1,0:T(8,128)(2,1)}, u32[]{:S(2)}, u32[]{:S(2)}) collective-permute-start(bf16[1008,768]{1,0:T(8,128)(2,1)} %pad_maximum_fusion.4), channel_id=1, source_target_pairs={{0,4},{4,0},{1,5},{5,1},{2,6},{6,2},{3,7},{7,3},{8,12},{12,8},{9,1... | collective-permute-start | bytes 4644872 | tf_op jit(solution)/shard_map/ppermute | solution.py:409
  (297 other events, 3620.6 us)
Sparse Core Ops, SparseCore 0:
  20.1 122.6 all-gather.4
  146.2 102.3 all-gather.6
  343.2 80.9 all-gather.8
  443.3 95.6 all-gather.10
  783.0 116.7 reduce-scatter.4
  950.7 140.4 reduce-scatter.6

commit v6 on v5

--- a/solution.py
+++ b/solution.py
@@ -372,7 +372,11 @@
         out_specs=pl.BlockSpec((rows, D), lambda i: (i, 0)),
         out_shape=jax.ShapeDtypeStruct((parts * rows, D), bf16),
         compiler_params=pltpu.CompilerParams(vmem_limit_bytes=VMEM_LIMIT),
-        cost_estimate=pl.CostEstimate(flops=1, bytes_accessed=rows, transcendentals=0),
+        cost_estimate=pl.CostEstimate(
+            flops=2 * sum(grads.shape[0] for _, grads in pairs) * parts * rows * D,
+            bytes_accessed=2 * parts * rows * D,
+            transcendentals=0,
+        ),
     )(*args)
 
 
@@ -456,16 +460,19 @@
     return scatter_last(scatter_second(scatter_first(value, seq_first), seq_first))
 
 
-def line_gather(value, axis):
+def line_gather(value, axis, before=None):
     size = lax.axis_size(axis)
     ups, downs = [value], [value]
-    for _ in range(1, size):
+    for step in range(1, size):
+        if step == 2 and before is not None:
+            ups[1], downs[1], before = lax.optimization_barrier((ups[1], downs[1], before))
         ups.append(lax.ppermute(ups[-1], axis, [(i, i + 1) for i in range(size - 1)]))
         downs.append(lax.ppermute(downs[-1], axis, [(i + 1, i) for i in range(size - 1)]))
-    return [value] + [ups[k] + downs[size - k] for k in range(1, size)]
-
-
-def line_scatter(parts, axis):
+    got = [value] + [ups[k] + downs[size - k] for k in range(1, size)]
+    return got if before is None else (got, before)
+
+
+def line_scatter(parts, axis, beside=None):
     size = lax.axis_size(axis)
     up, down = None, None
     for step in range(1, size):
@@ -475,14 +482,22 @@
             send_up, send_down = send_up + up, send_down + down
         up = lax.ppermute(send_up, axis, [(i, i + 1) for i in range(step)])
         down = lax.ppermute(send_down, axis, [(size - 1 - i, size - 2 - i) for i in range(step)])
+        if beside is not None:
+            up, down = beside(step, up, down)
     return parts[0].astype(f32) + up.astype(f32) + down.astype(f32)
 
 
-def plane_gather(table):
+def plane_near(table):
     if lax.axis_size("p") != 2:
-        return lax.all_gather(table, PLANE, axis=0, tiled=True)
+        return (lax.all_gather(table, PLANE, axis=0, tiled=True),)
+    return (swap(table, "seq"), swap(table, "p"))
+
+
+def plane_gather(table, near):
+    if len(near) == 1:
+        return near[0]
+    by_seq, by_p = near
     half = table.shape[0] // 2
-    by_seq, by_p = swap(table, "seq"), swap(table, "p")
     far = [swap(by_p[:half], "seq"), swap(by_seq[half:], "p")]
     mine = [table, by_seq, by_p] + far
     return jnp.concatenate(mine + [swap_core(item) for item in mine])
@@ -495,24 +510,24 @@
     return ((other >> 1) & 1) * 4 + (other >> 2) * 2 + (other & 1)
 
 
-def plane_scatter(pairs, rows, before, after):
-    pairs, before = lax.optimization_barrier((pairs, before))
+def plane_scatter(pairs, rows, after):
     count = lax.axis_size(PLANE)
     if lax.axis_size("p") != 2:
         placed = place_rows(pairs, 0, count, rows)
         placed = lax.psum_scatter(placed, PLANE, scatter_dimension=0, tiled=True)
-        return placed.astype(f32), before, after
+        return placed.astype(f32), after
     away = swap_core(place_rows(pairs, 4, 4, rows))
-    home, after = lax.optimization_barrier((place_rows(pairs, 0, 4, rows), after))
+    home = place_rows(pairs, 0, 4, rows)
     half = rows // 2
     part = lambda first, last: add16(home[first:last], away[first:last])
     got_low = swap(part(3 * rows, 3 * rows + half), "seq")
     got_high = swap(part(3 * rows + half, 4 * rows), "p")
+    got_low, got_high, after = lax.optimization_barrier((got_low, got_high, after))
     seq_high = add16(part(rows + half, 2 * rows), got_high)
     p_low = add16(part(2 * rows, 2 * rows + half), got_low)
     from_seq = swap(jnp.concatenate([part(rows, rows + half), seq_high]), "seq")
     from_p = swap(jnp.concatenate([p_low, part(2 * rows + half, 3 * rows)]), "p")
-    return part(0, rows).astype(f32) + from_seq.astype(f32) + from_p.astype(f32), before, after
+    return part(0, rows).astype(f32) + from_seq.astype(f32) + from_p.astype(f32), after
 
 
 def add_logs(left, right):
@@ -611,7 +626,6 @@
         [attn_in[1], attn_in[2], attn_out[1], attn_out[2]], axis=1
     ).astype(bf16)
     ffn_cast = jnp.concatenate([ffn_in[1].astype(bf16), flat_out[1]], axis=1)
-    plane_table = plane_gather(table_b)
     flat = jnp.concatenate(
         [
             enc_ids[0],
@@ -664,18 +678,31 @@
         places.append(
             jnp.where(inside, plane_slot(rel_id // shard) * padded + rel_id % shard, shard)
         )
-    dec_cast, enc_pack, plane_table, places = lax.optimization_barrier(
-        (dec_cast, enc_pack, plane_table, places)
-    )
+
+    def look(table):
+        return jnp.take(table, jnp.concatenate(places), axis=0, mode="clip")
+
+    def beside(step, up, down):
+        if step == 1:
+            up, down, held[0] = lax.optimization_barrier((up, down, plane_gather(high, far)))
+        elif step == 2:
+            up, down, held[0] = lax.optimization_barrier((up, down, look(held[0])))
+        return up, down
+
+    cut_line = lambda got: jnp.split(got, len(places))
+    low, high = table_b[:, : D // 2], table_b[:, D // 2 :]
+    near = plane_near(low)
+    near, high, places = lax.optimization_barrier((near, high, places))
+    far = plane_near(high)
+    got, far = lax.optimization_barrier((look(plane_gather(low, near)), far))
+    held = [None]
+    looked_low = line_scatter(cut_line(got), "z", beside)
+    looked_high = line_scatter(cut_line(held[0]), "z")
+    dec_cast, enc_pack, looked_low = lax.optimization_barrier((dec_cast, enc_pack, looked_low))
     dec_pack = lax.all_gather(dec_cast, ALL, axis=0, tiled=True)
+    looked = jnp.concatenate([looked_low, looked_high], axis=1)
     enc_places = [item[:enc_count] for item in places]
     dec_places = [item[enc_count:] for item in places]
-
-    def look(items):
-        got = jnp.take(plane_table, jnp.concatenate(items), axis=0, mode="clip")
-        return line_scatter(jnp.split(got, len(items)), "z")
-
-    looked = look(places)
     enc_x0, dec_y0 = looked[:enc_count], looked[enc_count:]
 
     cut = lambda pack, start, width: lax.slice_in_dim(pack, start, start + width, axis=1)
@@ -822,6 +849,7 @@
     late, dec_lines, enc_sums, g_dec_fo, d_enc_ob = lax.optimization_barrier(
         (d_dec_rest, dec_lines, enc_sums, g_dec_fo, d_enc_ob)
     )
+    g_dec_fo = scatter_last(g_dec_fo)
     late = lax.psum_scatter(late, ALL, scatter_dimension=0, tiled=True)
     early = early.astype(f32)
     enc_sums = [scatter_first(item, number == 0) for number, item in enumerate(enc_sums)]
@@ -835,16 +863,6 @@
     d_x0_norm, d_gain_eatt = norm_pull(enc_x0, gain[0], 1.0, input_grad(d_enc_qkv, enc_wi))
     d_x0 = d_x1 + d_x0_norm
 
-    d_x0, enc_sums = lax.optimization_barrier((d_x0.astype(bf16), enc_sums))
-    enc_sums = [scatter_second(item, number == 0) for number, item in enumerate(enc_sums)]
-    enc_lines = line_gather(d_x0, "z")
-    enc_lines, enc_sums = lax.optimization_barrier((enc_lines, enc_sums))
-    g_low, g_high, g_fo, g_dec_fo = [scatter_last(item) for item in (*enc_sums, g_dec_fo)]
-    far_place = lambda item: jnp.where(item == shard, -1, item)[None, :]
-    pairs = [
-        (far_place(item), grads)
-        for item, grads in zip(enc_places + dec_places, enc_lines + dec_lines)
-    ]
     d_gains = jnp.stack(
         [
             d_gain_eatt,
@@ -860,12 +878,23 @@
     d_rel = jnp.transpose(d_rel.reshape(2, -1, rel_table.shape[1]), (1, 0, 2)).reshape(D, 1)
     d_misc = jnp.pad(jnp.concatenate([d_gains.T, d_rel], axis=1), ((0, 0), (0, 120)))
     d_last = jnp.concatenate([d_enc_wi.astype(bf16), d_misc.astype(bf16)], axis=1)
+    d_x0, enc_sums = lax.optimization_barrier((d_x0.astype(bf16), enc_sums))
+    enc_sums = [scatter_second(item, number == 0) for number, item in enumerate(enc_sums)]
     last = [scatter_core(d_last[:, :1152]), scatter_core(d_last[:, 1152:])]
-    input_embed, late, last = plane_scatter(pairs, padded, late, last)
+    last = [scatter_first(item, number == 0) for number, item in enumerate(last)]
+    last = [scatter_second(item, number == 0) for number, item in enumerate(last)]
+    enc_lines, late = line_gather(d_x0, "z", late)
+    enc_lines, enc_sums, last = lax.optimization_barrier((enc_lines, enc_sums, last))
+    far_place = lambda item: jnp.where(item == shard, -1, item)[None, :]
+    pairs = [
+        (far_place(item), grads)
+        for item, grads in zip(enc_places + dec_places, enc_lines + dec_lines)
+    ]
+    input_embed, (enc_sums, last) = plane_scatter(pairs, padded, (enc_sums, last))
     late = late.astype(f32)
     grad_embed = head_embed[:shard] + input_embed[:shard]
-
-    last = [scatter_rest(item, number == 0) for number, item in enumerate(last)]
+    g_low, g_high, g_fo = [scatter_last(item) for item in enc_sums]
+    last = [scatter_last(item) for item in last]
     squares = sum(
         (jnp.sum(item * item) for item in (grad_embed, early, late, g_low, g_high, g_fo, g_dec_fo, *last))
     )

time: 1400 us -> 1440 us (1.029)
  starting transfers between devices: 169 us -> 217 us
  waiting for transfers between devices: 416 us -> 375 us
  local copies, waits for them, and re-layouts: 205 us -> 237 us
    ppermute x50 -> x59, waiting for transfers between devices: 106 us -> 140 us  [swap(): return lax.ppermute(value, axis, [(0, 1), (1, 0)])]
    all_gather x1, waiting for transfers between devices: 29.8 us -> 0.02 us  [body(): lax.all_gather(jnp.concatenate([enc_cast, flat_out[0]], axis=1), ALL, axi...]
    ppermute x3 -> x6, waiting for transfers between devices: 95.5 us -> 70.6 us  [line_scatter(): up = lax.ppermute(send_up, axis, [(i, i + 1) for i in range(step)])]
    ppermute x3 -> x6, starting transfers between devices: 11.4 us -> 29.6 us  [line_scatter(): up = lax.ppermute(send_up, axis, [(i, i + 1) for i in range(step)])]
    ppermute x30, waiting for transfers between devices: 52.4 us -> 35.4 us  [scatter_last(): got = lax.ppermute(send, 'z', [(i, (i + hop) % size) for i in range(size)])]
    unnamed x463 -> x461, local copies, waits for them, and re-layouts: 53.8 us -> 70.5 us
    ppermute x30, starting transfers between devices: 39 us -> 54.9 us  [scatter_last(): got = lax.ppermute(send, 'z', [(i, (i + hop) % size) for i in range(size)])]
    gather x1 -> x2, local copies, waits for them, and re-layouts: 20.7 us -> 30.7 us  [look(): return jnp.take(table, jnp.concatenate(places), axis=0, mode='clip')]
  transfers between devices with their start and end apart: 127 -> 142, of which waited for: 56 -> 66; matrix products, arithmetic and copies ran while one was open for 27% -> 28% of each run, Pallas kernels for 14% -> 13%
where the time goes in v6:
time: 1440 us; the launch traced here: 1430 us
  waiting for transfers between devices  375 us (26%)
  Pallas kernels  294 us (20%)
  local copies, waits for them, and re-layouts  237 us (16%)
  starting transfers between devices  217 us (15%)
  other arithmetic  150 us (10%)
  matrix products  123 us (9%)
  between operations  31.6 us (2%)
    ppermute x59, waiting for transfers between devices, swap(): return lax.ppermute(value, axis, [(0, 1), (1, 0)])  140 us
    pallas_call x3, Pallas kernels, attend_backward(): pl.pallas_call(functools.partial(attend_backward_kernel, cfg), grid=(HEAD...  102 us
    all_gather x1, waiting for transfers between devices, body(): hidden_all = lax.all_gather(hidden_b, ALL, axis=0, tiled=True)  71.3 us
    ppermute x6, waiting for transfers between devices, line_scatter(): up = lax.ppermute(send_up, axis, [(i, i + 1) for i in range(step)])  70.6 us
    unnamed x461, local copies, waits for them, and re-layouts  70.5 us
    pallas_call x4, Pallas kernels, head_grad(): pl.pallas_call(functools.partial(head_grad_kernel, count), grid_spec=pltp...  63.4 us
    pallas_call x3, Pallas kernels, attend_forward(): pl.pallas_call(functools.partial(attend_forward_kernel, cfg), grid=(HEADS...  55 us
    ppermute x30, starting transfers between devices, scatter_last(): got = lax.ppermute(send, 'z', [(i, (i + hop) % size) for i in range(size)])  54.9 us
  transfers between devices with their start and end apart: 142, of which 66 were waited for; matrix products, arithmetic and copies ran while one was open for 28% of the time, Pallas kernels for 13%

profile of v6, /device:TPU:0, one launch (start us, length us, event | category | flops | bytes accessed | tf_op | source)
XLA Modules:
  0.0 1428.3 jit_solution(5147241190375492707)
XLA Ops:
  19.8 5.6 collective-permute-start.3
  61.8 8.2 collective-permute-done.9
  79.7 14.4 %gather_fusion = bf16[3072,384]{1,0:T(8,128)(2,1)S(1)} fusion(bf16[8064,384]{1,0:T(8,128)(2,1)} %constant_dynamic-update-slice_fusion.4, s32[3072]{0:T(1024)S(1)} %broadcast_clamp_fusion), kind=kCustom, calls=%fused_computation | custom fusion | bytes 4730880 | tf_op jit(solution)/shard_map/jit(_take)/gather | solution.py:683
  110.5 11.2 collective-permute-done.20
  133.7 15.7 %collective-permute-done.18 = bf16[768,384]{1,0:T(8,128)(2,1)S(1)} collective-permute-done((bf16[768,384]{1,0:T(8,128)(2,1)S(1)}, bf16[768,384]{1,0:T(8,128)(2,1)S(1)}, u32[]{:S(2)}, u32[]{:S(2)}) %collective-permute-start.18) | collective-permute-done | bytes 589856 | tf_op jit(solution)/shard_map/ppermute | solution.py:483
  157.2 16.4 %gather_fusion.1 = bf16[3072,384]{1,0:T(8,128)(2,1)} fusion(bf16[8064,384]{1,0:T(8,128)(2,1)} %constant_dynamic-update-slice_fusion.15, s32[3072]{0:T(1024)S(1)} %broadcast_clamp_fusion), kind=kCustom, calls=%fused_computation.1 | custom fusion | bytes 4730880 | tf_op jit(solution)/shard_map/jit(_take)/gather | solution.py:683
  181.2 9.2 collective-permute-done.29
  204.7 14.6 %collective-permute-done.31 = bf16[768,384]{1,0:T(8,128)(2,1)S(1)} collective-permute-done((bf16[768,384]{1,0:T(8,128)(2,1)S(1)}, bf16[768,384]{1,0:T(8,128)(2,1)S(1)}, u32[]{:S(2)}, u32[]{:S(2)}) %collective-permute-start.31) | collective-permute-done | bytes 589856 | tf_op jit(solution)/shard_map/ppermute | solution.py:483
  220.4 5.2 collective-permute-start.32
  231.5 14.6 %collective-permute-done.32 = bf16[768,384]{1,0:T(8,128)(2,1)} collective-permute-done((bf16[768,384]{1,0:T(8,128)(2,1)}, bf16[768,384]{1,0:T(8,128)(2,1)}, u32[]{:S(2)}, u32[]{:S(2)}) %collective-permute-start.32) | collective-permute-done | bytes 589856 | tf_op jit(solution)/shard_map/ppermute | solution.py:483
  248.5 9.7 collective-permute-start.33
  261.3 16.4 %collective-permute-done.33 = bf16[768,384]{1,0:T(8,128)(2,1)} collective-permute-done((bf16[768,384]{1,0:T(8,128)(2,1)}, bf16[768,384]{1,0:T(8,128)(2,1)}, u32[]{:S(2)}, u32[]{:S(2)}) %collective-permute-start.33) | collective-permute-done | bytes 589856 | tf_op jit(solution)/shard_map/ppermute | solution.py:483
  277.7 10.1 collective-permute-done.36
  312.5 28.6 %shard_map.461 = bf16[512,768]{1,0:T(8,128)(2,1)} custom-call(bf16[512,768]{1,0:T(8,128)(2,1)} %convolution_convert_fusion.15.refs_0_, bf16[512,1536]{1,0:T(8,128)(2,1)} %copy-done.4, bf16[512,1536]{1,0:T(8,128)(2,1)} %copy-done.4, bf16[512,1536]{1,0:T(8,128)(2,1)} %collective-permute-done.37.refs_3_.refs_4_, ...), custom_call_target="tpu_custom_call" | custom-call | flops 2 | bytes 512 | tf_op jit(solution)/shard_map/pallas_call | solution.py:197
  347.9 7.0 reshape.679
  359.6 6.2 fusion.7
  391.1 13.9 shard_map.462
  411.1 12.4 shard_map.463
  469.0 71.3 %all-gather.11.cloned.1.call-done = bf16[8192,768]{1,0:T(8,128)(2,1)} async-done(((bf16[256,768]{1,0:T(8,128)(2,1)}), bf16[8192,768]{1,0:T(8,128)(2,1)}) %all-gather.11.cloned.1.call-update) | async-done | bytes 12582928 | tf_op jit(solution)/shard_map/all_gather | solution.py:763
  540.3 25.6 %shard_map.464 = (f32[1,8192]{1,0:T(1,128)}, f32[1,8192]{1,0:T(1,128)}) custom-call(bf16[8,2,2,256,768]{4,3,2,1,0:T(8,128)(2,1)} %bitcast.652, bf16[1008,768]{1,0:T(8,128)(2,1)} %pad.52.tab, s32[1,8192]{1,0:T(1,128)} %bitcast.611), custom_call_target="tpu_custom_call" | custom-call | flops 12683575296 | bytes 12582912 | tf_op jit(solution)/shard_map/pallas_call | solution.py:300
  587.8 15.8 %shard_map.465 = (bf16[8,2,64,768]{3,2,1,0:T(8,128)(2,1)}, bf16[8,2,64,768]{3,2,1,0:T(8,128)(2,1)}, f32[1008,768]{1,0:T(8,128)}) custom-call(s32[1]{0:T(128)} %bitcast.75.core, bf16[8,2,2,256,768]{4,3,2,1,0:T(8,128)(2,1)} %bitcast.653, bf16[1008,768]{1,0:T(8,128)(2,1)} %pad.52.tab, s32[1,8192]{1,0:T(1,128)} %bitcast.612, f32[1,8192]{1,0:T(1,128)} %bitcast.590, ...), custom_call_target="tpu_custom_call" | custom-call | flops 9512681472 | bytes 6291456 | tf_op jit(solution)/shard_map/pallas_call | solution.py:323
  603.6 15.8 %shard_map.467 = (bf16[8,2,64,768]{3,2,1,0:T(8,128)(2,1)}, bf16[8,2,64,768]{3,2,1,0:T(8,128)(2,1)}, f32[1008,768]{1,0:T(8,128)}) custom-call(s32[1]{0:T(128)} %bitcast.75.core, bf16[8,2,2,256,768]{4,3,2,1,0:T(8,128)(2,1)} %bitcast.654, bf16[1008,768]{1,0:T(8,128)(2,1)} %pad.52.tab, s32[1,8192]{1,0:T(1,128)} %bitcast.613, f32[1,8192]{1,0:T(1,128)} %bitcast.591, ...), custom_call_target="tpu_custom_call" | custom-call | flops 9512681472 | bytes 6291456 | tf_op jit(solution)/shard_map/pallas_call | solution.py:323
  620.1 15.7 %shard_map.466 = (bf16[8,2,64,768]{3,2,1,0:T(8,128)(2,1)}, bf16[8,2,64,768]{3,2,1,0:T(8,128)(2,1)}, f32[1008,768]{1,0:T(8,128)}) custom-call(s32[1]{0:T(128)} %bitcast.76.core, bf16[8,2,2,256,768]{4,3,2,1,0:T(8,128)(2,1)} %bitcast.655, bf16[1008,768]{1,0:T(8,128)(2,1)} %pad.52.tab, s32[1,8192]{1,0:T(1,128)} %bitcast.614, f32[1,8192]{1,0:T(1,128)} %bitcast.592, ...), custom_call_target="tpu_custom_call" | custom-call | flops 9512681472 | bytes 6291456 | tf_op jit(solution)/shard_map/pallas_call | solution.py:323
  636.4 16.0 %shard_map.468 = (bf16[8,2,64,768]{3,2,1,0:T(8,128)(2,1)}, bf16[8,2,64,768]{3,2,1,0:T(8,128)(2,1)}, f32[1008,768]{1,0:T(8,128)}) custom-call(s32[1]{0:T(128)} %bitcast.76.core, bf16[8,2,2,256,768]{4,3,2,1,0:T(8,128)(2,1)} %bitcast.656, bf16[1008,768]{1,0:T(8,128)(2,1)} %pad.52.tab, s32[1,8192]{1,0:T(1,128)} %bitcast.615, f32[1,8192]{1,0:T(1,128)} %bitcast.593, ...), custom_call_target="tpu_custom_call" | custom-call | flops 9512681472 | bytes 6291456 | tf_op jit(solution)/shard_map/pallas_call | solution.py:323
  661.6 13.3 collective-permute-done.52
  678.6 13.2 collective-permute-done.64
  695.4 7.0 collective-permute-done.53
  746.1 6.8 multiply_reduce_fusion.12
  756.6 22.0 %shard_map.469 = (bf16[256,768]{1,0:T(8,128)(2,1)}, f32[2,512,768]{2,1,0:T(8,128)}, bf16[2,512,768]{2,1,0:T(8,128)(2,1)}) custom-call(bf16[256,768]{1,0:T(8,128)(2,1)} %convolution_convert_fusion.18.refs_0_, bf16[512,1536]{1,0:T(8,128)(2,1)} %copy-done.2, bf16[512,1536]{1,0:T(8,128)(2,1)} %copy-done.2, bf16[512,1536]{1,0:T(8,128)(2,1)} %copy-done.3, ...), custom_call_target="tpu_custom_call" | custom-call | flops 5 | bytes 256 | tf_op jit(solution)/shard_map/pallas_call | solution.py:221
  813.6 25.1 %shard_map.470 = (bf16[256,768]{1,0:T(8,128)(2,1)}, f32[2,256,768]{2,1,0:T(8,128)}, bf16[2,256,768]{2,1,0:T(8,128)(2,1)}, f32[12,2,8,512]{3,2,1,0:T(8,128)}) custom-call(bf16[256,768]{1,0:T(8,128)(2,1)} %convolution_convert_fusion.19.refs_0_, bf16[256,1536]{1,0:T(8,128)(2,1)} %convolution_convert_fusion.9.refs_1_.refs_2_, ...), custom_call_target="tpu_custom_call" | custom-call | flops 5 | bytes 256 | tf_op jit(solution)/shard_map/pallas_call | solution.py:221
  838.8 8.7 fusion.65
  847.6 7.1 convolution_convert_fusion
  859.2 9.6 multiply_reduce_fusion.3
  959.4 55.1 %shard_map.471 = (bf16[512,768]{1,0:T(8,128)(2,1)}, f32[2,512,768]{2,1,0:T(8,128)}, bf16[2,512,768]{2,1,0:T(8,128)(2,1)}, f32[12,4,8,768]{3,2,1,0:T(8,128)}) custom-call(bf16[512,768]{1,0:T(8,128)(2,1)} %convolution_convert_fusion.15.refs_0_, bf16[512,1536]{1,0:T(8,128)(2,1)} %copy-done.4, bf16[512,1536]{1,0:T(8,128)(2,1)} %copy-done.4, ...), custom_call_target="tpu_custom_call" | custom-call | flops 5 | bytes 512 | tf_op jit(solution)/shard_map/pallas_call | solution.py:221
  1024.4 9.0 collective-permute-done.91
  1035.6 21.3 %collective-permute-done.92 = bf16[4,2,64,768]{3,2,0,1:T(8,128)(2,1)} collective-permute-done((bf16[4,2,64,768]{3,2,0,1:T(8,128)(2,1)}, bf16[4,2,64,768]{3,2,0,1:T(8,128)(2,1)}, u32[]{:S(2)}, u32[]{:S(2)}) %collective-permute-start.92) | collective-permute-done | bytes 786464 | tf_op jit(solution)/shard_map/ppermute | solution.py:413
  1087.3 5.3 copy.745
  1092.7 10.6 collective-permute-done.100
  1107.6 12.5 collective-permute-done.99
  1127.8 5.4 fusion
  1142.1 9.7 collective-permute-done.106
  1172.4 5.3 collective-permute-start.98
  1196.0 23.9 %shard_map.473 = bf16[4032,768]{1,0:T(8,128)(2,1)} custom-call(s32[1,512]{1,0:T(1,128)} %bitcast.638, bf16[512,768]{1,0:T(8,128)(2,1)} %fusion.54.refs_1_, s32[1,512]{1,0:T(1,128)} %bitcast.636, bf16[512,768]{1,0:T(8,128)(2,1)} %add.1367.refs_3_, s32[1,512]{1,0:T(1,128)} %bitcast.634, bf16[512,768]{1,0:T(8,128)(2,1)} %add.1368.refs_5_, s32[1,512]{1,0:T(1,128)} %bitcast.632, ...), custom_call_target="tpu_custom_call" | custom-call | flops 19025362944 | bytes 6193152 | tf_op jit(solution)/shard_map/pallas_call | solution.py:368
  1245.5 23.7 %shard_map.472 = bf16[4032,768]{1,0:T(8,128)(2,1)} custom-call(s32[1,512]{1,0:T(1,128)} %bitcast.639, bf16[512,768]{1,0:T(8,128)(2,1)} %fusion.54.refs_1_, s32[1,512]{1,0:T(1,128)} %bitcast.637, bf16[512,768]{1,0:T(8,128)(2,1)} %add.1367.refs_3_, s32[1,512]{1,0:T(1,128)} %bitcast.635, bf16[512,768]{1,0:T(8,128)(2,1)} %add.1368.refs_5_, s32[1,512]{1,0:T(1,128)} %bitcast.633, ...), custom_call_target="tpu_custom_call" | custom-call | flops 19025362944 | bytes 6193152 | tf_op jit(solution)/shard_map/pallas_call | solution.py:368
  1312.6 8.3 collective-permute-done.126
  1320.9 7.4 collective-permute-start.116
  1366.5 7.7 multiply_reduce_fusion.1
  1405.7 6.4 add_subtract_fusion
  (1105 shorter events, 692.4 us)
Async XLA Ops:
  7.2 189.7 %all-gather.5.cloned.1.call-start = ((), (), s32[]{:S(2)}) async-start(), calls=%async_computation.2 | async-start | bytes 14800896 | tf_op jit(solution)/shard_map/all_gather | solution.py:622
  12.7 328.4 %all-gather.7.cloned.1.call-start = ((), (), s32[]{:S(2)}) async-start(), calls=%async_computation.3 | async-start | bytes 9732096 | tf_op jit(solution)/shard_map/all_gather | solution.py:702
  26.7 25.1 %collective-permute-start.1 = (bf16[1008,384]{1,0:T(8,128)(2,1)}, bf16[1008,384]{1,0:T(8,128)(2,1)}, u32[]{:S(2)}, u32[]{:S(2)}) collective-permute-start(bf16[1008,384]{1,0:T(8,128)(2,1)} %get-tuple-element.496), channel_id=1, source_target_pairs={{0,1},{1,0},{2,3},{3,2},{4,5},{5,4},{6,7},{7,6},{8,9},{9,8},{10,11... | collective-permute-start | bytes 2322440 | tf_op jit(solution)/shard_map/ppermute | solution.py:413
  30.8 23.4 %collective-permute-start.2 = (bf16[1008,384]{1,0:T(8,128)(2,1)}, bf16[1008,384]{1,0:T(8,128)(2,1)S(1)}, u32[]{:S(2)}, u32[]{:S(2)}) collective-permute-start(bf16[1008,384]{1,0:T(8,128)(2,1)} %get-tuple-element.496), channel_id=1, source_target_pairs={{0,4},{4,0},{1,5},{5,1},{2,6},{6,2},{3,7},{7,3},{8,12},{12,8},{9,1... | collective-permute-start | bytes 2322440 | tf_op jit(solution)/shard_map/ppermute | solution.py:413
  32.3 41.0 %collective-permute-start.11 = (bf16[1008,384]{1,0:T(8,128)(2,1)}, bf16[1008,384]{1,0:T(8,128)(2,1)}, u32[]{:S(2)}, u32[]{:S(2)}) collective-permute-start(bf16[1008,384]{1,0:T(8,128)(2,1)} %get-tuple-element.496), channel_id=1, source_target_pairs={{0,2},{2,0},{1,3},{3,1},{4,6},{6,4},{5,7},{7,5},{8,10},{10,8},{9,1... | collective-permute-start | bytes 2322440 | tf_op jit(solution)/shard_map/ppermute | solution.py:413
  70.0 28.7 %collective-permute-start.16 = (bf16[1008,384]{1,0:T(8,128)(2,1)S(1)}, bf16[1008,384]{1,0:T(8,128)(2,1)}, u32[]{:S(2)}, u32[]{:S(2)}) collective-permute-start(bf16[1008,384]{1,0:T(8,128)(2,1)S(1)} %get-tuple-element.117), channel_id=1, source_target_pairs={{0,1},{1,0},{2,3},{3,2},{4,5},{5,4},{6,7},{7,6},{8,9},{9,8},{10,11... | collective-permute-start | bytes 2322440 | tf_op jit(solution)/shard_map/ppermute | solution.py:413
  70.3 28.9 %collective-permute-start.17 = (bf16[1008,384]{1,0:T(8,128)(2,1)S(1)}, bf16[1008,384]{1,0:T(8,128)(2,1)}, u32[]{:S(2)}, u32[]{:S(2)}) collective-permute-start(bf16[1008,384]{1,0:T(8,128)(2,1)S(1)} %get-tuple-element.117), channel_id=1, source_target_pairs={{0,4},{4,0},{1,5},{5,1},{2,6},{6,2},{3,7},{7,3},{8,12},{12,8},{9,1... | collective-permute-start | bytes 2322440 | tf_op jit(solution)/shard_map/ppermute | solution.py:413
  77.0 50.5 %collective-permute-start.22 = (bf16[1008,384]{1,0:T(8,128)(2,1)S(1)}, bf16[1008,384]{1,0:T(8,128)(2,1)}, u32[]{:S(2)}, u32[]{:S(2)}) collective-permute-start(bf16[1008,384]{1,0:T(8,128)(2,1)S(1)} %get-tuple-element.117), channel_id=1, source_target_pairs={{0,2},{2,0},{1,3},{3,1},{4,6},{6,4},{5,7},{7,5},{8,10},{10,8},{9,1... | collective-permute-start | bytes 2322440 | tf_op jit(solution)/shard_map/ppermute | solution.py:413
  100.2 27.3 %collective-permute-start.23 = (bf16[1008,384]{1,0:T(8,128)(2,1)}, bf16[1008,384]{1,0:T(8,128)(2,1)S(1)}, u32[]{:S(2)}, u32[]{:S(2)}) collective-permute-start(bf16[1008,384]{1,0:T(8,128)(2,1)} %collective-permute-done.16), channel_id=1, source_target_pairs={{0,2},{2,0},{1,3},{3,1},{4,6},{6,4},{5,7},{7,5},{8,10},{10,8},{9,1... | collective-permute-start | bytes 2322440 | tf_op jit(solution)/shard_map/ppermute | solution.py:413
  101.3 29.7 %collective-permute-start.24 = (bf16[1008,384]{1,0:T(8,128)(2,1)}, bf16[1008,384]{1,0:T(8,128)(2,1)S(1)}, u32[]{:S(2)}, u32[]{:S(2)}) collective-permute-start(bf16[1008,384]{1,0:T(8,128)(2,1)} %collective-permute-done.17), channel_id=1, source_target_pairs={{0,2},{2,0},{1,3},{3,1},{4,6},{6,4},{5,7},{7,5},{8,10},{10,8},{9,1... | collective-permute-start | bytes 2322440 | tf_op jit(solution)/shard_map/ppermute | solution.py:413
  103.7 22.3 %collective-permute-start.21 = (bf16[504,384]{1,0:T(8,128)(2,1)S(1)}, bf16[504,384]{1,0:T(8,128)(2,1)S(1)}, u32[]{:S(2)}, u32[]{:S(2)}) collective-permute-start(bf16[504,384]{1,0:T(8,128)(2,1)S(1)} %slice.492), channel_id=1, source_target_pairs={{0,4},{4,0},{1,5},{5,1},{2,6},{6,2},{3,7},{7,3},{8,12},{12,8},{9,1... | collective-permute-start | bytes 1161224 | tf_op jit(solution)/shard_map/ppermute | solution.py:413
  121.7 27.7 %collective-permute-start.18 = (bf16[768,384]{1,0:T(8,128)(2,1)S(1)}, bf16[768,384]{1,0:T(8,128)(2,1)S(1)}, u32[]{:S(2)}, u32[]{:S(2)}) collective-permute-start(bf16[768,384]{1,0:T(8,128)(2,1)S(1)} %get-tuple-element.472), channel_id=1, source_target_pairs={{0,8},{1,9},{2,10},{3,11},{4,12},{5,13},{6,14},{7,15}} | collective-permute-start | bytes 1769480 | tf_op jit(solution)/shard_map/ppermute | solution.py:483
  126.0 23.5 %collective-permute-start.19 = (bf16[768,384]{1,0:T(8,128)(2,1)S(1)}, bf16[768,384]{1,0:T(8,128)(2,1)S(1)}, u32[]{:S(2)}, u32[]{:S(2)}) collective-permute-start(bf16[768,384]{1,0:T(8,128)(2,1)S(1)} %get-tuple-element.471), channel_id=1, source_target_pairs={{24,16},{25,17},{26,18},{27,19},{28,20},{29,21},{30,22},{31,23}} | collective-permute-start | bytes 1769480 | tf_op jit(solution)/shard_map/ppermute | solution.py:484
  150.6 23.0 %collective-permute-start.27 = (bf16[768,384]{1,0:T(8,128)(2,1)}, bf16[768,384]{1,0:T(8,128)(2,1)S(1)}, u32[]{:S(2)}, u32[]{:S(2)}) collective-permute-start(bf16[768,384]{1,0:T(8,128)(2,1)} %get-tuple-element.470), channel_id=1, source_target_pairs={{0,8},{8,16},{1,9},{9,17},{2,10},{10,18},{3,11},{11,19},{4,12},{12... | collective-permute-start | bytes 1769480 | tf_op jit(solution)/shard_map/ppermute | solution.py:483
  197.0 228.6 %all-gather.9.cloned.1.call-start = ((), (), s32[]{:S(2)}) async-start(), calls=%async_computation.4 | async-start | bytes 9732096 | tf_op jit(solution)/shard_map/all_gather | solution.py:738
  220.4 25.7 %collective-permute-start.32 = (bf16[768,384]{1,0:T(8,128)(2,1)}, bf16[768,384]{1,0:T(8,128)(2,1)}, u32[]{:S(2)}, u32[]{:S(2)}) collective-permute-start(bf16[768,384]{1,0:T(8,128)(2,1)} %get-tuple-element.463), channel_id=1, source_target_pairs={{0,8},{8,16},{1,9},{9,17},{2,10},{10,18},{3,11},{11,19},{4,12},{12... | collective-permute-start | bytes 1769480 | tf_op jit(solution)/shard_map/ppermute | solution.py:483
  248.5 29.2 %collective-permute-start.33 = (bf16[768,384]{1,0:T(8,128)(2,1)}, bf16[768,384]{1,0:T(8,128)(2,1)}, u32[]{:S(2)}, u32[]{:S(2)}) collective-permute-start(bf16[768,384]{1,0:T(8,128)(2,1)} %get-tuple-element.461), channel_id=1, source_target_pairs={{0,8},{8,16},{16,24},{1,9},{9,17},{17,25},{2,10},{10,18},{18,26},{... | collective-permute-start | bytes 1769480 | tf_op jit(solution)/shard_map/ppermute | solution.py:483
  258.2 29.6 %collective-permute-start.36 = (bf16[768,384]{1,0:T(8,128)(2,1)}, bf16[768,384]{1,0:T(8,128)(2,1)}, u32[]{:S(2)}, u32[]{:S(2)}) collective-permute-start(bf16[768,384]{1,0:T(8,128)(2,1)} %get-tuple-element.462), channel_id=1, source_target_pairs={{24,16},{16,8},{8,0},{25,17},{17,9},{9,1},{26,18},{18,10},{10,2},{... | collective-permute-start | bytes 1769480 | tf_op jit(solution)/shard_map/ppermute | solution.py:484
  341.1 199.2 %all-gather.11.cloned.1.call-start = ((), (), s32[]{:S(2)}) async-start(), calls=%async_computation.5 | async-start | bytes 12976128 | tf_op jit(solution)/shard_map/all_gather | solution.py:763
  376.3 33.6 %collective-permute-start.39 = (bf16[512,1536]{1,0:T(8,128)(2,1)S(1)}, bf16[512,1536]{1,0:T(8,128)(2,1)S(1)}, u32[]{:S(2)}, u32[]{:S(2)}) collective-permute-start(bf16[512,1536]{1,0:T(8,128)(2,1)S(1)} %convolution_convert_fusion.7.refs_1_.refs_2_), channel_id=1, source_target_pairs={{0,2},{2,0},{1,3},{3,1},{4,6},{6,4},{5,7},{7,5},{8,10},{10,8},{9,1... | collective-permute-start | bytes 4718600 | tf_op jit(solution)/shard_map/ppermute | solution.py:413
  443.5 488.3 %reduce-scatter.5.cloned.1.call-start = ((), (), s32[]{:S(2)}) async-start(), calls=%async_computation.6 | async-start | bytes 6488064 | tf_op jit(solution)/shard_map/reduce_scatter | solution.py:802
  619.5 32.9 %collective-permute-start.51 = (bf16[8,2,64,768]{3,2,1,0:T(8,128)(2,1)}, bf16[8,2,64,768]{3,2,1,0:T(8,128)(2,1)S(1)}, u32[]{:S(2)}, u32[]{:S(2)}) collective-permute-start(bf16[8,2,64,768]{3,2,1,0:T(8,128)(2,1)} %get-tuple-element.140), channel_id=1, source_target_pairs={{0,2},{2,0},{1,3},{3,1},{4,6},{6,4},{5,7},{7,5},{8,10},{10,8},{9,1... | collective-permute-start | bytes 4718600 | tf_op jit(solution)/shard_map/ppermute | solution.py:413
  619.6 36.4 %collective-permute-start.57 = (bf16[8,2,64,768]{3,2,1,0:T(8,128)(2,1)}, bf16[8,2,64,768]{3,2,1,0:T(8,128)(2,1)S(1)}, u32[]{:S(2)}, u32[]{:S(2)}) collective-permute-start(bf16[8,2,64,768]{3,2,1,0:T(8,128)(2,1)} %get-tuple-element.142), channel_id=1, source_target_pairs={{0,2},{2,0},{1,3},{3,1},{4,6},{6,4},{5,7},{7,5},{8,10},{10,8},{9,1... | collective-permute-start | bytes 4718600 | tf_op jit(solution)/shard_map/ppermute | solution.py:413
  635.8 22.1 %collective-permute-start.63 = (bf16[8,2,64,768]{3,2,1,0:T(8,128)(2,1)}, bf16[8,2,64,768]{3,2,1,0:T(8,128)(2,1)S(1)}, u32[]{:S(2)}, u32[]{:S(2)}) collective-permute-start(bf16[8,2,64,768]{3,2,1,0:T(8,128)(2,1)} %get-tuple-element.144), channel_id=1, source_target_pairs={{0,2},{2,0},{1,3},{3,1},{4,6},{6,4},{5,7},{7,5},{8,10},{10,8},{9,1... | collective-permute-start | bytes 4718600 | tf_op jit(solution)/shard_map/ppermute | solution.py:413
  636.0 23.8 %collective-permute-start.69 = (bf16[8,2,64,768]{3,2,1,0:T(8,128)(2,1)}, bf16[8,2,64,768]{3,2,1,0:T(8,128)(2,1)S(1)}, u32[]{:S(2)}, u32[]{:S(2)}) collective-permute-start(bf16[8,2,64,768]{3,2,1,0:T(8,128)(2,1)} %get-tuple-element.146), channel_id=1, source_target_pairs={{0,2},{2,0},{1,3},{3,1},{4,6},{6,4},{5,7},{7,5},{8,10},{10,8},{9,1... | collective-permute-start | bytes 4718600 | tf_op jit(solution)/shard_map/ppermute | solution.py:413
  658.6 33.2 %collective-permute-start.64 = (bf16[4,2,64,768]{3,2,0,1:T(8,128)(2,1)S(1)}, bf16[4,2,64,768]{3,2,0,1:T(8,128)(2,1)S(1)}, u32[]{:S(2)}, u32[]{:S(2)}) collective-permute-start(bf16[4,2,64,768]{3,2,0,1:T(8,128)(2,1)S(1)} %bitcast.583), channel_id=1, source_target_pairs={{0,1},{1,0},{2,3},{3,2},{4,5},{5,4},{6,7},{7,6},{8,9},{9,8},{10,11... | collective-permute-start | bytes 2359304 | tf_op jit(solution)/shard_map/ppermute | solution.py:413
  660.4 33.6 %collective-permute-start.70 = (bf16[4,2,64,768]{3,2,0,1:T(8,128)(2,1)S(1)}, bf16[4,2,64,768]{3,2,0,1:T(8,128)(2,1)S(1)}, u32[]{:S(2)}, u32[]{:S(2)}) collective-permute-start(bf16[4,2,64,768]{3,2,0,1:T(8,128)(2,1)S(1)} %bitcast.584), channel_id=1, source_target_pairs={{0,4},{4,0},{1,5},{5,1},{2,6},{6,2},{3,7},{7,3},{8,12},{12,8},{9,1... | collective-permute-start | bytes 2359304 | tf_op jit(solution)/shard_map/ppermute | solution.py:413
  675.2 27.3 %collective-permute-start.53 = (bf16[4,64,768]{2,1,0:T(8,128)(2,1)S(1)}, bf16[4,64,768]{2,1,0:T(8,128)(2,1)S(1)}, u32[]{:S(2)}, u32[]{:S(2)}) collective-permute-start(bf16[4,64,768]{2,1,0:T(8,128)(2,1)S(1)} %dynamic-slice_bitcast_fusion.16), channel_id=1, source_target_pairs={{0,4},{4,0},{1,5},{5,1},{2,6},{6,2},{3,7},{7,3},{8,12},{12,8},{9,1... | collective-permute-start | bytes 1179656 | tf_op jit(solution)/shard_map/ppermute | solution.py:413
  677.4 27.3 %collective-permute-start.59 = (bf16[4,64,768]{2,1,0:T(8,128)(2,1)S(1)}, bf16[4,64,768]{2,1,0:T(8,128)(2,1)S(1)}, u32[]{:S(2)}, u32[]{:S(2)}) collective-permute-start(bf16[4,64,768]{2,1,0:T(8,128)(2,1)S(1)} %dynamic-slice_bitcast_fusion.15), channel_id=1, source_target_pairs={{0,1},{1,0},{2,3},{3,2},{4,5},{5,4},{6,7},{7,6},{8,9},{9,8},{10,11... | collective-permute-start | bytes 1179656 | tf_op jit(solution)/shard_map/ppermute | solution.py:413
  786.2 367.7 %reduce-scatter.7.cloned.1.call-start = ((), (), s32[]{:S(2)}) async-start(), calls=%async_computation.7 | async-start | bytes 9732096
  805.1 115.4 %collective-permute-start.76 = (bf16[4,2,64,768]{3,2,0,1:T(8,128)(2,1)}, bf16[4,2,64,768]{3,2,0,1:T(8,128)(2,1)}, u32[]{:S(2)}, u32[]{:S(2)}) collective-permute-start(bf16[4,2,64,768]{3,2,0,1:T(8,128)(2,1)} %dynamic-slice_bitcast_fusion.7), channel_id=1, source_target_pairs={{0,4},{4,0},{1,5},{5,1},{2,6},{6,2},{3,7},{7,3},{8,12},{12,8},{9,1... | collective-permute-start | bytes 2359304 | tf_op jit(solution)/shard_map/ppermute | solution.py:413
  813.2 111.6 %collective-permute-start.87 = (bf16[4,2,2,64,768]{4,3,0,2,1:T(8,128)(2,1)}, bf16[4,2,2,64,768]{4,3,0,2,1:T(8,128)(2,1)}, u32[]{:S(2)}, u32[]{:S(2)}) collective-permute-start(bf16[4,2,2,64,768]{4,3,0,2,1:T(8,128)(2,1)} %bitcast.561), channel_id=1, source_target_pairs={{0,2},{2,0},{1,3},{3,1},{4,6},{6,4},{5,7},{7,5},{8,10},{10,8},{9,1... | collective-permute-start | bytes 4718600 | tf_op jit(solution)/shard_map/ppermute | solution.py:413
  878.0 66.6 %collective-permute-start.85 = (bf16[4,2,2,24,3456]{4,3,0,1,2:T(8,128)(2,1)}, bf16[4,2,2,24,3456]{4,3,0,1,2:T(8,128)(2,1)}, u32[]{:S(2)}, u32[]{:S(2)}) collective-permute-start(bf16[4,2,2,24,3456]{4,3,0,1,2:T(8,128)(2,1)} %bitcast.560), channel_id=1, source_target_pairs={{0,2},{2,0},{1,3},{3,1},{4,6},{6,4},{5,7},{7,5},{8,10},{10,8},{9,1... | collective-permute-start | bytes 7962632 | tf_op jit(solution)/shard_map/ppermute | solution.py:413
  1014.6 46.6 %collective-permute-start.89 = (bf16[2,512,768]{2,1,0:T(8,128)(2,1)}, bf16[2,512,768]{2,1,0:T(8,128)(2,1)}, u32[]{:S(2)}, u32[]{:S(2)}) collective-permute-start(bf16[2,512,768]{2,1,0:T(8,128)(2,1)} %get-tuple-element.163), channel_id=1, source_target_pairs={{0,2},{2,0},{1,3},{3,1},{4,6},{6,4},{5,7},{7,5},{8,10},{10,8},{9,1... | collective-permute-start | bytes 4718600 | tf_op jit(solution)/shard_map/ppermute | solution.py:413
  1015.8 43.3 %collective-permute-start.90 = (bf16[4,2,24,3456]{3,2,0,1:T(8,128)(2,1)}, bf16[4,2,24,3456]{3,2,0,1:T(8,128)(2,1)}, u32[]{:S(2)}, u32[]{:S(2)}) collective-permute-start(bf16[4,2,24,3456]{3,2,0,1:T(8,128)(2,1)} %dynamic-slice_bitcast_fusion), channel_id=1, source_target_pairs={{0,1},{1,0},{2,3},{3,2},{4,5},{5,4},{6,7},{7,6},{8,9},{9,8},{10,11... | collective-permute-start | bytes 3981320 | tf_op jit(solution)/shard_map/ppermute | solution.py:413
  1019.4 37.5 %collective-permute-start.92 = (bf16[4,2,64,768]{3,2,0,1:T(8,128)(2,1)}, bf16[4,2,64,768]{3,2,0,1:T(8,128)(2,1)}, u32[]{:S(2)}, u32[]{:S(2)}) collective-permute-start(bf16[4,2,64,768]{3,2,0,1:T(8,128)(2,1)} %dynamic-slice_bitcast_fusion.6), channel_id=1, source_target_pairs={{0,4},{4,0},{1,5},{5,1},{2,6},{6,2},{3,7},{7,3},{8,12},{12,8},{9,1... | collective-permute-start | bytes 2359304 | tf_op jit(solution)/shard_map/ppermute | solution.py:413
  1071.3 84.3 %collective-permute-start.93 = (bf16[512,768]{1,0:T(8,128)(2,1)}, bf16[512,768]{1,0:T(8,128)(2,1)}, u32[]{:S(2)}, u32[]{:S(2)}) collective-permute-start(bf16[512,768]{1,0:T(8,128)(2,1)} %fusion.54.refs_1_), channel_id=1, source_target_pairs={{0,8},{8,16},{16,24},{1,9},{9,17},{17,25},{2,10},{10,18},{18,26},{... | collective-permute-start | bytes 2359304 | tf_op jit(solution)/shard_map/ppermute | solution.py:469
  1075.7 79.8 %collective-permute-start.94 = (bf16[512,768]{1,0:T(8,128)(2,1)}, bf16[512,768]{1,0:T(8,128)(2,1)}, u32[]{:S(2)}, u32[]{:S(2)}) collective-permute-start(bf16[512,768]{1,0:T(8,128)(2,1)} %fusion.54.refs_1_), channel_id=1, source_target_pairs={{8,0},{16,8},{24,16},{9,1},{17,9},{25,17},{10,2},{18,10},{26,18},{... | collective-permute-start | bytes 2359304 | tf_op jit(solution)/shard_map/ppermute | solution.py:470
  1082.8 40.2 %collective-permute-start.105 = (bf16[4,2,2,24,1280]{4,3,2,1,0:T(8,128)(2,1)}, bf16[4,2,2,24,1280]{4,3,2,1,0:T(8,128)(2,1)}, u32[]{:S(2)}, u32[]{:S(2)}) collective-permute-start(bf16[4,2,2,24,1280]{4,3,2,1,0:T(8,128)(2,1)} %get-tuple-element.482), channel_id=1, source_target_pairs={{0,2},{2,0},{1,3},{3,1},{4,6},{6,4},{5,7},{7,5},{8,10},{10,8},{9,1... | collective-permute-start | bytes 2949128 | tf_op jit(solution)/shard_map/ppermute | solution.py:413
  1083.6 23.1 %collective-permute-start.101 = (bf16[4,64,768]{2,1,0:T(8,128)(2,1)}, bf16[4,64,768]{2,1,0:T(8,128)(2,1)S(1)}, u32[]{:S(2)}, u32[]{:S(2)}) collective-permute-start(bf16[4,64,768]{2,1,0:T(8,128)(2,1)} %dynamic-slice_bitcast_fusion.11), channel_id=1, source_target_pairs={{0,1},{1,0},{2,3},{3,2},{4,5},{5,4},{6,7},{7,6},{8,9},{9,8},{10,11... | collective-permute-start | bytes 1179656 | tf_op jit(solution)/shard_map/ppermute | solution.py:413
  1141.8 37.2 %collective-permute-start.104 = (bf16[4,24,1152]{2,1,0:T(8,128)(2,1)}, bf16[4,24,1152]{2,1,0:T(8,128)(2,1)S(1)}, u32[]{:S(2)}, u32[]{:S(2)}) collective-permute-start(bf16[4,24,1152]{2,1,0:T(8,128)(2,1)} %dynamic-slice_bitcast_fusion.23), channel_id=1, source_target_pairs={{0,4},{4,0},{1,5},{5,1},{2,6},{6,2},{3,7},{7,3},{8,12},{12,8},{9,1... | collective-permute-start | bytes 663560 | tf_op jit(solution)/shard_map/ppermute | solution.py:413
  1219.9 49.3 %collective-permute-start.108 = (bf16[4032,768]{1,0:T(8,128)(2,1)}, bf16[4032,768]{1,0:T(8,128)(2,1)}, u32[]{:S(2)}, u32[]{:S(2)}) collective-permute-start(bf16[4032,768]{1,0:T(8,128)(2,1)} %shard_map.473), channel_id=1, source_target_pairs={{0,2},{2,0},{1,3},{3,1},{4,6},{6,4},{5,7},{7,5},{8,10},{10,8},{9,1... | collective-permute-start | bytes 18579464 | tf_op jit(solution)/shard_map/ppermute | solution.py:413
  1293.0 39.4 %collective-permute-start.128 = (bf16[24,1280]{0,1:T(8,128)(2,1)S(1)}, bf16[24,1280]{0,1:T(8,128)(2,1)S(1)}, u32[]{:S(2)}, u32[]{:S(2)}) collective-permute-start(bf16[24,1280]{0,1:T(8,128)(2,1)S(1)} %get-tuple-element.498), channel_id=1, source_target_pairs={{0,8},{8,16},{16,24},{24,0},{1,9},{9,17},{17,25},{25,1},{2,10},{10... | collective-permute-start | bytes 184328 | tf_op jit(solution)/shard_map/ppermute | solution.py:454
  1295.9 36.8 %collective-permute-start.129 = (bf16[24,1280]{0,1:T(8,128)(2,1)S(1)}, bf16[24,1280]{0,1:T(8,128)(2,1)S(1)}, u32[]{:S(2)}, u32[]{:S(2)}) collective-permute-start(bf16[24,1280]{0,1:T(8,128)(2,1)S(1)} %get-tuple-element.500), channel_id=1, source_target_pairs={{0,16},{8,24},{16,0},{24,8},{1,17},{9,25},{17,1},{25,9},{2,18},{10... | collective-permute-start | bytes 184328 | tf_op jit(solution)/shard_map/ppermute | solution.py:454
  1297.7 23.2 %collective-permute-start.126 = (bf16[24,1152]{1,0:T(8,128)(2,1)S(1)}, bf16[24,1152]{1,0:T(8,128)(2,1)S(1)}, u32[]{:S(2)}, u32[]{:S(2)}) collective-permute-start(bf16[24,1152]{1,0:T(8,128)(2,1)S(1)} %get-tuple-element.541), channel_id=1, source_target_pairs={{0,16},{8,24},{16,0},{24,8},{1,17},{9,25},{17,1},{25,9},{2,18},{10... | collective-permute-start | bytes 165896 | tf_op jit(solution)/shard_map/ppermute | solution.py:454
  1299.0 29.3 %collective-permute-start.127 = (bf16[24,1152]{1,0:T(8,128)(2,1)S(1)}, bf16[24,1152]{1,0:T(8,128)(2,1)S(1)}, u32[]{:S(2)}, u32[]{:S(2)}) collective-permute-start(bf16[24,1152]{1,0:T(8,128)(2,1)S(1)} %get-tuple-element.540), channel_id=1, source_target_pairs={{0,24},{8,0},{16,8},{24,16},{1,25},{9,1},{17,9},{25,17},{2,26},{10... | collective-permute-start | bytes 165896 | tf_op jit(solution)/shard_map/ppermute | solution.py:454
  1332.7 32.3 %collective-permute-start.111 = (bf16[1008,768]{1,0:T(8,128)(2,1)}, bf16[1008,768]{1,0:T(8,128)(2,1)}, u32[]{:S(2)}, u32[]{:S(2)}) collective-permute-start(bf16[1008,768]{1,0:T(8,128)(2,1)} %pad_maximum_fusion.4), channel_id=1, source_target_pairs={{0,1},{1,0},{2,3},{3,2},{4,5},{5,4},{6,7},{7,6},{8,9},{9,8},{10,11... | collective-permute-start | bytes 4644872 | tf_op jit(solution)/shard_map/ppermute | solution.py:413
  1334.4 32.0 %collective-permute-start.112 = (bf16[1008,768]{1,0:T(8,128)(2,1)}, bf16[1008,768]{1,0:T(8,128)(2,1)}, u32[]{:S(2)}, u32[]{:S(2)}) collective-permute-start(bf16[1008,768]{1,0:T(8,128)(2,1)} %pad_maximum_fusion.5), channel_id=1, source_target_pairs={{0,4},{4,0},{1,5},{5,1},{2,6},{6,2},{3,7},{7,3},{8,12},{12,8},{9,1... | collective-permute-start | bytes 4644872 | tf_op jit(solution)/shard_map/ppermute | solution.py:413
  (304 other events, 3269.5 us)
Sparse Core Ops, SparseCore 0:
  12.8 136.2 all-gather.4
  197.1 92.8 all-gather.6
  341.3 81.9 all-gather.8
  443.6 96.6 all-gather.10
  786.3 116.9 reduce-scatter.4
  955.4 146.5 reduce-scatter.6

commit v7 on v5

--- a/solution.py
+++ b/solution.py
@@ -81,28 +81,22 @@
     return have
 
 
-def probs_of(cfg, refs, block, head):
+def scores_of(cfg, refs, block, head):
     bq, has_bias, causal = cfg
     rows = slice(block * bq, (block + 1) * bq)
     cols = slice(head * HEAD_DIM, (head + 1) * HEAD_DIM)
-    query = refs["q"][rows, cols]
+    query = refs["q"][rows, cols] * jnp.asarray(HEAD_DIM ** (-0.5), bf16)
     scores = []
     for part in range(2):
         keys = refs["k"][part][:, cols]
-        s = dot_nt(query, keys) * HEAD_DIM ** (-0.5)
+        s = dot_nt(query, keys)
         if has_bias:
             s = s + spread(refs["x8"][head, block * 2 + part], bq, keys.shape[0])
         allowed = refs["qseg"][rows, :] == refs["kseg"][part]
         if causal:
             allowed = allowed & (refs["kpos"][part] <= refs["qpos"][rows, :])
         scores.append(jnp.where(allowed, s, masked_out))
-    top = jnp.maximum(
-        jnp.max(scores[0], axis=1, keepdims=True), jnp.max(scores[1], axis=1, keepdims=True)
-    )
-    exps = [jnp.exp(s - top) for s in scores]
-    total = jnp.sum(exps[0], axis=1, keepdims=True) + jnp.sum(exps[1], axis=1, keepdims=True)
-    scale = 1.0 / total
-    return query, [e * scale for e in exps]
+    return query, scores
 
 
 def name_refs(cfg, refs):
@@ -120,39 +114,48 @@
 
 
 def attend_forward_kernel(cfg, *refs):
-    named, (out,) = name_refs(cfg, refs)
+    named, (out, lse) = name_refs(cfg, refs)
     bq = cfg[0]
     for block in range(named["q"].shape[0] // bq):
+        rows = slice(block * bq, (block + 1) * bq)
         for head in range(2):
             cols = slice(head * HEAD_DIM, (head + 1) * HEAD_DIM)
-            _, probs = probs_of(cfg, named, block, head)
-            acc = dot_nn(probs[0].astype(bf16), named["v"][0][:, cols])
-            acc = acc + dot_nn(probs[1].astype(bf16), named["v"][1][:, cols])
-            out[block * bq : (block + 1) * bq, cols] = acc.astype(bf16)
+            _, scores = scores_of(cfg, named, block, head)
+            top = jnp.maximum(
+                jnp.max(scores[0], axis=1, keepdims=True), jnp.max(scores[1], axis=1, keepdims=True)
+            )
+            exps = [jnp.exp(s - top) for s in scores]
+            total = jnp.sum(exps[0] + exps[1], axis=1, keepdims=True)
+            scale = 1.0 / total
+            acc = dot_nn((exps[0] * scale).astype(bf16), named["v"][0][:, cols])
+            acc = acc + dot_nn((exps[1] * scale).astype(bf16), named["v"][1][:, cols])
+            out[rows, cols] = acc.astype(bf16)
+            lse[rows, cols] = jnp.broadcast_to(top + jnp.log(total), (bq, HEAD_DIM))
 
 
 def attend_backward_kernel(cfg, *refs):
     named, rest = name_refs(cfg, refs)
     bq, has_bias, causal = cfg
     if has_bias:
-        grad, dq, own, other, y8 = rest
+        grad, lse, dq, own, other, y8 = rest
     else:
-        grad, dq, own, other = rest
+        grad, lse, dq, own, other = rest
     blocks = named["q"].shape[0] // bq
     for head in range(2):
         cols = slice(head * HEAD_DIM, (head + 1) * HEAD_DIM)
         dk, dv = [None, None], [None, None]
         for block in range(blocks):
             rows = slice(block * bq, (block + 1) * bq)
-            query, probs = probs_of(cfg, named, block, head)
+            query, scores = scores_of(cfg, named, block, head)
+            level = lse[rows, head * HEAD_DIM : head * HEAD_DIM + 1]
+            probs = [jnp.exp(s - level) for s in scores]
             do = grad[rows, cols]
             dp = [dot_nt(do, named["v"][part][:, cols]) for part in range(2)]
-            delta = jnp.sum(probs[0] * dp[0], axis=1, keepdims=True) + jnp.sum(
-                probs[1] * dp[1], axis=1, keepdims=True
-            )
+            delta = jnp.sum(probs[0] * dp[0] + probs[1] * dp[1], axis=1, keepdims=True)
             acc = None
             for part in range(2):
-                ds = (probs[part] * (dp[part] - delta)).astype(bf16)
+                ds_wide = probs[part] * (dp[part] - delta)
+                ds = ds_wide.astype(bf16)
                 term = dot_nn(ds, named["k"][part][:, cols])
                 acc = term if acc is None else acc + term
                 k_term = dot_tn(query, ds)
@@ -160,10 +163,10 @@
                 dk[part] = k_term if dk[part] is None else dk[part] + k_term
                 dv[part] = v_term if dv[part] is None else dv[part] + v_term
                 if has_bias:
-                    y8[head, block * 2 + part] = collect(ds.astype(f32), y8.shape[-1])
+                    y8[head, block * 2 + part] = collect(ds_wide, y8.shape[-1])
             dq[rows, cols] = (acc * HEAD_DIM ** (-0.5)).astype(bf16)
         for part, target in enumerate((own, other)):
-            target[0, :, cols] = (dk[part] * HEAD_DIM ** (-0.5)).T.astype(target.dtype)
+            target[0, :, cols] = dk[part].T.astype(target.dtype)
             target[1, :, cols] = dv[part].T.astype(target.dtype)
 
 
@@ -198,14 +201,17 @@
         functools.partial(attend_forward_kernel, cfg),
         grid=(HEADS // 2,),
         in_specs=attend_specs(q_len, k_len, x8 is not None, x8),
-        out_specs=pl.BlockSpec((q_len, 128), lambda i: (0, i)),
-        out_shape=jax.ShapeDtypeStruct((q_len, D), bf16),
+        out_specs=[pl.BlockSpec((q_len, 128), lambda i: (0, i))] * 2,
+        out_shape=[
+            jax.ShapeDtypeStruct((q_len, D), bf16),
+            jax.ShapeDtypeStruct((q_len, D), f32),
+        ],
         compiler_params=pltpu.CompilerParams(vmem_limit_bytes=VMEM_LIMIT),
         cost_estimate=attend_cost(q_len, k_len, 2),
     )(*attend_args(q, kv_own, kv_other, ids, x8))
 
 
-def attend_backward(grad, q, kv_own, kv_other, ids, x8, causal):
+def attend_backward(grad, lse, q, kv_own, kv_other, ids, x8, causal):
     q_len, k_len = q.shape[0], kv_own.shape[0]
     cfg = (256, x8 is not None, causal)
     kv_spec = pl.BlockSpec((2, k_len, 128), lambda i: (0, 0, i))
@@ -222,12 +228,12 @@
         functools.partial(attend_backward_kernel, cfg),
         grid=(HEADS // 2,),
         in_specs=attend_specs(q_len, k_len, x8 is not None, x8)
-        + [pl.BlockSpec((q_len, 128), lambda i: (0, i))],
+        + [pl.BlockSpec((q_len, 128), lambda i: (0, i))] * 2,
         out_specs=out_specs,
         out_shape=out_shape,
         compiler_params=pltpu.CompilerParams(vmem_limit_bytes=VMEM_LIMIT),
         cost_estimate=attend_cost(q_len, k_len, 5),
-    )(*attend_args(q, kv_own, kv_other, ids, x8), grad)
+    )(*attend_args(q, kv_own, kv_other, ids, x8), grad, lse)
 
 
 def bias_bases(core, q_len, k_len, offset):
@@ -465,7 +471,7 @@
     return [value] + [ups[k] + downs[size - k] for k in range(1, size)]
 
 
-def line_scatter(parts, axis):
+def line_scatter(parts, axis, beside=None):
     size = lax.axis_size(axis)
     up, down = None, None
     for step in range(1, size):
@@ -475,6 +481,8 @@
             send_up, send_down = send_up + up, send_down + down
         up = lax.ppermute(send_up, axis, [(i, i + 1) for i in range(step)])
         down = lax.ppermute(send_down, axis, [(size - 1 - i, size - 2 - i) for i in range(step)])
+        if beside is not None:
+            up, down = beside(step, up, down)
     return parts[0].astype(f32) + up.astype(f32) + down.astype(f32)
 
 
@@ -503,11 +511,12 @@
         placed = lax.psum_scatter(placed, PLANE, scatter_dimension=0, tiled=True)
         return placed.astype(f32), before, after
     away = swap_core(place_rows(pairs, 4, 4, rows))
-    home, after = lax.optimization_barrier((place_rows(pairs, 0, 4, rows), after))
+    home = place_rows(pairs, 0, 4, rows)
     half = rows // 2
     part = lambda first, last: add16(home[first:last], away[first:last])
     got_low = swap(part(3 * rows, 3 * rows + half), "seq")
     got_high = swap(part(3 * rows + half, 4 * rows), "p")
+    got_low, got_high, after = lax.optimization_barrier((got_low, got_high, after))
     seq_high = add16(part(rows + half, 2 * rows), got_high)
     p_low = add16(part(2 * rows, 2 * rows + half), got_low)
     from_seq = swap(jnp.concatenate([part(rows, rows + half), seq_high]), "seq")
@@ -671,12 +680,6 @@
     enc_places = [item[:enc_count] for item in places]
     dec_places = [item[enc_count:] for item in places]
 
-    def look(items):
-        got = jnp.take(plane_table, jnp.concatenate(items), axis=0, mode="clip")
-        return line_scatter(jnp.split(got, len(items)), "z")
-
-    looked = look(places)
-    enc_x0, dec_y0 = looked[:enc_count], looked[enc_count:]
 
     cut = lambda pack, start, width: lax.slice_in_dim(pack, start, start + width, axis=1)
     enc_wi, enc_fi = cut(enc_pack, 0, 3 * D), cut(enc_pack, 3 * D, 2 * FF)
@@ -688,6 +691,19 @@
 
     enc_x8, enc_picks = bias_lines(rel_all[0], buckets[0], core, enc_count, enc_count)
     dec_x8, dec_picks = bias_lines(rel_all[1], buckets[1], core, dec_count, dec_count)
+    held = (enc_fo, gain, enc_x8, dec_x8, enc_picks, dec_picks)
+
+    def beside(step, up, down):
+        nonlocal held
+        if step == 2:
+            up, down, held = lax.optimization_barrier((up, down, held))
+        return up, down
+
+    got = jnp.take(plane_table, jnp.concatenate(places), axis=0, mode="clip")
+    looked = line_scatter(jnp.split(got, len(places)), "z", beside)
+    enc_fo, gain, enc_x8, dec_x8, enc_picks, dec_picks = held
+    enc_x0, dec_y0 = looked[:enc_count], looked[enc_count:]
+
     col, line = (lambda v: v[:, None]), (lambda v: v[None, :])
     enc_info = (
         col(enc_seg), line(enc_seg), line(enc_seg_other),
@@ -706,7 +722,7 @@
     enc_q = project(enc_n1, enc_wi[:, :D]).astype(bf16)
     enc_kv = project(enc_n1, enc_wi[:, D:]).astype(bf16)
     enc_kv2 = swap_core(enc_kv)
-    enc_ob = attend_forward(enc_q, enc_kv, enc_kv2, enc_info, enc_x8, False)
+    enc_ob, enc_lse = attend_forward(enc_q, enc_kv, enc_kv2, enc_info, enc_x8, False)
     ffn_cast, dec_pack, enc_ob = lax.optimization_barrier((ffn_cast, dec_pack, enc_ob))
     ffn_pack = lax.all_gather(ffn_cast, ALL, axis=0, tiled=True)
     dec_wi, cross_wi = cut(dec_pack, 0, 3 * D), cut(dec_pack, 3 * D, 3 * D)
@@ -721,13 +737,13 @@
     dec_q = project(dec_n1, dec_wi[:, :D]).astype(bf16)
     dec_kv = project(dec_n1, dec_wi[:, D:]).astype(bf16)
     dec_kv2 = swap_core(dec_kv)
-    dec_ob = attend_forward(dec_q, dec_kv, dec_kv2, dec_info, dec_x8, True)
+    dec_ob, dec_lse = attend_forward(dec_q, dec_kv, dec_kv2, dec_info, dec_x8, True)
     dec_y1 = dec_y0 + project(dec_ob, dec_wo)
     cross_kv = project(enc_out, cross_wi[:, D:]).astype(bf16)
     cross_kv2 = swap_core(cross_kv)
     cross_n = rms_scale(dec_y1, gain[4]).astype(bf16)
     cross_q = project(cross_n, cross_wi[:, :D]).astype(bf16)
-    cross_ob = attend_forward(cross_q, cross_kv, cross_kv2, cross_info, None, False)
+    cross_ob, cross_lse = attend_forward(cross_q, cross_kv, cross_kv2, cross_info, None, False)
     dec_y2 = dec_y1 + project(cross_ob, cross_wo)
     dec_y3, dec_saved = ffn_forward(dec_y2, gain[5], dec_fi, dec_fo)
     head_scale = D ** (-0.5)
@@ -774,7 +790,7 @@
     g_dec_fo = scatter_core(d_dec_fo)
     early = lax.psum_scatter(early, ALL, scatter_dimension=0, tiled=True)
     d_cross_q, own, other = attend_backward(
-        d_cross_ob, cross_q, cross_kv, cross_kv2, cross_info, None, False
+        d_cross_ob, cross_lse, cross_q, cross_kv, cross_kv2, cross_info, None, False
     )
     got = (own + swap_core(other).astype(f32)).astype(bf16)
     d_cross_kv = jnp.concatenate([got[0], got[1]], axis=1)
@@ -788,7 +804,7 @@
     g_dec_fo, d_dec_ob = lax.optimization_barrier((g_dec_fo, d_dec_ob))
     g_dec_fo = scatter_first(g_dec_fo, False)
     d_dec_q, own, other, dec_y8 = attend_backward(
-        d_dec_ob, dec_q, dec_kv, dec_kv2, dec_info, dec_x8, True
+        d_dec_ob, dec_lse, dec_q, dec_kv, dec_kv2, dec_info, dec_x8, True
     )
     got = (own + swap_core(other).astype(f32)).astype(bf16)
     d_dec_qkv = jnp.concatenate([d_dec_q, got[0], got[1]], axis=1)
@@ -826,7 +842,7 @@
     early = early.astype(f32)
     enc_sums = [scatter_first(item, number == 0) for number, item in enumerate(enc_sums)]
     d_enc_q, own, other, enc_y8 = attend_backward(
-        d_enc_ob, enc_q, enc_kv, enc_kv2, enc_info, enc_x8, False
+        d_enc_ob, enc_lse, enc_q, enc_kv, enc_kv2, enc_info, enc_x8, False
     )
     got = (own + swap_core(other).astype(f32)).astype(bf16)
     d_enc_qkv = jnp.concatenate([d_enc_q, got[0], got[1]], axis=1)
@@ -835,11 +851,12 @@
     d_x0_norm, d_gain_eatt = norm_pull(enc_x0, gain[0], 1.0, input_grad(d_enc_qkv, enc_wi))
     d_x0 = d_x1 + d_x0_norm
 
-    d_x0, enc_sums = lax.optimization_barrier((d_x0.astype(bf16), enc_sums))
+    d_x0, enc_sums, g_dec_fo = lax.optimization_barrier(
+        (d_x0.astype(bf16), enc_sums, scatter_last(g_dec_fo))
+    )
     enc_sums = [scatter_second(item, number == 0) for number, item in enumerate(enc_sums)]
     enc_lines = line_gather(d_x0, "z")
     enc_lines, enc_sums = lax.optimization_barrier((enc_lines, enc_sums))
-    g_low, g_high, g_fo, g_dec_fo = [scatter_last(item) for item in (*enc_sums, g_dec_fo)]
     far_place = lambda item: jnp.where(item == shard, -1, item)[None, :]
     pairs = [
         (far_place(item), grads)
@@ -861,11 +878,12 @@
     d_misc = jnp.pad(jnp.concatenate([d_gains.T, d_rel], axis=1), ((0, 0), (0, 120)))
     d_last = jnp.concatenate([d_enc_wi.astype(bf16), d_misc.astype(bf16)], axis=1)
     last = [scatter_core(d_last[:, :1152]), scatter_core(d_last[:, 1152:])]
-    input_embed, late, last = plane_scatter(pairs, padded, late, last)
+    input_embed, late, (last, enc_sums) = plane_scatter(pairs, padded, late, (last, enc_sums))
     late = late.astype(f32)
     grad_embed = head_embed[:shard] + input_embed[:shard]
 
     last = [scatter_rest(item, number == 0) for number, item in enumerate(last)]
+    g_low, g_high, g_fo = [scatter_last(item) for item in enc_sums]
     squares = sum(
         (jnp.sum(item * item) for item in (grad_embed, early, late, g_low, g_high, g_fo, g_dec_fo, *last))
     )

time: 1400 us -> 1430 us (1.021)
  starting transfers between devices: 169 us -> 198 us
  waiting for transfers between devices: 416 us -> 439 us
  Pallas kernels: 294 us -> 277 us
  local copies, waits for them, and re-layouts: 205 us -> 189 us
    ppermute x9, waiting for transfers between devices: 24.3 us -> 62.8 us  [line_gather(): lax.ppermute(ups[-1], axis, [(i, i + 1) for i in range(size - 1)])]
    ppermute x3, waiting for transfers between devices: 95.5 us -> 66.5 us  [line_scatter(): up = lax.ppermute(send_up, axis, [(i, i + 1) for i in range(step)])]
    all_gather x1, waiting for transfers between devices: 29.8 us -> 9.41 us  [body(): lax.all_gather(jnp.concatenate([enc_cast, flat_out[0]], axis=1), ALL, axi...]
    all_gather x1, waiting for transfers between devices: 0.02 us -> 19.7 us  [body(): ffn_pack = lax.all_gather(ffn_cast, ALL, axis=0, tiled=True)]
    ppermute x50, waiting for transfers between devices: 106 us -> 125 us  [swap(): return lax.ppermute(value, axis, [(0, 1), (1, 0)])]
    ppermute x50, starting transfers between devices: 42.6 us -> 57.5 us  [swap(): return lax.ppermute(value, axis, [(0, 1), (1, 0)])]
    unnamed x463 -> x399, local copies, waits for them, and re-layouts: 53.8 us -> 50.6 us
  transfers between devices with their start and end apart: 127 -> 127, of which waited for: 56 -> 52; matrix products, arithmetic and copies ran while one was open for 27% -> 25% of each run, Pallas kernels for 14% -> 13%
where the time goes in v7:
time: 1430 us; the launch traced here: 1410 us
  waiting for transfers between devices  439 us (31%)
  Pallas kernels  277 us (19%)
  starting transfers between devices  198 us (14%)
  local copies, waits for them, and re-layouts  189 us (13%)
  other arithmetic  147 us (10%)
  matrix products  131 us (9%)
  between operations  31.4 us (2%)
    ppermute x50, waiting for transfers between devices, swap(): return lax.ppermute(value, axis, [(0, 1), (1, 0)])  125 us
    pallas_call x3, Pallas kernels, attend_backward(): pl.pallas_call(functools.partial(attend_backward_kernel, cfg), grid=(HEAD...  87.3 us
    all_gather x1, waiting for transfers between devices, body(): hidden_all = lax.all_gather(hidden_b, ALL, axis=0, tiled=True)  76.8 us
    ppermute x3, waiting for transfers between devices, line_scatter(): up = lax.ppermute(send_up, axis, [(i, i + 1) for i in range(step)])  66.5 us
    pallas_call x4, Pallas kernels, head_grad(): pl.pallas_call(functools.partial(head_grad_kernel, count), grid_spec=pltp...  63.5 us
    ppermute x9, waiting for transfers between devices, line_gather(): lax.ppermute(ups[-1], axis, [(i, i + 1) for i in range(size - 1)])  62.8 us
    ppermute x50, starting transfers between devices, swap(): return lax.ppermute(value, axis, [(0, 1), (1, 0)])  57.5 us
    pallas_call x3, Pallas kernels, attend_forward(): pl.pallas_call(functools.partial(attend_forward_kernel, cfg), grid=(HEADS...  53.9 us
  transfers between devices with their start and end apart: 127, of which 52 were waited for; matrix products, arithmetic and copies ran while one was open for 25% of the time, Pallas kernels for 13%

profile of v7, /device:TPU:0, one launch (start us, length us, event | category | flops | bytes accessed | tf_op | source)
XLA Modules:
  0.0 1413.3 jit_solution(8727244478380470792)
XLA Ops:
  48.3 22.4 %collective-permute-done.1 = bf16[1008,768]{1,0:T(8,128)(2,1)} collective-permute-done((bf16[1008,768]{1,0:T(8,128)(2,1)}, bf16[1008,768]{1,0:T(8,128)(2,1)}, u32[]{:S(2)}, u32[]{:S(2)}) %collective-permute-start.1) | collective-permute-done | bytes 1548320 | tf_op jit(solution)/shard_map/ppermute | solution.py:415
  70.7 19.0 %collective-permute-start.6 = (bf16[1008,768]{1,0:T(8,128)(2,1)}, bf16[1008,768]{1,0:T(8,128)(2,1)}, u32[]{:S(2)}, u32[]{:S(2)}) collective-permute-start(bf16[1008,768]{1,0:T(8,128)(2,1)} %collective-permute-done.1), channel_id=1, source_target_pairs={{0,2},{2,0},{1,3},{3,1},{4,6},{6,4},{5,7},{7,5},{8,10},{10,8},{9,1... | collective-permute-start | bytes 4644872 | tf_op jit(solution)/shard_map/ppermute | solution.py:415
  99.1 30.8 %collective-permute-done.3 = bf16[504,768]{1,0:T(8,128)(2,1)S(1)} collective-permute-done((bf16[504,768]{1,0:T(8,128)(2,1)S(1)}, bf16[504,768]{1,0:T(8,128)(2,1)S(1)}, u32[]{:S(2)}, u32[]{:S(2)}) %collective-permute-start.3) | collective-permute-done | bytes 774176 | tf_op jit(solution)/shard_map/ppermute | solution.py:415
  145.0 9.4 all-gather.5.cloned.1.call-done
  159.3 20.8 %gather_fusion = bf16[3072,768]{1,0:T(8,128)(2,1)} fusion(bf16[8064,768]{1,0:T(8,128)(2,1)} %constant_dynamic-update-slice_fusion.4, s32[3072]{0:T(1024)S(1)} %add_clamp_fusion), kind=kCustom, calls=%fused_computation | custom fusion | bytes 9449472 | tf_op jit(solution)/shard_map/jit(_take)/gather | solution.py:702
  194.4 32.5 %collective-permute-done.16 = bf16[768,768]{1,0:T(8,128)(2,1)S(1)} collective-permute-done((bf16[768,768]{1,0:T(8,128)(2,1)}, bf16[768,768]{1,0:T(8,128)(2,1)S(1)}, u32[]{:S(2)}, u32[]{:S(2)}) %collective-permute-start.16) | collective-permute-done | bytes 1179680 | tf_op jit(solution)/shard_map/ppermute | solution.py:482
  230.1 5.6 collective-permute-start.17
  256.9 14.5 %collective-permute-done.17 = bf16[768,768]{1,0:T(8,128)(2,1)} collective-permute-done((bf16[768,768]{1,0:T(8,128)(2,1)}, bf16[768,768]{1,0:T(8,128)(2,1)}, u32[]{:S(2)}, u32[]{:S(2)}) %collective-permute-start.17) | collective-permute-done | bytes 1179680 | tf_op jit(solution)/shard_map/ppermute | solution.py:482
  274.0 5.5 collective-permute-start.20
  284.0 19.4 %collective-permute-done.20 = bf16[768,768]{1,0:T(8,128)(2,1)} collective-permute-done((bf16[768,768]{1,0:T(8,128)(2,1)S(1)}, bf16[768,768]{1,0:T(8,128)(2,1)}, u32[]{:S(2)}, u32[]{:S(2)}) %collective-permute-start.20) | collective-permute-done | bytes 1179680 | tf_op jit(solution)/shard_map/ppermute | solution.py:482
  303.4 5.2 collective-permute-done.21
  320.9 28.7 %shard_map.461 = (bf16[512,768]{1,0:T(8,128)(2,1)}, f32[512,768]{1,0:T(8,128)}) custom-call(bf16[512,768]{1,0:T(8,128)(2,1)} %convolution_convert_fusion.15.refs_0_, bf16[512,1536]{1,0:T(8,128)(2,1)} %convolution_convert_fusion.8.refs_1_.refs_2_, bf16[512,1536]{1,0:T(8,128)(2,1)} %convolution_convert_fusion.8.refs_1_.refs_2_, ...), custom_call_target="tpu_custom_call" | custom-call | flops 2 | bytes 512 | tf_op jit(solution)/shard_map/pallas_call | solution.py:200
  356.1 6.3 fusion.7
  379.6 13.2 shard_map.462
  397.6 12.0 shard_map.463
  411.6 19.7 %all-gather.9.cloned.1.call-done = bf16[768,6144]{1,0:T(8,128)(2,1)} async-done(((bf16[24,6144]{1,0:T(8,128)(2,1)}), bf16[768,6144]{1,0:T(8,128)(2,1)}) %all-gather.9.cloned.1.call-update) | async-done | bytes 9437200 | tf_op jit(solution)/shard_map/all_gather | solution.py:727
  468.0 76.8 %all-gather.11.cloned.1.call-done = bf16[8192,768]{1,0:T(8,128)(2,1)} async-done(((bf16[256,768]{1,0:T(8,128)(2,1)}), bf16[8192,768]{1,0:T(8,128)(2,1)}) %all-gather.11.cloned.1.call-update) | async-done | bytes 12582928 | tf_op jit(solution)/shard_map/all_gather | solution.py:752
  544.7 25.4 %shard_map.464 = (f32[1,8192]{1,0:T(1,128)}, f32[1,8192]{1,0:T(1,128)}) custom-call(bf16[8,2,2,256,768]{4,3,2,1,0:T(8,128)(2,1)} %bitcast.646, bf16[1008,768]{1,0:T(8,128)(2,1)} %get-tuple-element.515.tab, s32[1,8192]{1,0:T(1,128)} %bitcast.605), custom_call_target="tpu_custom_call" | custom-call | flops 12683575296 | bytes 12582912 | tf_op jit(solution)/shard_map/pallas_call | solution.py:306
  592.1 15.8 %shard_map.465 = (bf16[8,2,64,768]{3,2,1,0:T(8,128)(2,1)}, bf16[8,2,64,768]{3,2,1,0:T(8,128)(2,1)}, f32[1008,768]{1,0:T(8,128)}) custom-call(s32[1]{0:T(128)} %bitcast.97.core, bf16[8,2,2,256,768]{4,3,2,1,0:T(8,128)(2,1)} %bitcast.647, bf16[1008,768]{1,0:T(8,128)(2,1)} %get-tuple-element.515.tab, s32[1,8192]{1,0:T(1,128)} %bitcast.606, f32[1,8192]{1,0:T(1,128)} %bitcast.584, ...), custom_call_target="tpu_custom_call" | custom-call | flops 9512681472 | bytes 6291456 | tf_op jit(solution)/shard_map/pallas_call | solution.py:329
  607.9 15.8 %shard_map.467 = (bf16[8,2,64,768]{3,2,1,0:T(8,128)(2,1)}, bf16[8,2,64,768]{3,2,1,0:T(8,128)(2,1)}, f32[1008,768]{1,0:T(8,128)}) custom-call(s32[1]{0:T(128)} %bitcast.97.core, bf16[8,2,2,256,768]{4,3,2,1,0:T(8,128)(2,1)} %bitcast.648, bf16[1008,768]{1,0:T(8,128)(2,1)} %get-tuple-element.515.tab, s32[1,8192]{1,0:T(1,128)} %bitcast.607, f32[1,8192]{1,0:T(1,128)} %bitcast.585, ...), custom_call_target="tpu_custom_call" | custom-call | flops 9512681472 | bytes 6291456 | tf_op jit(solution)/shard_map/pallas_call | solution.py:329
  624.3 15.8 %shard_map.466 = (bf16[8,2,64,768]{3,2,1,0:T(8,128)(2,1)}, bf16[8,2,64,768]{3,2,1,0:T(8,128)(2,1)}, f32[1008,768]{1,0:T(8,128)}) custom-call(s32[1]{0:T(128)} %bitcast.98.core, bf16[8,2,2,256,768]{4,3,2,1,0:T(8,128)(2,1)} %bitcast.649, bf16[1008,768]{1,0:T(8,128)(2,1)} %get-tuple-element.515.tab, s32[1,8192]{1,0:T(1,128)} %bitcast.608, f32[1,8192]{1,0:T(1,128)} %bitcast.586, ...), custom_call_target="tpu_custom_call" | custom-call | flops 9512681472 | bytes 6291456 | tf_op jit(solution)/shard_map/pallas_call | solution.py:329
  640.7 16.0 %shard_map.468 = (bf16[8,2,64,768]{3,2,1,0:T(8,128)(2,1)}, bf16[8,2,64,768]{3,2,1,0:T(8,128)(2,1)}, f32[1008,768]{1,0:T(8,128)}) custom-call(s32[1]{0:T(128)} %bitcast.98.core, bf16[8,2,2,256,768]{4,3,2,1,0:T(8,128)(2,1)} %bitcast.650, bf16[1008,768]{1,0:T(8,128)(2,1)} %get-tuple-element.515.tab, s32[1,8192]{1,0:T(1,128)} %bitcast.609, f32[1,8192]{1,0:T(1,128)} %bitcast.587, ...), custom_call_target="tpu_custom_call" | custom-call | flops 9512681472 | bytes 6291456 | tf_op jit(solution)/shard_map/pallas_call | solution.py:329
  666.0 13.3 collective-permute-done.37
  683.0 13.2 collective-permute-done.49
  699.8 7.0 collective-permute-done.38
  750.5 6.8 multiply_reduce_fusion.12
  761.0 16.6 %shard_map.469 = (bf16[256,768]{1,0:T(8,128)(2,1)}, f32[2,512,768]{2,1,0:T(8,128)}, bf16[2,512,768]{2,1,0:T(8,128)(2,1)}) custom-call(bf16[256,768]{1,0:T(8,128)(2,1)} %convolution_convert_fusion.18.refs_0_, bf16[512,1536]{1,0:T(8,128)(2,1)} %convolution_convert_fusion.7.refs_1_.refs_2_, bf16[512,1536]{1,0:T(8,128)(2,1)} %convolution_convert_fusion.7.refs_1_.refs_2_, ...), custom_call_target="tpu_custom_call" | custom-call | flops 5 | bytes 256 | tf_op jit(solution)/shard_map/pallas_call | solution.py:227
  807.7 22.8 %shard_map.470 = (bf16[256,768]{1,0:T(8,128)(2,1)}, f32[2,256,768]{2,1,0:T(8,128)}, bf16[2,256,768]{2,1,0:T(8,128)(2,1)}, f32[12,2,8,512]{3,2,1,0:T(8,128)}) custom-call(bf16[256,768]{1,0:T(8,128)(2,1)} %convolution_convert_fusion.19.refs_0_, bf16[256,1536]{1,0:T(8,128)(2,1)} %copy-done.5, bf16[256,1536]{1,0:T(8,128)(2,1)} %copy-done.5, ...), custom_call_target="tpu_custom_call" | custom-call | flops 5 | bytes 256 | tf_op jit(solution)/shard_map/pallas_call | solution.py:227
  830.6 9.1 fusion.58
  839.6 7.1 convolution_convert_fusion
  851.3 9.7 multiply_reduce_fusion.3
  879.3 5.2 collective-permute-start.64
  961.9 47.9 %shard_map.471 = (bf16[512,768]{1,0:T(8,128)(2,1)}, f32[2,512,768]{2,1,0:T(8,128)}, bf16[2,512,768]{2,1,0:T(8,128)(2,1)}, f32[12,4,8,768]{3,2,1,0:T(8,128)}) custom-call(bf16[512,768]{1,0:T(8,128)(2,1)} %convolution_convert_fusion.15.refs_0_, bf16[512,1536]{1,0:T(8,128)(2,1)} %convolution_convert_fusion.8.refs_1_.refs_2_, ...), custom_call_target="tpu_custom_call" | custom-call | flops 5 | bytes 512 | tf_op jit(solution)/shard_map/pallas_call | solution.py:227
  1029.8 12.8 collective-permute-done.81
  1051.2 24.2 %collective-permute-done.85 = bf16[512,768]{1,0:T(8,128)(2,1)S(1)} collective-permute-done((bf16[512,768]{1,0:T(8,128)(2,1)S(1)}, bf16[512,768]{1,0:T(8,128)(2,1)S(1)}, u32[]{:S(2)}, u32[]{:S(2)}) %collective-permute-start.85) | collective-permute-done | bytes 786464 | tf_op jit(solution)/shard_map/ppermute | solution.py:469
  1083.3 19.4 %collective-permute-done.86 = bf16[512,768]{1,0:T(8,128)(2,1)S(1)} collective-permute-done((bf16[512,768]{1,0:T(8,128)(2,1)S(1)}, bf16[512,768]{1,0:T(8,128)(2,1)S(1)}, u32[]{:S(2)}, u32[]{:S(2)}) %collective-permute-start.86) | collective-permute-done | bytes 786464 | tf_op jit(solution)/shard_map/ppermute | solution.py:469
  1109.8 23.8 %shard_map.473 = bf16[4032,768]{1,0:T(8,128)(2,1)} custom-call(s32[1,512]{1,0:T(1,128)} %bitcast.616, bf16[512,768]{1,0:T(8,128)(2,1)} %copy-done.23, s32[1,512]{1,0:T(1,128)} %bitcast.614, bf16[512,768]{1,0:T(8,128)(2,1)} %add.1346.refs_3_, s32[1,512]{1,0:T(1,128)} %bitcast.612, bf16[512,768]{1,0:T(8,128)(2,1)} %add.1347.refs_5_, s32[1,512]{1,0:T(1,128)} %bitcast.610, ...), custom_call_target="tpu_custom_call" | custom-call | flops 1 | bytes 1008 | tf_op jit(solution)/shard_map/pallas_call | solution.py:374
  1153.1 5.3 copy.745
  1166.3 7.8 fusion
  1174.1 23.7 %shard_map.472 = bf16[4032,768]{1,0:T(8,128)(2,1)} custom-call(s32[1,512]{1,0:T(1,128)} %bitcast.617, bf16[512,768]{1,0:T(8,128)(2,1)} %copy-done.23, s32[1,512]{1,0:T(1,128)} %bitcast.615, bf16[512,768]{1,0:T(8,128)(2,1)} %add.1346.refs_3_, s32[1,512]{1,0:T(1,128)} %bitcast.613, bf16[512,768]{1,0:T(8,128)(2,1)} %add.1347.refs_5_, s32[1,512]{1,0:T(1,128)} %bitcast.611, ...), custom_call_target="tpu_custom_call" | custom-call | flops 1 | bytes 1008 | tf_op jit(solution)/shard_map/pallas_call | solution.py:374
  1215.1 9.6 collective-permute-done.91
  1262.9 5.0 collective-permute-done.98
  1283.1 23.7 %collective-permute-done.107 = bf16[4,24,1152]{2,1,0:T(8,128)(2,1)S(1)} collective-permute-done((bf16[4,24,1152]{2,1,0:T(8,128)(2,1)S(1)}, bf16[4,24,1152]{2,1,0:T(8,128)(2,1)S(1)}, u32[]{:S(2)}, u32[]{:S(2)}) %collective-permute-start.107) | collective-permute-done | bytes 221216 | tf_op jit(solution)/shard_map/ppermute | solution.py:415
  1323.8 6.0 collective-permute-done.113
  1329.8 10.9 collective-permute-done.114
  1343.8 8.5 multiply_reduce_fusion.1
  1368.2 7.5 collective-permute-start.119
  1389.1 8.3 add_subtract_fusion
  (1007 shorter events, 596.1 us)
Async XLA Ops:
  7.2 147.2 %all-gather.5.cloned.1.call-start = ((), (), s32[]{:S(2)}) async-start(), calls=%async_computation.2 | async-start | bytes 14800896 | tf_op jit(solution)/shard_map/all_gather | solution.py:616
  19.9 329.8 %all-gather.7.cloned.1.call-start = ((), (), s32[]{:S(2)}) async-start(), calls=%async_computation.3 | async-start | bytes 9732096 | tf_op jit(solution)/shard_map/all_gather | solution.py:679
  22.0 48.6 %collective-permute-start.1 = (bf16[1008,768]{1,0:T(8,128)(2,1)}, bf16[1008,768]{1,0:T(8,128)(2,1)}, u32[]{:S(2)}, u32[]{:S(2)}) collective-permute-start(bf16[1008,768]{1,0:T(8,128)(2,1)} %get-tuple-element.515.tab), channel_id=1, source_target_pairs={{0,1},{1,0},{2,3},{3,2},{4,5},{5,4},{6,7},{7,6},{8,9},{9,8},{10,11... | collective-permute-start | bytes 4644872 | tf_op jit(solution)/shard_map/ppermute | solution.py:415
  25.0 64.7 %collective-permute-start.2 = (bf16[1008,768]{1,0:T(8,128)(2,1)}, bf16[1008,768]{1,0:T(8,128)(2,1)}, u32[]{:S(2)}, u32[]{:S(2)}) collective-permute-start(bf16[1008,768]{1,0:T(8,128)(2,1)} %get-tuple-element.515.tab), channel_id=1, source_target_pairs={{0,4},{4,0},{1,5},{5,1},{2,6},{6,2},{3,7},{7,3},{8,12},{12,8},{9,1... | collective-permute-start | bytes 4644872 | tf_op jit(solution)/shard_map/ppermute | solution.py:415
  26.5 108.5 %collective-permute-start.5 = (bf16[1008,768]{1,0:T(8,128)(2,1)}, bf16[1008,768]{1,0:T(8,128)(2,1)}, u32[]{:S(2)}, u32[]{:S(2)}) collective-permute-start(bf16[1008,768]{1,0:T(8,128)(2,1)} %get-tuple-element.515.tab), channel_id=1, source_target_pairs={{0,2},{2,0},{1,3},{3,1},{4,6},{6,4},{5,7},{7,5},{8,10},{10,8},{9,1... | collective-permute-start | bytes 4644872 | tf_op jit(solution)/shard_map/ppermute | solution.py:415
  42.4 50.9 %collective-permute-start.13 = (s32[768]{0:T(1024)S(1)}, s32[768]{0:T(1024)S(1)}, u32[]{:S(2)}, u32[]{:S(2)}) collective-permute-start(s32[768]{0:T(1024)S(1)} %collective-permute-done.12), channel_id=1, source_target_pairs={{8,0},{16,8},{24,16},{9,1},{17,9},{25,17},{10,2},{18,10},{26,18},{... | collective-permute-start | bytes 9224 | tf_op jit(solution)/shard_map/ppermute | solution.py:470
  43.7 50.8 %collective-permute-start.15 = (s32[768]{0:T(1024)S(1)}, s32[768]{0:T(1024)S(1)}, u32[]{:S(2)}, u32[]{:S(2)}) collective-permute-start(s32[768]{0:T(1024)S(1)} %collective-permute-done.14), channel_id=1, source_target_pairs={{0,8},{8,16},{16,24},{1,9},{9,17},{17,25},{2,10},{10,18},{18,26},{... | collective-permute-start | bytes 9224 | tf_op jit(solution)/shard_map/ppermute | solution.py:469
  70.7 67.1 %collective-permute-start.6 = (bf16[1008,768]{1,0:T(8,128)(2,1)}, bf16[1008,768]{1,0:T(8,128)(2,1)}, u32[]{:S(2)}, u32[]{:S(2)}) collective-permute-start(bf16[1008,768]{1,0:T(8,128)(2,1)} %collective-permute-done.1), channel_id=1, source_target_pairs={{0,2},{2,0},{1,3},{3,1},{4,6},{6,4},{5,7},{7,5},{8,10},{10,8},{9,1... | collective-permute-start | bytes 4644872 | tf_op jit(solution)/shard_map/ppermute | solution.py:415
  89.7 50.7 %collective-permute-start.7 = (bf16[1008,768]{1,0:T(8,128)(2,1)}, bf16[1008,768]{1,0:T(8,128)(2,1)}, u32[]{:S(2)}, u32[]{:S(2)}) collective-permute-start(bf16[1008,768]{1,0:T(8,128)(2,1)} %collective-permute-done.2), channel_id=1, source_target_pairs={{0,2},{2,0},{1,3},{3,1},{4,6},{6,4},{5,7},{7,5},{8,10},{10,8},{9,1... | collective-permute-start | bytes 4644872 | tf_op jit(solution)/shard_map/ppermute | solution.py:415
  93.3 36.6 %collective-permute-start.3 = (bf16[504,768]{1,0:T(8,128)(2,1)S(1)}, bf16[504,768]{1,0:T(8,128)(2,1)S(1)}, u32[]{:S(2)}, u32[]{:S(2)}) collective-permute-start(bf16[504,768]{1,0:T(8,128)(2,1)S(1)} %slice.614), channel_id=1, source_target_pairs={{0,1},{1,0},{2,3},{3,2},{4,5},{5,4},{6,7},{7,6},{8,9},{9,8},{10,11... | collective-permute-start | bytes 2322440 | tf_op jit(solution)/shard_map/ppermute | solution.py:415
  94.5 38.1 %collective-permute-start.4 = (bf16[504,768]{1,0:T(8,128)(2,1)S(1)}, bf16[504,768]{1,0:T(8,128)(2,1)S(1)}, u32[]{:S(2)}, u32[]{:S(2)}) collective-permute-start(bf16[504,768]{1,0:T(8,128)(2,1)S(1)} %slice.615), channel_id=1, source_target_pairs={{0,4},{4,0},{1,5},{5,1},{2,6},{6,2},{3,7},{7,3},{8,12},{12,8},{9,1... | collective-permute-start | bytes 2322440 | tf_op jit(solution)/shard_map/ppermute | solution.py:415
  154.4 276.9 %all-gather.9.cloned.1.call-start = ((), (), s32[]{:S(2)}) async-start(), calls=%async_computation.4 | async-start | bytes 9732096 | tf_op jit(solution)/shard_map/all_gather | solution.py:727
  182.8 44.1 %collective-permute-start.16 = (bf16[768,768]{1,0:T(8,128)(2,1)}, bf16[768,768]{1,0:T(8,128)(2,1)S(1)}, u32[]{:S(2)}, u32[]{:S(2)}) collective-permute-start(bf16[768,768]{1,0:T(8,128)(2,1)} %get-tuple-element.484), channel_id=1, source_target_pairs={{0,8},{1,9},{2,10},{3,11},{4,12},{5,13},{6,14},{7,15}} | collective-permute-start | bytes 3538952 | tf_op jit(solution)/shard_map/ppermute | solution.py:482
  185.4 41.5 %collective-permute-start.18 = (bf16[768,768]{1,0:T(8,128)(2,1)S(1)}, bf16[768,768]{1,0:T(8,128)(2,1)}, u32[]{:S(2)}, u32[]{:S(2)}) collective-permute-start(bf16[768,768]{1,0:T(8,128)(2,1)S(1)} %get-tuple-element.483), channel_id=1, source_target_pairs={{24,16},{25,17},{26,18},{27,19},{28,20},{29,21},{30,22},{31,23}} | collective-permute-start | bytes 3538952 | tf_op jit(solution)/shard_map/ppermute | solution.py:483
  230.1 41.3 %collective-permute-start.17 = (bf16[768,768]{1,0:T(8,128)(2,1)}, bf16[768,768]{1,0:T(8,128)(2,1)}, u32[]{:S(2)}, u32[]{:S(2)}) collective-permute-start(bf16[768,768]{1,0:T(8,128)(2,1)} %get-tuple-element.482), channel_id=1, source_target_pairs={{0,8},{8,16},{1,9},{9,17},{2,10},{10,18},{3,11},{11,19},{4,12},{12... | collective-permute-start | bytes 3538952 | tf_op jit(solution)/shard_map/ppermute | solution.py:482
  235.7 35.8 %collective-permute-start.19 = (bf16[768,768]{1,0:T(8,128)(2,1)}, bf16[768,768]{1,0:T(8,128)(2,1)}, u32[]{:S(2)}, u32[]{:S(2)}) collective-permute-start(bf16[768,768]{1,0:T(8,128)(2,1)} %get-tuple-element.481), channel_id=1, source_target_pairs={{24,16},{16,8},{25,17},{17,9},{26,18},{18,10},{27,19},{19,11},{28,... | collective-permute-start | bytes 3538952 | tf_op jit(solution)/shard_map/ppermute | solution.py:483
  274.0 29.4 %collective-permute-start.20 = (bf16[768,768]{1,0:T(8,128)(2,1)S(1)}, bf16[768,768]{1,0:T(8,128)(2,1)}, u32[]{:S(2)}, u32[]{:S(2)}) collective-permute-start(bf16[768,768]{1,0:T(8,128)(2,1)S(1)} %get-tuple-element.479), channel_id=1, source_target_pairs={{0,8},{8,16},{16,24},{1,9},{9,17},{17,25},{2,10},{10,18},{18,26},{... | collective-permute-start | bytes 3538952 | tf_op jit(solution)/shard_map/ppermute | solution.py:482
  279.5 29.1 %collective-permute-start.21 = (bf16[768,768]{1,0:T(8,128)(2,1)S(1)}, bf16[768,768]{1,0:T(8,128)(2,1)}, u32[]{:S(2)}, u32[]{:S(2)}) collective-permute-start(bf16[768,768]{1,0:T(8,128)(2,1)S(1)} %get-tuple-element.480), channel_id=1, source_target_pairs={{24,16},{16,8},{8,0},{25,17},{17,9},{9,1},{26,18},{18,10},{10,2},{... | collective-permute-start | bytes 3538952 | tf_op jit(solution)/shard_map/ppermute | solution.py:483
  349.7 195.0 %all-gather.11.cloned.1.call-start = ((), (), s32[]{:S(2)}) async-start(), calls=%async_computation.5 | async-start | bytes 12976128 | tf_op jit(solution)/shard_map/all_gather | solution.py:752
  353.3 26.3 %collective-permute-start.23 = (bf16[256,1536]{1,0:T(8,128)(2,1)S(1)}, bf16[256,1536]{1,0:T(8,128)(2,1)}, u32[]{:S(2)}, u32[]{:S(2)}) collective-permute-start(bf16[256,1536]{1,0:T(8,128)(2,1)S(1)} %convolution_convert_fusion.9.refs_1_.refs_2_), channel_id=1, source_target_pairs={{0,2},{2,0},{1,3},{3,1},{4,6},{6,4},{5,7},{7,5},{8,10},{10,8},{9,1... | collective-permute-start | bytes 2359304 | tf_op jit(solution)/shard_map/ppermute | solution.py:415
  449.2 476.8 %reduce-scatter.5.cloned.1.call-start = ((), (), s32[]{:S(2)}) async-start(), calls=%async_computation.6 | async-start | bytes 6488064 | tf_op jit(solution)/shard_map/reduce_scatter | solution.py:791
  623.8 33.0 %collective-permute-start.36 = (bf16[8,2,64,768]{3,2,1,0:T(8,128)(2,1)}, bf16[8,2,64,768]{3,2,1,0:T(8,128)(2,1)S(1)}, u32[]{:S(2)}, u32[]{:S(2)}) collective-permute-start(bf16[8,2,64,768]{3,2,1,0:T(8,128)(2,1)} %get-tuple-element.152), channel_id=1, source_target_pairs={{0,2},{2,0},{1,3},{3,1},{4,6},{6,4},{5,7},{7,5},{8,10},{10,8},{9,1... | collective-permute-start | bytes 4718600 | tf_op jit(solution)/shard_map/ppermute | solution.py:415
  623.8 36.5 %collective-permute-start.42 = (bf16[8,2,64,768]{3,2,1,0:T(8,128)(2,1)}, bf16[8,2,64,768]{3,2,1,0:T(8,128)(2,1)S(1)}, u32[]{:S(2)}, u32[]{:S(2)}) collective-permute-start(bf16[8,2,64,768]{3,2,1,0:T(8,128)(2,1)} %get-tuple-element.154), channel_id=1, source_target_pairs={{0,2},{2,0},{1,3},{3,1},{4,6},{6,4},{5,7},{7,5},{8,10},{10,8},{9,1... | collective-permute-start | bytes 4718600 | tf_op jit(solution)/shard_map/ppermute | solution.py:415
  663.0 33.2 %collective-permute-start.49 = (bf16[4,2,64,768]{3,2,0,1:T(8,128)(2,1)S(1)}, bf16[4,2,64,768]{3,2,0,1:T(8,128)(2,1)S(1)}, u32[]{:S(2)}, u32[]{:S(2)}) collective-permute-start(bf16[4,2,64,768]{3,2,0,1:T(8,128)(2,1)S(1)} %bitcast.578), channel_id=1, source_target_pairs={{0,1},{1,0},{2,3},{3,2},{4,5},{5,4},{6,7},{7,6},{8,9},{9,8},{10,11... | collective-permute-start | bytes 2359304 | tf_op jit(solution)/shard_map/ppermute | solution.py:415
  664.8 33.6 %collective-permute-start.55 = (bf16[4,2,64,768]{3,2,0,1:T(8,128)(2,1)S(1)}, bf16[4,2,64,768]{3,2,0,1:T(8,128)(2,1)S(1)}, u32[]{:S(2)}, u32[]{:S(2)}) collective-permute-start(bf16[4,2,64,768]{3,2,0,1:T(8,128)(2,1)S(1)} %bitcast.579), channel_id=1, source_target_pairs={{0,4},{4,0},{1,5},{5,1},{2,6},{6,2},{3,7},{7,3},{8,12},{12,8},{9,1... | collective-permute-start | bytes 2359304 | tf_op jit(solution)/shard_map/ppermute | solution.py:415
  679.6 27.3 %collective-permute-start.38 = (bf16[4,64,768]{2,1,0:T(8,128)(2,1)S(1)}, bf16[4,64,768]{2,1,0:T(8,128)(2,1)S(1)}, u32[]{:S(2)}, u32[]{:S(2)}) collective-permute-start(bf16[4,64,768]{2,1,0:T(8,128)(2,1)S(1)} %dynamic-slice_bitcast_fusion.16), channel_id=1, source_target_pairs={{0,4},{4,0},{1,5},{5,1},{2,6},{6,2},{3,7},{7,3},{8,12},{12,8},{9,1... | collective-permute-start | bytes 1179656 | tf_op jit(solution)/shard_map/ppermute | solution.py:415
  681.8 27.3 %collective-permute-start.44 = (bf16[4,64,768]{2,1,0:T(8,128)(2,1)S(1)}, bf16[4,64,768]{2,1,0:T(8,128)(2,1)S(1)}, u32[]{:S(2)}, u32[]{:S(2)}) collective-permute-start(bf16[4,64,768]{2,1,0:T(8,128)(2,1)S(1)} %dynamic-slice_bitcast_fusion.15), channel_id=1, source_target_pairs={{0,1},{1,0},{2,3},{3,2},{4,5},{5,4},{6,7},{7,6},{8,9},{9,8},{10,11... | collective-permute-start | bytes 1179656 | tf_op jit(solution)/shard_map/ppermute | solution.py:415
  780.9 326.8 %reduce-scatter.7.cloned.1.call-start = ((), (), s32[]{:S(2)}) async-start(), calls=%async_computation.7 | async-start | bytes 9732096
  799.4 115.4 %collective-permute-start.61 = (bf16[4,2,64,768]{3,2,0,1:T(8,128)(2,1)}, bf16[4,2,64,768]{3,2,0,1:T(8,128)(2,1)}, u32[]{:S(2)}, u32[]{:S(2)}) collective-permute-start(bf16[4,2,64,768]{3,2,0,1:T(8,128)(2,1)} %dynamic-slice_bitcast_fusion.5), channel_id=1, source_target_pairs={{0,4},{4,0},{1,5},{5,1},{2,6},{6,2},{3,7},{7,3},{8,12},{12,8},{9,1... | collective-permute-start | bytes 2359304 | tf_op jit(solution)/shard_map/ppermute | solution.py:415
  807.5 110.5 %collective-permute-start.72 = (bf16[4,2,2,64,768]{4,3,0,2,1:T(8,128)(2,1)}, bf16[4,2,2,64,768]{4,3,0,2,1:T(8,128)(2,1)}, u32[]{:S(2)}, u32[]{:S(2)}) collective-permute-start(bf16[4,2,2,64,768]{4,3,0,2,1:T(8,128)(2,1)} %bitcast.558), channel_id=1, source_target_pairs={{0,2},{2,0},{1,3},{3,1},{4,6},{6,4},{5,7},{7,5},{8,10},{10,8},{9,1... | collective-permute-start | bytes 4718600 | tf_op jit(solution)/shard_map/ppermute | solution.py:415
  870.3 67.6 %collective-permute-start.70 = (bf16[4,2,2,24,3456]{4,3,0,1,2:T(8,128)(2,1)}, bf16[4,2,2,24,3456]{4,3,0,1,2:T(8,128)(2,1)}, u32[]{:S(2)}, u32[]{:S(2)}) collective-permute-start(bf16[4,2,2,24,3456]{4,3,0,1,2:T(8,128)(2,1)} %bitcast.557), channel_id=1, source_target_pairs={{0,2},{2,0},{1,3},{3,1},{4,6},{6,4},{5,7},{7,5},{8,10},{10,8},{9,1... | collective-permute-start | bytes 7962632 | tf_op jit(solution)/shard_map/ppermute | solution.py:415
  951.7 58.0 %collective-permute-start.79 = (bf16[64,768]{1,0:T(8,128)(2,1)S(1)}, bf16[64,768]{1,0:T(8,128)(2,1)S(1)}, u32[]{:S(2)}, u32[]{:S(2)}) collective-permute-start(bf16[64,768]{1,0:T(8,128)(2,1)S(1)} %get-tuple-element.538), channel_id=1, source_target_pairs={{0,16},{8,24},{16,0},{24,8},{1,17},{9,25},{17,1},{25,9},{2,18},{10... | collective-permute-start | bytes 294920 | tf_op jit(solution)/shard_map/ppermute | solution.py:456
  952.5 57.3 %collective-permute-start.80 = (bf16[64,768]{1,0:T(8,128)(2,1)S(1)}, bf16[64,768]{1,0:T(8,128)(2,1)S(1)}, u32[]{:S(2)}, u32[]{:S(2)}) collective-permute-start(bf16[64,768]{1,0:T(8,128)(2,1)S(1)} %get-tuple-element.537), channel_id=1, source_target_pairs={{0,24},{8,0},{16,8},{24,16},{1,25},{9,1},{17,9},{25,17},{2,26},{10... | collective-permute-start | bytes 294920 | tf_op jit(solution)/shard_map/ppermute | solution.py:456
  955.2 56.5 %collective-permute-start.76 = (bf16[4,2,24,1408]{3,2,1,0:T(8,128)(2,1)S(1)}, bf16[4,2,24,1408]{3,2,1,0:T(8,128)(2,1)}, u32[]{:S(2)}, u32[]{:S(2)}) collective-permute-start(bf16[4,2,24,1408]{3,2,1,0:T(8,128)(2,1)S(1)} %copy_bitcast_fusion.15), channel_id=1, source_target_pairs={{0,4},{4,0},{1,5},{5,1},{2,6},{6,2},{3,7},{7,3},{8,12},{12,8},{9,1... | collective-permute-start | bytes 1622024 | tf_op jit(solution)/shard_map/ppermute | solution.py:415
  959.0 55.2 %collective-permute-start.75 = (bf16[4,2,24,3456]{3,2,0,1:T(8,128)(2,1)}, bf16[4,2,24,3456]{3,2,0,1:T(8,128)(2,1)}, u32[]{:S(2)}, u32[]{:S(2)}) collective-permute-start(bf16[4,2,24,3456]{3,2,0,1:T(8,128)(2,1)} %dynamic-slice_bitcast_fusion), channel_id=1, source_target_pairs={{0,1},{1,0},{2,3},{3,2},{4,5},{5,4},{6,7},{7,6},{8,9},{9,8},{10,11... | collective-permute-start | bytes 3981320 | tf_op jit(solution)/shard_map/ppermute | solution.py:415
  960.0 52.8 %collective-permute-start.77 = (bf16[4,2,64,768]{3,2,0,1:T(8,128)(2,1)S(1)}, bf16[4,2,64,768]{3,2,0,1:T(8,128)(2,1)}, u32[]{:S(2)}, u32[]{:S(2)}) collective-permute-start(bf16[4,2,64,768]{3,2,0,1:T(8,128)(2,1)S(1)} %dynamic-slice_bitcast_fusion.4), channel_id=1, source_target_pairs={{0,4},{4,0},{1,5},{5,1},{2,6},{6,2},{3,7},{7,3},{8,12},{12,8},{9,1... | collective-permute-start | bytes 2359304 | tf_op jit(solution)/shard_map/ppermute | solution.py:415
  1042.6 32.9 %collective-permute-start.85 = (bf16[512,768]{1,0:T(8,128)(2,1)S(1)}, bf16[512,768]{1,0:T(8,128)(2,1)S(1)}, u32[]{:S(2)}, u32[]{:S(2)}) collective-permute-start(bf16[512,768]{1,0:T(8,128)(2,1)S(1)} %collective-permute-done.81), channel_id=1, source_target_pairs={{0,8},{8,16},{16,24},{1,9},{9,17},{17,25},{2,10},{10,18},{18,26},{... | collective-permute-start | bytes 2359304 | tf_op jit(solution)/shard_map/ppermute | solution.py:469
  1047.4 32.5 %collective-permute-start.83 = (bf16[512,768]{1,0:T(8,128)(2,1)S(1)}, bf16[512,768]{1,0:T(8,128)(2,1)S(1)}, u32[]{:S(2)}, u32[]{:S(2)}) collective-permute-start(bf16[512,768]{1,0:T(8,128)(2,1)S(1)} %collective-permute-done.82), channel_id=1, source_target_pairs={{8,0},{16,8},{24,16},{9,1},{17,9},{25,17},{10,2},{18,10},{26,18},{... | collective-permute-start | bytes 2359304 | tf_op jit(solution)/shard_map/ppermute | solution.py:470
  1048.7 32.5 %collective-permute-start.87 = (bf16[4,24,3456]{2,1,0:T(8,128)(2,1)S(1)}, bf16[4,24,3456]{2,1,0:T(8,128)(2,1)S(1)}, u32[]{:S(2)}, u32[]{:S(2)}) collective-permute-start(bf16[4,24,3456]{2,1,0:T(8,128)(2,1)S(1)} %dynamic-slice_bitcast_fusion.8), channel_id=1, source_target_pairs={{0,4},{4,0},{1,5},{5,1},{2,6},{6,2},{3,7},{7,3},{8,12},{12,8},{9,1... | collective-permute-start | bytes 1990664 | tf_op jit(solution)/shard_map/ppermute | solution.py:415
  1075.5 27.3 %collective-permute-start.86 = (bf16[512,768]{1,0:T(8,128)(2,1)S(1)}, bf16[512,768]{1,0:T(8,128)(2,1)S(1)}, u32[]{:S(2)}, u32[]{:S(2)}) collective-permute-start(bf16[512,768]{1,0:T(8,128)(2,1)S(1)} %collective-permute-done.85), channel_id=1, source_target_pairs={{0,8},{8,16},{16,24},{1,9},{9,17},{17,25},{2,10},{10,18},{18,26},{... | collective-permute-start | bytes 2359304 | tf_op jit(solution)/shard_map/ppermute | solution.py:469
  1079.9 26.8 %collective-permute-start.84 = (bf16[512,768]{1,0:T(8,128)(2,1)S(1)}, bf16[512,768]{1,0:T(8,128)(2,1)S(1)}, u32[]{:S(2)}, u32[]{:S(2)}) collective-permute-start(bf16[512,768]{1,0:T(8,128)(2,1)S(1)} %collective-permute-done.83), channel_id=1, source_target_pairs={{8,0},{16,8},{24,16},{9,1},{17,9},{25,17},{10,2},{18,10},{26,18},{... | collective-permute-start | bytes 2359304 | tf_op jit(solution)/shard_map/ppermute | solution.py:470
  1133.5 67.8 %collective-permute-start.90 = (bf16[4032,768]{1,0:T(8,128)(2,1)}, bf16[4032,768]{1,0:T(8,128)(2,1)}, u32[]{:S(2)}, u32[]{:S(2)}) collective-permute-start(bf16[4032,768]{1,0:T(8,128)(2,1)} %shard_map.473), channel_id=1, source_target_pairs={{0,2},{2,0},{1,3},{3,1},{4,6},{6,4},{5,7},{7,5},{8,10},{10,8},{9,1... | collective-permute-start | bytes 18579464 | tf_op jit(solution)/shard_map/ppermute | solution.py:415
  1229.6 43.8 %collective-permute-start.111 = (bf16[4,2,24,1280]{3,2,1,0:T(8,128)(2,1)}, bf16[4,2,24,1280]{3,2,1,0:T(8,128)(2,1)S(1)}, u32[]{:S(2)}, u32[]{:S(2)}) collective-permute-start(bf16[4,2,24,1280]{3,2,1,0:T(8,128)(2,1)} %bitcast.580), channel_id=1, source_target_pairs={{0,4},{4,0},{1,5},{5,1},{2,6},{6,2},{3,7},{7,3},{8,12},{12,8},{9,1... | collective-permute-start | bytes 1474568 | tf_op jit(solution)/shard_map/ppermute | solution.py:415
  1230.7 40.8 %collective-permute-start.106 = (bf16[4,2,24,1152]{3,2,1,0:T(8,128)(2,1)S(1)}, bf16[4,2,24,1152]{3,2,1,0:T(8,128)(2,1)S(1)}, u32[]{:S(2)}, u32[]{:S(2)}) collective-permute-start(bf16[4,2,24,1152]{3,2,1,0:T(8,128)(2,1)S(1)} %dynamic-slice_bitcast_fusion.10), channel_id=1, source_target_pairs={{0,1},{1,0},{2,3},{3,2},{4,5},{5,4},{6,7},{7,6},{8,9},{9,8},{10,11... | collective-permute-start | bytes 1327112 | tf_op jit(solution)/shard_map/ppermute | solution.py:415
  1262.0 81.7 %collective-permute-start.95 = (bf16[1008,768]{1,0:T(8,128)(2,1)}, bf16[1008,768]{1,0:T(8,128)(2,1)}, u32[]{:S(2)}, u32[]{:S(2)}) collective-permute-start(bf16[1008,768]{1,0:T(8,128)(2,1)} %pad_maximum_fusion.4), channel_id=1, source_target_pairs={{0,1},{1,0},{2,3},{3,2},{4,5},{5,4},{6,7},{7,6},{8,9},{9,8},{10,11... | collective-permute-start | bytes 4644872 | tf_op jit(solution)/shard_map/ppermute | solution.py:415
  1267.9 75.7 %collective-permute-start.96 = (bf16[1008,768]{1,0:T(8,128)(2,1)}, bf16[1008,768]{1,0:T(8,128)(2,1)}, u32[]{:S(2)}, u32[]{:S(2)}) collective-permute-start(bf16[1008,768]{1,0:T(8,128)(2,1)} %pad_maximum_fusion.5), channel_id=1, source_target_pairs={{0,4},{4,0},{1,5},{5,1},{2,6},{6,2},{3,7},{7,3},{8,12},{12,8},{9,1... | collective-permute-start | bytes 4644872 | tf_op jit(solution)/shard_map/ppermute | solution.py:415
  1272.4 34.4 %collective-permute-start.107 = (bf16[4,24,1152]{2,1,0:T(8,128)(2,1)S(1)}, bf16[4,24,1152]{2,1,0:T(8,128)(2,1)S(1)}, u32[]{:S(2)}, u32[]{:S(2)}) collective-permute-start(bf16[4,24,1152]{2,1,0:T(8,128)(2,1)S(1)} %dynamic-slice_bitcast_fusion.23), channel_id=1, source_target_pairs={{0,4},{4,0},{1,5},{5,1},{2,6},{6,2},{3,7},{7,3},{8,12},{12,8},{9,1... | collective-permute-start | bytes 663560 | tf_op jit(solution)/shard_map/ppermute | solution.py:415
  1282.2 30.8 %collective-permute-start.112 = (bf16[4,24,1280]{2,1,0:T(8,128)(2,1)}, bf16[4,24,1280]{2,1,0:T(8,128)(2,1)}, u32[]{:S(2)}, u32[]{:S(2)}) collective-permute-start(bf16[4,24,1280]{2,1,0:T(8,128)(2,1)} %bitcast.218), channel_id=1, source_target_pairs={{0,1},{1,0},{2,3},{3,2},{4,5},{5,4},{6,7},{7,6},{8,9},{9,8},{10,11... | collective-permute-start | bytes 737288 | tf_op jit(solution)/shard_map/ppermute | solution.py:415
  (266 other events, 3583.2 us)
Sparse Core Ops, SparseCore 0:
  20.0 134.3 all-gather.4
  157.9 99.4 all-gather.6
  349.8 81.4 all-gather.8
  449.3 95.3 all-gather.10
  781.1 117.2 reduce-scatter.4
  947.8 149.9 reduce-scatter.6

commit v8 on v7

--- a/solution.py
+++ b/solution.py
@@ -504,24 +504,25 @@
 
 
 def plane_scatter(pairs, rows, before, after):
-    pairs, before = lax.optimization_barrier((pairs, before))
     count = lax.axis_size(PLANE)
     if lax.axis_size("p") != 2:
         placed = place_rows(pairs, 0, count, rows)
         placed = lax.psum_scatter(placed, PLANE, scatter_dimension=0, tiled=True)
-        return placed.astype(f32), before, after
+        return placed.astype(f32), after(after(before))
+    pairs, before = lax.optimization_barrier((pairs, before))
     away = swap_core(place_rows(pairs, 4, 4, rows))
+    pairs, sums = lax.optimization_barrier((pairs, after(before)))
     home = place_rows(pairs, 0, 4, rows)
     half = rows // 2
     part = lambda first, last: add16(home[first:last], away[first:last])
-    got_low = swap(part(3 * rows, 3 * rows + half), "seq")
-    got_high = swap(part(3 * rows + half, 4 * rows), "p")
-    got_low, got_high, after = lax.optimization_barrier((got_low, got_high, after))
+    far_low, far_high = part(3 * rows, 3 * rows + half), part(3 * rows + half, 4 * rows)
+    far_low, far_high, sums = lax.optimization_barrier((far_low, far_high, after(sums)))
+    got_low, got_high = swap(far_low, "seq"), swap(far_high, "p")
     seq_high = add16(part(rows + half, 2 * rows), got_high)
     p_low = add16(part(2 * rows, 2 * rows + half), got_low)
     from_seq = swap(jnp.concatenate([part(rows, rows + half), seq_high]), "seq")
     from_p = swap(jnp.concatenate([p_low, part(2 * rows + half, 3 * rows)]), "p")
-    return part(0, rows).astype(f32) + from_seq.astype(f32) + from_p.astype(f32), before, after
+    return part(0, rows).astype(f32) + from_seq.astype(f32) + from_p.astype(f32), sums
 
 
 def add_logs(left, right):
@@ -702,6 +703,12 @@
     got = jnp.take(plane_table, jnp.concatenate(places), axis=0, mode="clip")
     looked = line_scatter(jnp.split(got, len(places)), "z", beside)
     enc_fo, gain, enc_x8, dec_x8, enc_picks, dec_picks = held
+    ffn_cast, dec_pack, looked = lax.optimization_barrier((ffn_cast, dec_pack, looked))
+    ffn_pack = lax.all_gather(ffn_cast, ALL, axis=0, tiled=True)
+    dec_wi, cross_wi = cut(dec_pack, 0, 3 * D), cut(dec_pack, 3 * D, 3 * D)
+    dec_wo, cross_wo = cut(dec_pack, 6 * D, D), cut(dec_pack, 7 * D, D)
+    dec_fi = cut(ffn_pack, 0, 2 * FF)
+    dec_fo = cut(ffn_pack, 2 * FF, FF).reshape(FF, D)
     enc_x0, dec_y0 = looked[:enc_count], looked[enc_count:]
 
     col, line = (lambda v: v[:, None]), (lambda v: v[None, :])
@@ -723,12 +730,6 @@
     enc_kv = project(enc_n1, enc_wi[:, D:]).astype(bf16)
     enc_kv2 = swap_core(enc_kv)
     enc_ob, enc_lse = attend_forward(enc_q, enc_kv, enc_kv2, enc_info, enc_x8, False)
-    ffn_cast, dec_pack, enc_ob = lax.optimization_barrier((ffn_cast, dec_pack, enc_ob))
-    ffn_pack = lax.all_gather(ffn_cast, ALL, axis=0, tiled=True)
-    dec_wi, cross_wi = cut(dec_pack, 0, 3 * D), cut(dec_pack, 3 * D, 3 * D)
-    dec_wo, cross_wo = cut(dec_pack, 6 * D, D), cut(dec_pack, 7 * D, D)
-    dec_fi = cut(ffn_pack, 0, 2 * FF)
-    dec_fo = cut(ffn_pack, 2 * FF, FF).reshape(FF, D)
     enc_x1 = enc_x0 + project(enc_ob, enc_wo)
     enc_x2, enc_saved = ffn_forward(enc_x1, gain[1], enc_fi, enc_fo)
     enc_out = rms_scale(enc_x2, gain[2]).astype(bf16)
@@ -878,23 +879,32 @@
     d_misc = jnp.pad(jnp.concatenate([d_gains.T, d_rel], axis=1), ((0, 0), (0, 120)))
     d_last = jnp.concatenate([d_enc_wi.astype(bf16), d_misc.astype(bf16)], axis=1)
     last = [scatter_core(d_last[:, :1152]), scatter_core(d_last[:, 1152:])]
-    input_embed, late, (last, enc_sums) = plane_scatter(pairs, padded, late, (last, enc_sums))
+
+    def beside_place(sums):
+        if len(sums) == 3:
+            late, last, enc_sums = sums
+            last = [scatter_first(item, number == 0) for number, item in enumerate(last)]
+            wide = jnp.concatenate(enc_sums[:2], axis=2)
+            return late, last, [scatter_last(wide), scatter_last(enc_sums[2])], None
+        late, last, enc_sums, _ = sums
+        return late, [scatter_second(item, not number) for number, item in enumerate(last)], enc_sums
+
+    input_embed, (late, last, (g_wide, g_fo)) = plane_scatter(
+        pairs, padded, (late, last, enc_sums), beside_place
+    )
     late = late.astype(f32)
     grad_embed = head_embed[:shard] + input_embed[:shard]
 
-    last = [scatter_rest(item, number == 0) for number, item in enumerate(last)]
-    g_low, g_high, g_fo = [scatter_last(item) for item in enc_sums]
+    last = [scatter_last(item) for item in last]
     squares = sum(
-        (jnp.sum(item * item) for item in (grad_embed, early, late, g_low, g_high, g_fo, g_dec_fo, *last))
+        (jnp.sum(item * item) for item in (grad_embed, early, late, g_wide, g_fo, g_dec_fo, *last))
     )
     sums = fold_all(jnp.stack([jnp.sum(mask), loss_local, squares]), jnp.add)
     last = jnp.concatenate(last, axis=1)
     owned = (
         jnp.stack([cut(last, 0, 3 * D), cut(late, 0, 3 * D), cut(late, 3 * D, 3 * D)]),
-        jnp.stack([cut(g_high, 640, D), cut(late, 6 * D, D), cut(late, 7 * D, D)]),
-        jnp.stack(
-            [jnp.concatenate([g_low, cut(g_high, 0, 640)], axis=1), early]
-        ),
+        jnp.stack([cut(g_wide, 2 * FF, D), cut(late, 6 * D, D), cut(late, 7 * D, D)]),
+        jnp.stack([cut(g_wide, 0, 2 * FF), early]),
         jnp.stack([g_fo, g_dec_fo]),
         last[:, 3 * D + 7].reshape(2, -1),
         last[:, 3 * D : 3 * D + 7].T,

time: 1430 us -> 1400 us (0.979)
  waiting for transfers between devices: 439 us -> 389 us
  other arithmetic: 147 us -> 164 us
    ppermute x9, waiting for transfers between devices: 62.8 us -> 15.2 us  [line_gather(): lax.ppermute(ups[-1], axis, [(i, i + 1) for i in range(size - 1)])]
    all_gather x1, waiting for transfers between devices: 19.7 us -> 0.02 us  [body(): ffn_pack = lax.all_gather(ffn_cast, ALL, axis=0, tiled=True)]
    ppermute x50, waiting for transfers between devices: 125 us -> 140 us  [swap(): return lax.ppermute(value, axis, [(0, 1), (1, 0)])]
    unnamed x399 -> x416, local copies, waits for them, and re-layouts: 50.6 us -> 42.2 us
    ppermute x30 -> x27, waiting for transfers between devices: 38.3 us -> 35.3 us  [scatter_last(): got = lax.ppermute(send, 'z', [(i, (i + hop) % size) for i in range(size)])]
    ppermute x30 -> x27, starting transfers between devices: 47.4 us -> 49 us  [scatter_last(): got = lax.ppermute(send, 'z', [(i, (i + hop) % size) for i in range(size)])]
  transfers between devices with their start and end apart: 127 -> 124, of which waited for: 52 -> 50; matrix products, arithmetic and copies ran while one was open for 25% -> 27% of each run, Pallas kernels for 13% -> 13%
where the time goes in v8:
time: 1400 us; the launch traced here: 1380 us
  waiting for transfers between devices  389 us (28%)
  Pallas kernels  278 us (20%)
  starting transfers between devices  203 us (14%)
  local copies, waits for them, and re-layouts  185 us (13%)
  other arithmetic  164 us (12%)
  matrix products  134 us (10%)
  between operations  30.8 us (2%)
    ppermute x50, waiting for transfers between devices, swap(): return lax.ppermute(value, axis, [(0, 1), (1, 0)])  140 us
    pallas_call x3, Pallas kernels, attend_backward(): pl.pallas_call(functools.partial(attend_backward_kernel, cfg), grid=(HEAD...  87.7 us
    all_gather x1, waiting for transfers between devices, body(): hidden_all = lax.all_gather(hidden_b, ALL, axis=0, tiled=True)  76.9 us
    ppermute x3, waiting for transfers between devices, line_scatter(): up = lax.ppermute(send_up, axis, [(i, i + 1) for i in range(step)])  66.5 us
    pallas_call x4, Pallas kernels, head_grad(): pl.pallas_call(functools.partial(head_grad_kernel, count), grid_spec=pltp...  63.7 us
    ppermute x50, starting transfers between devices, swap(): return lax.ppermute(value, axis, [(0, 1), (1, 0)])  59.1 us
    pallas_call x3, Pallas kernels, attend_forward(): pl.pallas_call(functools.partial(attend_forward_kernel, cfg), grid=(HEADS...  54.1 us
    convert_element_type x32, other arithmetic, add16(): return (left.astype(f32) + right.astype(f32)).astype(bf16)  54 us
  transfers between devices with their start and end apart: 124, of which 50 were waited for; matrix products, arithmetic and copies ran while one was open for 27% of the time, Pallas kernels for 13%

profile of v8, /device:TPU:0, one launch (start us, length us, event | category | flops | bytes accessed | tf_op | source)
XLA Modules:
  0.0 1383.1 jit_solution(3000710817302775797)
XLA Ops:
  49.5 21.3 %collective-permute-done.1 = bf16[1008,768]{1,0:T(8,128)(2,1)S(1)} collective-permute-done((bf16[1008,768]{1,0:T(8,128)(2,1)}, bf16[1008,768]{1,0:T(8,128)(2,1)S(1)}, u32[]{:S(2)}, u32[]{:S(2)}) %collective-permute-start.1) | collective-permute-done | bytes 1548320 | tf_op jit(solution)/shard_map/ppermute | solution.py:415
  70.7 19.0 %collective-permute-start.6 = (bf16[1008,768]{1,0:T(8,128)(2,1)S(1)}, bf16[1008,768]{1,0:T(8,128)(2,1)}, u32[]{:S(2)}, u32[]{:S(2)}) collective-permute-start(bf16[1008,768]{1,0:T(8,128)(2,1)S(1)} %collective-permute-done.1), channel_id=1, source_target_pairs={{0,2},{2,0},{1,3},{3,1},{4,6},{6,4},{5,7},{7,5},{8,10},{10,8},{9,1... | collective-permute-start | bytes 4644872 | tf_op jit(solution)/shard_map/ppermute | solution.py:415
  94.4 31.8 %collective-permute-done.3 = bf16[504,768]{1,0:T(8,128)(2,1)S(1)} collective-permute-done((bf16[504,768]{1,0:T(8,128)(2,1)S(1)}, bf16[504,768]{1,0:T(8,128)(2,1)S(1)}, u32[]{:S(2)}, u32[]{:S(2)}) %collective-permute-start.3) | collective-permute-done | bytes 774176 | tf_op jit(solution)/shard_map/ppermute | solution.py:415
  140.0 14.5 %all-gather.5.cloned.1.call-done = bf16[768,9344]{1,0:T(8,128)(2,1)} async-done(((bf16[24,9344]{1,0:T(8,128)(2,1)}), bf16[768,9344]{1,0:T(8,128)(2,1)}) %all-gather.5.cloned.1.call-update) | async-done | bytes 14352400 | tf_op jit(solution)/shard_map/all_gather | solution.py:617
  159.8 20.8 %gather_fusion = bf16[3072,768]{1,0:T(8,128)(2,1)} fusion(bf16[8064,768]{1,0:T(8,128)(2,1)} %constant_dynamic-update-slice_fusion.4, s32[3072]{0:T(1024)S(1)} %add_clamp_fusion), kind=kCustom, calls=%fused_computation | custom fusion | bytes 9449472 | tf_op jit(solution)/shard_map/jit(_take)/gather | solution.py:703
  196.8 30.5 %collective-permute-done.16 = bf16[768,768]{1,0:T(8,128)(2,1)S(1)} collective-permute-done((bf16[768,768]{1,0:T(8,128)(2,1)}, bf16[768,768]{1,0:T(8,128)(2,1)S(1)}, u32[]{:S(2)}, u32[]{:S(2)}) %collective-permute-start.16) | collective-permute-done | bytes 1179680 | tf_op jit(solution)/shard_map/ppermute | solution.py:482
  230.6 5.6 collective-permute-start.17
  257.5 14.1 %collective-permute-done.17 = bf16[768,768]{1,0:T(8,128)(2,1)} collective-permute-done((bf16[768,768]{1,0:T(8,128)(2,1)}, bf16[768,768]{1,0:T(8,128)(2,1)}, u32[]{:S(2)}, u32[]{:S(2)}) %collective-permute-start.17) | collective-permute-done | bytes 1179680 | tf_op jit(solution)/shard_map/ppermute | solution.py:482
  274.1 5.4 collective-permute-start.20
  281.6 21.9 %collective-permute-done.20 = bf16[768,768]{1,0:T(8,128)(2,1)} collective-permute-done((bf16[768,768]{1,0:T(8,128)(2,1)S(1)}, bf16[768,768]{1,0:T(8,128)(2,1)}, u32[]{:S(2)}, u32[]{:S(2)}) %collective-permute-start.20) | collective-permute-done | bytes 1179680 | tf_op jit(solution)/shard_map/ppermute | solution.py:482
  303.5 5.3 collective-permute-done.21
  327.2 29.1 %shard_map.462 = (bf16[512,768]{1,0:T(8,128)(2,1)}, f32[512,768]{1,0:T(8,128)}) custom-call(bf16[512,768]{1,0:T(8,128)(2,1)} %convolution_convert_fusion.15.refs_0_, bf16[512,1536]{1,0:T(8,128)(2,1)} %convolution_convert_fusion.8.refs_1_.refs_2_, bf16[512,1536]{1,0:T(8,128)(2,1)} %convolution_convert_fusion.8.refs_1_.refs_2_, ...), custom_call_target="tpu_custom_call" | custom-call | flops 2 | bytes 512 | tf_op jit(solution)/shard_map/pallas_call | solution.py:200
  358.8 6.9 fusion.7
  382.9 13.2 shard_map.461
  401.0 11.8 shard_map.463
  452.0 76.9 %all-gather.11.cloned.1.call-done = bf16[8192,768]{1,0:T(8,128)(2,1)} async-done(((bf16[256,768]{1,0:T(8,128)(2,1)}), bf16[8192,768]{1,0:T(8,128)(2,1)}) %all-gather.11.cloned.1.call-update) | async-done | bytes 12582928 | tf_op jit(solution)/shard_map/all_gather | solution.py:753
  528.9 25.6 %shard_map.464 = (f32[1,8192]{1,0:T(1,128)}, f32[1,8192]{1,0:T(1,128)}) custom-call(bf16[8,2,2,256,768]{4,3,2,1,0:T(8,128)(2,1)} %bitcast.631, bf16[1008,768]{1,0:T(8,128)(2,1)} %get-tuple-element.559.tab, s32[1,8192]{1,0:T(1,128)} %bitcast.590), custom_call_target="tpu_custom_call" | custom-call | flops 12683575296 | bytes 12582912 | tf_op jit(solution)/shard_map/pallas_call | solution.py:306
  576.5 15.8 %shard_map.465 = (bf16[8,2,64,768]{3,2,1,0:T(8,128)(2,1)}, bf16[8,2,64,768]{3,2,1,0:T(8,128)(2,1)}, f32[1008,768]{1,0:T(8,128)}) custom-call(s32[1]{0:T(128)} %bitcast.97.core, bf16[8,2,2,256,768]{4,3,2,1,0:T(8,128)(2,1)} %bitcast.632, bf16[1008,768]{1,0:T(8,128)(2,1)} %get-tuple-element.559.tab, s32[1,8192]{1,0:T(1,128)} %bitcast.591, f32[1,8192]{1,0:T(1,128)} %bitcast.569, ...), custom_call_target="tpu_custom_call" | custom-call | flops 9512681472 | bytes 6291456 | tf_op jit(solution)/shard_map/pallas_call | solution.py:329
  592.3 15.8 %shard_map.467 = (bf16[8,2,64,768]{3,2,1,0:T(8,128)(2,1)}, bf16[8,2,64,768]{3,2,1,0:T(8,128)(2,1)}, f32[1008,768]{1,0:T(8,128)}) custom-call(s32[1]{0:T(128)} %bitcast.97.core, bf16[8,2,2,256,768]{4,3,2,1,0:T(8,128)(2,1)} %bitcast.633, bf16[1008,768]{1,0:T(8,128)(2,1)} %get-tuple-element.559.tab, s32[1,8192]{1,0:T(1,128)} %bitcast.592, f32[1,8192]{1,0:T(1,128)} %bitcast.570, ...), custom_call_target="tpu_custom_call" | custom-call | flops 9512681472 | bytes 6291456 | tf_op jit(solution)/shard_map/pallas_call | solution.py:329
  608.7 15.8 %shard_map.466 = (bf16[8,2,64,768]{3,2,1,0:T(8,128)(2,1)}, bf16[8,2,64,768]{3,2,1,0:T(8,128)(2,1)}, f32[1008,768]{1,0:T(8,128)}) custom-call(s32[1]{0:T(128)} %bitcast.98.core, bf16[8,2,2,256,768]{4,3,2,1,0:T(8,128)(2,1)} %bitcast.634, bf16[1008,768]{1,0:T(8,128)(2,1)} %get-tuple-element.559.tab, s32[1,8192]{1,0:T(1,128)} %bitcast.593, f32[1,8192]{1,0:T(1,128)} %bitcast.571, ...), custom_call_target="tpu_custom_call" | custom-call | flops 9512681472 | bytes 6291456 | tf_op jit(solution)/shard_map/pallas_call | solution.py:329
  625.1 16.2 %shard_map.468 = (bf16[8,2,64,768]{3,2,1,0:T(8,128)(2,1)}, bf16[8,2,64,768]{3,2,1,0:T(8,128)(2,1)}, f32[1008,768]{1,0:T(8,128)}) custom-call(s32[1]{0:T(128)} %bitcast.98.core, bf16[8,2,2,256,768]{4,3,2,1,0:T(8,128)(2,1)} %bitcast.635, bf16[1008,768]{1,0:T(8,128)(2,1)} %get-tuple-element.559.tab, s32[1,8192]{1,0:T(1,128)} %bitcast.594, f32[1,8192]{1,0:T(1,128)} %bitcast.572, ...), custom_call_target="tpu_custom_call" | custom-call | flops 9512681472 | bytes 6291456 | tf_op jit(solution)/shard_map/pallas_call | solution.py:329
  650.6 13.3 collective-permute-done.37
  667.5 13.2 collective-permute-done.49
  684.4 7.0 collective-permute-done.38
  720.3 5.0 collective-permute-done.58
  735.0 6.8 multiply_reduce_fusion.12
  745.6 16.6 %shard_map.469 = (bf16[256,768]{1,0:T(8,128)(2,1)}, f32[2,512,768]{2,1,0:T(8,128)}, bf16[2,512,768]{2,1,0:T(8,128)(2,1)}) custom-call(bf16[256,768]{1,0:T(8,128)(2,1)} %convolution_convert_fusion.18.refs_0_, bf16[512,1536]{1,0:T(8,128)(2,1)} %convolution_convert_fusion.7.refs_1_.refs_2_, bf16[512,1536]{1,0:T(8,128)(2,1)} %convolution_convert_fusion.7.refs_1_.refs_2_, ...), custom_call_target="tpu_custom_call" | custom-call | flops 5 | bytes 256 | tf_op jit(solution)/shard_map/pallas_call | solution.py:227
  793.4 22.8 %shard_map.470 = (bf16[256,768]{1,0:T(8,128)(2,1)}, f32[2,256,768]{2,1,0:T(8,128)}, bf16[2,256,768]{2,1,0:T(8,128)(2,1)}, f32[12,2,8,512]{3,2,1,0:T(8,128)}) custom-call(bf16[256,768]{1,0:T(8,128)(2,1)} %convolution_convert_fusion.19.refs_0_, bf16[256,1536]{1,0:T(8,128)(2,1)} %copy-done.5, bf16[256,1536]{1,0:T(8,128)(2,1)} %copy-done.5, ...), custom_call_target="tpu_custom_call" | custom-call | flops 5 | bytes 256 | tf_op jit(solution)/shard_map/pallas_call | solution.py:227
  816.3 8.4 fusion.59
  826.7 5.8 convolution_convert_fusion
  833.4 12.2 multiply_reduce_fusion.3
  862.1 5.2 collective-permute-start.64
  951.1 48.2 %shard_map.471 = (bf16[512,768]{1,0:T(8,128)(2,1)}, f32[2,512,768]{2,1,0:T(8,128)}, bf16[2,512,768]{2,1,0:T(8,128)(2,1)}, f32[12,4,8,768]{3,2,1,0:T(8,128)}) custom-call(bf16[512,768]{1,0:T(8,128)(2,1)} %convolution_convert_fusion.15.refs_0_, bf16[512,1536]{1,0:T(8,128)(2,1)} %convolution_convert_fusion.8.refs_1_.refs_2_, ...), custom_call_target="tpu_custom_call" | custom-call | flops 5 | bytes 512 | tf_op jit(solution)/shard_map/pallas_call | solution.py:227
  1011.2 21.2 %collective-permute-done.77 = bf16[4,2,64,768]{3,2,0,1:T(8,128)(2,1)} collective-permute-done((bf16[4,2,64,768]{3,2,0,1:T(8,128)(2,1)}, bf16[4,2,64,768]{3,2,0,1:T(8,128)(2,1)}, u32[]{:S(2)}, u32[]{:S(2)}) %collective-permute-start.77) | collective-permute-done | bytes 786464 | tf_op jit(solution)/shard_map/ppermute | solution.py:415
  1061.2 5.0 copy.745
  1066.2 10.0 collective-permute-done.88
  1081.6 5.5 collective-permute-start.85
  1110.4 7.7 fusion
  1133.8 23.7 %shard_map.473 = bf16[4032,768]{1,0:T(8,128)(2,1)} custom-call(s32[1,512]{1,0:T(1,128)} %bitcast.601, bf16[512,768]{1,0:T(8,128)(2,1)} %fusion.47.refs_1_, s32[1,512]{1,0:T(1,128)} %bitcast.599, bf16[512,768]{1,0:T(8,128)(2,1)} %add.1323.refs_3_, s32[1,512]{1,0:T(1,128)} %bitcast.597, bf16[512,768]{1,0:T(8,128)(2,1)} %add.1324.refs_5_, s32[1,512]{1,0:T(1,128)} %bitcast.595, ...), custom_call_target="tpu_custom_call" | custom-call | flops 1 | bytes 1008 | tf_op jit(solution)/shard_map/pallas_call | solution.py:374
  1184.4 8.9 collective-permute-done.95
  1205.9 23.7 %shard_map.472 = bf16[4032,768]{1,0:T(8,128)(2,1)} custom-call(s32[1,512]{1,0:T(1,128)} %bitcast.602, bf16[512,768]{1,0:T(8,128)(2,1)} %fusion.47.refs_1_, s32[1,512]{1,0:T(1,128)} %bitcast.600, bf16[512,768]{1,0:T(8,128)(2,1)} %add.1323.refs_3_, s32[1,512]{1,0:T(1,128)} %bitcast.598, bf16[512,768]{1,0:T(8,128)(2,1)} %add.1324.refs_5_, s32[1,512]{1,0:T(1,128)} %bitcast.596, ...), custom_call_target="tpu_custom_call" | custom-call | flops 1 | bytes 1008 | tf_op jit(solution)/shard_map/pallas_call | solution.py:374
  1242.8 7.3 collective-permute-start.107
  1259.5 12.7 collective-permute-done.103
  1293.5 6.2 collective-permute-done.110
  1299.7 9.3 collective-permute-done.111
  1314.7 8.5 multiply_reduce_fusion.1
  1338.7 6.6 collective-permute-start.116
  1358.7 8.3 add_subtract_fusion
  (1018 shorter events, 605.7 us)
Async XLA Ops:
  7.2 147.2 %all-gather.5.cloned.1.call-start = ((), (), s32[]{:S(2)}) async-start(), calls=%async_computation.2 | async-start | bytes 14800896 | tf_op jit(solution)/shard_map/all_gather | solution.py:617
  19.9 291.3 %all-gather.7.cloned.1.call-start = ((), (), s32[]{:S(2)}) async-start(), calls=%async_computation.3 | async-start | bytes 9732096 | tf_op jit(solution)/shard_map/all_gather | solution.py:680
  22.1 48.7 %collective-permute-start.1 = (bf16[1008,768]{1,0:T(8,128)(2,1)}, bf16[1008,768]{1,0:T(8,128)(2,1)S(1)}, u32[]{:S(2)}, u32[]{:S(2)}) collective-permute-start(bf16[1008,768]{1,0:T(8,128)(2,1)} %get-tuple-element.559.tab), channel_id=1, source_target_pairs={{0,1},{1,0},{2,3},{3,2},{4,5},{5,4},{6,7},{7,6},{8,9},{9,8},{10,11... | collective-permute-start | bytes 4644872 | tf_op jit(solution)/shard_map/ppermute | solution.py:415
  25.0 64.7 %collective-permute-start.2 = (bf16[1008,768]{1,0:T(8,128)(2,1)}, bf16[1008,768]{1,0:T(8,128)(2,1)S(1)}, u32[]{:S(2)}, u32[]{:S(2)}) collective-permute-start(bf16[1008,768]{1,0:T(8,128)(2,1)} %get-tuple-element.559.tab), channel_id=1, source_target_pairs={{0,4},{4,0},{1,5},{5,1},{2,6},{6,2},{3,7},{7,3},{8,12},{12,8},{9,1... | collective-permute-start | bytes 4644872 | tf_op jit(solution)/shard_map/ppermute | solution.py:415
  26.5 103.5 %collective-permute-start.5 = (bf16[1008,768]{1,0:T(8,128)(2,1)}, bf16[1008,768]{1,0:T(8,128)(2,1)}, u32[]{:S(2)}, u32[]{:S(2)}) collective-permute-start(bf16[1008,768]{1,0:T(8,128)(2,1)} %get-tuple-element.559.tab), channel_id=1, source_target_pairs={{0,2},{2,0},{1,3},{3,1},{4,6},{6,4},{5,7},{7,5},{8,10},{10,8},{9,1... | collective-permute-start | bytes 4644872 | tf_op jit(solution)/shard_map/ppermute | solution.py:415
  43.6 46.4 %collective-permute-start.13 = (s32[768]{0:T(1024)S(1)}, s32[768]{0:T(1024)S(1)}, u32[]{:S(2)}, u32[]{:S(2)}) collective-permute-start(s32[768]{0:T(1024)S(1)} %collective-permute-done.12), channel_id=1, source_target_pairs={{8,0},{16,8},{24,16},{9,1},{17,9},{25,17},{10,2},{18,10},{26,18},{... | collective-permute-start | bytes 9224 | tf_op jit(solution)/shard_map/ppermute | solution.py:470
  44.9 46.5 %collective-permute-start.15 = (s32[768]{0:T(1024)S(1)}, s32[768]{0:T(1024)S(1)}, u32[]{:S(2)}, u32[]{:S(2)}) collective-permute-start(s32[768]{0:T(1024)S(1)} %collective-permute-done.14), channel_id=1, source_target_pairs={{0,8},{8,16},{16,24},{1,9},{9,17},{17,25},{2,10},{10,18},{18,26},{... | collective-permute-start | bytes 9224 | tf_op jit(solution)/shard_map/ppermute | solution.py:469
  70.7 62.0 %collective-permute-start.6 = (bf16[1008,768]{1,0:T(8,128)(2,1)S(1)}, bf16[1008,768]{1,0:T(8,128)(2,1)}, u32[]{:S(2)}, u32[]{:S(2)}) collective-permute-start(bf16[1008,768]{1,0:T(8,128)(2,1)S(1)} %collective-permute-done.1), channel_id=1, source_target_pairs={{0,2},{2,0},{1,3},{3,1},{4,6},{6,4},{5,7},{7,5},{8,10},{10,8},{9,1... | collective-permute-start | bytes 4644872 | tf_op jit(solution)/shard_map/ppermute | solution.py:415
  89.7 45.7 %collective-permute-start.7 = (bf16[1008,768]{1,0:T(8,128)(2,1)S(1)}, bf16[1008,768]{1,0:T(8,128)(2,1)}, u32[]{:S(2)}, u32[]{:S(2)}) collective-permute-start(bf16[1008,768]{1,0:T(8,128)(2,1)S(1)} %collective-permute-done.2), channel_id=1, source_target_pairs={{0,2},{2,0},{1,3},{3,1},{4,6},{6,4},{5,7},{7,5},{8,10},{10,8},{9,1... | collective-permute-start | bytes 4644872 | tf_op jit(solution)/shard_map/ppermute | solution.py:415
  90.0 36.3 %collective-permute-start.3 = (bf16[504,768]{1,0:T(8,128)(2,1)S(1)}, bf16[504,768]{1,0:T(8,128)(2,1)S(1)}, u32[]{:S(2)}, u32[]{:S(2)}) collective-permute-start(bf16[504,768]{1,0:T(8,128)(2,1)S(1)} %slice.616), channel_id=1, source_target_pairs={{0,1},{1,0},{2,3},{3,2},{4,5},{5,4},{6,7},{7,6},{8,9},{9,8},{10,11... | collective-permute-start | bytes 2322440 | tf_op jit(solution)/shard_map/ppermute | solution.py:415
  91.4 36.2 %collective-permute-start.4 = (bf16[504,768]{1,0:T(8,128)(2,1)S(1)}, bf16[504,768]{1,0:T(8,128)(2,1)S(1)}, u32[]{:S(2)}, u32[]{:S(2)}) collective-permute-start(bf16[504,768]{1,0:T(8,128)(2,1)S(1)} %slice.617), channel_id=1, source_target_pairs={{0,4},{4,0},{1,5},{5,1},{2,6},{6,2},{3,7},{7,3},{8,12},{12,8},{9,1... | collective-permute-start | bytes 2322440 | tf_op jit(solution)/shard_map/ppermute | solution.py:415
  154.5 260.3 %all-gather.9.cloned.1.call-start = ((), (), s32[]{:S(2)}) async-start(), calls=%async_computation.4 | async-start | bytes 9732096 | tf_op jit(solution)/shard_map/all_gather | solution.py:707
  183.4 43.9 %collective-permute-start.16 = (bf16[768,768]{1,0:T(8,128)(2,1)}, bf16[768,768]{1,0:T(8,128)(2,1)S(1)}, u32[]{:S(2)}, u32[]{:S(2)}) collective-permute-start(bf16[768,768]{1,0:T(8,128)(2,1)} %get-tuple-element.530), channel_id=1, source_target_pairs={{0,8},{1,9},{2,10},{3,11},{4,12},{5,13},{6,14},{7,15}} | collective-permute-start | bytes 3538952 | tf_op jit(solution)/shard_map/ppermute | solution.py:482
  185.8 41.5 %collective-permute-start.18 = (bf16[768,768]{1,0:T(8,128)(2,1)S(1)}, bf16[768,768]{1,0:T(8,128)(2,1)}, u32[]{:S(2)}, u32[]{:S(2)}) collective-permute-start(bf16[768,768]{1,0:T(8,128)(2,1)S(1)} %get-tuple-element.529), channel_id=1, source_target_pairs={{24,16},{25,17},{26,18},{27,19},{28,20},{29,21},{30,22},{31,23}} | collective-permute-start | bytes 3538952 | tf_op jit(solution)/shard_map/ppermute | solution.py:483
  230.6 41.0 %collective-permute-start.17 = (bf16[768,768]{1,0:T(8,128)(2,1)}, bf16[768,768]{1,0:T(8,128)(2,1)}, u32[]{:S(2)}, u32[]{:S(2)}) collective-permute-start(bf16[768,768]{1,0:T(8,128)(2,1)} %get-tuple-element.528), channel_id=1, source_target_pairs={{0,8},{8,16},{1,9},{9,17},{2,10},{10,18},{3,11},{11,19},{4,12},{12... | collective-permute-start | bytes 3538952 | tf_op jit(solution)/shard_map/ppermute | solution.py:482
  236.2 35.4 %collective-permute-start.19 = (bf16[768,768]{1,0:T(8,128)(2,1)}, bf16[768,768]{1,0:T(8,128)(2,1)}, u32[]{:S(2)}, u32[]{:S(2)}) collective-permute-start(bf16[768,768]{1,0:T(8,128)(2,1)} %get-tuple-element.527), channel_id=1, source_target_pairs={{24,16},{16,8},{25,17},{17,9},{26,18},{18,10},{27,19},{19,11},{28,... | collective-permute-start | bytes 3538952 | tf_op jit(solution)/shard_map/ppermute | solution.py:483
  274.1 29.4 %collective-permute-start.20 = (bf16[768,768]{1,0:T(8,128)(2,1)S(1)}, bf16[768,768]{1,0:T(8,128)(2,1)}, u32[]{:S(2)}, u32[]{:S(2)}) collective-permute-start(bf16[768,768]{1,0:T(8,128)(2,1)S(1)} %get-tuple-element.525), channel_id=1, source_target_pairs={{0,8},{8,16},{16,24},{1,9},{9,17},{17,25},{2,10},{10,18},{18,26},{... | collective-permute-start | bytes 3538952 | tf_op jit(solution)/shard_map/ppermute | solution.py:482
  279.6 29.2 %collective-permute-start.21 = (bf16[768,768]{1,0:T(8,128)(2,1)S(1)}, bf16[768,768]{1,0:T(8,128)(2,1)}, u32[]{:S(2)}, u32[]{:S(2)}) collective-permute-start(bf16[768,768]{1,0:T(8,128)(2,1)S(1)} %get-tuple-element.526), channel_id=1, source_target_pairs={{24,16},{16,8},{8,0},{25,17},{17,9},{9,1},{26,18},{18,10},{10,2},{... | collective-permute-start | bytes 3538952 | tf_op jit(solution)/shard_map/ppermute | solution.py:483
  311.2 217.7 %all-gather.11.cloned.1.call-start = ((), (), s32[]{:S(2)}) async-start(), calls=%async_computation.5 | async-start | bytes 12976128 | tf_op jit(solution)/shard_map/all_gather | solution.py:753
  323.7 59.3 %collective-permute-start.22 = (bf16[256,1536]{1,0:T(8,128)(2,1)S(1)}, bf16[256,1536]{1,0:T(8,128)(2,1)}, u32[]{:S(2)}, u32[]{:S(2)}) collective-permute-start(bf16[256,1536]{1,0:T(8,128)(2,1)S(1)} %convolution_convert_fusion.9.refs_1_.refs_2_), channel_id=1, source_target_pairs={{0,2},{2,0},{1,3},{3,1},{4,6},{6,4},{5,7},{7,5},{8,10},{10,8},{9,1... | collective-permute-start | bytes 2359304 | tf_op jit(solution)/shard_map/ppermute | solution.py:415
  432.7 476.3 %reduce-scatter.7.cloned.1.call-start = ((), (), s32[]{:S(2)}) async-start(), calls=%async_computation.6 | async-start | bytes 6488064
  608.2 33.2 %collective-permute-start.36 = (bf16[8,2,64,768]{3,2,1,0:T(8,128)(2,1)}, bf16[8,2,64,768]{3,2,1,0:T(8,128)(2,1)S(1)}, u32[]{:S(2)}, u32[]{:S(2)}) collective-permute-start(bf16[8,2,64,768]{3,2,1,0:T(8,128)(2,1)} %get-tuple-element.178), channel_id=1, source_target_pairs={{0,2},{2,0},{1,3},{3,1},{4,6},{6,4},{5,7},{7,5},{8,10},{10,8},{9,1... | collective-permute-start | bytes 4718600 | tf_op jit(solution)/shard_map/ppermute | solution.py:415
  608.2 36.7 %collective-permute-start.42 = (bf16[8,2,64,768]{3,2,1,0:T(8,128)(2,1)}, bf16[8,2,64,768]{3,2,1,0:T(8,128)(2,1)S(1)}, u32[]{:S(2)}, u32[]{:S(2)}) collective-permute-start(bf16[8,2,64,768]{3,2,1,0:T(8,128)(2,1)} %get-tuple-element.180), channel_id=1, source_target_pairs={{0,2},{2,0},{1,3},{3,1},{4,6},{6,4},{5,7},{7,5},{8,10},{10,8},{9,1... | collective-permute-start | bytes 4718600 | tf_op jit(solution)/shard_map/ppermute | solution.py:415
  647.6 33.2 %collective-permute-start.49 = (bf16[4,2,64,768]{3,2,0,1:T(8,128)(2,1)S(1)}, bf16[4,2,64,768]{3,2,0,1:T(8,128)(2,1)S(1)}, u32[]{:S(2)}, u32[]{:S(2)}) collective-permute-start(bf16[4,2,64,768]{3,2,0,1:T(8,128)(2,1)S(1)} %bitcast.563), channel_id=1, source_target_pairs={{0,1},{1,0},{2,3},{3,2},{4,5},{5,4},{6,7},{7,6},{8,9},{9,8},{10,11... | collective-permute-start | bytes 2359304 | tf_op jit(solution)/shard_map/ppermute | solution.py:415
  649.4 33.6 %collective-permute-start.55 = (bf16[4,2,64,768]{3,2,0,1:T(8,128)(2,1)S(1)}, bf16[4,2,64,768]{3,2,0,1:T(8,128)(2,1)S(1)}, u32[]{:S(2)}, u32[]{:S(2)}) collective-permute-start(bf16[4,2,64,768]{3,2,0,1:T(8,128)(2,1)S(1)} %bitcast.564), channel_id=1, source_target_pairs={{0,4},{4,0},{1,5},{5,1},{2,6},{6,2},{3,7},{7,3},{8,12},{12,8},{9,1... | collective-permute-start | bytes 2359304 | tf_op jit(solution)/shard_map/ppermute | solution.py:415
  664.2 27.3 %collective-permute-start.38 = (bf16[4,64,768]{2,1,0:T(8,128)(2,1)S(1)}, bf16[4,64,768]{2,1,0:T(8,128)(2,1)S(1)}, u32[]{:S(2)}, u32[]{:S(2)}) collective-permute-start(bf16[4,64,768]{2,1,0:T(8,128)(2,1)S(1)} %dynamic-slice_bitcast_fusion.18), channel_id=1, source_target_pairs={{0,4},{4,0},{1,5},{5,1},{2,6},{6,2},{3,7},{7,3},{8,12},{12,8},{9,1... | collective-permute-start | bytes 1179656 | tf_op jit(solution)/shard_map/ppermute | solution.py:415
  666.4 27.3 %collective-permute-start.44 = (bf16[4,64,768]{2,1,0:T(8,128)(2,1)S(1)}, bf16[4,64,768]{2,1,0:T(8,128)(2,1)S(1)}, u32[]{:S(2)}, u32[]{:S(2)}) collective-permute-start(bf16[4,64,768]{2,1,0:T(8,128)(2,1)S(1)} %dynamic-slice_bitcast_fusion.17), channel_id=1, source_target_pairs={{0,1},{1,0},{2,3},{3,2},{4,5},{5,4},{6,7},{7,6},{8,9},{9,8},{10,11... | collective-permute-start | bytes 1179656 | tf_op jit(solution)/shard_map/ppermute | solution.py:415
  766.7 365.4 %reduce-scatter.9.cloned.1.call-start = ((), (), s32[]{:S(2)}) async-start(), calls=%async_computation.7 | async-start | bytes 9732096
  785.2 113.0 %collective-permute-start.61 = (bf16[4,2,64,768]{3,2,0,1:T(8,128)(2,1)}, bf16[4,2,64,768]{3,2,0,1:T(8,128)(2,1)}, u32[]{:S(2)}, u32[]{:S(2)}) collective-permute-start(bf16[4,2,64,768]{3,2,0,1:T(8,128)(2,1)} %dynamic-slice_bitcast_fusion.6), channel_id=1, source_target_pairs={{0,4},{4,0},{1,5},{5,1},{2,6},{6,2},{3,7},{7,3},{8,12},{12,8},{9,1... | collective-permute-start | bytes 2359304 | tf_op jit(solution)/shard_map/ppermute | solution.py:415
  793.2 108.3 %collective-permute-start.72 = (bf16[4,2,2,64,768]{4,3,0,2,1:T(8,128)(2,1)}, bf16[4,2,2,64,768]{4,3,0,2,1:T(8,128)(2,1)}, u32[]{:S(2)}, u32[]{:S(2)}) collective-permute-start(bf16[4,2,2,64,768]{4,3,0,2,1:T(8,128)(2,1)} %bitcast.538), channel_id=1, source_target_pairs={{0,2},{2,0},{1,3},{3,1},{4,6},{6,4},{5,7},{7,5},{8,10},{10,8},{9,1... | collective-permute-start | bytes 4718600 | tf_op jit(solution)/shard_map/ppermute | solution.py:415
  851.0 71.1 %collective-permute-start.70 = (bf16[4,2,2,24,3456]{4,3,2,1,0:T(8,128)(2,1)}, bf16[4,2,2,24,3456]{4,3,2,1,0:T(8,128)(2,1)}, u32[]{:S(2)}, u32[]{:S(2)}) collective-permute-start(bf16[4,2,2,24,3456]{4,3,2,1,0:T(8,128)(2,1)} %dynamic-slice_bitcast_fusion), channel_id=1, source_target_pairs={{0,2},{2,0},{1,3},{3,1},{4,6},{6,4},{5,7},{7,5},{8,10},{10,8},{9,1... | collective-permute-start | bytes 7962632 | tf_op jit(solution)/shard_map/ppermute | solution.py:415
  943.2 61.4 %collective-permute-start.78 = (bf16[64,768]{1,0:T(8,128)(2,1)}, bf16[64,768]{1,0:T(8,128)(2,1)S(1)}, u32[]{:S(2)}, u32[]{:S(2)}) collective-permute-start(bf16[64,768]{1,0:T(8,128)(2,1)} %get-tuple-element.578), channel_id=1, source_target_pairs={{0,8},{8,16},{16,24},{24,0},{1,9},{9,17},{17,25},{25,1},{2,10},{10... | collective-permute-start | bytes 294920 | tf_op jit(solution)/shard_map/ppermute | solution.py:456
  944.1 62.8 %collective-permute-start.79 = (bf16[64,768]{1,0:T(8,128)(2,1)}, bf16[64,768]{1,0:T(8,128)(2,1)}, u32[]{:S(2)}, u32[]{:S(2)}) collective-permute-start(bf16[64,768]{1,0:T(8,128)(2,1)} %get-tuple-element.580), channel_id=1, source_target_pairs={{0,16},{8,24},{16,0},{24,8},{1,17},{9,25},{17,1},{25,9},{2,18},{10... | collective-permute-start | bytes 294920 | tf_op jit(solution)/shard_map/ppermute | solution.py:456
  944.1 62.9 %collective-permute-start.80 = (bf16[64,768]{1,0:T(8,128)(2,1)}, bf16[64,768]{1,0:T(8,128)(2,1)}, u32[]{:S(2)}, u32[]{:S(2)}) collective-permute-start(bf16[64,768]{1,0:T(8,128)(2,1)} %get-tuple-element.579), channel_id=1, source_target_pairs={{0,24},{8,0},{16,8},{24,16},{1,25},{9,1},{17,9},{25,17},{2,26},{10... | collective-permute-start | bytes 294920 | tf_op jit(solution)/shard_map/ppermute | solution.py:456
  947.9 61.0 %collective-permute-start.76 = (bf16[4,2,24,1408]{3,2,1,0:T(8,128)(2,1)}, bf16[4,2,24,1408]{3,2,1,0:T(8,128)(2,1)}, u32[]{:S(2)}, u32[]{:S(2)}) collective-permute-start(bf16[4,2,24,1408]{3,2,1,0:T(8,128)(2,1)} %dynamic-slice_bitcast_fusion.10), channel_id=1, source_target_pairs={{0,4},{4,0},{1,5},{5,1},{2,6},{6,2},{3,7},{7,3},{8,12},{12,8},{9,1... | collective-permute-start | bytes 1622024 | tf_op jit(solution)/shard_map/ppermute | solution.py:415
  949.1 85.5 %collective-permute-start.75 = (bf16[4,2,24,3456]{3,2,1,0:T(8,128)(2,1)}, bf16[4,2,24,3456]{3,2,1,0:T(8,128)(2,1)}, u32[]{:S(2)}, u32[]{:S(2)}) collective-permute-start(bf16[4,2,24,3456]{3,2,1,0:T(8,128)(2,1)} %dynamic-slice_bitcast_fusion.1), channel_id=1, source_target_pairs={{0,1},{1,0},{2,3},{3,2},{4,5},{5,4},{6,7},{7,6},{8,9},{9,8},{10,11... | collective-permute-start | bytes 3981320 | tf_op jit(solution)/shard_map/ppermute | solution.py:415
  1004.6 27.8 %collective-permute-start.77 = (bf16[4,2,64,768]{3,2,0,1:T(8,128)(2,1)}, bf16[4,2,64,768]{3,2,0,1:T(8,128)(2,1)}, u32[]{:S(2)}, u32[]{:S(2)}) collective-permute-start(bf16[4,2,64,768]{3,2,0,1:T(8,128)(2,1)} %dynamic-slice_bitcast_fusion.5), channel_id=1, source_target_pairs={{0,4},{4,0},{1,5},{5,1},{2,6},{6,2},{3,7},{7,3},{8,12},{12,8},{9,1... | collective-permute-start | bytes 2359304 | tf_op jit(solution)/shard_map/ppermute | solution.py:415
  1007.0 30.6 %collective-permute-start.74 = (bf16[2,512,768]{2,1,0:T(8,128)(2,1)}, bf16[2,512,768]{2,1,0:T(8,128)(2,1)S(1)}, u32[]{:S(2)}, u32[]{:S(2)}) collective-permute-start(bf16[2,512,768]{2,1,0:T(8,128)(2,1)} %get-tuple-element.204), channel_id=1, source_target_pairs={{0,2},{2,0},{1,3},{3,1},{4,6},{6,4},{5,7},{7,5},{8,10},{10,8},{9,1... | collective-permute-start | bytes 4718600 | tf_op jit(solution)/shard_map/ppermute | solution.py:415
  1045.0 36.5 %collective-permute-start.81 = (bf16[512,768]{1,0:T(8,128)(2,1)}, bf16[512,768]{1,0:T(8,128)(2,1)}, u32[]{:S(2)}, u32[]{:S(2)}) collective-permute-start(bf16[512,768]{1,0:T(8,128)(2,1)} %fusion.47.refs_1_), channel_id=1, source_target_pairs={{0,8},{8,16},{16,24},{1,9},{9,17},{17,25},{2,10},{10,18},{18,26},{... | collective-permute-start | bytes 2359304 | tf_op jit(solution)/shard_map/ppermute | solution.py:469
  1048.5 38.5 %collective-permute-start.82 = (bf16[512,768]{1,0:T(8,128)(2,1)}, bf16[512,768]{1,0:T(8,128)(2,1)}, u32[]{:S(2)}, u32[]{:S(2)}) collective-permute-start(bf16[512,768]{1,0:T(8,128)(2,1)} %fusion.47.refs_1_), channel_id=1, source_target_pairs={{8,0},{16,8},{24,16},{9,1},{17,9},{25,17},{10,2},{18,10},{26,18},{... | collective-permute-start | bytes 2359304 | tf_op jit(solution)/shard_map/ppermute | solution.py:470
  1055.7 39.5 %collective-permute-start.91 = (bf16[4,2,2,24,1280]{4,3,2,1,0:T(8,128)(2,1)}, bf16[4,2,2,24,1280]{4,3,2,1,0:T(8,128)(2,1)}, u32[]{:S(2)}, u32[]{:S(2)}) collective-permute-start(bf16[4,2,2,24,1280]{4,3,2,1,0:T(8,128)(2,1)} %get-tuple-element.546), channel_id=1, source_target_pairs={{0,2},{2,0},{1,3},{3,1},{4,6},{6,4},{5,7},{7,5},{8,10},{10,8},{9,1... | collective-permute-start | bytes 2949128 | tf_op jit(solution)/shard_map/ppermute | solution.py:415
  1157.5 78.0 %collective-permute-start.100 = (bf16[4032,768]{1,0:T(8,128)(2,1)}, bf16[4032,768]{1,0:T(8,128)(2,1)}, u32[]{:S(2)}, u32[]{:S(2)}) collective-permute-start(bf16[4032,768]{1,0:T(8,128)(2,1)} %shard_map.473), channel_id=1, source_target_pairs={{0,2},{2,0},{1,3},{3,1},{4,6},{6,4},{5,7},{7,5},{8,10},{10,8},{9,1... | collective-permute-start | bytes 18579464 | tf_op jit(solution)/shard_map/ppermute | solution.py:415
  1202.7 26.9 %collective-permute-start.101 = (bf16[4,24,1152]{2,1,0:T(8,128)(2,1)}, bf16[4,24,1152]{2,1,0:T(8,128)(2,1)}, u32[]{:S(2)}, u32[]{:S(2)}) collective-permute-start(bf16[4,24,1152]{2,1,0:T(8,128)(2,1)} %dynamic-slice_bitcast_fusion.28), channel_id=1, source_target_pairs={{0,4},{4,0},{1,5},{5,1},{2,6},{6,2},{3,7},{7,3},{8,12},{12,8},{9,1... | collective-permute-start | bytes 663560 | tf_op jit(solution)/shard_map/ppermute | solution.py:415
  1242.8 44.4 %collective-permute-start.107 = (bf16[24,1152]{1,0:T(8,128)(2,1)}, bf16[24,1152]{1,0:T(8,128)(2,1)}, u32[]{:S(2)}, u32[]{:S(2)}) collective-permute-start(bf16[24,1152]{1,0:T(8,128)(2,1)} %get-tuple-element.595), channel_id=1, source_target_pairs={{0,8},{8,16},{16,24},{24,0},{1,9},{9,17},{17,25},{25,1},{2,10},{10... | collective-permute-start | bytes 165896 | tf_op jit(solution)/shard_map/ppermute | solution.py:456
  1250.1 37.2 %collective-permute-start.108 = (bf16[24,1152]{1,0:T(8,128)(2,1)}, bf16[24,1152]{1,0:T(8,128)(2,1)}, u32[]{:S(2)}, u32[]{:S(2)}) collective-permute-start(bf16[24,1152]{1,0:T(8,128)(2,1)} %get-tuple-element.597), channel_id=1, source_target_pairs={{0,16},{8,24},{16,0},{24,8},{1,17},{9,25},{17,1},{25,9},{2,18},{10... | collective-permute-start | bytes 165896 | tf_op jit(solution)/shard_map/ppermute | solution.py:456
  1252.1 35.9 %collective-permute-start.109 = (bf16[24,1152]{1,0:T(8,128)(2,1)}, bf16[24,1152]{1,0:T(8,128)(2,1)}, u32[]{:S(2)}, u32[]{:S(2)}) collective-permute-start(bf16[24,1152]{1,0:T(8,128)(2,1)} %get-tuple-element.596), channel_id=1, source_target_pairs={{0,24},{8,0},{16,8},{24,16},{1,25},{9,1},{17,9},{25,17},{2,26},{10... | collective-permute-start | bytes 165896 | tf_op jit(solution)/shard_map/ppermute | solution.py:456
  1277.1 37.5 %collective-permute-start.104 = (bf16[1008,768]{1,0:T(8,128)(2,1)}, bf16[1008,768]{1,0:T(8,128)(2,1)}, u32[]{:S(2)}, u32[]{:S(2)}) collective-permute-start(bf16[1008,768]{1,0:T(8,128)(2,1)} %pad_maximum_fusion.4), channel_id=1, source_target_pairs={{0,1},{1,0},{2,3},{3,2},{4,5},{5,4},{6,7},{7,6},{8,9},{9,8},{10,11... | collective-permute-start | bytes 4644872 | tf_op jit(solution)/shard_map/ppermute | solution.py:415
  1280.0 34.6 %collective-permute-start.106 = (bf16[1008,768]{1,0:T(8,128)(2,1)}, bf16[1008,768]{1,0:T(8,128)(2,1)}, u32[]{:S(2)}, u32[]{:S(2)}) collective-permute-start(bf16[1008,768]{1,0:T(8,128)(2,1)} %pad_maximum_fusion.5), channel_id=1, source_target_pairs={{0,4},{4,0},{1,5},{5,1},{2,6},{6,2},{3,7},{7,3},{8,12},{12,8},{9,1... | collective-permute-start | bytes 4644872 | tf_op jit(solution)/shard_map/ppermute | solution.py:415
  (269 other events, 3585.7 us)
Sparse Core Ops, SparseCore 0:
  20.0 134.4 all-gather.4
  157.9 99.1 all-gather.6
  311.3 81.2 all-gather.8
  432.8 96.0 all-gather.10
  766.8 116.8 reduce-scatter.6
  933.3 148.7 reduce-scatter.8

commit v9 on v8

--- a/solution.py
+++ b/solution.py
@@ -674,9 +674,8 @@
         places.append(
             jnp.where(inside, plane_slot(rel_id // shard) * padded + rel_id % shard, shard)
         )
-    dec_cast, enc_pack, plane_table, places = lax.optimization_barrier(
-        (dec_cast, enc_pack, plane_table, places)
-    )
+    got = jnp.take(plane_table, jnp.concatenate(places), axis=0, mode="clip")
+    dec_cast, enc_pack, got = lax.optimization_barrier((dec_cast, enc_pack, got))
     dec_pack = lax.all_gather(dec_cast, ALL, axis=0, tiled=True)
     enc_places = [item[:enc_count] for item in places]
     dec_places = [item[enc_count:] for item in places]
@@ -700,7 +699,6 @@
             up, down, held = lax.optimization_barrier((up, down, held))
         return up, down
 
-    got = jnp.take(plane_table, jnp.concatenate(places), axis=0, mode="clip")
     looked = line_scatter(jnp.split(got, len(places)), "z", beside)
     enc_fo, gain, enc_x8, dec_x8, enc_picks, dec_picks = held
     ffn_cast, dec_pack, looked = lax.optimization_barrier((ffn_cast, dec_pack, looked))
@@ -852,9 +850,8 @@
     d_x0_norm, d_gain_eatt = norm_pull(enc_x0, gain[0], 1.0, input_grad(d_enc_qkv, enc_wi))
     d_x0 = d_x1 + d_x0_norm
 
-    d_x0, enc_sums, g_dec_fo = lax.optimization_barrier(
-        (d_x0.astype(bf16), enc_sums, scatter_last(g_dec_fo))
-    )
+    d_x0, wides = lax.optimization_barrier((d_x0.astype(bf16), enc_sums[:2]))
+    enc_sums = wides + enc_sums[2:]
     enc_sums = [scatter_second(item, number == 0) for number, item in enumerate(enc_sums)]
     enc_lines = line_gather(d_x0, "z")
     enc_lines, enc_sums = lax.optimization_barrier((enc_lines, enc_sums))
@@ -885,27 +882,28 @@
             late, last, enc_sums = sums
             last = [scatter_first(item, number == 0) for number, item in enumerate(last)]
             wide = jnp.concatenate(enc_sums[:2], axis=2)
-            return late, last, [scatter_last(wide), scatter_last(enc_sums[2])], None
+            both = jnp.concatenate([enc_sums[2], g_dec_fo], axis=1)
+            return late, last, [scatter_last(wide), scatter_last(both)], None
         late, last, enc_sums, _ = sums
-        return late, [scatter_second(item, not number) for number, item in enumerate(last)], enc_sums
-
-    input_embed, (late, last, (g_wide, g_fo)) = plane_scatter(
+        last = [scatter_second(item, number == 0) for number, item in enumerate(last)]
+        return late, jnp.concatenate(last, axis=2), enc_sums
+
+    input_embed, (late, last, (g_wide, g_out)) = plane_scatter(
         pairs, padded, (late, last, enc_sums), beside_place
     )
     late = late.astype(f32)
     grad_embed = head_embed[:shard] + input_embed[:shard]
 
-    last = [scatter_last(item) for item in last]
+    last = scatter_last(last)
     squares = sum(
-        (jnp.sum(item * item) for item in (grad_embed, early, late, g_wide, g_fo, g_dec_fo, *last))
+        (jnp.sum(item * item) for item in (grad_embed, early, late, g_wide, g_out, last))
     )
     sums = fold_all(jnp.stack([jnp.sum(mask), loss_local, squares]), jnp.add)
-    last = jnp.concatenate(last, axis=1)
     owned = (
         jnp.stack([cut(last, 0, 3 * D), cut(late, 0, 3 * D), cut(late, 3 * D, 3 * D)]),
         jnp.stack([cut(g_wide, 2 * FF, D), cut(late, 6 * D, D), cut(late, 7 * D, D)]),
         jnp.stack([cut(g_wide, 0, 2 * FF), early]),
-        jnp.stack([g_fo, g_dec_fo]),
+        g_out.reshape(2, -1, D),
         last[:, 3 * D + 7].reshape(2, -1),
         last[:, 3 * D : 3 * D + 7].T,
     )

time: 1400 us -> 1370 us (0.979)
  other arithmetic: 164 us -> 143 us
  waiting for transfers between devices: 389 us -> 407 us
    convert_element_type x32, other arithmetic: 54 us -> 35.2 us  [add16(): return (left.astype(f32) + right.astype(f32)).astype(bf16)]
    ppermute x9, waiting for transfers between devices: 15.2 us -> 33.7 us  [line_gather(): lax.ppermute(ups[-1], axis, [(i, i + 1) for i in range(size - 1)])]
    all_gather x1, waiting for transfers between devices: 14.5 us -> 0.01 us  [body(): lax.all_gather(jnp.concatenate([enc_cast, flat_out[0]], axis=1), ALL, axi...]
    ppermute x27 -> x21, starting transfers between devices: 49 us -> 40.4 us  [scatter_last(): got = lax.ppermute(send, 'z', [(i, (i + hop) % size) for i in range(size)])]
    unnamed x416 -> x404, local copies, waits for them, and re-layouts: 42.2 us -> 43.6 us
    ppermute x27 -> x21, waiting for transfers between devices: 35.3 us -> 35.3 us  [scatter_last(): got = lax.ppermute(send, 'z', [(i, (i + hop) % size) for i in range(size)])]
  transfers between devices with their start and end apart: 124 -> 118, of which waited for: 50 -> 54; matrix products, arithmetic and copies ran while one was open for 27% -> 25% of each run, Pallas kernels for 13% -> 13%
where the time goes in v9:
time: 1370 us; the launch traced here: 1360 us
  waiting for transfers between devices  407 us (30%)
  Pallas kernels  278 us (20%)
  starting transfers between devices  191 us (14%)
  local copies, waits for them, and re-layouts  176 us (13%)
  other arithmetic  143 us (10%)
  matrix products  132 us (10%)
  between operations  29.6 us (2%)
    ppermute x50, waiting for transfers between devices, swap(): return lax.ppermute(value, axis, [(0, 1), (1, 0)])  145 us
    pallas_call x3, Pallas kernels, attend_backward(): pl.pallas_call(functools.partial(attend_backward_kernel, cfg), grid=(HEAD...  87.5 us
    all_gather x1, waiting for transfers between devices, body(): hidden_all = lax.all_gather(hidden_b, ALL, axis=0, tiled=True)  77.3 us
    ppermute x3, waiting for transfers between devices, line_scatter(): up = lax.ppermute(send_up, axis, [(i, i + 1) for i in range(step)])  75.2 us
    pallas_call x4, Pallas kernels, head_grad(): pl.pallas_call(functools.partial(head_grad_kernel, count), grid_spec=pltp...  63.5 us
    ppermute x50, starting transfers between devices, swap(): return lax.ppermute(value, axis, [(0, 1), (1, 0)])  58.1 us
    pallas_call x3, Pallas kernels, attend_forward(): pl.pallas_call(functools.partial(attend_forward_kernel, cfg), grid=(HEADS...  54.2 us
    dot_general x11, matrix products, input_grad(): return jnp.einsum('te,de->td', grads, weight, preferred_element_type=f32)  52.7 us
  transfers between devices with their start and end apart: 118, of which 54 were waited for; matrix products, arithmetic and copies ran while one was open for 25% of the time, Pallas kernels for 13%

profile of v9, /device:TPU:0, one launch (start us, length us, event | category | flops | bytes accessed | tf_op | source)
XLA Modules:
  0.0 1356.6 jit_solution(11048765120909446635)
XLA Ops:
  60.1 10.5 collective-permute-done.1
  70.6 18.0 %collective-permute-start.6 = (bf16[1008,768]{1,0:T(8,128)(2,1)S(1)}, bf16[1008,768]{1,0:T(8,128)(2,1)S(1)}, u32[]{:S(2)}, u32[]{:S(2)}) collective-permute-start(bf16[1008,768]{1,0:T(8,128)(2,1)S(1)} %collective-permute-done.1), channel_id=1, source_target_pairs={{0,2},{2,0},{1,3},{3,1},{4,6},{6,4},{5,7},{7,5},{8,10},{10,8},{9,1... | collective-permute-start | bytes 4644872 | tf_op jit(solution)/shard_map/ppermute | solution.py:415
  98.6 31.4 %collective-permute-done.3 = bf16[504,768]{1,0:T(8,128)(2,1)S(1)} collective-permute-done((bf16[504,768]{1,0:T(8,128)(2,1)S(1)}, bf16[504,768]{1,0:T(8,128)(2,1)S(1)}, u32[]{:S(2)}, u32[]{:S(2)}) %collective-permute-start.3) | collective-permute-done | bytes 774176 | tf_op jit(solution)/shard_map/ppermute | solution.py:415
  141.0 21.0 %gather_fusion = bf16[3072,768]{1,0:T(8,128)(2,1)} fusion(bf16[8064,768]{1,0:T(8,128)(2,1)} %constant_dynamic-update-slice_fusion.4, s32[3072]{0:T(1024)S(1)} %add_clamp_fusion), kind=kCustom, calls=%fused_computation | custom fusion | bytes 9449472 | tf_op jit(solution)/shard_map/jit(_take)/gather | solution.py:677
  194.6 27.3 %collective-permute-done.16 = bf16[768,768]{1,0:T(8,128)(2,1)S(1)} collective-permute-done((bf16[768,768]{1,0:T(8,128)(2,1)S(1)}, bf16[768,768]{1,0:T(8,128)(2,1)S(1)}, u32[]{:S(2)}, u32[]{:S(2)}) %collective-permute-start.16) | collective-permute-done | bytes 1179680 | tf_op jit(solution)/shard_map/ppermute | solution.py:482
  224.4 5.8 collective-permute-start.17
  249.7 25.9 %collective-permute-done.17 = bf16[768,768]{1,0:T(8,128)(2,1)} collective-permute-done((bf16[768,768]{1,0:T(8,128)(2,1)}, bf16[768,768]{1,0:T(8,128)(2,1)}, u32[]{:S(2)}, u32[]{:S(2)}) %collective-permute-start.17) | collective-permute-done | bytes 1179680 | tf_op jit(solution)/shard_map/ppermute | solution.py:482
  278.2 6.6 collective-permute-start.20
  286.8 22.0 %collective-permute-done.20 = bf16[768,768]{1,0:T(8,128)(2,1)} collective-permute-done((bf16[768,768]{1,0:T(8,128)(2,1)S(1)}, bf16[768,768]{1,0:T(8,128)(2,1)}, u32[]{:S(2)}, u32[]{:S(2)}) %collective-permute-start.20) | collective-permute-done | bytes 1179680 | tf_op jit(solution)/shard_map/ppermute | solution.py:482
  308.8 5.2 collective-permute-done.21
  332.9 28.9 %shard_map.462 = (bf16[512,768]{1,0:T(8,128)(2,1)}, f32[512,768]{1,0:T(8,128)}) custom-call(bf16[512,768]{1,0:T(8,128)(2,1)} %convolution_convert_fusion.15.refs_0_, bf16[512,1536]{1,0:T(8,128)(2,1)} %convolution_convert_fusion.8.refs_1_.refs_2_, bf16[512,1536]{1,0:T(8,128)(2,1)} %convolution_convert_fusion.8.refs_1_.refs_2_, ...), custom_call_target="tpu_custom_call" | custom-call | flops 2 | bytes 512 | tf_op jit(solution)/shard_map/pallas_call | solution.py:200
  364.3 6.3 fusion.6
  387.9 13.2 shard_map.461
  405.9 12.0 shard_map.463
  420.0 4.9 fusion.2
  456.2 77.3 %all-gather.11.cloned.1.call-done = bf16[8192,768]{1,0:T(8,128)(2,1)} async-done(((bf16[256,768]{1,0:T(8,128)(2,1)}), bf16[8192,768]{1,0:T(8,128)(2,1)}) %all-gather.11.cloned.1.call-update) | async-done | bytes 12582928 | tf_op jit(solution)/shard_map/all_gather | solution.py:751
  533.5 25.6 %shard_map.464 = (f32[1,8192]{1,0:T(1,128)}, f32[1,8192]{1,0:T(1,128)}) custom-call(bf16[8,2,2,256,768]{4,3,2,1,0:T(8,128)(2,1)} %bitcast.612, bf16[1008,768]{1,0:T(8,128)(2,1)} %get-tuple-element.537.tab, s32[1,8192]{1,0:T(1,128)} %bitcast.571), custom_call_target="tpu_custom_call" | custom-call | flops 12683575296 | bytes 12582912 | tf_op jit(solution)/shard_map/pallas_call | solution.py:306
  581.1 15.8 %shard_map.465 = (bf16[8,2,64,768]{3,2,1,0:T(8,128)(2,1)}, bf16[8,2,64,768]{3,2,1,0:T(8,128)(2,1)}, f32[1008,768]{1,0:T(8,128)}) custom-call(s32[1]{0:T(128)} %bitcast.97.core, bf16[8,2,2,256,768]{4,3,2,1,0:T(8,128)(2,1)} %bitcast.613, bf16[1008,768]{1,0:T(8,128)(2,1)} %get-tuple-element.537.tab, s32[1,8192]{1,0:T(1,128)} %bitcast.572, f32[1,8192]{1,0:T(1,128)} %bitcast.550, ...), custom_call_target="tpu_custom_call" | custom-call | flops 9512681472 | bytes 6291456 | tf_op jit(solution)/shard_map/pallas_call | solution.py:329
  596.9 15.8 %shard_map.467 = (bf16[8,2,64,768]{3,2,1,0:T(8,128)(2,1)}, bf16[8,2,64,768]{3,2,1,0:T(8,128)(2,1)}, f32[1008,768]{1,0:T(8,128)}) custom-call(s32[1]{0:T(128)} %bitcast.97.core, bf16[8,2,2,256,768]{4,3,2,1,0:T(8,128)(2,1)} %bitcast.614, bf16[1008,768]{1,0:T(8,128)(2,1)} %get-tuple-element.537.tab, s32[1,8192]{1,0:T(1,128)} %bitcast.573, f32[1,8192]{1,0:T(1,128)} %bitcast.551, ...), custom_call_target="tpu_custom_call" | custom-call | flops 9512681472 | bytes 6291456 | tf_op jit(solution)/shard_map/pallas_call | solution.py:329
  613.3 15.8 %shard_map.466 = (bf16[8,2,64,768]{3,2,1,0:T(8,128)(2,1)}, bf16[8,2,64,768]{3,2,1,0:T(8,128)(2,1)}, f32[1008,768]{1,0:T(8,128)}) custom-call(s32[1]{0:T(128)} %bitcast.98.core, bf16[8,2,2,256,768]{4,3,2,1,0:T(8,128)(2,1)} %bitcast.615, bf16[1008,768]{1,0:T(8,128)(2,1)} %get-tuple-element.537.tab, s32[1,8192]{1,0:T(1,128)} %bitcast.574, f32[1,8192]{1,0:T(1,128)} %bitcast.552, ...), custom_call_target="tpu_custom_call" | custom-call | flops 9512681472 | bytes 6291456 | tf_op jit(solution)/shard_map/pallas_call | solution.py:329
  629.7 16.0 %shard_map.468 = (bf16[8,2,64,768]{3,2,1,0:T(8,128)(2,1)}, bf16[8,2,64,768]{3,2,1,0:T(8,128)(2,1)}, f32[1008,768]{1,0:T(8,128)}) custom-call(s32[1]{0:T(128)} %bitcast.98.core, bf16[8,2,2,256,768]{4,3,2,1,0:T(8,128)(2,1)} %bitcast.616, bf16[1008,768]{1,0:T(8,128)(2,1)} %get-tuple-element.537.tab, s32[1,8192]{1,0:T(1,128)} %bitcast.575, f32[1,8192]{1,0:T(1,128)} %bitcast.553, ...), custom_call_target="tpu_custom_call" | custom-call | flops 9512681472 | bytes 6291456 | tf_op jit(solution)/shard_map/pallas_call | solution.py:329
  655.0 13.3 collective-permute-done.37
  671.9 13.2 collective-permute-done.49
  688.8 7.0 collective-permute-done.38
  724.7 4.9 collective-permute-done.58
  739.4 6.8 multiply_reduce_fusion.13
  750.0 16.6 %shard_map.469 = (bf16[256,768]{1,0:T(8,128)(2,1)}, f32[2,512,768]{2,1,0:T(8,128)}, bf16[2,512,768]{2,1,0:T(8,128)(2,1)}) custom-call(bf16[256,768]{1,0:T(8,128)(2,1)} %convolution_convert_fusion.18.refs_0_, bf16[512,1536]{1,0:T(8,128)(2,1)} %convolution_convert_fusion.7.refs_1_.refs_2_, bf16[512,1536]{1,0:T(8,128)(2,1)} %convolution_convert_fusion.7.refs_1_.refs_2_, ...), custom_call_target="tpu_custom_call" | custom-call | flops 5 | bytes 256 | tf_op jit(solution)/shard_map/pallas_call | solution.py:227
  797.6 22.8 %shard_map.470 = (bf16[256,768]{1,0:T(8,128)(2,1)}, f32[2,256,768]{2,1,0:T(8,128)}, bf16[2,256,768]{2,1,0:T(8,128)(2,1)}, f32[12,2,8,512]{3,2,1,0:T(8,128)}) custom-call(bf16[256,768]{1,0:T(8,128)(2,1)} %convolution_convert_fusion.19.refs_0_, bf16[256,1536]{1,0:T(8,128)(2,1)} %copy-done.5, bf16[256,1536]{1,0:T(8,128)(2,1)} %copy-done.5, ...), custom_call_target="tpu_custom_call" | custom-call | flops 5 | bytes 256 | tf_op jit(solution)/shard_map/pallas_call | solution.py:227
  820.4 9.0 fusion.57
  831.5 5.8 convolution_convert_fusion
  838.2 12.2 multiply_reduce_fusion.3
  925.9 4.8 fusion.8
  952.6 48.1 %shard_map.471 = (bf16[512,768]{1,0:T(8,128)(2,1)}, f32[2,512,768]{2,1,0:T(8,128)}, bf16[2,512,768]{2,1,0:T(8,128)(2,1)}, f32[12,4,8,768]{3,2,1,0:T(8,128)}) custom-call(bf16[512,768]{1,0:T(8,128)(2,1)} %convolution_convert_fusion.15.refs_0_, bf16[512,1536]{1,0:T(8,128)(2,1)} %convolution_convert_fusion.8.refs_1_.refs_2_, ...), custom_call_target="tpu_custom_call" | custom-call | flops 5 | bytes 512 | tf_op jit(solution)/shard_map/pallas_call | solution.py:227
  1011.3 19.9 %collective-permute-done.85 = bf16[4,2,64,768]{3,2,0,1:T(8,128)(2,1)} collective-permute-done((bf16[4,2,64,768]{3,2,0,1:T(8,128)(2,1)}, bf16[4,2,64,768]{3,2,0,1:T(8,128)(2,1)}, u32[]{:S(2)}, u32[]{:S(2)}) %collective-permute-start.85) | collective-permute-done | bytes 786464 | tf_op jit(solution)/shard_map/ppermute | solution.py:415
  1035.0 7.0 collective-permute-done.76
  1044.0 14.3 %collective-permute-done.86 = bf16[4,64,768]{2,1,0:T(8,128)(2,1)S(1)} collective-permute-done((bf16[4,64,768]{2,1,0:T(8,128)(2,1)S(1)}, bf16[4,64,768]{2,1,0:T(8,128)(2,1)S(1)}, u32[]{:S(2)}, u32[]{:S(2)}) %collective-permute-start.86) | collective-permute-done | bytes 393248 | tf_op jit(solution)/shard_map/ppermute | solution.py:415
  1081.3 6.2 collective-permute-done.84
  1098.4 13.1 collective-permute-done.81
  1119.3 11.8 collective-permute-done.82
  1138.4 23.8 %shard_map.473 = bf16[4032,768]{1,0:T(8,128)(2,1)} custom-call(s32[1,512]{1,0:T(1,128)} %bitcast.576, bf16[512,768]{1,0:T(8,128)(2,1)} %copy-done.25, s32[1,512]{1,0:T(1,128)} %bitcast.580, bf16[512,768]{1,0:T(8,128)(2,1)} %add.1275.refs_3_, s32[1,512]{1,0:T(1,128)} %bitcast.578, bf16[512,768]{1,0:T(8,128)(2,1)} %add.1276.refs_5_, s32[1,512]{1,0:T(1,128)} %bitcast.582, ...), custom_call_target="tpu_custom_call" | custom-call | flops 1 | bytes 1008 | tf_op jit(solution)/shard_map/pallas_call | solution.py:374
  1167.2 4.9 collective-permute-done.94
  1172.1 8.4 collective-permute-done.95
  1180.5 4.8 collective-permute-start.93
  1187.9 11.4 collective-permute-done.92
  1202.7 23.7 %shard_map.472 = bf16[4032,768]{1,0:T(8,128)(2,1)} custom-call(s32[1,512]{1,0:T(1,128)} %bitcast.577, bf16[512,768]{1,0:T(8,128)(2,1)} %copy-done.25, s32[1,512]{1,0:T(1,128)} %bitcast.581, bf16[512,768]{1,0:T(8,128)(2,1)} %add.1275.refs_3_, s32[1,512]{1,0:T(1,128)} %bitcast.579, bf16[512,768]{1,0:T(8,128)(2,1)} %add.1276.refs_5_, s32[1,512]{1,0:T(1,128)} %bitcast.583, ...), custom_call_target="tpu_custom_call" | custom-call | flops 1 | bytes 1008 | tf_op jit(solution)/shard_map/pallas_call | solution.py:374
  1239.6 12.6 collective-permute-done.100
  1293.3 8.5 multiply_reduce_fusion.1
  1335.8 6.7 add_subtract_fusion
  (996 shorter events, 579.9 us)
Async XLA Ops:
  7.2 154.8 %all-gather.5.cloned.1.call-start = ((), (), s32[]{:S(2)}) async-start(), calls=%async_computation.2 | async-start | bytes 14800896 | tf_op jit(solution)/shard_map/all_gather | solution.py:617
  19.8 296.6 %all-gather.7.cloned.1.call-start = ((), (), s32[]{:S(2)}) async-start(), calls=%async_computation.3 | async-start | bytes 9732096 | tf_op jit(solution)/shard_map/all_gather | solution.py:679
  22.0 48.6 %collective-permute-start.1 = (bf16[1008,768]{1,0:T(8,128)(2,1)}, bf16[1008,768]{1,0:T(8,128)(2,1)S(1)}, u32[]{:S(2)}, u32[]{:S(2)}) collective-permute-start(bf16[1008,768]{1,0:T(8,128)(2,1)} %get-tuple-element.537.tab), channel_id=1, source_target_pairs={{0,1},{1,0},{2,3},{3,2},{4,5},{5,4},{6,7},{7,6},{8,9},{9,8},{10,11... | collective-permute-start | bytes 4644872 | tf_op jit(solution)/shard_map/ppermute | solution.py:415
  24.9 68.7 %collective-permute-start.2 = (bf16[1008,768]{1,0:T(8,128)(2,1)}, bf16[1008,768]{1,0:T(8,128)(2,1)S(1)}, u32[]{:S(2)}, u32[]{:S(2)}) collective-permute-start(bf16[1008,768]{1,0:T(8,128)(2,1)} %get-tuple-element.537.tab), channel_id=1, source_target_pairs={{0,4},{4,0},{1,5},{5,1},{2,6},{6,2},{3,7},{7,3},{8,12},{12,8},{9,1... | collective-permute-start | bytes 4644872 | tf_op jit(solution)/shard_map/ppermute | solution.py:415
  26.5 107.3 %collective-permute-start.5 = (bf16[1008,768]{1,0:T(8,128)(2,1)}, bf16[1008,768]{1,0:T(8,128)(2,1)}, u32[]{:S(2)}, u32[]{:S(2)}) collective-permute-start(bf16[1008,768]{1,0:T(8,128)(2,1)} %get-tuple-element.537.tab), channel_id=1, source_target_pairs={{0,2},{2,0},{1,3},{3,1},{4,6},{6,4},{5,7},{7,5},{8,10},{10,8},{9,1... | collective-permute-start | bytes 4644872 | tf_op jit(solution)/shard_map/ppermute | solution.py:415
  54.3 35.1 %collective-permute-start.14 = (s32[768]{0:T(1024)S(1)}, s32[768]{0:T(1024)S(1)}, u32[]{:S(2)}, u32[]{:S(2)}) collective-permute-start(s32[768]{0:T(1024)S(1)} %collective-permute-done.10), channel_id=1, source_target_pairs={{0,8},{8,16},{16,24},{1,9},{9,17},{17,25},{2,10},{10,18},{18,26},{... | collective-permute-start | bytes 9224 | tf_op jit(solution)/shard_map/ppermute | solution.py:469
  58.8 35.5 %collective-permute-start.13 = (s32[768]{0:T(1024)S(1)}, s32[768]{0:T(1024)S(1)}, u32[]{:S(2)}, u32[]{:S(2)}) collective-permute-start(s32[768]{0:T(1024)S(1)} %collective-permute-done.12), channel_id=1, source_target_pairs={{8,0},{16,8},{24,16},{9,1},{17,9},{25,17},{10,2},{18,10},{26,18},{... | collective-permute-start | bytes 9224 | tf_op jit(solution)/shard_map/ppermute | solution.py:470
  70.6 65.9 %collective-permute-start.6 = (bf16[1008,768]{1,0:T(8,128)(2,1)S(1)}, bf16[1008,768]{1,0:T(8,128)(2,1)S(1)}, u32[]{:S(2)}, u32[]{:S(2)}) collective-permute-start(bf16[1008,768]{1,0:T(8,128)(2,1)S(1)} %collective-permute-done.1), channel_id=1, source_target_pairs={{0,2},{2,0},{1,3},{3,1},{4,6},{6,4},{5,7},{7,5},{8,10},{10,8},{9,1... | collective-permute-start | bytes 4644872 | tf_op jit(solution)/shard_map/ppermute | solution.py:415
  93.7 36.4 %collective-permute-start.3 = (bf16[504,768]{1,0:T(8,128)(2,1)S(1)}, bf16[504,768]{1,0:T(8,128)(2,1)S(1)}, u32[]{:S(2)}, u32[]{:S(2)}) collective-permute-start(bf16[504,768]{1,0:T(8,128)(2,1)S(1)} %slice.616), channel_id=1, source_target_pairs={{0,1},{1,0},{2,3},{3,2},{4,5},{5,4},{6,7},{7,6},{8,9},{9,8},{10,11... | collective-permute-start | bytes 2322440 | tf_op jit(solution)/shard_map/ppermute | solution.py:415
  94.4 43.4 %collective-permute-start.7 = (bf16[1008,768]{1,0:T(8,128)(2,1)S(1)}, bf16[1008,768]{1,0:T(8,128)(2,1)S(1)}, u32[]{:S(2)}, u32[]{:S(2)}) collective-permute-start(bf16[1008,768]{1,0:T(8,128)(2,1)S(1)} %collective-permute-done.2), channel_id=1, source_target_pairs={{0,2},{2,0},{1,3},{3,1},{4,6},{6,4},{5,7},{7,5},{8,10},{10,8},{9,1... | collective-permute-start | bytes 4644872 | tf_op jit(solution)/shard_map/ppermute | solution.py:415
  94.9 36.4 %collective-permute-start.4 = (bf16[504,768]{1,0:T(8,128)(2,1)S(1)}, bf16[504,768]{1,0:T(8,128)(2,1)S(1)}, u32[]{:S(2)}, u32[]{:S(2)}) collective-permute-start(bf16[504,768]{1,0:T(8,128)(2,1)S(1)} %slice.617), channel_id=1, source_target_pairs={{0,4},{4,0},{1,5},{5,1},{2,6},{6,2},{3,7},{7,3},{8,12},{12,8},{9,1... | collective-permute-start | bytes 2322440 | tf_op jit(solution)/shard_map/ppermute | solution.py:415
  162.0 257.9 %all-gather.9.cloned.1.call-start = ((), (), s32[]{:S(2)}) async-start(), calls=%async_computation.4 | async-start | bytes 9732096 | tf_op jit(solution)/shard_map/all_gather | solution.py:705
  179.0 43.0 %collective-permute-start.16 = (bf16[768,768]{1,0:T(8,128)(2,1)S(1)}, bf16[768,768]{1,0:T(8,128)(2,1)S(1)}, u32[]{:S(2)}, u32[]{:S(2)}) collective-permute-start(bf16[768,768]{1,0:T(8,128)(2,1)S(1)} %get-tuple-element.512), channel_id=1, source_target_pairs={{0,8},{1,9},{2,10},{3,11},{4,12},{5,13},{6,14},{7,15}} | collective-permute-start | bytes 3538952 | tf_op jit(solution)/shard_map/ppermute | solution.py:482
  193.0 56.8 %collective-permute-start.19 = (bf16[768,768]{1,0:T(8,128)(2,1)}, bf16[768,768]{1,0:T(8,128)(2,1)}, u32[]{:S(2)}, u32[]{:S(2)}) collective-permute-start(bf16[768,768]{1,0:T(8,128)(2,1)} %get-tuple-element.511), channel_id=1, source_target_pairs={{24,16},{16,8},{25,17},{17,9},{26,18},{18,10},{27,19},{19,11},{28,... | collective-permute-start | bytes 3538952 | tf_op jit(solution)/shard_map/ppermute | solution.py:483
  224.4 51.2 %collective-permute-start.17 = (bf16[768,768]{1,0:T(8,128)(2,1)}, bf16[768,768]{1,0:T(8,128)(2,1)}, u32[]{:S(2)}, u32[]{:S(2)}) collective-permute-start(bf16[768,768]{1,0:T(8,128)(2,1)} %slice_add_fusion.4), channel_id=1, source_target_pairs={{0,8},{8,16},{1,9},{9,17},{2,10},{10,18},{3,11},{11,19},{4,12},{12... | collective-permute-start | bytes 3538952 | tf_op jit(solution)/shard_map/ppermute | solution.py:482
  278.2 30.7 %collective-permute-start.20 = (bf16[768,768]{1,0:T(8,128)(2,1)S(1)}, bf16[768,768]{1,0:T(8,128)(2,1)}, u32[]{:S(2)}, u32[]{:S(2)}) collective-permute-start(bf16[768,768]{1,0:T(8,128)(2,1)S(1)} %get-tuple-element.509), channel_id=1, source_target_pairs={{0,8},{8,16},{16,24},{1,9},{9,17},{17,25},{2,10},{10,18},{18,26},{... | collective-permute-start | bytes 3538952 | tf_op jit(solution)/shard_map/ppermute | solution.py:482
  284.8 29.3 %collective-permute-start.21 = (bf16[768,768]{1,0:T(8,128)(2,1)S(1)}, bf16[768,768]{1,0:T(8,128)(2,1)}, u32[]{:S(2)}, u32[]{:S(2)}) collective-permute-start(bf16[768,768]{1,0:T(8,128)(2,1)S(1)} %get-tuple-element.510), channel_id=1, source_target_pairs={{24,16},{16,8},{8,0},{25,17},{17,9},{9,1},{26,18},{18,10},{10,2},{... | collective-permute-start | bytes 3538952 | tf_op jit(solution)/shard_map/ppermute | solution.py:483
  316.5 217.0 %all-gather.11.cloned.1.call-start = ((), (), s32[]{:S(2)}) async-start(), calls=%async_computation.5 | async-start | bytes 12976128 | tf_op jit(solution)/shard_map/all_gather | solution.py:751
  329.4 58.5 %collective-permute-start.22 = (bf16[256,1536]{1,0:T(8,128)(2,1)S(1)}, bf16[256,1536]{1,0:T(8,128)(2,1)}, u32[]{:S(2)}, u32[]{:S(2)}) collective-permute-start(bf16[256,1536]{1,0:T(8,128)(2,1)S(1)} %convolution_convert_fusion.9.refs_1_.refs_2_), channel_id=1, source_target_pairs={{0,2},{2,0},{1,3},{3,1},{4,6},{6,4},{5,7},{7,5},{8,10},{10,8},{9,1... | collective-permute-start | bytes 2359304 | tf_op jit(solution)/shard_map/ppermute | solution.py:415
  381.7 24.3 %collective-permute-start.24 = (bf16[512,1536]{1,0:T(8,128)(2,1)}, bf16[512,1536]{1,0:T(8,128)(2,1)}, u32[]{:S(2)}, u32[]{:S(2)}) collective-permute-start(bf16[512,1536]{1,0:T(8,128)(2,1)} %convolution_convert_fusion.7.refs_1_.refs_2_), channel_id=1, source_target_pairs={{0,2},{2,0},{1,3},{3,1},{4,6},{6,4},{5,7},{7,5},{8,10},{10,8},{9,1... | collective-permute-start | bytes 4718600 | tf_op jit(solution)/shard_map/ppermute | solution.py:415
  437.9 475.0 %reduce-scatter.7.cloned.1.call-start = ((), (), s32[]{:S(2)}) async-start(), calls=%async_computation.6 | async-start | bytes 6488064
  612.7 33.0 %collective-permute-start.36 = (bf16[8,2,64,768]{3,2,1,0:T(8,128)(2,1)}, bf16[8,2,64,768]{3,2,1,0:T(8,128)(2,1)S(1)}, u32[]{:S(2)}, u32[]{:S(2)}) collective-permute-start(bf16[8,2,64,768]{3,2,1,0:T(8,128)(2,1)} %get-tuple-element.167), channel_id=1, source_target_pairs={{0,2},{2,0},{1,3},{3,1},{4,6},{6,4},{5,7},{7,5},{8,10},{10,8},{9,1... | collective-permute-start | bytes 4718600 | tf_op jit(solution)/shard_map/ppermute | solution.py:415
  612.8 36.5 %collective-permute-start.42 = (bf16[8,2,64,768]{3,2,1,0:T(8,128)(2,1)}, bf16[8,2,64,768]{3,2,1,0:T(8,128)(2,1)S(1)}, u32[]{:S(2)}, u32[]{:S(2)}) collective-permute-start(bf16[8,2,64,768]{3,2,1,0:T(8,128)(2,1)} %get-tuple-element.169), channel_id=1, source_target_pairs={{0,2},{2,0},{1,3},{3,1},{4,6},{6,4},{5,7},{7,5},{8,10},{10,8},{9,1... | collective-permute-start | bytes 4718600 | tf_op jit(solution)/shard_map/ppermute | solution.py:415
  629.2 23.8 %collective-permute-start.54 = (bf16[8,2,64,768]{3,2,1,0:T(8,128)(2,1)}, bf16[8,2,64,768]{3,2,1,0:T(8,128)(2,1)S(1)}, u32[]{:S(2)}, u32[]{:S(2)}) collective-permute-start(bf16[8,2,64,768]{3,2,1,0:T(8,128)(2,1)} %get-tuple-element.173), channel_id=1, source_target_pairs={{0,2},{2,0},{1,3},{3,1},{4,6},{6,4},{5,7},{7,5},{8,10},{10,8},{9,1... | collective-permute-start | bytes 4718600 | tf_op jit(solution)/shard_map/ppermute | solution.py:415
  651.9 33.2 %collective-permute-start.49 = (bf16[4,2,64,768]{3,2,0,1:T(8,128)(2,1)S(1)}, bf16[4,2,64,768]{3,2,0,1:T(8,128)(2,1)S(1)}, u32[]{:S(2)}, u32[]{:S(2)}) collective-permute-start(bf16[4,2,64,768]{3,2,0,1:T(8,128)(2,1)S(1)} %bitcast.545), channel_id=1, source_target_pairs={{0,1},{1,0},{2,3},{3,2},{4,5},{5,4},{6,7},{7,6},{8,9},{9,8},{10,11... | collective-permute-start | bytes 2359304 | tf_op jit(solution)/shard_map/ppermute | solution.py:415
  653.8 33.6 %collective-permute-start.55 = (bf16[4,2,64,768]{3,2,0,1:T(8,128)(2,1)S(1)}, bf16[4,2,64,768]{3,2,0,1:T(8,128)(2,1)S(1)}, u32[]{:S(2)}, u32[]{:S(2)}) collective-permute-start(bf16[4,2,64,768]{3,2,0,1:T(8,128)(2,1)S(1)} %bitcast.546), channel_id=1, source_target_pairs={{0,4},{4,0},{1,5},{5,1},{2,6},{6,2},{3,7},{7,3},{8,12},{12,8},{9,1... | collective-permute-start | bytes 2359304 | tf_op jit(solution)/shard_map/ppermute | solution.py:415
  668.5 27.3 %collective-permute-start.38 = (bf16[4,64,768]{2,1,0:T(8,128)(2,1)S(1)}, bf16[4,64,768]{2,1,0:T(8,128)(2,1)S(1)}, u32[]{:S(2)}, u32[]{:S(2)}) collective-permute-start(bf16[4,64,768]{2,1,0:T(8,128)(2,1)S(1)} %dynamic-slice_bitcast_fusion.20), channel_id=1, source_target_pairs={{0,4},{4,0},{1,5},{5,1},{2,6},{6,2},{3,7},{7,3},{8,12},{12,8},{9,1... | collective-permute-start | bytes 1179656 | tf_op jit(solution)/shard_map/ppermute | solution.py:415
  670.8 27.3 %collective-permute-start.44 = (bf16[4,64,768]{2,1,0:T(8,128)(2,1)S(1)}, bf16[4,64,768]{2,1,0:T(8,128)(2,1)S(1)}, u32[]{:S(2)}, u32[]{:S(2)}) collective-permute-start(bf16[4,64,768]{2,1,0:T(8,128)(2,1)S(1)} %dynamic-slice_bitcast_fusion.19), channel_id=1, source_target_pairs={{0,1},{1,0},{2,3},{3,2},{4,5},{5,4},{6,7},{7,6},{8,9},{9,8},{10,11... | collective-permute-start | bytes 1179656 | tf_op jit(solution)/shard_map/ppermute | solution.py:415
  770.3 366.3 %reduce-scatter.9.cloned.1.call-start = ((), (), s32[]{:S(2)}) async-start(), calls=%async_computation.7 | async-start | bytes 9732096
  789.4 111.9 %collective-permute-start.61 = (bf16[4,2,64,768]{3,2,1,0:T(8,128)(2,1)}, bf16[4,2,64,768]{3,2,1,0:T(8,128)(2,1)}, u32[]{:S(2)}, u32[]{:S(2)}) collective-permute-start(bf16[4,2,64,768]{3,2,1,0:T(8,128)(2,1)} %dynamic-slice_bitcast_fusion.7), channel_id=1, source_target_pairs={{0,4},{4,0},{1,5},{5,1},{2,6},{6,2},{3,7},{7,3},{8,12},{12,8},{9,1... | collective-permute-start | bytes 2359304 | tf_op jit(solution)/shard_map/ppermute | solution.py:415
  797.5 108.2 %collective-permute-start.72 = (bf16[4,2,2,64,768]{4,3,0,2,1:T(8,128)(2,1)}, bf16[4,2,2,64,768]{4,3,0,2,1:T(8,128)(2,1)}, u32[]{:S(2)}, u32[]{:S(2)}) collective-permute-start(bf16[4,2,2,64,768]{4,3,0,2,1:T(8,128)(2,1)} %bitcast.518), channel_id=1, source_target_pairs={{0,2},{2,0},{1,3},{3,1},{4,6},{6,4},{5,7},{7,5},{8,10},{10,8},{9,1... | collective-permute-start | bytes 4718600 | tf_op jit(solution)/shard_map/ppermute | solution.py:415
  837.7 22.4 %collective-permute-start.63 = (bf16[2,256,768]{2,1,0:T(8,128)(2,1)}, bf16[2,256,768]{2,1,0:T(8,128)(2,1)}, u32[]{:S(2)}, u32[]{:S(2)}) collective-permute-start(bf16[2,256,768]{2,1,0:T(8,128)(2,1)} %get-tuple-element.187), channel_id=1, source_target_pairs={{0,2},{2,0},{1,3},{3,1},{4,6},{6,4},{5,7},{7,5},{8,10},{10,8},{9,1... | collective-permute-start | bytes 2359304 | tf_op jit(solution)/shard_map/ppermute | solution.py:415
  855.9 70.0 %collective-permute-start.70 = (bf16[4,2,2,24,3456]{4,3,2,1,0:T(8,128)(2,1)}, bf16[4,2,2,24,3456]{4,3,2,1,0:T(8,128)(2,1)}, u32[]{:S(2)}, u32[]{:S(2)}) collective-permute-start(bf16[4,2,2,24,3456]{4,3,2,1,0:T(8,128)(2,1)} %dynamic-slice_bitcast_fusion), channel_id=1, source_target_pairs={{0,2},{2,0},{1,3},{3,1},{4,6},{6,4},{5,7},{7,5},{8,10},{10,8},{9,1... | collective-permute-start | bytes 7962632 | tf_op jit(solution)/shard_map/ppermute | solution.py:415
  1000.7 61.4 %collective-permute-start.74 = (bf16[2,512,768]{2,1,0:T(8,128)(2,1)}, bf16[2,512,768]{2,1,0:T(8,128)(2,1)}, u32[]{:S(2)}, u32[]{:S(2)}) collective-permute-start(bf16[2,512,768]{2,1,0:T(8,128)(2,1)} %get-tuple-element.193), channel_id=1, source_target_pairs={{0,2},{2,0},{1,3},{3,1},{4,6},{6,4},{5,7},{7,5},{8,10},{10,8},{9,1... | collective-permute-start | bytes 4718600 | tf_op jit(solution)/shard_map/ppermute | solution.py:415
  1002.1 29.1 %collective-permute-start.85 = (bf16[4,2,64,768]{3,2,0,1:T(8,128)(2,1)}, bf16[4,2,64,768]{3,2,0,1:T(8,128)(2,1)}, u32[]{:S(2)}, u32[]{:S(2)}) collective-permute-start(bf16[4,2,64,768]{3,2,0,1:T(8,128)(2,1)} %dynamic-slice_bitcast_fusion.6), channel_id=1, source_target_pairs={{0,4},{4,0},{1,5},{5,1},{2,6},{6,2},{3,7},{7,3},{8,12},{12,8},{9,1... | collective-permute-start | bytes 2359304 | tf_op jit(solution)/shard_map/ppermute | solution.py:415
  1002.9 39.1 %collective-permute-start.76 = (bf16[4,2,24,1408]{3,2,1,0:T(8,128)(2,1)}, bf16[4,2,24,1408]{3,2,1,0:T(8,128)(2,1)}, u32[]{:S(2)}, u32[]{:S(2)}) collective-permute-start(bf16[4,2,24,1408]{3,2,1,0:T(8,128)(2,1)} %dynamic-slice_bitcast_fusion.11), channel_id=1, source_target_pairs={{0,4},{4,0},{1,5},{5,1},{2,6},{6,2},{3,7},{7,3},{8,12},{12,8},{9,1... | collective-permute-start | bytes 1622024 | tf_op jit(solution)/shard_map/ppermute | solution.py:415
  1006.1 53.0 %collective-permute-start.75 = (bf16[4,2,24,3456]{3,2,1,0:T(8,128)(2,1)}, bf16[4,2,24,3456]{3,2,1,0:T(8,128)(2,1)}, u32[]{:S(2)}, u32[]{:S(2)}) collective-permute-start(bf16[4,2,24,3456]{3,2,1,0:T(8,128)(2,1)} %dynamic-slice_bitcast_fusion.2), channel_id=1, source_target_pairs={{0,1},{1,0},{2,3},{3,2},{4,5},{5,4},{6,7},{7,6},{8,9},{9,8},{10,11... | collective-permute-start | bytes 3981320 | tf_op jit(solution)/shard_map/ppermute | solution.py:415
  1032.9 25.4 %collective-permute-start.86 = (bf16[4,64,768]{2,1,0:T(8,128)(2,1)S(1)}, bf16[4,64,768]{2,1,0:T(8,128)(2,1)S(1)}, u32[]{:S(2)}, u32[]{:S(2)}) collective-permute-start(bf16[4,64,768]{2,1,0:T(8,128)(2,1)S(1)} %dynamic-slice_bitcast_fusion.15), channel_id=1, source_target_pairs={{0,1},{1,0},{2,3},{3,2},{4,5},{5,4},{6,7},{7,6},{8,9},{9,8},{10,11... | collective-permute-start | bytes 1179656 | tf_op jit(solution)/shard_map/ppermute | solution.py:415
  1072.4 23.0 %collective-permute-start.78 = (bf16[512,768]{1,0:T(8,128)(2,1)S(1)}, bf16[512,768]{1,0:T(8,128)(2,1)S(1)}, u32[]{:S(2)}, u32[]{:S(2)}) collective-permute-start(bf16[512,768]{1,0:T(8,128)(2,1)S(1)} %fusion.45.refs_1_), channel_id=1, source_target_pairs={{8,0},{16,8},{24,16},{9,1},{17,9},{25,17},{10,2},{18,10},{26,18},{... | collective-permute-start | bytes 2359304 | tf_op jit(solution)/shard_map/ppermute | solution.py:470
  1078.4 39.6 %collective-permute-start.88 = (bf16[4,2,2,24,1280]{4,3,2,1,0:T(8,128)(2,1)S(1)}, bf16[4,2,2,24,1280]{4,3,2,1,0:T(8,128)(2,1)S(1)}, u32[]{:S(2)}, u32[]{:S(2)}) collective-permute-start(bf16[4,2,2,24,1280]{4,3,2,1,0:T(8,128)(2,1)S(1)} %dynamic-slice_bitcast_fusion.4), channel_id=1, source_target_pairs={{0,2},{2,0},{1,3},{3,1},{4,6},{6,4},{5,7},{7,5},{8,10},{10,8},{9,1... | collective-permute-start | bytes 2949128 | tf_op jit(solution)/shard_map/ppermute | solution.py:415
  1087.4 30.2 %collective-permute-start.87 = (bf16[4,2,2,24,1152]{4,3,2,1,0:T(8,128)(2,1)S(1)}, bf16[4,2,2,24,1152]{4,3,2,1,0:T(8,128)(2,1)S(1)}, u32[]{:S(2)}, u32[]{:S(2)}) collective-permute-start(bf16[4,2,2,24,1152]{4,3,2,1,0:T(8,128)(2,1)S(1)} %dynamic-slice_bitcast_fusion.5), channel_id=1, source_target_pairs={{0,2},{2,0},{1,3},{3,1},{4,6},{6,4},{5,7},{7,5},{8,10},{10,8},{9,1... | collective-permute-start | bytes 2654216 | tf_op jit(solution)/shard_map/ppermute | solution.py:415
  1162.2 64.4 %collective-permute-start.97 = (bf16[4032,768]{1,0:T(8,128)(2,1)}, bf16[4032,768]{1,0:T(8,128)(2,1)}, u32[]{:S(2)}, u32[]{:S(2)}) collective-permute-start(bf16[4032,768]{1,0:T(8,128)(2,1)} %shard_map.473), channel_id=1, source_target_pairs={{0,2},{2,0},{1,3},{3,1},{4,6},{6,4},{5,7},{7,5},{8,10},{10,8},{9,1... | collective-permute-start | bytes 18579464 | tf_op jit(solution)/shard_map/ppermute | solution.py:415
  1172.1 27.2 %collective-permute-start.92 = (bf16[24,4864]{1,0:T(8,128)(2,1)S(1)}, bf16[24,4864]{1,0:T(8,128)(2,1)S(1)}, u32[]{:S(2)}, u32[]{:S(2)}) collective-permute-start(bf16[24,4864]{1,0:T(8,128)(2,1)S(1)} %get-tuple-element.541), channel_id=1, source_target_pairs={{0,16},{8,24},{16,0},{24,8},{1,17},{9,25},{17,1},{25,9},{2,18},{10... | collective-permute-start | bytes 700424 | tf_op jit(solution)/shard_map/ppermute | solution.py:456
  1199.8 26.6 %collective-permute-start.98 = (bf16[4,24,1152]{2,1,0:T(8,128)(2,1)S(1)}, bf16[4,24,1152]{2,1,0:T(8,128)(2,1)S(1)}, u32[]{:S(2)}, u32[]{:S(2)}) collective-permute-start(bf16[4,24,1152]{2,1,0:T(8,128)(2,1)S(1)} %dynamic-slice_bitcast_fusion.28), channel_id=1, source_target_pairs={{0,4},{4,0},{1,5},{5,1},{2,6},{6,2},{3,7},{7,3},{8,12},{12,8},{9,1... | collective-permute-start | bytes 663560 | tf_op jit(solution)/shard_map/ppermute | solution.py:415
  1200.7 25.8 %collective-permute-start.99 = (bf16[4,24,1280]{2,1,0:T(8,128)(2,1)S(1)}, bf16[4,24,1280]{2,1,0:T(8,128)(2,1)S(1)}, u32[]{:S(2)}, u32[]{:S(2)}) collective-permute-start(bf16[4,24,1280]{2,1,0:T(8,128)(2,1)S(1)} %dynamic-slice_bitcast_fusion.24), channel_id=1, source_target_pairs={{0,1},{1,0},{2,3},{3,2},{4,5},{5,4},{6,7},{7,6},{8,9},{9,8},{10,11... | collective-permute-start | bytes 737288 | tf_op jit(solution)/shard_map/ppermute | solution.py:415
  1229.7 50.3 %collective-permute-start.106 = (bf16[24,2432]{1,0:T(8,128)(2,1)}, bf16[24,2432]{1,0:T(8,128)(2,1)}, u32[]{:S(2)}, u32[]{:S(2)}) collective-permute-start(bf16[24,2432]{1,0:T(8,128)(2,1)} %get-tuple-element.554), channel_id=1, source_target_pairs={{0,24},{8,0},{16,8},{24,16},{1,25},{9,1},{17,9},{25,17},{2,26},{10... | collective-permute-start | bytes 350216 | tf_op jit(solution)/shard_map/ppermute | solution.py:456
  1257.6 33.8 %collective-permute-start.101 = (bf16[1008,768]{1,0:T(8,128)(2,1)}, bf16[1008,768]{1,0:T(8,128)(2,1)}, u32[]{:S(2)}, u32[]{:S(2)}) collective-permute-start(bf16[1008,768]{1,0:T(8,128)(2,1)} %pad_maximum_fusion.4), channel_id=1, source_target_pairs={{0,1},{1,0},{2,3},{3,2},{4,5},{5,4},{6,7},{7,6},{8,9},{9,8},{10,11... | collective-permute-start | bytes 4644872 | tf_op jit(solution)/shard_map/ppermute | solution.py:415
  1259.8 33.5 %collective-permute-start.103 = (bf16[1008,768]{1,0:T(8,128)(2,1)}, bf16[1008,768]{1,0:T(8,128)(2,1)}, u32[]{:S(2)}, u32[]{:S(2)}) collective-permute-start(bf16[1008,768]{1,0:T(8,128)(2,1)} %pad_maximum_fusion.5), channel_id=1, source_target_pairs={{0,4},{4,0},{1,5},{5,1},{2,6},{6,2},{3,7},{7,3},{8,12},{12,8},{9,1... | collective-permute-start | bytes 4644872 | tf_op jit(solution)/shard_map/ppermute | solution.py:415
  (257 other events, 2865.5 us)
Sparse Core Ops, SparseCore 0:
  20.0 134.2 all-gather.4
  162.2 108.7 all-gather.6
  316.6 80.3 all-gather.8
  438.0 95.4 all-gather.10
  770.4 116.8 reduce-scatter.6
  937.2 142.8 reduce-scatter.8

commit v10 on v9

--- a/solution.py
+++ b/solution.py
@@ -839,7 +839,7 @@
     )
     late = lax.psum_scatter(late, ALL, scatter_dimension=0, tiled=True)
     early = early.astype(f32)
-    enc_sums = [scatter_first(item, number == 0) for number, item in enumerate(enc_sums)]
+    enc_sums = [scatter_first(enc_sums[0], True), scatter_first(enc_sums[1], False), enc_sums[2]]
     d_enc_q, own, other, enc_y8 = attend_backward(
         d_enc_ob, enc_lse, enc_q, enc_kv, enc_kv2, enc_info, enc_x8, False
     )
@@ -850,8 +850,8 @@
     d_x0_norm, d_gain_eatt = norm_pull(enc_x0, gain[0], 1.0, input_grad(d_enc_qkv, enc_wi))
     d_x0 = d_x1 + d_x0_norm
 
-    d_x0, wides = lax.optimization_barrier((d_x0.astype(bf16), enc_sums[:2]))
-    enc_sums = wides + enc_sums[2:]
+    d_x0, enc_sums = lax.optimization_barrier((d_x0.astype(bf16), enc_sums))
+    enc_sums[2] = scatter_first(enc_sums[2], False)
     enc_sums = [scatter_second(item, number == 0) for number, item in enumerate(enc_sums)]
     enc_lines = line_gather(d_x0, "z")
     enc_lines, enc_sums = lax.optimization_barrier((enc_lines, enc_sums))

time: 1370 us -> 1340 us (0.978)
  waiting for transfers between devices: 407 us -> 379 us
    ppermute x50, waiting for transfers between devices: 145 us -> 128 us  [swap(): return lax.ppermute(value, axis, [(0, 1), (1, 0)])]
    unnamed x404 -> x398, local copies, waits for them, and re-layouts: 43.6 us -> 43.5 us
  transfers between devices with their start and end apart: 118 -> 118, of which waited for: 54 -> 53; matrix products, arithmetic and copies ran while one was open for 25% -> 26% of each run, Pallas kernels for 13% -> 14%
where the time goes in v10:
time: 1340 us; the launch traced here: 1330 us
  waiting for transfers between devices  379 us (28%)
  Pallas kernels  278 us (21%)
  starting transfers between devices  192 us (14%)
  local copies, waits for them, and re-layouts  178 us (13%)
  other arithmetic  141 us (11%)
  matrix products  133 us (10%)
  between operations  29.6 us (2%)
    ppermute x50, waiting for transfers between devices, swap(): return lax.ppermute(value, axis, [(0, 1), (1, 0)])  128 us
    pallas_call x3, Pallas kernels, attend_backward(): pl.pallas_call(functools.partial(attend_backward_kernel, cfg), grid=(HEAD...  87.5 us
    all_gather x1, waiting for transfers between devices, body(): hidden_all = lax.all_gather(hidden_b, ALL, axis=0, tiled=True)  77.3 us
    ppermute x3, waiting for transfers between devices, line_scatter(): up = lax.ppermute(send_up, axis, [(i, i + 1) for i in range(step)])  75.1 us
    pallas_call x4, Pallas kernels, head_grad(): pl.pallas_call(functools.partial(head_grad_kernel, count), grid_spec=pltp...  63.4 us
    ppermute x50, starting transfers between devices, swap(): return lax.ppermute(value, axis, [(0, 1), (1, 0)])  58 us
    pallas_call x3, Pallas kernels, attend_forward(): pl.pallas_call(functools.partial(attend_forward_kernel, cfg), grid=(HEADS...  53.9 us
    dot_general x11, matrix products, input_grad(): return jnp.einsum('te,de->td', grads, weight, preferred_element_type=f32)  52.6 us
  transfers between devices with their start and end apart: 118, of which 53 were waited for; matrix products, arithmetic and copies ran while one was open for 26% of the time, Pallas kernels for 14%

profile of v10, /device:TPU:0, one launch (start us, length us, event | category | flops | bytes accessed | tf_op | source)
XLA Modules:
  0.0 1330.0 jit_solution(5162085542285483990)
XLA Ops:
  60.1 10.5 collective-permute-done.1
  70.6 18.0 %collective-permute-start.6 = (bf16[1008,768]{1,0:T(8,128)(2,1)S(1)}, bf16[1008,768]{1,0:T(8,128)(2,1)S(1)}, u32[]{:S(2)}, u32[]{:S(2)}) collective-permute-start(bf16[1008,768]{1,0:T(8,128)(2,1)S(1)} %collective-permute-done.1), channel_id=1, source_target_pairs={{0,2},{2,0},{1,3},{3,1},{4,6},{6,4},{5,7},{7,5},{8,10},{10,8},{9,1... | collective-permute-start | bytes 4644872 | tf_op jit(solution)/shard_map/ppermute | solution.py:415
  98.5 31.5 %collective-permute-done.3 = bf16[504,768]{1,0:T(8,128)(2,1)S(1)} collective-permute-done((bf16[504,768]{1,0:T(8,128)(2,1)S(1)}, bf16[504,768]{1,0:T(8,128)(2,1)S(1)}, u32[]{:S(2)}, u32[]{:S(2)}) %collective-permute-start.3) | collective-permute-done | bytes 774176 | tf_op jit(solution)/shard_map/ppermute | solution.py:415
  140.9 20.9 %gather_fusion = bf16[3072,768]{1,0:T(8,128)(2,1)} fusion(bf16[8064,768]{1,0:T(8,128)(2,1)} %constant_dynamic-update-slice_fusion.4, s32[3072]{0:T(1024)S(1)} %add_clamp_fusion), kind=kCustom, calls=%fused_computation | custom fusion | bytes 9449472 | tf_op jit(solution)/shard_map/jit(_take)/gather | solution.py:677
  194.4 27.4 %collective-permute-done.16 = bf16[768,768]{1,0:T(8,128)(2,1)S(1)} collective-permute-done((bf16[768,768]{1,0:T(8,128)(2,1)S(1)}, bf16[768,768]{1,0:T(8,128)(2,1)S(1)}, u32[]{:S(2)}, u32[]{:S(2)}) %collective-permute-start.16) | collective-permute-done | bytes 1179680 | tf_op jit(solution)/shard_map/ppermute | solution.py:482
  224.3 6.1 collective-permute-start.17
  249.8 25.6 %collective-permute-done.17 = bf16[768,768]{1,0:T(8,128)(2,1)} collective-permute-done((bf16[768,768]{1,0:T(8,128)(2,1)}, bf16[768,768]{1,0:T(8,128)(2,1)}, u32[]{:S(2)}, u32[]{:S(2)}) %collective-permute-start.17) | collective-permute-done | bytes 1179680 | tf_op jit(solution)/shard_map/ppermute | solution.py:482
  278.0 6.6 collective-permute-start.20
  286.7 22.1 %collective-permute-done.20 = bf16[768,768]{1,0:T(8,128)(2,1)} collective-permute-done((bf16[768,768]{1,0:T(8,128)(2,1)S(1)}, bf16[768,768]{1,0:T(8,128)(2,1)}, u32[]{:S(2)}, u32[]{:S(2)}) %collective-permute-start.20) | collective-permute-done | bytes 1179680 | tf_op jit(solution)/shard_map/ppermute | solution.py:482
  308.7 5.2 collective-permute-done.21
  332.8 28.9 %shard_map.462 = (bf16[512,768]{1,0:T(8,128)(2,1)}, f32[512,768]{1,0:T(8,128)}) custom-call(bf16[512,768]{1,0:T(8,128)(2,1)} %convolution_convert_fusion.15.refs_0_, bf16[512,1536]{1,0:T(8,128)(2,1)} %convolution_convert_fusion.8.refs_1_.refs_2_, bf16[512,1536]{1,0:T(8,128)(2,1)} %convolution_convert_fusion.8.refs_1_.refs_2_, ...), custom_call_target="tpu_custom_call" | custom-call | flops 2 | bytes 512 | tf_op jit(solution)/shard_map/pallas_call | solution.py:200
  364.2 6.3 fusion.6
  387.8 13.2 shard_map.461
  405.8 11.8 shard_map.463
  419.7 4.9 fusion.2
  455.9 77.3 %all-gather.11.cloned.1.call-done = bf16[8192,768]{1,0:T(8,128)(2,1)} async-done(((bf16[256,768]{1,0:T(8,128)(2,1)}), bf16[8192,768]{1,0:T(8,128)(2,1)}) %all-gather.11.cloned.1.call-update) | async-done | bytes 12582928 | tf_op jit(solution)/shard_map/all_gather | solution.py:751
  533.2 25.8 %shard_map.464 = (f32[1,8192]{1,0:T(1,128)}, f32[1,8192]{1,0:T(1,128)}) custom-call(bf16[8,2,2,256,768]{4,3,2,1,0:T(8,128)(2,1)} %bitcast.612, bf16[1008,768]{1,0:T(8,128)(2,1)} %get-tuple-element.539.tab, s32[1,8192]{1,0:T(1,128)} %bitcast.571), custom_call_target="tpu_custom_call" | custom-call | flops 12683575296 | bytes 12582912 | tf_op jit(solution)/shard_map/pallas_call | solution.py:306
  581.0 15.8 %shard_map.465 = (bf16[8,2,64,768]{3,2,1,0:T(8,128)(2,1)}, bf16[8,2,64,768]{3,2,1,0:T(8,128)(2,1)}, f32[1008,768]{1,0:T(8,128)}) custom-call(s32[1]{0:T(128)} %bitcast.97.core, bf16[8,2,2,256,768]{4,3,2,1,0:T(8,128)(2,1)} %bitcast.613, bf16[1008,768]{1,0:T(8,128)(2,1)} %get-tuple-element.539.tab, s32[1,8192]{1,0:T(1,128)} %bitcast.572, f32[1,8192]{1,0:T(1,128)} %bitcast.550, ...), custom_call_target="tpu_custom_call" | custom-call | flops 9512681472 | bytes 6291456 | tf_op jit(solution)/shard_map/pallas_call | solution.py:329
  596.8 15.8 %shard_map.467 = (bf16[8,2,64,768]{3,2,1,0:T(8,128)(2,1)}, bf16[8,2,64,768]{3,2,1,0:T(8,128)(2,1)}, f32[1008,768]{1,0:T(8,128)}) custom-call(s32[1]{0:T(128)} %bitcast.97.core, bf16[8,2,2,256,768]{4,3,2,1,0:T(8,128)(2,1)} %bitcast.614, bf16[1008,768]{1,0:T(8,128)(2,1)} %get-tuple-element.539.tab, s32[1,8192]{1,0:T(1,128)} %bitcast.573, f32[1,8192]{1,0:T(1,128)} %bitcast.551, ...), custom_call_target="tpu_custom_call" | custom-call | flops 9512681472 | bytes 6291456 | tf_op jit(solution)/shard_map/pallas_call | solution.py:329
  613.2 15.8 %shard_map.466 = (bf16[8,2,64,768]{3,2,1,0:T(8,128)(2,1)}, bf16[8,2,64,768]{3,2,1,0:T(8,128)(2,1)}, f32[1008,768]{1,0:T(8,128)}) custom-call(s32[1]{0:T(128)} %bitcast.98.core, bf16[8,2,2,256,768]{4,3,2,1,0:T(8,128)(2,1)} %bitcast.615, bf16[1008,768]{1,0:T(8,128)(2,1)} %get-tuple-element.539.tab, s32[1,8192]{1,0:T(1,128)} %bitcast.574, f32[1,8192]{1,0:T(1,128)} %bitcast.552, ...), custom_call_target="tpu_custom_call" | custom-call | flops 9512681472 | bytes 6291456 | tf_op jit(solution)/shard_map/pallas_call | solution.py:329
  629.6 16.0 %shard_map.468 = (bf16[8,2,64,768]{3,2,1,0:T(8,128)(2,1)}, bf16[8,2,64,768]{3,2,1,0:T(8,128)(2,1)}, f32[1008,768]{1,0:T(8,128)}) custom-call(s32[1]{0:T(128)} %bitcast.98.core, bf16[8,2,2,256,768]{4,3,2,1,0:T(8,128)(2,1)} %bitcast.616, bf16[1008,768]{1,0:T(8,128)(2,1)} %get-tuple-element.539.tab, s32[1,8192]{1,0:T(1,128)} %bitcast.575, f32[1,8192]{1,0:T(1,128)} %bitcast.553, ...), custom_call_target="tpu_custom_call" | custom-call | flops 9512681472 | bytes 6291456 | tf_op jit(solution)/shard_map/pallas_call | solution.py:329
  654.8 13.3 %collective-permute-done.37 = bf16[4,2,64,768]{3,2,0,1:T(8,128)(2,1)S(1)} collective-permute-done((bf16[4,2,64,768]{3,2,0,1:T(8,128)(2,1)S(1)}, bf16[4,2,64,768]{3,2,0,1:T(8,128)(2,1)S(1)}, u32[]{:S(2)}, u32[]{:S(2)}) %collective-permute-start.37) | collective-permute-done | bytes 786464 | tf_op jit(solution)/shard_map/ppermute | solution.py:415
  671.8 13.2 collective-permute-done.49
  688.6 7.0 collective-permute-done.38
  724.5 5.0 collective-permute-done.58
  734.6 4.6 convolution_convert_fusion.1
  739.3 6.8 multiply_reduce_fusion.13
  749.8 16.6 %shard_map.469 = (bf16[256,768]{1,0:T(8,128)(2,1)}, f32[2,512,768]{2,1,0:T(8,128)}, bf16[2,512,768]{2,1,0:T(8,128)(2,1)}) custom-call(bf16[256,768]{1,0:T(8,128)(2,1)} %convolution_convert_fusion.18.refs_0_, bf16[512,1536]{1,0:T(8,128)(2,1)} %convolution_convert_fusion.7.refs_1_.refs_2_, bf16[512,1536]{1,0:T(8,128)(2,1)} %convolution_convert_fusion.7.refs_1_.refs_2_, ...), custom_call_target="tpu_custom_call" | custom-call | flops 5 | bytes 256 | tf_op jit(solution)/shard_map/pallas_call | solution.py:227
  797.4 22.8 %shard_map.470 = (bf16[256,768]{1,0:T(8,128)(2,1)}, f32[2,256,768]{2,1,0:T(8,128)}, bf16[2,256,768]{2,1,0:T(8,128)(2,1)}, f32[12,2,8,512]{3,2,1,0:T(8,128)}) custom-call(bf16[256,768]{1,0:T(8,128)(2,1)} %convolution_convert_fusion.19.refs_0_, bf16[256,1536]{1,0:T(8,128)(2,1)} %copy-done.5, bf16[256,1536]{1,0:T(8,128)(2,1)} %copy-done.5, ...), custom_call_target="tpu_custom_call" | custom-call | flops 5 | bytes 256 | tf_op jit(solution)/shard_map/pallas_call | solution.py:227
  820.2 8.8 fusion.57
  831.0 5.8 convolution_convert_fusion
  837.8 12.2 multiply_reduce_fusion.3
  925.4 4.8 fusion.8
  958.7 48.2 %shard_map.471 = (bf16[512,768]{1,0:T(8,128)(2,1)}, f32[2,512,768]{2,1,0:T(8,128)}, bf16[2,512,768]{2,1,0:T(8,128)(2,1)}, f32[12,4,8,768]{3,2,1,0:T(8,128)}) custom-call(bf16[512,768]{1,0:T(8,128)(2,1)} %convolution_convert_fusion.15.refs_0_, bf16[512,1536]{1,0:T(8,128)(2,1)} %convolution_convert_fusion.8.refs_1_.refs_2_, ...), custom_call_target="tpu_custom_call" | custom-call | flops 5 | bytes 512 | tf_op jit(solution)/shard_map/pallas_call | solution.py:227
  1036.7 6.6 collective-permute-done.84
  1044.1 11.8 collective-permute-done.83
  1064.0 13.5 %collective-permute-done.85 = bf16[4,2,64,768]{3,2,0,1:T(8,128)(2,1)S(1)} collective-permute-done((bf16[4,2,64,768]{3,2,0,1:T(8,128)(2,1)S(1)}, bf16[4,2,64,768]{3,2,0,1:T(8,128)(2,1)S(1)}, u32[]{:S(2)}, u32[]{:S(2)}) %collective-permute-start.85) | collective-permute-done | bytes 786464 | tf_op jit(solution)/shard_map/ppermute | solution.py:415
  1092.0 11.0 collective-permute-done.82
  1111.1 23.8 %shard_map.473 = bf16[4032,768]{1,0:T(8,128)(2,1)} custom-call(s32[1,512]{1,0:T(1,128)} %bitcast.576, bf16[512,768]{1,0:T(8,128)(2,1)} %copy-done.23, s32[1,512]{1,0:T(1,128)} %bitcast.580, bf16[512,768]{1,0:T(8,128)(2,1)} %add.1275.refs_3_, s32[1,512]{1,0:T(1,128)} %bitcast.578, bf16[512,768]{1,0:T(8,128)(2,1)} %add.1276.refs_5_, s32[1,512]{1,0:T(1,128)} %bitcast.582, ...), custom_call_target="tpu_custom_call" | custom-call | flops 1 | bytes 1008 | tf_op jit(solution)/shard_map/pallas_call | solution.py:374
  1140.0 4.8 collective-permute-done.94
  1144.8 8.4 collective-permute-done.95
  1153.3 4.7 collective-permute-start.93
  1161.4 10.6 collective-permute-done.92
  1176.0 23.7 %shard_map.472 = bf16[4032,768]{1,0:T(8,128)(2,1)} custom-call(s32[1,512]{1,0:T(1,128)} %bitcast.577, bf16[512,768]{1,0:T(8,128)(2,1)} %copy-done.23, s32[1,512]{1,0:T(1,128)} %bitcast.581, bf16[512,768]{1,0:T(8,128)(2,1)} %add.1275.refs_3_, s32[1,512]{1,0:T(1,128)} %bitcast.579, bf16[512,768]{1,0:T(8,128)(2,1)} %add.1276.refs_5_, s32[1,512]{1,0:T(1,128)} %bitcast.583, ...), custom_call_target="tpu_custom_call" | custom-call | flops 1 | bytes 1008 | tf_op jit(solution)/shard_map/pallas_call | solution.py:374
  1203.0 4.9 collective-permute-start.106
  1212.6 13.4 %collective-permute-done.100 = bf16[504,768]{1,0:T(8,128)(2,1)S(1)} collective-permute-done((bf16[504,768]{1,0:T(8,128)(2,1)S(1)}, bf16[504,768]{1,0:T(8,128)(2,1)S(1)}, u32[]{:S(2)}, u32[]{:S(2)}) %collective-permute-start.100) | collective-permute-done | bytes 774176 | tf_op jit(solution)/shard_map/ppermute | solution.py:415
  1266.9 8.5 multiply_reduce_fusion.1
  1309.3 6.7 add_subtract_fusion
  (990 shorter events, 573.0 us)
Async XLA Ops:
  7.2 154.6 %all-gather.5.cloned.1.call-start = ((), (), s32[]{:S(2)}) async-start(), calls=%async_computation.2 | async-start | bytes 14800896 | tf_op jit(solution)/shard_map/all_gather | solution.py:617
  19.8 296.5 %all-gather.7.cloned.1.call-start = ((), (), s32[]{:S(2)}) async-start(), calls=%async_computation.3 | async-start | bytes 9732096 | tf_op jit(solution)/shard_map/all_gather | solution.py:679
  22.0 48.6 %collective-permute-start.1 = (bf16[1008,768]{1,0:T(8,128)(2,1)}, bf16[1008,768]{1,0:T(8,128)(2,1)S(1)}, u32[]{:S(2)}, u32[]{:S(2)}) collective-permute-start(bf16[1008,768]{1,0:T(8,128)(2,1)} %get-tuple-element.539.tab), channel_id=1, source_target_pairs={{0,1},{1,0},{2,3},{3,2},{4,5},{5,4},{6,7},{7,6},{8,9},{9,8},{10,11... | collective-permute-start | bytes 4644872 | tf_op jit(solution)/shard_map/ppermute | solution.py:415
  24.9 68.6 %collective-permute-start.2 = (bf16[1008,768]{1,0:T(8,128)(2,1)}, bf16[1008,768]{1,0:T(8,128)(2,1)S(1)}, u32[]{:S(2)}, u32[]{:S(2)}) collective-permute-start(bf16[1008,768]{1,0:T(8,128)(2,1)} %get-tuple-element.539.tab), channel_id=1, source_target_pairs={{0,4},{4,0},{1,5},{5,1},{2,6},{6,2},{3,7},{7,3},{8,12},{12,8},{9,1... | collective-permute-start | bytes 4644872 | tf_op jit(solution)/shard_map/ppermute | solution.py:415
  26.4 107.3 %collective-permute-start.5 = (bf16[1008,768]{1,0:T(8,128)(2,1)}, bf16[1008,768]{1,0:T(8,128)(2,1)}, u32[]{:S(2)}, u32[]{:S(2)}) collective-permute-start(bf16[1008,768]{1,0:T(8,128)(2,1)} %get-tuple-element.539.tab), channel_id=1, source_target_pairs={{0,2},{2,0},{1,3},{3,1},{4,6},{6,4},{5,7},{7,5},{8,10},{10,8},{9,1... | collective-permute-start | bytes 4644872 | tf_op jit(solution)/shard_map/ppermute | solution.py:415
  54.2 35.1 %collective-permute-start.14 = (s32[768]{0:T(1024)S(1)}, s32[768]{0:T(1024)S(1)}, u32[]{:S(2)}, u32[]{:S(2)}) collective-permute-start(s32[768]{0:T(1024)S(1)} %collective-permute-done.10), channel_id=1, source_target_pairs={{0,8},{8,16},{16,24},{1,9},{9,17},{17,25},{2,10},{10,18},{18,26},{... | collective-permute-start | bytes 9224 | tf_op jit(solution)/shard_map/ppermute | solution.py:469
  58.8 35.5 %collective-permute-start.13 = (s32[768]{0:T(1024)S(1)}, s32[768]{0:T(1024)S(1)}, u32[]{:S(2)}, u32[]{:S(2)}) collective-permute-start(s32[768]{0:T(1024)S(1)} %collective-permute-done.12), channel_id=1, source_target_pairs={{8,0},{16,8},{24,16},{9,1},{17,9},{25,17},{10,2},{18,10},{26,18},{... | collective-permute-start | bytes 9224 | tf_op jit(solution)/shard_map/ppermute | solution.py:470
  70.6 65.9 %collective-permute-start.6 = (bf16[1008,768]{1,0:T(8,128)(2,1)S(1)}, bf16[1008,768]{1,0:T(8,128)(2,1)S(1)}, u32[]{:S(2)}, u32[]{:S(2)}) collective-permute-start(bf16[1008,768]{1,0:T(8,128)(2,1)S(1)} %collective-permute-done.1), channel_id=1, source_target_pairs={{0,2},{2,0},{1,3},{3,1},{4,6},{6,4},{5,7},{7,5},{8,10},{10,8},{9,1... | collective-permute-start | bytes 4644872 | tf_op jit(solution)/shard_map/ppermute | solution.py:415
  93.6 36.4 %collective-permute-start.3 = (bf16[504,768]{1,0:T(8,128)(2,1)S(1)}, bf16[504,768]{1,0:T(8,128)(2,1)S(1)}, u32[]{:S(2)}, u32[]{:S(2)}) collective-permute-start(bf16[504,768]{1,0:T(8,128)(2,1)S(1)} %slice.616), channel_id=1, source_target_pairs={{0,1},{1,0},{2,3},{3,2},{4,5},{5,4},{6,7},{7,6},{8,9},{9,8},{10,11... | collective-permute-start | bytes 2322440 | tf_op jit(solution)/shard_map/ppermute | solution.py:415
  94.3 43.4 %collective-permute-start.7 = (bf16[1008,768]{1,0:T(8,128)(2,1)S(1)}, bf16[1008,768]{1,0:T(8,128)(2,1)S(1)}, u32[]{:S(2)}, u32[]{:S(2)}) collective-permute-start(bf16[1008,768]{1,0:T(8,128)(2,1)S(1)} %collective-permute-done.2), channel_id=1, source_target_pairs={{0,2},{2,0},{1,3},{3,1},{4,6},{6,4},{5,7},{7,5},{8,10},{10,8},{9,1... | collective-permute-start | bytes 4644872 | tf_op jit(solution)/shard_map/ppermute | solution.py:415
  94.9 36.4 %collective-permute-start.4 = (bf16[504,768]{1,0:T(8,128)(2,1)S(1)}, bf16[504,768]{1,0:T(8,128)(2,1)S(1)}, u32[]{:S(2)}, u32[]{:S(2)}) collective-permute-start(bf16[504,768]{1,0:T(8,128)(2,1)S(1)} %slice.617), channel_id=1, source_target_pairs={{0,4},{4,0},{1,5},{5,1},{2,6},{6,2},{3,7},{7,3},{8,12},{12,8},{9,1... | collective-permute-start | bytes 2322440 | tf_op jit(solution)/shard_map/ppermute | solution.py:415
  161.9 257.8 %all-gather.9.cloned.1.call-start = ((), (), s32[]{:S(2)}) async-start(), calls=%async_computation.4 | async-start | bytes 9732096 | tf_op jit(solution)/shard_map/all_gather | solution.py:705
  178.8 43.0 %collective-permute-start.16 = (bf16[768,768]{1,0:T(8,128)(2,1)S(1)}, bf16[768,768]{1,0:T(8,128)(2,1)S(1)}, u32[]{:S(2)}, u32[]{:S(2)}) collective-permute-start(bf16[768,768]{1,0:T(8,128)(2,1)S(1)} %get-tuple-element.514), channel_id=1, source_target_pairs={{0,8},{1,9},{2,10},{3,11},{4,12},{5,13},{6,14},{7,15}} | collective-permute-start | bytes 3538952 | tf_op jit(solution)/shard_map/ppermute | solution.py:482
  192.7 57.1 %collective-permute-start.19 = (bf16[768,768]{1,0:T(8,128)(2,1)}, bf16[768,768]{1,0:T(8,128)(2,1)}, u32[]{:S(2)}, u32[]{:S(2)}) collective-permute-start(bf16[768,768]{1,0:T(8,128)(2,1)} %get-tuple-element.513), channel_id=1, source_target_pairs={{24,16},{16,8},{25,17},{17,9},{26,18},{18,10},{27,19},{19,11},{28,... | collective-permute-start | bytes 3538952 | tf_op jit(solution)/shard_map/ppermute | solution.py:483
  224.3 51.1 %collective-permute-start.17 = (bf16[768,768]{1,0:T(8,128)(2,1)}, bf16[768,768]{1,0:T(8,128)(2,1)}, u32[]{:S(2)}, u32[]{:S(2)}) collective-permute-start(bf16[768,768]{1,0:T(8,128)(2,1)} %slice_add_fusion.4), channel_id=1, source_target_pairs={{0,8},{8,16},{1,9},{9,17},{2,10},{10,18},{3,11},{11,19},{4,12},{12... | collective-permute-start | bytes 3538952 | tf_op jit(solution)/shard_map/ppermute | solution.py:482
  278.0 30.8 %collective-permute-start.20 = (bf16[768,768]{1,0:T(8,128)(2,1)S(1)}, bf16[768,768]{1,0:T(8,128)(2,1)}, u32[]{:S(2)}, u32[]{:S(2)}) collective-permute-start(bf16[768,768]{1,0:T(8,128)(2,1)S(1)} %get-tuple-element.511), channel_id=1, source_target_pairs={{0,8},{8,16},{16,24},{1,9},{9,17},{17,25},{2,10},{10,18},{18,26},{... | collective-permute-start | bytes 3538952 | tf_op jit(solution)/shard_map/ppermute | solution.py:482
  284.6 29.4 %collective-permute-start.21 = (bf16[768,768]{1,0:T(8,128)(2,1)S(1)}, bf16[768,768]{1,0:T(8,128)(2,1)}, u32[]{:S(2)}, u32[]{:S(2)}) collective-permute-start(bf16[768,768]{1,0:T(8,128)(2,1)S(1)} %get-tuple-element.512), channel_id=1, source_target_pairs={{24,16},{16,8},{8,0},{25,17},{17,9},{9,1},{26,18},{18,10},{10,2},{... | collective-permute-start | bytes 3538952 | tf_op jit(solution)/shard_map/ppermute | solution.py:483
  316.4 216.8 %all-gather.11.cloned.1.call-start = ((), (), s32[]{:S(2)}) async-start(), calls=%async_computation.5 | async-start | bytes 12976128 | tf_op jit(solution)/shard_map/all_gather | solution.py:751
  329.3 58.5 %collective-permute-start.22 = (bf16[256,1536]{1,0:T(8,128)(2,1)S(1)}, bf16[256,1536]{1,0:T(8,128)(2,1)}, u32[]{:S(2)}, u32[]{:S(2)}) collective-permute-start(bf16[256,1536]{1,0:T(8,128)(2,1)S(1)} %convolution_convert_fusion.9.refs_1_.refs_2_), channel_id=1, source_target_pairs={{0,2},{2,0},{1,3},{3,1},{4,6},{6,4},{5,7},{7,5},{8,10},{10,8},{9,1... | collective-permute-start | bytes 2359304 | tf_op jit(solution)/shard_map/ppermute | solution.py:415
  381.5 24.3 %collective-permute-start.24 = (bf16[512,1536]{1,0:T(8,128)(2,1)}, bf16[512,1536]{1,0:T(8,128)(2,1)}, u32[]{:S(2)}, u32[]{:S(2)}) collective-permute-start(bf16[512,1536]{1,0:T(8,128)(2,1)} %convolution_convert_fusion.7.refs_1_.refs_2_), channel_id=1, source_target_pairs={{0,2},{2,0},{1,3},{3,1},{4,6},{6,4},{5,7},{7,5},{8,10},{10,8},{9,1... | collective-permute-start | bytes 4718600 | tf_op jit(solution)/shard_map/ppermute | solution.py:415
  437.6 474.8 %reduce-scatter.7.cloned.1.call-start = ((), (), s32[]{:S(2)}) async-start(), calls=%async_computation.6 | async-start | bytes 6488064
  612.6 32.9 %collective-permute-start.36 = (bf16[8,2,64,768]{3,2,1,0:T(8,128)(2,1)}, bf16[8,2,64,768]{3,2,1,0:T(8,128)(2,1)S(1)}, u32[]{:S(2)}, u32[]{:S(2)}) collective-permute-start(bf16[8,2,64,768]{3,2,1,0:T(8,128)(2,1)} %get-tuple-element.168), channel_id=1, source_target_pairs={{0,2},{2,0},{1,3},{3,1},{4,6},{6,4},{5,7},{7,5},{8,10},{10,8},{9,1... | collective-permute-start | bytes 4718600 | tf_op jit(solution)/shard_map/ppermute | solution.py:415
  612.7 36.5 %collective-permute-start.42 = (bf16[8,2,64,768]{3,2,1,0:T(8,128)(2,1)}, bf16[8,2,64,768]{3,2,1,0:T(8,128)(2,1)S(1)}, u32[]{:S(2)}, u32[]{:S(2)}) collective-permute-start(bf16[8,2,64,768]{3,2,1,0:T(8,128)(2,1)} %get-tuple-element.170), channel_id=1, source_target_pairs={{0,2},{2,0},{1,3},{3,1},{4,6},{6,4},{5,7},{7,5},{8,10},{10,8},{9,1... | collective-permute-start | bytes 4718600 | tf_op jit(solution)/shard_map/ppermute | solution.py:415
  629.1 23.8 %collective-permute-start.54 = (bf16[8,2,64,768]{3,2,1,0:T(8,128)(2,1)}, bf16[8,2,64,768]{3,2,1,0:T(8,128)(2,1)S(1)}, u32[]{:S(2)}, u32[]{:S(2)}) collective-permute-start(bf16[8,2,64,768]{3,2,1,0:T(8,128)(2,1)} %get-tuple-element.174), channel_id=1, source_target_pairs={{0,2},{2,0},{1,3},{3,1},{4,6},{6,4},{5,7},{7,5},{8,10},{10,8},{9,1... | collective-permute-start | bytes 4718600 | tf_op jit(solution)/shard_map/ppermute | solution.py:415
  651.8 33.2 %collective-permute-start.49 = (bf16[4,2,64,768]{3,2,0,1:T(8,128)(2,1)S(1)}, bf16[4,2,64,768]{3,2,0,1:T(8,128)(2,1)S(1)}, u32[]{:S(2)}, u32[]{:S(2)}) collective-permute-start(bf16[4,2,64,768]{3,2,0,1:T(8,128)(2,1)S(1)} %bitcast.545), channel_id=1, source_target_pairs={{0,1},{1,0},{2,3},{3,2},{4,5},{5,4},{6,7},{7,6},{8,9},{9,8},{10,11... | collective-permute-start | bytes 2359304 | tf_op jit(solution)/shard_map/ppermute | solution.py:415
  653.6 33.6 %collective-permute-start.55 = (bf16[4,2,64,768]{3,2,0,1:T(8,128)(2,1)S(1)}, bf16[4,2,64,768]{3,2,0,1:T(8,128)(2,1)S(1)}, u32[]{:S(2)}, u32[]{:S(2)}) collective-permute-start(bf16[4,2,64,768]{3,2,0,1:T(8,128)(2,1)S(1)} %bitcast.546), channel_id=1, source_target_pairs={{0,4},{4,0},{1,5},{5,1},{2,6},{6,2},{3,7},{7,3},{8,12},{12,8},{9,1... | collective-permute-start | bytes 2359304 | tf_op jit(solution)/shard_map/ppermute | solution.py:415
  668.4 27.3 %collective-permute-start.38 = (bf16[4,64,768]{2,1,0:T(8,128)(2,1)S(1)}, bf16[4,64,768]{2,1,0:T(8,128)(2,1)S(1)}, u32[]{:S(2)}, u32[]{:S(2)}) collective-permute-start(bf16[4,64,768]{2,1,0:T(8,128)(2,1)S(1)} %dynamic-slice_bitcast_fusion.20), channel_id=1, source_target_pairs={{0,4},{4,0},{1,5},{5,1},{2,6},{6,2},{3,7},{7,3},{8,12},{12,8},{9,1... | collective-permute-start | bytes 1179656 | tf_op jit(solution)/shard_map/ppermute | solution.py:415
  670.6 27.3 %collective-permute-start.44 = (bf16[4,64,768]{2,1,0:T(8,128)(2,1)S(1)}, bf16[4,64,768]{2,1,0:T(8,128)(2,1)S(1)}, u32[]{:S(2)}, u32[]{:S(2)}) collective-permute-start(bf16[4,64,768]{2,1,0:T(8,128)(2,1)S(1)} %dynamic-slice_bitcast_fusion.19), channel_id=1, source_target_pairs={{0,1},{1,0},{2,3},{3,2},{4,5},{5,4},{6,7},{7,6},{8,9},{9,8},{10,11... | collective-permute-start | bytes 1179656 | tf_op jit(solution)/shard_map/ppermute | solution.py:415
  770.1 339.0 %reduce-scatter.9.cloned.1.call-start = ((), (), s32[]{:S(2)}) async-start(), calls=%async_computation.7 | async-start | bytes 9732096
  789.2 111.7 %collective-permute-start.61 = (bf16[4,2,64,768]{3,2,1,0:T(8,128)(2,1)}, bf16[4,2,64,768]{3,2,1,0:T(8,128)(2,1)}, u32[]{:S(2)}, u32[]{:S(2)}) collective-permute-start(bf16[4,2,64,768]{3,2,1,0:T(8,128)(2,1)} %dynamic-slice_bitcast_fusion.7), channel_id=1, source_target_pairs={{0,4},{4,0},{1,5},{5,1},{2,6},{6,2},{3,7},{7,3},{8,12},{12,8},{9,1... | collective-permute-start | bytes 2359304 | tf_op jit(solution)/shard_map/ppermute | solution.py:415
  797.2 108.1 %collective-permute-start.72 = (bf16[4,2,2,64,768]{4,3,0,2,1:T(8,128)(2,1)}, bf16[4,2,2,64,768]{4,3,0,2,1:T(8,128)(2,1)}, u32[]{:S(2)}, u32[]{:S(2)}) collective-permute-start(bf16[4,2,2,64,768]{4,3,0,2,1:T(8,128)(2,1)} %bitcast.518), channel_id=1, source_target_pairs={{0,2},{2,0},{1,3},{3,1},{4,6},{6,4},{5,7},{7,5},{8,10},{10,8},{9,1... | collective-permute-start | bytes 4718600 | tf_op jit(solution)/shard_map/ppermute | solution.py:415
  837.3 22.4 %collective-permute-start.63 = (bf16[2,256,768]{2,1,0:T(8,128)(2,1)}, bf16[2,256,768]{2,1,0:T(8,128)(2,1)}, u32[]{:S(2)}, u32[]{:S(2)}) collective-permute-start(bf16[2,256,768]{2,1,0:T(8,128)(2,1)} %get-tuple-element.188), channel_id=1, source_target_pairs={{0,2},{2,0},{1,3},{3,1},{4,6},{6,4},{5,7},{7,5},{8,10},{10,8},{9,1... | collective-permute-start | bytes 2359304 | tf_op jit(solution)/shard_map/ppermute | solution.py:415
  855.6 69.8 %collective-permute-start.70 = (bf16[4,2,2,24,3456]{4,3,2,1,0:T(8,128)(2,1)}, bf16[4,2,2,24,3456]{4,3,2,1,0:T(8,128)(2,1)}, u32[]{:S(2)}, u32[]{:S(2)}) collective-permute-start(bf16[4,2,2,24,3456]{4,3,2,1,0:T(8,128)(2,1)} %dynamic-slice_bitcast_fusion), channel_id=1, source_target_pairs={{0,2},{2,0},{1,3},{3,1},{4,6},{6,4},{5,7},{7,5},{8,10},{10,8},{9,1... | collective-permute-start | bytes 7962632 | tf_op jit(solution)/shard_map/ppermute | solution.py:415
  949.1 64.6 %collective-permute-start.75 = (bf16[4,2,24,3456]{3,2,1,0:T(8,128)(2,1)}, bf16[4,2,24,3456]{3,2,1,0:T(8,128)(2,1)}, u32[]{:S(2)}, u32[]{:S(2)}) collective-permute-start(bf16[4,2,24,3456]{3,2,1,0:T(8,128)(2,1)} %dynamic-slice_bitcast_fusion.2), channel_id=1, source_target_pairs={{0,1},{1,0},{2,3},{3,2},{4,5},{5,4},{6,7},{7,6},{8,9},{9,8},{10,11... | collective-permute-start | bytes 3981320 | tf_op jit(solution)/shard_map/ppermute | solution.py:415
  957.5 54.1 %collective-permute-start.76 = (bf16[4,2,24,1408]{3,2,1,0:T(8,128)(2,1)}, bf16[4,2,24,1408]{3,2,1,0:T(8,128)(2,1)}, u32[]{:S(2)}, u32[]{:S(2)}) collective-permute-start(bf16[4,2,24,1408]{3,2,1,0:T(8,128)(2,1)} %dynamic-slice_bitcast_fusion.11), channel_id=1, source_target_pairs={{0,4},{4,0},{1,5},{5,1},{2,6},{6,2},{3,7},{7,3},{8,12},{12,8},{9,1... | collective-permute-start | bytes 1622024 | tf_op jit(solution)/shard_map/ppermute | solution.py:415
  1025.1 32.1 %collective-permute-start.77 = (bf16[512,768]{1,0:T(8,128)(2,1)S(1)}, bf16[512,768]{1,0:T(8,128)(2,1)S(1)}, u32[]{:S(2)}, u32[]{:S(2)}) collective-permute-start(bf16[512,768]{1,0:T(8,128)(2,1)S(1)} %fusion.45.refs_1_), channel_id=1, source_target_pairs={{0,8},{8,16},{16,24},{1,9},{9,17},{17,25},{2,10},{10,18},{18,26},{... | collective-permute-start | bytes 2359304 | tf_op jit(solution)/shard_map/ppermute | solution.py:469
  1027.4 34.3 %collective-permute-start.78 = (bf16[512,768]{1,0:T(8,128)(2,1)S(1)}, bf16[512,768]{1,0:T(8,128)(2,1)S(1)}, u32[]{:S(2)}, u32[]{:S(2)}) collective-permute-start(bf16[512,768]{1,0:T(8,128)(2,1)S(1)} %fusion.45.refs_1_), channel_id=1, source_target_pairs={{8,0},{16,8},{24,16},{9,1},{17,9},{25,17},{10,2},{18,10},{26,18},{... | collective-permute-start | bytes 2359304 | tf_op jit(solution)/shard_map/ppermute | solution.py:470
  1033.3 56.5 %collective-permute-start.88 = (bf16[4,2,2,24,1280]{4,3,2,1,0:T(8,128)(2,1)S(1)}, bf16[4,2,2,24,1280]{4,3,2,1,0:T(8,128)(2,1)S(1)}, u32[]{:S(2)}, u32[]{:S(2)}) collective-permute-start(bf16[4,2,2,24,1280]{4,3,2,1,0:T(8,128)(2,1)S(1)} %dynamic-slice_bitcast_fusion.4), channel_id=1, source_target_pairs={{0,2},{2,0},{1,3},{3,1},{4,6},{6,4},{5,7},{7,5},{8,10},{10,8},{9,1... | collective-permute-start | bytes 2949128 | tf_op jit(solution)/shard_map/ppermute | solution.py:415
  1043.3 46.2 %collective-permute-start.87 = (bf16[4,2,2,24,1152]{4,3,2,1,0:T(8,128)(2,1)S(1)}, bf16[4,2,2,24,1152]{4,3,2,1,0:T(8,128)(2,1)S(1)}, u32[]{:S(2)}, u32[]{:S(2)}) collective-permute-start(bf16[4,2,2,24,1152]{4,3,2,1,0:T(8,128)(2,1)S(1)} %dynamic-slice_bitcast_fusion.5), channel_id=1, source_target_pairs={{0,2},{2,0},{1,3},{3,1},{4,6},{6,4},{5,7},{7,5},{8,10},{10,8},{9,1... | collective-permute-start | bytes 2654216 | tf_op jit(solution)/shard_map/ppermute | solution.py:415
  1057.2 26.5 %collective-permute-start.81 = (bf16[512,768]{1,0:T(8,128)(2,1)S(1)}, bf16[512,768]{1,0:T(8,128)(2,1)S(1)}, u32[]{:S(2)}, u32[]{:S(2)}) collective-permute-start(bf16[512,768]{1,0:T(8,128)(2,1)S(1)} %collective-permute-done.77), channel_id=1, source_target_pairs={{0,8},{8,16},{16,24},{1,9},{9,17},{17,25},{2,10},{10,18},{18,26},{... | collective-permute-start | bytes 2359304 | tf_op jit(solution)/shard_map/ppermute | solution.py:469
  1061.7 26.6 %collective-permute-start.79 = (bf16[512,768]{1,0:T(8,128)(2,1)S(1)}, bf16[512,768]{1,0:T(8,128)(2,1)S(1)}, u32[]{:S(2)}, u32[]{:S(2)}) collective-permute-start(bf16[512,768]{1,0:T(8,128)(2,1)S(1)} %collective-permute-done.78), channel_id=1, source_target_pairs={{8,0},{16,8},{24,16},{9,1},{17,9},{25,17},{10,2},{18,10},{26,18},{... | collective-permute-start | bytes 2359304 | tf_op jit(solution)/shard_map/ppermute | solution.py:470
  1134.9 65.0 %collective-permute-start.97 = (bf16[4032,768]{1,0:T(8,128)(2,1)}, bf16[4032,768]{1,0:T(8,128)(2,1)}, u32[]{:S(2)}, u32[]{:S(2)}) collective-permute-start(bf16[4032,768]{1,0:T(8,128)(2,1)} %shard_map.473), channel_id=1, source_target_pairs={{0,2},{2,0},{1,3},{3,1},{4,6},{6,4},{5,7},{7,5},{8,10},{10,8},{9,1... | collective-permute-start | bytes 18579464 | tf_op jit(solution)/shard_map/ppermute | solution.py:415
  1144.8 27.2 %collective-permute-start.92 = (bf16[24,4864]{1,0:T(8,128)(2,1)S(1)}, bf16[24,4864]{1,0:T(8,128)(2,1)S(1)}, u32[]{:S(2)}, u32[]{:S(2)}) collective-permute-start(bf16[24,4864]{1,0:T(8,128)(2,1)S(1)} %get-tuple-element.543), channel_id=1, source_target_pairs={{0,16},{8,24},{16,0},{24,8},{1,17},{9,25},{17,1},{25,9},{2,18},{10... | collective-permute-start | bytes 700424 | tf_op jit(solution)/shard_map/ppermute | solution.py:456
  1172.5 27.2 %collective-permute-start.98 = (bf16[4,24,1152]{2,1,0:T(8,128)(2,1)S(1)}, bf16[4,24,1152]{2,1,0:T(8,128)(2,1)S(1)}, u32[]{:S(2)}, u32[]{:S(2)}) collective-permute-start(bf16[4,24,1152]{2,1,0:T(8,128)(2,1)S(1)} %dynamic-slice_bitcast_fusion.28), channel_id=1, source_target_pairs={{0,4},{4,0},{1,5},{5,1},{2,6},{6,2},{3,7},{7,3},{8,12},{12,8},{9,1... | collective-permute-start | bytes 663560 | tf_op jit(solution)/shard_map/ppermute | solution.py:415
  1175.9 23.9 %collective-permute-start.99 = (bf16[4,24,1280]{2,1,0:T(8,128)(2,1)S(1)}, bf16[4,24,1280]{2,1,0:T(8,128)(2,1)S(1)}, u32[]{:S(2)}, u32[]{:S(2)}) collective-permute-start(bf16[4,24,1280]{2,1,0:T(8,128)(2,1)S(1)} %dynamic-slice_bitcast_fusion.24), channel_id=1, source_target_pairs={{0,1},{1,0},{2,3},{3,2},{4,5},{5,4},{6,7},{7,6},{8,9},{9,8},{10,11... | collective-permute-start | bytes 737288 | tf_op jit(solution)/shard_map/ppermute | solution.py:415
  1203.0 51.4 %collective-permute-start.106 = (bf16[24,2432]{1,0:T(8,128)(2,1)}, bf16[24,2432]{1,0:T(8,128)(2,1)}, u32[]{:S(2)}, u32[]{:S(2)}) collective-permute-start(bf16[24,2432]{1,0:T(8,128)(2,1)} %get-tuple-element.556), channel_id=1, source_target_pairs={{0,24},{8,0},{16,8},{24,16},{1,25},{9,1},{17,9},{25,17},{2,26},{10... | collective-permute-start | bytes 350216 | tf_op jit(solution)/shard_map/ppermute | solution.py:456
  1230.6 33.8 %collective-permute-start.101 = (bf16[1008,768]{1,0:T(8,128)(2,1)}, bf16[1008,768]{1,0:T(8,128)(2,1)}, u32[]{:S(2)}, u32[]{:S(2)}) collective-permute-start(bf16[1008,768]{1,0:T(8,128)(2,1)} %pad_maximum_fusion.4), channel_id=1, source_target_pairs={{0,1},{1,0},{2,3},{3,2},{4,5},{5,4},{6,7},{7,6},{8,9},{9,8},{10,11... | collective-permute-start | bytes 4644872 | tf_op jit(solution)/shard_map/ppermute | solution.py:415
  1233.0 33.8 %collective-permute-start.103 = (bf16[1008,768]{1,0:T(8,128)(2,1)}, bf16[1008,768]{1,0:T(8,128)(2,1)}, u32[]{:S(2)}, u32[]{:S(2)}) collective-permute-start(bf16[1008,768]{1,0:T(8,128)(2,1)} %pad_maximum_fusion.5), channel_id=1, source_target_pairs={{0,4},{4,0},{1,5},{5,1},{2,6},{6,2},{3,7},{7,3},{8,12},{12,8},{9,1... | collective-permute-start | bytes 4644872 | tf_op jit(solution)/shard_map/ppermute | solution.py:415
  (254 other events, 2710.1 us)
Sparse Core Ops, SparseCore 0:
  20.0 134.2 all-gather.4
  162.0 108.7 all-gather.6
  316.5 80.3 all-gather.8
  437.7 95.4 all-gather.10
  770.2 117.0 reduce-scatter.6
  936.7 144.9 reduce-scatter.8
